TPU v7x, 32 devices: a whole 2x2x4 slice. The times are simulated.
32 devices in a mesh: group: 2 (over x), seq: 16 (over z, y, core).
Axes of the slice: x: 2, y: 2, z: 4, core: 2. Of those that a mesh axis runs over, the one named last changes fastest.
Arguments:
- queries: bfloat16 [8192, 5120], P(('group', 'seq')), parts along dimension 0, may hold values from -30 to 30
- packed_keys: bfloat16 [8192, 5120], P(('group', 'seq')), parts along dimension 0, may hold values from -30 to 30
- packed_values: bfloat16 [8192, 5120], P(('group', 'seq')), parts along dimension 0, may hold values from -6 to 6
- clip_begin_position: int32 [8192], P(('group', 'seq')), parts along dimension 0, may hold values from 0 to 4095, as said below
- clip_stop_position: int32 [8192], P(('group', 'seq')), parts along dimension 0, may hold values from 1 to 4096
- adapter_down_factor: bfloat16 [5120, 128], P('seq'), may hold values from -6 to 6
- adapter_up_factor: bfloat16 [128, 5120], P(None, 'seq'), may hold values from -0.5 to 0.5
- frozen_projection: bfloat16 [5120, 5120], P('seq'), may hold values from -0.078125 to 0.078125
Outputs:
- attended: bfloat16 [8192, 5120], P(('group', 'seq')), parts along dimension 0
- merged_weight: bfloat16 [10240, 5120], P(('group', 'seq')), parts along dimension 0
There are 2 independent parts, one for each index of `group`. A program takes and returns all parts, laid end to end along the dimension named above; an argument that names none is the same for every part. Nothing has to cross between parts.
Inputs may be any that keep to these rules, and one draw needn't show every extreme that they name: Each token lies in the run of positions [clip_begin_position, clip_stop_position) of its clip; clips are consecutive and cover all 4096 positions; each clip is a whole number of frames of 64 positions, at most 2 frames, except that the last clip may be cut by the end of the pack; one clip holds exactly 128 positions.
All inputs are finite; a program needn't handle non-finite values.
Results may differ from a plain program's by a relative error of at most 0.012.
Values may be sent and summed in bfloat16 or wider, within the bound.
No kernel may reach another device: no remote copies, remote signals or barrier semaphores. Data moves between devices by JAX's collectives and lax.ppermute only.
A program may use at most 192 MiB of HBM per device.

v0:
```python
import jax
import jax.numpy as jnp
from jax import lax
from jax.sharding import PartitionSpec as P

MODEL_WIDTH = 5120
HEADS = 40
HD = 128


def extended(cells, sides, width):
    for axis, dim in sides:
        count = lax.axis_size(axis)
        ends = count - 1
        head = lax.slice_in_dim(cells, 0, width, axis=dim)
        tail = lax.slice_in_dim(cells, cells.shape[dim] - width, cells.shape[dim], axis=dim)
        cells = jnp.concatenate(
            [
                lax.ppermute(tail, axis, [(i, (i + 1) % count) for i in range(ends)]),
                cells,
                lax.ppermute(head, axis, [((i + 1) % count, i) for i in range(ends)]),
            ],
            axis=dim,
        )
    return cells


def attend(query_block, key_block, value_block, clip_lo, clip_hi, offset):
    query_rows = query_block.shape[0]
    key_count = key_block.shape[0]
    query_heads = query_block.reshape(query_rows, HEADS, HD)
    key_heads = key_block.reshape(key_count, HEADS, HD)
    value_heads = value_block.reshape(key_count, HEADS, HD)
    scores = jnp.einsum(
        "thd,shd->hts", query_heads, key_heads, preferred_element_type=jnp.float32
    ) * HD ** (-0.5)
    position = offset + jnp.arange(key_count, dtype=jnp.int32)
    allowed = (position[None, :] >= clip_lo[:, None]) & (position[None, :] < clip_hi[:, None])
    scores = jnp.where(allowed[None], scores, jnp.float32(-1e30))
    highest = jnp.max(scores, axis=-1, keepdims=True)
    weights = jnp.exp(scores - highest)
    denominator = jnp.sum(weights, axis=-1, keepdims=True)
    weights_bf = (weights / denominator).astype(jnp.bfloat16)
    mixed = jnp.einsum("hts,shd->thd", weights_bf, value_heads, preferred_element_type=jnp.float32)
    return mixed.reshape(query_rows, HEADS * HD).astype(jnp.bfloat16)


def body(
    queries,
    packed_keys,
    packed_values,
    clip_begin_position,
    clip_stop_position,
    adapter_down_factor,
    adapter_up_factor,
    frozen_projection,
):
    shard_rows = queries.shape[0]
    stacked = jnp.stack([packed_keys, packed_values])
    padded = extended(stacked, (("seq", 1),), shard_rows)
    offset = lax.axis_index("seq") * shard_rows - shard_rows
    clip_attention = attend(
        queries, padded[0], padded[1], clip_begin_position, clip_stop_position, offset
    )
    down_full, gathered_up_factor = (
        lax.all_gather(adapter_down_factor, "seq", axis=0, tiled=True),
        lax.all_gather(adapter_up_factor, "seq", axis=1, tiled=True),
    )
    adapter_scale = MODEL_WIDTH ** (-0.5)
    summed_partial = jnp.dot(clip_attention, down_full, preferred_element_type=jnp.float32).astype(
        jnp.bfloat16
    )
    weight_delta = jnp.dot(summed_partial, gathered_up_factor, preferred_element_type=jnp.float32)
    attended = (clip_attention.astype(jnp.float32) + adapter_scale * weight_delta).astype(
        jnp.bfloat16
    )
    factor_product = jnp.dot(
        adapter_down_factor, gathered_up_factor, preferred_element_type=jnp.float32
    )
    merged_weight = (frozen_projection.astype(jnp.float32) + adapter_scale * factor_product).astype(
        jnp.bfloat16
    )
    return (attended, merged_weight)


def solution(mesh):
    return jax.shard_map(
        body,
        mesh=mesh,
        in_specs=(
            P(("group", "seq"), None),
            P(("group", "seq"), None),
            P(("group", "seq"), None),
            P(("group", "seq")),
            P(("group", "seq")),
            P("seq", None),
            P(None, "seq"),
            P("seq", None),
        ),
        out_specs=(P(("group", "seq"), None), P(("group", "seq"), None)),
        check_vma=False,
    )
```

profile of v0, /device:TPU:1, one launch (start us, length us, event | category | flops | bytes accessed | tf_op | source)
XLA Modules:
  0.0 240.0 jit_solution(10811502397740273118)
XLA Ops:
  7.2 0.0 copy-start
  7.2 0.0 all-gather.5.cloned.1.call-start
  7.2 4.6 %copy.14 = bf16[256,5120]{0,1:T(8,128)(2,1)} copy(bf16[256,5120]{1,0:T(8,128)(2,1)} %param.9) | data formatting | bytes 5242880 | tf_op args[1]
  11.8 4.4 %copy.15 = bf16[256,5120]{0,1:T(8,128)(2,1)} copy(bf16[256,5120]{1,0:T(8,128)(2,1)} %param.10) | data formatting | bytes 5242880 | tf_op args[2]
  16.2 0.0 copy-start.5
  16.2 0.0 copy-start.6
  16.2 0.0 copy-start.4
  16.2 5.4 %pad_maximum_fusion.1 = bf16[2,256,5120]{1,2,0:T(8,128)(2,1)} fusion(bf16[1,256,5120]{1,2,0:T(8,128)(2,1)} %bitcast.35, bf16[1,256,5120]{1,2,0:T(8,128)(2,1)} %bitcast.33), kind=kLoop, calls=%fused_computation.16 | loop fusion | flops 2621440 | bytes 10485760 | tf_op jit(solution)/shard_map/stack | solution.py:59
  21.6 4.5 %collective-permute-start = (bf16[2,256,5120]{1,2,0:T(8,128)(2,1)}, bf16[2,256,5120]{1,2,0:T(8,128)(2,1)}, u32[]{:S(2)}, u32[]{:S(2)}) collective-permute-start(bf16[2,256,5120]{1,2,0:T(8,128)(2,1)} %pad_maximum_fusion.1), channel_id=1, source_target_pairs={{0,1},{1,2},{2,3},{3,4},{4,5},{5,6},{6,7},{7,8},{8,9},{9,10},{10,1... | collective-permute-start | bytes 15728648 | tf_op jit(solution)/shard_map/ppermute | solution.py:19
  26.1 2.1 collective-permute-start.1
  28.3 0.0 all-gather.5.cloned.1.call-update
  28.3 0.0 all-gather.3.cloned.1.call-start
  28.3 0.7 all-gather.3.cloned.1.call-update
  29.1 0.0 copy-done.5
  29.1 0.0 copy-done.6
  29.1 0.2 compare_and_fusion
  29.3 72.3 %all-gather.5.cloned.1.call-done = bf16[128,5120]{0,1:T(8,128)(2,1)} async-done(((bf16[128,320]{0,1:T(8,128)(2,1)}), bf16[128,5120]{0,1:T(8,128)(2,1)}) %all-gather.5.cloned.1.call-update) | async-done | bytes 1310736 | tf_op jit(solution)/shard_map/all_gather | solution.py:67
  101.6 0.0 copy-done.4
  101.6 0.0 copy-start.2
  101.7 0.0 copy-start.3
  101.7 5.2 %fusion.8 = bf16[320,5120]{1,0:T(8,128)(2,1)} fusion(bf16[320,128]{1,0:T(8,128)(2,1)S(1)} %copy-done.4, bf16[128,5120]{0,1:T(8,128)(2,1)} %all-gather.5.cloned.1.call-done, bf16[320,5120]{1,0:T(8,128)(2,1)} %param.15), kind=kOutput, calls=%fused_computation.14 | convolution fusion | flops 425984000 | bytes 7946240 | tf_op jit(solution)/shard_map/dot_general | solution.py:77
  106.8 41.2 %collective-permute-done = bf16[2,256,5120]{1,2,0:T(8,128)(2,1)} collective-permute-done((bf16[2,256,5120]{1,2,0:T(8,128)(2,1)}, bf16[2,256,5120]{1,2,0:T(8,128)(2,1)}, u32[]{:S(2)}, u32[]{:S(2)}) %collective-permute-start) | collective-permute-done | bytes 5242912 | tf_op jit(solution)/shard_map/ppermute | solution.py:19
  148.1 0.0 collective-permute-done.1
  148.1 0.0 copy-done.2
  148.1 0.0 copy-done.3
  148.1 6.4 %pad_maximum_fusion = bf16[2,768,5120]{1,2,0:T(8,128)(2,1)S(1)} fusion(bf16[2,256,5120]{1,2,0:T(8,128)(2,1)} %collective-permute-done.1, bf16[1,256,5120]{1,2,0:T(8,128)(2,1)S(1)} %bitcast.36, bf16[1,256,5120]{1,2,0:T(8,128)(2,1)S(1)} %bitcast.34, bf16[2,256,5120]{1,2,0:T(8,128)(2,1)} %collective-permute-done), kind=kLoop, calls=%fused_computation.5 | loop fusion | flops 62914560 | bytes 31457280 | tf_op jit(solution)/shard_map/concatenate | solution.py:17
  154.5 5.8 %fusion.16 = (bf16[1,768,5120]{1,2,0:T(8,128)(2,1)}, bf16[1,768,5120]{1,2,0:T(8,128)(2,1)}) fusion(bf16[2,768,5120]{1,2,0:T(8,128)(2,1)S(1)} %pad_maximum_fusion), kind=kLoop, calls=%fused_computation.26 | loop fusion | bytes 31457280 | tf_op jit(solution)/shard_map/slice | solution.py:63
  160.3 0.0 copy-done
  160.3 14.5 %fusion.10 = f32[40,768,256]{2,1,0:T(8,128)} fusion(bf16[768,40,128]{0,2,1:T(8,128)(2,1)} %bitcast.32, bf16[256,5120]{1,0:T(8,128)(2,1)S(1)} %copy-done), kind=kOutput, calls=%fused_computation.17 | convolution fusion | flops 2013265920 | bytes 41943040 | tf_op jit(solution)/shard_map/thd,shd->hts/dot_general | solution.py:34
  174.7 31.4 %fusion.17 = (f32[40,256]{1,0:T(8,128)S(1)}, f32[40,256,768]{1,2,0:T(8,128)}) fusion(f32[40,768,256]{2,1,0:T(8,128)} %fusion.10, pred[256,768]{0,1:T(8,128)(4,1)S(1)} %compare_and_fusion), kind=kOutput, calls=%fused_computation.27 | output fusion | flops 47186688 | bytes 63152128 | tf_op jit(solution)/shard_map/sub | solution.py:41
  206.1 16.1 %fusion.13 = bf16[40,128,256]{2,1,0:T(8,128)(2,1)} fusion(bf16[768,40,128]{0,2,1:T(8,128)(2,1)} %bitcast.39, f32[40,256,768]{1,2,0:T(8,128)} %get-tuple-element.5, f32[40,256]{1,0:T(8,128)S(1)} %get-tuple-element.4), kind=kOutput, calls=%fused_computation.20 | convolution fusion | flops 2030305280 | bytes 41984000 | tf_op jit(solution)/shard_map/hts,shd->thd/dot_general | solution.py:44
  222.2 0.0 copy-start.1
  222.2 4.5 %copy.19 = bf16[256,5120]{1,0:T(8,128)(2,1)} copy(bf16[256,5120]{0,1:T(8,128)(2,1)} %bitcast.37) | data formatting | bytes 5242880 | tf_op jit(solution)/shard_map/convert_element_type | solution.py:45
  226.7 0.0 all-gather.3.cloned.1.call-done
  226.7 6.5 %fusion.9 = bf16[256,5120]{1,0:T(8,128)(2,1)} fusion(bf16[128,5120]{0,1:T(8,128)(2,1)} %all-gather.5.cloned.1.call-done, bf16[256,5120]{1,0:T(8,128)(2,1)} %copy.19, bf16[256,5120]{0,1:T(8,128)(2,1)} %bitcast.38, bf16[5120,128]{1,0:T(8,128)(2,1)} %all-gather.3.cloned.1.call-done), kind=kOutput, calls=%fused_computation.15 | convolution fusion | flops 676364288 | bytes 10485760 | tf_op jit(solution)/shard_map/dot_general | solution.py:73
  233.2 0.0 copy-done.1
  (1 shorter events, 0.0 us)
Async XLA Ops:
  7.2 153.1 %copy-start = (bf16[256,5120]{1,0:T(8,128)(2,1)S(1)}, bf16[256,5120]{1,0:T(8,128)(2,1)}, u32[]{:S(2)}) copy-start(bf16[256,5120]{1,0:T(8,128)(2,1)} %param.8) | copy-start | bytes 7864324
  7.2 94.5 %all-gather.5.cloned.1.call-start = ((), (), s32[]{:S(2)}) async-start(), calls=%async_computation.1 | async-start | bytes 1392640 | tf_op jit(solution)/shard_map/all_gather | solution.py:67
  16.2 12.9 %copy-start.5 = (s32[256]{0:T(256)S(1)}, s32[256]{0:T(256)}, u32[]{:S(2)}) copy-start(s32[256]{0:T(256)} %param.12) | copy-start | bytes 3076
  16.2 12.9 %copy-start.6 = (s32[256]{0:T(256)S(1)}, s32[256]{0:T(256)}, u32[]{:S(2)}) copy-start(s32[256]{0:T(256)} %param.11) | copy-start | bytes 3076
  16.2 85.5 %copy-start.4 = (bf16[320,128]{1,0:T(8,128)(2,1)S(1)}, bf16[320,128]{1,0:T(8,128)(2,1)}, u32[]{:S(2)}) copy-start(bf16[320,128]{1,0:T(8,128)(2,1)} %param.13) | copy-start | bytes 245764
  21.6 126.5 %collective-permute-start = (bf16[2,256,5120]{1,2,0:T(8,128)(2,1)}, bf16[2,256,5120]{1,2,0:T(8,128)(2,1)}, u32[]{:S(2)}, u32[]{:S(2)}) collective-permute-start(bf16[2,256,5120]{1,2,0:T(8,128)(2,1)} %pad_maximum_fusion.1), channel_id=1, source_target_pairs={{0,1},{1,2},{2,3},{3,4},{4,5},{5,6},{6,7},{7,8},{8,9},{9,10},{10,1... | collective-permute-start | bytes 15728648 | tf_op jit(solution)/shard_map/ppermute | solution.py:19
  26.1 121.9 %collective-permute-start.1 = (bf16[2,256,5120]{1,2,0:T(8,128)(2,1)}, bf16[2,256,5120]{1,2,0:T(8,128)(2,1)}, u32[]{:S(2)}, u32[]{:S(2)}) collective-permute-start(bf16[2,256,5120]{1,2,0:T(8,128)(2,1)} %pad_maximum_fusion.1), channel_id=1, source_target_pairs={{1,0},{2,1},{3,2},{4,3},{5,4},{6,5},{7,6},{8,7},{9,8},{10,9},{11,1... | collective-permute-start | bytes 15728648 | tf_op jit(solution)/shard_map/ppermute | solution.py:21
  28.3 198.4 %all-gather.3.cloned.1.call-start = ((), (), s32[]{:S(2)}) async-start(), calls=%async_computation | async-start | bytes 1392640 | tf_op jit(solution)/shard_map/all_gather | solution.py:66
  101.6 46.4 %copy-start.2 = (bf16[256,5120]{0,1:T(8,128)(2,1)S(1)}, bf16[256,5120]{0,1:T(8,128)(2,1)}, u32[]{:S(2)}) copy-start(bf16[256,5120]{0,1:T(8,128)(2,1)} %copy.14) | copy-start | bytes 7864324
  101.7 46.4 %copy-start.3 = (bf16[256,5120]{0,1:T(8,128)(2,1)S(1)}, bf16[256,5120]{0,1:T(8,128)(2,1)}, u32[]{:S(2)}) copy-start(bf16[256,5120]{0,1:T(8,128)(2,1)} %copy.15) | copy-start | bytes 7864324
  222.2 11.0 %copy-start.1 = (bf16[256,5120]{1,0:T(8,128)(2,1)S(1)}, bf16[256,5120]{1,0:T(8,128)(2,1)}, u32[]{:S(2)}) copy-start(bf16[256,5120]{1,0:T(8,128)(2,1)} %param.8) | copy-start | bytes 7864324
Sparse Core Ops, SparseCore 0:
  28.4 73.1 all-gather.4
  103.9 41.8 all-gather.2
where the time goes:
time: 241 us; the launch traced here: 240 us
  waiting for transfers between devices  114 us (47%)
  other arithmetic  43.4 us (18%)
  matrix products  42.2 us (18%)
  local copies, waits for them, and re-layouts  19.3 us (8%)
  between operations  14.1 us (6%)
  starting transfers between devices  6.72 us (3%)
    all_gather x1, waiting for transfers between devices, body(): lax.all_gather(adapter_up_factor, 'seq', axis=1, tiled=True)  72.3 us
    ppermute x1, waiting for transfers between devices, extended(): lax.ppermute(tail, axis, [(i, (i + 1) % count) for i in range(ends)])  41.2 us
    sub x1, other arithmetic, attend(): weights = jnp.exp(scores - highest)  31.4 us
    dot_general x1, matrix products, attend(): jnp.einsum('hts,shd->thd', weights_bf, value_heads, preferred_element_typ...  16.1 us
    dot_general x1, matrix products, attend(): jnp.einsum('thd,shd->hts', query_heads, key_heads, preferred_element_type...  14.5 us
    unnamed x16, local copies, waits for them, and re-layouts  8.99 us
    dot_general x1, matrix products, body(): jnp.dot(summed_partial, gathered_up_factor, preferred_element_type=jnp.fl...  6.48 us
    concatenate x1, other arithmetic, extended(): jnp.concatenate([lax.ppermute(tail, axis, [(i, (i + 1) % count) for i in...  6.39 us
  transfers between devices with their start and end apart: 4, of which 2 were waited for; matrix products, arithmetic and copies ran while one was open for 35% of the time, Pallas kernels for 0%

commit v1 on v0

v1 whole, which is shorter than its diff:
```python
import functools

import jax
import jax.numpy as jnp
from jax import lax
from jax.experimental import pallas as pl
from jax.experimental.pallas import tpu as pltpu
from jax.sharding import PartitionSpec as P

MODEL_WIDTH = 5120
HEADS = 40
HD = 128
FRAME = 64
CHUNK = 512
SCORE_SCALE = HD ** (-0.5) * 1.4426950408889634
ADAPTER_SCALE = MODEL_WIDTH ** (-0.5)
FAR = -1e30
NT = (((1,), (1,)), ((), ()))
NN = (((1,), (0,)), ((), ()))


def dot(a, b, dims):
    return lax.dot_general(a, b, dims, preferred_element_type=jnp.float32)


def softmax_mix(q, k, v, bias):
    scores = dot(q, k, NT) * SCORE_SCALE + bias
    weights = jnp.exp2(scores - jnp.max(scores, axis=-1, keepdims=True))
    total = jnp.sum(weights, axis=-1, keepdims=True)
    mixed = dot(weights.astype(jnp.bfloat16), v, NN)
    return (mixed * (1.0 / total)).astype(jnp.bfloat16)


def frame_bias(lo, hi, first, keys):
    position = first + lax.broadcasted_iota(jnp.int32, (FRAME, keys), 1)
    return jnp.where((position >= lo) & (position < hi), 0.0, FAR).astype(jnp.float32)


def local_kernel(lo_ref, hi_ref, q_ref, k_ref, v_ref, o_ref, bias_ref):
    rows = q_ref.shape[0]
    base = lax.axis_index("seq") * rows

    @pl.when(pl.program_id(0) == 0)
    def _():
        for at in range(0, rows, FRAME):
            bias_ref[at : at + FRAME, :] = frame_bias(lo_ref[at], hi_ref[at], base, rows)

    for col in range(0, CHUNK, HD):
        part = slice(col, col + HD)
        o_ref[:, part] = softmax_mix(q_ref[:, part], k_ref[:, part], v_ref[:, part], bias_ref[...])


def local_attention(lo, hi, q, k, v):
    rows, width = q.shape
    smem = pl.BlockSpec(memory_space=pltpu.SMEM)
    block = pl.BlockSpec((rows, CHUNK), lambda i: (0, i))
    return pl.pallas_call(
        local_kernel,
        grid=(width // CHUNK,),
        out_shape=jax.ShapeDtypeStruct((rows, width), jnp.bfloat16),
        in_specs=[smem, smem, block, block, block],
        out_specs=block,
        scratch_shapes=[pltpu.VMEM((rows, rows), jnp.float32)],
        compiler_params=pltpu.CompilerParams(vmem_limit_bytes=16 << 20),
        cost_estimate=pl.CostEstimate(
            flops=4 * rows * rows * width,
            bytes_accessed=8 * rows * width,
            transcendentals=rows * rows * HEADS,
        ),
        name="local_attention",
    )(lo, hi, q, k, v)


def piece_copies(pieces, half, shard, whole, sems):
    me = lax.axis_index("seq")
    copies = []
    for mask, ref, where in pieces:
        source = ref.at[where] if where is not None else ref
        start = pl.multiple_of((me ^ mask) * shard, shard)
        copies.append(
            pltpu.make_async_copy(
                source.at[pl.ds(half * shard, shard)],
                whole.at[pl.ds(start, shard)],
                sems.at[len(copies)],
            )
        )
    return copies


def merge_kernel(layout, shard, frozen_ref, down_ref, *rest):
    refs = rest[: len(rest) - 3]
    out_ref, up_ref, sems = rest[len(rest) - 3 :]

    @pl.when(pl.program_id(0) == 0)
    def _():
        pieces = [(mask, refs[i], where) for mask, i, where in layout]
        copies = piece_copies(pieces, 1, shard, up_ref, sems)
        for copy in copies:
            copy.start()
        for copy in copies:
            copy.wait()

    first = pl.multiple_of(pl.program_id(0) * CHUNK, CHUNK)
    product = dot(down_ref[...], up_ref[pl.ds(first, CHUNK), :], NT)
    out_ref[...] = (frozen_ref[...].astype(jnp.float32) + ADAPTER_SCALE * product).astype(
        jnp.bfloat16
    )


def merge(frozen, down, layout, pieces):
    shard, width = frozen.shape
    rank = down.shape[1]
    block = pl.BlockSpec((shard, CHUNK), lambda i: (0, i))
    return pl.pallas_call(
        functools.partial(merge_kernel, layout, shard),
        grid=(width // CHUNK,),
        out_shape=jax.ShapeDtypeStruct((shard, width), jnp.bfloat16),
        in_specs=[block, pl.BlockSpec((shard, rank), lambda i: (0, 0))]
        + [pl.BlockSpec(memory_space=pl.ANY)] * len(pieces),
        out_specs=block,
        scratch_shapes=[
            pltpu.VMEM((width, rank), jnp.bfloat16),
            pltpu.SemaphoreType.DMA((len(layout),)),
        ],
        compiler_params=pltpu.CompilerParams(vmem_limit_bytes=16 << 20),
        cost_estimate=pl.CostEstimate(
            flops=2 * shard * width * rank,
            bytes_accessed=4 * shard * width + 2 * width * rank,
            transcendentals=0,
        ),
        name="merge_weight",
    )(frozen, down, *pieces)


def final_kernel(layout, shard, lo_ref, hi_ref, q, k, v, att, k_left, v_left, k_right, v_right, *rest):
    refs = rest[: len(rest) - 11]
    (
        out,
        q_edge,
        k_edge,
        v_edge,
        mixed,
        result,
        down,
        up,
        reduced,
        piece_sems,
        sems,
    ) = rest[len(rest) - 11 :]
    rows, width = q.shape
    near = 2 * FRAME
    base = lax.axis_index("seq") * rows
    pieces = [(mask, refs[i], where) for mask, i, where in layout]

    def local(source, target, i):
        return pltpu.make_async_copy(source, target, sems.at[i])

    head, tail = pl.ds(0, FRAME), pl.ds(rows - FRAME, FRAME)
    front, back = pl.ds(0, near), pl.ds(rows - near, near)
    edges = [
        local(q.at[head], q_edge.at[0], 0),
        local(q.at[tail], q_edge.at[1], 1),
        local(k_left, k_edge.at[0, pl.ds(0, FRAME)], 2),
        local(k.at[front], k_edge.at[0, pl.ds(FRAME, near)], 3),
        local(k.at[back], k_edge.at[1, pl.ds(0, near)], 4),
        local(k_right, k_edge.at[1, pl.ds(near, FRAME)], 5),
        local(v_left, v_edge.at[0, pl.ds(0, FRAME)], 6),
        local(v.at[front], v_edge.at[0, pl.ds(FRAME, near)], 7),
        local(v.at[back], v_edge.at[1, pl.ds(0, near)], 8),
        local(v_right, v_edge.at[1, pl.ds(near, FRAME)], 9),
        local(att.at[pl.ds(FRAME, rows - near)], mixed.at[pl.ds(FRAME, rows - near)], 10),
    ]
    downs = piece_copies(pieces, 0, shard, down, piece_sems.at[0])
    ups = piece_copies(pieces, 1, shard, up, piece_sems.at[1])
    for copy in edges + downs + ups:
        copy.start()
    bias = [
        frame_bias(lo_ref[0], hi_ref[0], base - FRAME, near + FRAME),
        frame_bias(lo_ref[rows - FRAME], hi_ref[rows - FRAME], base + rows - near, near + FRAME),
    ]
    reduced[...] = jnp.zeros_like(reduced)
    for copy in edges + downs:
        copy.wait()

    def attend(step, _):
        for col in range(0, CHUNK, HD):
            part = pl.ds(pl.multiple_of(step * CHUNK + col, HD), HD)
            for e, row in ((0, 0), (1, rows - FRAME)):
                mixed[row : row + FRAME, part] = softmax_mix(
                    q_edge[e, :, part], k_edge[e, :, part], v_edge[e, :, part], bias[e]
                )
        wide = pl.ds(pl.multiple_of(step * CHUNK, CHUNK), CHUNK)
        reduced[...] += dot(mixed[:, wide], down[wide, :], NN)
        return 0

    steps = width // CHUNK
    lax.fori_loop(0, steps, attend, 0)
    for copy in ups:
        copy.wait()
    narrow = reduced[...].astype(jnp.bfloat16)
    stores = []
    for step in range(steps):
        wide = pl.ds(step * CHUNK, CHUNK)
        delta = dot(narrow, up[wide, :], NT)
        result[:, wide] = (mixed[:, wide].astype(jnp.float32) + ADAPTER_SCALE * delta).astype(
            jnp.bfloat16
        )
        store = local(result.at[:, wide], out.at[:, wide], 11 + step)
        store.start()
        stores.append(store)
    for store in stores:
        store.wait()


def final(lo, hi, q, k, v, att, halos, layout, pieces, shard):
    rows, width = q.shape
    rank = pieces[0].shape[-1]
    any_spec = pl.BlockSpec(memory_space=pl.ANY)
    smem = pl.BlockSpec(memory_space=pltpu.SMEM)
    window = 3 * FRAME
    bf16 = jnp.bfloat16
    return pl.pallas_call(
        functools.partial(final_kernel, layout, shard),
        out_shape=jax.ShapeDtypeStruct((rows, width), bf16),
        in_specs=[smem, smem] + [any_spec] * (8 + len(pieces)),
        out_specs=any_spec,
        scratch_shapes=[
            pltpu.VMEM((2, FRAME, width), bf16),
            pltpu.VMEM((2, window, width), bf16),
            pltpu.VMEM((2, window, width), bf16),
            pltpu.VMEM((rows, width), bf16),
            pltpu.VMEM((rows, width), bf16),
            pltpu.VMEM((width, rank), bf16),
            pltpu.VMEM((width, rank), bf16),
            pltpu.VMEM((rows, rank), jnp.float32),
            pltpu.SemaphoreType.DMA((2, len(layout))),
            pltpu.SemaphoreType.DMA((11 + width // CHUNK,)),
        ],
        compiler_params=pltpu.CompilerParams(vmem_limit_bytes=32 << 20),
        cost_estimate=pl.CostEstimate(
            flops=4 * rows * width * rank + 8 * FRAME * window * width,
            bytes_accessed=14 * rows * width,
            transcendentals=2 * FRAME * window * HEADS,
        ),
        name="edge_attention_adapter",
    )(lo, hi, q, k, v, att, *halos, *pieces)


def gather_pieces(own, axis):
    count = lax.axis_size(axis)
    if own.shape[0] % 32:
        full = lax.all_gather(own, axis, axis=0)
        me = lax.axis_index(axis)
        order = jnp.arange(count, dtype=jnp.int32) ^ me
        return [(mask, 0, mask) for mask in range(count)], [full[order]]

    def swap(cells, mask):
        return lax.ppermute(cells, axis, [(i, i ^ mask) for i in range(count)])

    groups = []
    bit = count
    while bit > 4:
        low = max(bit // 4, 4)
        groups.append([low * j for j in range(1, bit // low)])
        bit = low
    while bit > 1:
        bit //= 2
        groups.append([bit])
    cells, masks = own[None], [0]
    for group in groups[:-1]:
        cells = jnp.concatenate([cells] + [swap(cells, mask) for mask in group])
        masks = masks + [have ^ mask for mask in group for have in masks]
    last = groups[-1][0]
    far = swap(cells, last)
    layout = [(mask, 0, i) for i, mask in enumerate(masks)]
    layout += [(mask ^ last, 1, i) for i, mask in enumerate(masks)]
    return layout, [cells, far]


def body(q, k, v, lo, hi, down, up, frozen):
    shard = down.shape[0]
    count = lax.axis_size("seq")
    layout, pieces = gather_pieces(jnp.concatenate([down, up.T]), "seq")
    forward = [(i, i + 1) for i in range(count - 1)]
    backward = [(i + 1, i) for i in range(count - 1)]
    rows = q.shape[0]
    k_left = lax.ppermute(k[rows - FRAME :], "seq", forward)
    v_left = lax.ppermute(v[rows - FRAME :], "seq", forward)
    k_right = lax.ppermute(k[:FRAME], "seq", backward)
    v_right = lax.ppermute(v[:FRAME], "seq", backward)
    att = local_attention(lo, hi, q, k, v)
    merged = merge(frozen, down, layout, pieces)
    attended = final(
        lo, hi, q, k, v, att, (k_left, v_left, k_right, v_right), layout, pieces, shard
    )
    return (attended, merged)


def solution(mesh):
    rows = P(("group", "seq"), None)
    flat = P(("group", "seq"))
    return jax.shard_map(
        body,
        mesh=mesh,
        in_specs=(rows, rows, rows, flat, flat, P("seq", None), P(None, "seq"), P("seq", None)),
        out_specs=(rows, rows),
        check_vma=False,
    )
```

time: 241 us -> 101 us (0.42)
  waiting for transfers between devices: 114 us -> 25.3 us
  Pallas kernels: 0 us -> 48.9 us
  other arithmetic: 43.4 us -> 1.04 us
  matrix products: 42.2 us -> 0 us
  local copies, waits for them, and re-layouts: 19.3 us -> 1.8 us
  starting transfers between devices: 6.72 us -> 22 us
  between operations: 14.1 us -> 0.87 us
    all_gather x2 -> x0, waiting for transfers between devices: 72.3 us -> none  [the longest x1 72.3 us: body(): lax.all_gather(adapter_up_factor, 'seq', axis=1, tiled=True)]
    pallas_call x0 -> x3, Pallas kernels: none -> 48.9 us  [the longest x1 31.9 us: final(): pl.pallas_call(functools.partial(final_kernel, layout, shard), out_shape=...]
    dot_general x4 -> x0, matrix products: 42.2 us -> none  [the longest x1 16.1 us: attend(): jnp.einsum('hts,shd->thd', weights_bf, value_heads, preferred_element_typ...]
    sub x1 -> x0, other arithmetic: 31.4 us -> none  [attend(): weights = jnp.exp(scores - highest)]
    ppermute x2 -> x9, waiting for transfers between devices: 41.2 us -> 25.3 us  [the longest x5 25.3 us: swap(): return lax.ppermute(cells, axis, [(i, i ^ mask) for i in range(count)])]
    ppermute x2 -> x9, starting transfers between devices: 6.65 us -> 22 us  [the longest x5 10.1 us: swap(): return lax.ppermute(cells, axis, [(i, i ^ mask) for i in range(count)])]
    unnamed x16 -> x19, local copies, waits for them, and re-layouts: 8.99 us -> 0.11 us
    concatenate x1, other arithmetic: 6.39 us -> 0.08 us  [gather_pieces(): cells = jnp.concatenate([cells] + [swap(cells, mask) for mask in group])]
  transfers between devices with their start and end apart: 4 -> 9, of which waited for: 2 -> 3; matrix products, arithmetic and copies ran while one was open for 35% -> 2% of each run, Pallas kernels for 0% -> 17%
where the time goes in v1:
time: 101 us; the launch traced here: 99.9 us
  Pallas kernels  48.9 us (48%)
  waiting for transfers between devices  25.3 us (25%)
  starting transfers between devices  22 us (22%)
  local copies, waits for them, and re-layouts  1.8 us (2%)
  other arithmetic  1.04 us (1%)
    pallas_call x1, Pallas kernels, final(): pl.pallas_call(functools.partial(final_kernel, layout, shard), out_shape=...  31.9 us
    ppermute x5, waiting for transfers between devices, swap(): return lax.ppermute(cells, axis, [(i, i ^ mask) for i in range(count)])  25.3 us
    ppermute x5, starting transfers between devices, swap(): return lax.ppermute(cells, axis, [(i, i ^ mask) for i in range(count)])  10.1 us
    pallas_call x1, Pallas kernels, local_attention(): pl.pallas_call(local_kernel, grid=(width // CHUNK,), out_shape=jax.ShapeD...  9.81 us
    pallas_call x1, Pallas kernels, merge(): pl.pallas_call(functools.partial(merge_kernel, layout, shard), grid=(widt...  7.26 us
    ppermute x1, starting transfers between devices, body(): v_left = lax.ppermute(v[rows - FRAME:], 'seq', forward)  4.01 us
    ppermute x1, starting transfers between devices, body(): k_right = lax.ppermute(k[:FRAME], 'seq', backward)  3.55 us
    ppermute x1, starting transfers between devices, body(): k_left = lax.ppermute(k[rows - FRAME:], 'seq', forward)  2.3 us
  transfers between devices with their start and end apart: 9, of which 3 were waited for; matrix products, arithmetic and copies ran while one was open for 2% of the time, Pallas kernels for 17%

profile of v1, /device:TPU:1, one launch (start us, length us, event | category | flops | bytes accessed | tf_op | source)
XLA Modules:
  0.0 99.9 jit_solution(7132990913528303081)
XLA Ops:
  0.6 0.9 maximum_bitcast_fusion
  1.6 4.2 %collective-permute-start.6 = (bf16[1,640,128]{2,1,0:T(8,128)(2,1)S(1)}, bf16[1,640,128]{2,1,0:T(8,128)(2,1)S(1)}, u32[]{:S(2)}, u32[]{:S(2)}) collective-permute-start(bf16[1,640,128]{2,1,0:T(8,128)(2,1)S(1)} %maximum_bitcast_fusion), channel_id=1, source_target_pairs={{0,12},{1,13},{2,14},{3,15},{4,8},{5,9},{6,10},{7,11},{8,4},{9,5},... | collective-permute-start | bytes 491528 | tf_op jit(solution)/shard_map/ppermute | solution.py:258
  5.8 0.0 collective-permute-start.5
  5.8 0.4 collective-permute-start.4
  6.2 3.6 %collective-permute-done.6 = bf16[1,640,128]{2,1,0:T(8,128)(2,1)S(1)} collective-permute-done((bf16[1,640,128]{2,1,0:T(8,128)(2,1)S(1)}, bf16[1,640,128]{2,1,0:T(8,128)(2,1)S(1)}, u32[]{:S(2)}, u32[]{:S(2)}) %collective-permute-start.6) | collective-permute-done | bytes 163872 | tf_op jit(solution)/shard_map/ppermute | solution.py:258
  9.8 9.5 %collective-permute-done.5 = bf16[1,640,128]{2,1,0:T(8,128)(2,1)S(1)} collective-permute-done((bf16[1,640,128]{2,1,0:T(8,128)(2,1)S(1)}, bf16[1,640,128]{2,1,0:T(8,128)(2,1)S(1)}, u32[]{:S(2)}, u32[]{:S(2)}) %collective-permute-start.5) | collective-permute-done | bytes 163872 | tf_op jit(solution)/shard_map/ppermute | solution.py:258
  19.3 0.0 collective-permute-done.4
  19.3 0.0 copy-start.4
  19.3 0.0 copy-start.7
  19.3 0.1 pad_maximum_fusion
  19.4 1.3 %collective-permute-start.7 = (bf16[4,640,128]{2,1,0:T(8,128)(2,1)S(1)}, bf16[4,640,128]{2,1,0:T(8,128)(2,1)S(1)}, u32[]{:S(2)}, u32[]{:S(2)}) collective-permute-start(bf16[4,640,128]{2,1,0:T(8,128)(2,1)S(1)} %pad_maximum_fusion), channel_id=1, source_target_pairs={{0,2},{1,3},{2,0},{3,1},{4,6},{5,7},{6,4},{7,5},{8,10},{9,11},{10,... | collective-permute-start | bytes 1966088 | tf_op jit(solution)/shard_map/ppermute | solution.py:258
  20.7 0.0 copy-start.2
  20.7 1.5 %fusion.1 = (bf16[64,5120]{1,0:T(8,128)(2,1)S(1)}, bf16[64,5120]{1,0:T(8,128)(2,1)S(1)}) fusion(bf16[256,5120]{1,0:T(8,128)(2,1)} %k.1), kind=kLoop, calls=%fused_computation.8 | loop fusion | bytes 2621440 | tf_op jit(solution)/shard_map/slice | solution.py:289
  22.2 3.5 %collective-permute-start.2 = (bf16[64,5120]{1,0:T(8,128)(2,1)S(1)}, bf16[64,5120]{1,0:T(8,128)(2,1)S(1)}, u32[]{:S(2)}, u32[]{:S(2)}) collective-permute-start(bf16[64,5120]{1,0:T(8,128)(2,1)S(1)} %get-tuple-element.4), channel_id=1, source_target_pairs={{1,0},{2,1},{3,2},{4,3},{5,4},{6,5},{7,6},{8,7},{9,8},{10,9},{11,1... | collective-permute-start | bytes 1966088 | tf_op jit(solution)/shard_map/ppermute | solution.py:289
  25.8 0.0 copy-start.1
  25.8 2.3 %collective-permute-start = (bf16[64,5120]{1,0:T(8,128)(2,1)S(1)}, bf16[64,5120]{1,0:T(8,128)(2,1)S(1)}, u32[]{:S(2)}, u32[]{:S(2)}) collective-permute-start(bf16[64,5120]{1,0:T(8,128)(2,1)S(1)} %get-tuple-element.5), channel_id=1, source_target_pairs={{0,1},{1,2},{2,3},{3,4},{4,5},{5,6},{6,7},{7,8},{8,9},{9,10},{10,1... | collective-permute-start | bytes 1966088 | tf_op jit(solution)/shard_map/ppermute | solution.py:287
  28.1 0.0 copy-done.4
  28.1 0.0 copy-done.7
  28.2 12.2 %collective-permute-done.7 = bf16[4,640,128]{2,1,0:T(8,128)(2,1)S(1)} collective-permute-done((bf16[4,640,128]{2,1,0:T(8,128)(2,1)S(1)}, bf16[4,640,128]{2,1,0:T(8,128)(2,1)S(1)}, u32[]{:S(2)}, u32[]{:S(2)}) %collective-permute-start.7) | collective-permute-done | bytes 655392 | tf_op jit(solution)/shard_map/ppermute | solution.py:258
  40.4 0.1 constant_dynamic-update-slice_fusion.rest_0_
  40.4 0.0 copy-start
  40.5 0.0 copy-start.5
  40.5 0.0 copy-start.6
  40.5 4.2 %collective-permute-start.8 = (bf16[8,640,128]{2,1,0:T(8,128)(2,1)S(1)}, bf16[8,640,128]{2,1,0:T(8,128)(2,1)S(1)}, u32[]{:S(2)}, u32[]{:S(2)}) collective-permute-start(bf16[8,640,128]{2,1,0:T(8,128)(2,1)S(1)} %constant_dynamic-update-slice_fusion.rest_0_), channel_id=1, source_target_pairs={{0,1},{1,0},{2,3},{3,2},{4,5},{5,4},{6,7},{7,6},{8,9},{9,8},{10,11... | collective-permute-start | bytes 3932168 | tf_op jit(solution)/shard_map/ppermute | solution.py:258
  44.7 0.0 copy-done.1
  44.7 0.1 fusion
  44.8 2.1 %collective-permute-start.3 = (bf16[64,5120]{1,0:T(8,128)(2,1)S(1)}, bf16[64,5120]{1,0:T(8,128)(2,1)S(1)}, u32[]{:S(2)}, u32[]{:S(2)}) collective-permute-start(bf16[64,5120]{1,0:T(8,128)(2,1)S(1)} %get-tuple-element.2), channel_id=1, source_target_pairs={{1,0},{2,1},{3,2},{4,3},{5,4},{6,5},{7,6},{8,7},{9,8},{10,9},{11,1... | collective-permute-start | bytes 1966088 | tf_op jit(solution)/shard_map/ppermute | solution.py:290
  46.9 4.0 %collective-permute-start.1 = (bf16[64,5120]{1,0:T(8,128)(2,1)S(1)}, bf16[64,5120]{1,0:T(8,128)(2,1)S(1)}, u32[]{:S(2)}, u32[]{:S(2)}) collective-permute-start(bf16[64,5120]{1,0:T(8,128)(2,1)S(1)} %get-tuple-element.3), channel_id=1, source_target_pairs={{0,1},{1,2},{2,3},{3,4},{4,5},{5,6},{6,7},{7,8},{8,9},{9,10},{10,1... | collective-permute-start | bytes 1966088 | tf_op jit(solution)/shard_map/ppermute | solution.py:288
  50.9 0.0 copy-done.2
  50.9 0.0 copy-done
  50.9 0.0 copy-done.5
  50.9 0.0 copy-done.6
  50.9 0.0 copy-start.3
  50.9 9.8 %local_attention.1.att = bf16[256,5120]{1,0:T(8,128)(2,1)S(1)} custom-call(s32[256]{0:T(256)S(1)} %copy-done.5, s32[256]{0:T(256)S(1)} %copy-done.6, bf16[256,5120]{1,0:T(8,128)(2,1)S(1)} %copy-done.2, bf16[256,5120]{1,0:T(8,128)(2,1)S(1)} %copy-done, bf16[256,5120]{1,0:T(8,128)(2,1)S(1)} %copy-done.1), custom_call_target="tpu_custom_call" | custom-call | flops 1342177280 | bytes 10485760 | tf_op jit(solution)/shard_map/local_attention/pallas_call | solution.py:57
  60.8 0.0 collective-permute-done.8.rest_1_
  60.8 0.0 copy-done.3
  60.8 7.3 %merge_weight.1 = bf16[320,5120]{1,0:T(8,128)(2,1)} custom-call(bf16[320,5120]{1,0:T(8,128)(2,1)S(1)} %copy-done.3, bf16[320,128]{1,0:T(8,128)(2,1)S(1)} %copy-done.4, bf16[8,640,128]{2,1,0:T(8,128)(2,1)S(1)} %constant_dynamic-update-slice_fusion.rest_0_, bf16[8,640,128]{2,1,0:T(8,128)(2,1)S(1)} %collective-permute-done.8.rest_1_), custom_call_target="tpu_custom_call" | custom-call | flops 419430400 | bytes 7864320 | tf_op jit(solution)/shard_map/merge_weight/pallas_call | solution.py:114
  68.0 0.0 collective-permute-done.2.k_right
  68.1 0.0 collective-permute-done.k_left
  68.1 0.0 collective-permute-done.3.v_right
  68.1 0.0 collective-permute-done.1.v_left
  68.1 31.9 %edge_attention_adapter.1 = bf16[256,5120]{1,0:T(8,128)(2,1)} custom-call(s32[256]{0:T(256)S(1)} %copy-done.5, s32[256]{0:T(256)S(1)} %copy-done.6, bf16[256,5120]{1,0:T(8,128)(2,1)S(1)} %copy-done.2, bf16[256,5120]{1,0:T(8,128)(2,1)S(1)} %copy-done, bf16[256,5120]{1,0:T(8,128)(2,1)S(1)} %copy-done.1, bf16[256,5120]{1,0:T(8,128)(2,1)S(1)} %local_attention.1.att, ...), custom_call_target="tpu_custom_call" | custom-call | flops 1174405120 | bytes 18350080 | tf_op jit(solution)/shard_map/edge_attention_adapter/pallas_call | solution.py:222
  (4 shorter events, 0.1 us)
Async XLA Ops:
  1.6 8.2 %collective-permute-start.6 = (bf16[1,640,128]{2,1,0:T(8,128)(2,1)S(1)}, bf16[1,640,128]{2,1,0:T(8,128)(2,1)S(1)}, u32[]{:S(2)}, u32[]{:S(2)}) collective-permute-start(bf16[1,640,128]{2,1,0:T(8,128)(2,1)S(1)} %maximum_bitcast_fusion), channel_id=1, source_target_pairs={{0,12},{1,13},{2,14},{3,15},{4,8},{5,9},{6,10},{7,11},{8,4},{9,5},... | collective-permute-start | bytes 491528 | tf_op jit(solution)/shard_map/ppermute | solution.py:258
  5.8 13.5 %collective-permute-start.5 = (bf16[1,640,128]{2,1,0:T(8,128)(2,1)S(1)}, bf16[1,640,128]{2,1,0:T(8,128)(2,1)S(1)}, u32[]{:S(2)}, u32[]{:S(2)}) collective-permute-start(bf16[1,640,128]{2,1,0:T(8,128)(2,1)S(1)} %maximum_bitcast_fusion), channel_id=1, source_target_pairs={{0,8},{1,9},{2,10},{3,11},{4,12},{5,13},{6,14},{7,15},{8,0},{9,1},... | collective-permute-start | bytes 491528 | tf_op jit(solution)/shard_map/ppermute | solution.py:258
  5.8 13.5 %collective-permute-start.4 = (bf16[1,640,128]{2,1,0:T(8,128)(2,1)S(1)}, bf16[1,640,128]{2,1,0:T(8,128)(2,1)S(1)}, u32[]{:S(2)}, u32[]{:S(2)}) collective-permute-start(bf16[1,640,128]{2,1,0:T(8,128)(2,1)S(1)} %maximum_bitcast_fusion), channel_id=1, source_target_pairs={{0,4},{1,5},{2,6},{3,7},{4,0},{5,1},{6,2},{7,3},{8,12},{9,13},{10,... | collective-permute-start | bytes 491528 | tf_op jit(solution)/shard_map/ppermute | solution.py:258
  19.3 8.8 %copy-start.4 = (bf16[320,128]{1,0:T(8,128)(2,1)S(1)}, bf16[320,128]{1,0:T(8,128)(2,1)}, u32[]{:S(2)}) copy-start(bf16[320,128]{1,0:T(8,128)(2,1)} %down_ref.1) | copy-start | bytes 245764
  19.3 8.8 %copy-start.7 = (bf16[128,320]{0,1:T(8,128)(2,1)S(1)}, bf16[128,320]{0,1:T(8,128)(2,1)}, u32[]{:S(2)}) copy-start(bf16[128,320]{0,1:T(8,128)(2,1)} %param.14) | copy-start | bytes 245764
  19.4 21.0 %collective-permute-start.7 = (bf16[4,640,128]{2,1,0:T(8,128)(2,1)S(1)}, bf16[4,640,128]{2,1,0:T(8,128)(2,1)S(1)}, u32[]{:S(2)}, u32[]{:S(2)}) collective-permute-start(bf16[4,640,128]{2,1,0:T(8,128)(2,1)S(1)} %pad_maximum_fusion), channel_id=1, source_target_pairs={{0,2},{1,3},{2,0},{3,1},{4,6},{5,7},{6,4},{7,5},{8,10},{9,11},{10,... | collective-permute-start | bytes 1966088 | tf_op jit(solution)/shard_map/ppermute | solution.py:258
  20.7 30.2 %copy-start.2 = (bf16[256,5120]{1,0:T(8,128)(2,1)S(1)}, bf16[256,5120]{1,0:T(8,128)(2,1)}, u32[]{:S(2)}) copy-start(bf16[256,5120]{1,0:T(8,128)(2,1)} %q.1) | copy-start | bytes 7864324
  22.2 45.9 %collective-permute-start.2 = (bf16[64,5120]{1,0:T(8,128)(2,1)S(1)}, bf16[64,5120]{1,0:T(8,128)(2,1)S(1)}, u32[]{:S(2)}, u32[]{:S(2)}) collective-permute-start(bf16[64,5120]{1,0:T(8,128)(2,1)S(1)} %get-tuple-element.4), channel_id=1, source_target_pairs={{1,0},{2,1},{3,2},{4,3},{5,4},{6,5},{7,6},{8,7},{9,8},{10,9},{11,1... | collective-permute-start | bytes 1966088 | tf_op jit(solution)/shard_map/ppermute | solution.py:289
  25.8 19.0 %copy-start.1 = (bf16[256,5120]{1,0:T(8,128)(2,1)S(1)}, bf16[256,5120]{1,0:T(8,128)(2,1)}, u32[]{:S(2)}) copy-start(bf16[256,5120]{1,0:T(8,128)(2,1)} %v.1) | copy-start | bytes 7864324
  25.8 42.3 %collective-permute-start = (bf16[64,5120]{1,0:T(8,128)(2,1)S(1)}, bf16[64,5120]{1,0:T(8,128)(2,1)S(1)}, u32[]{:S(2)}, u32[]{:S(2)}) collective-permute-start(bf16[64,5120]{1,0:T(8,128)(2,1)S(1)} %get-tuple-element.5), channel_id=1, source_target_pairs={{0,1},{1,2},{2,3},{3,4},{4,5},{5,6},{6,7},{7,8},{8,9},{9,10},{10,1... | collective-permute-start | bytes 1966088 | tf_op jit(solution)/shard_map/ppermute | solution.py:287
  40.4 10.5 %copy-start = (bf16[256,5120]{1,0:T(8,128)(2,1)S(1)}, bf16[256,5120]{1,0:T(8,128)(2,1)}, u32[]{:S(2)}) copy-start(bf16[256,5120]{1,0:T(8,128)(2,1)} %k.1) | copy-start | bytes 7864324
  40.5 10.5 %copy-start.5 = (s32[256]{0:T(256)S(1)}, s32[256]{0:T(256)}, u32[]{:S(2)}) copy-start(s32[256]{0:T(256)} %lo_ref.3) | copy-start | bytes 3076
  40.5 10.5 %copy-start.6 = (s32[256]{0:T(256)S(1)}, s32[256]{0:T(256)}, u32[]{:S(2)}) copy-start(s32[256]{0:T(256)} %hi_ref.3) | copy-start | bytes 3076
  40.5 20.3 %collective-permute-start.8 = (bf16[8,640,128]{2,1,0:T(8,128)(2,1)S(1)}, bf16[8,640,128]{2,1,0:T(8,128)(2,1)S(1)}, u32[]{:S(2)}, u32[]{:S(2)}) collective-permute-start(bf16[8,640,128]{2,1,0:T(8,128)(2,1)S(1)} %constant_dynamic-update-slice_fusion.rest_0_), channel_id=1, source_target_pairs={{0,1},{1,0},{2,3},{3,2},{4,5},{5,4},{6,7},{7,6},{8,9},{9,8},{10,11... | collective-permute-start | bytes 3932168 | tf_op jit(solution)/shard_map/ppermute | solution.py:258
  44.8 23.3 %collective-permute-start.3 = (bf16[64,5120]{1,0:T(8,128)(2,1)S(1)}, bf16[64,5120]{1,0:T(8,128)(2,1)S(1)}, u32[]{:S(2)}, u32[]{:S(2)}) collective-permute-start(bf16[64,5120]{1,0:T(8,128)(2,1)S(1)} %get-tuple-element.2), channel_id=1, source_target_pairs={{1,0},{2,1},{3,2},{4,3},{5,4},{6,5},{7,6},{8,7},{9,8},{10,9},{11,1... | collective-permute-start | bytes 1966088 | tf_op jit(solution)/shard_map/ppermute | solution.py:290
  46.9 21.2 %collective-permute-start.1 = (bf16[64,5120]{1,0:T(8,128)(2,1)S(1)}, bf16[64,5120]{1,0:T(8,128)(2,1)S(1)}, u32[]{:S(2)}, u32[]{:S(2)}) collective-permute-start(bf16[64,5120]{1,0:T(8,128)(2,1)S(1)} %get-tuple-element.3), channel_id=1, source_target_pairs={{0,1},{1,2},{2,3},{3,4},{4,5},{5,6},{6,7},{7,8},{8,9},{9,10},{10,1... | collective-permute-start | bytes 1966088 | tf_op jit(solution)/shard_map/ppermute | solution.py:288
  50.9 9.8 %copy-start.3 = (bf16[320,5120]{1,0:T(8,128)(2,1)S(1)}, bf16[320,5120]{1,0:T(8,128)(2,1)}, u32[]{:S(2)}) copy-start(bf16[320,5120]{1,0:T(8,128)(2,1)} %frozen_ref.1) | copy-start | bytes 9830404

commit v2 on v0

v2 whole, which is shorter than its diff:
```python
import functools

import jax
import jax.numpy as jnp
from jax import lax
from jax.experimental import pallas as pl
from jax.experimental.pallas import tpu as pltpu
from jax.sharding import PartitionSpec as P

MODEL_WIDTH = 5120
HEADS = 40
HD = 128
FRAME = 64
NEAR = 2 * FRAME
WINDOW = 3 * FRAME
CHUNK = 512
SCORE_SCALE = HD ** (-0.5) * 1.4426950408889634
ADAPTER_SCALE = MODEL_WIDTH ** (-0.5)
FAR = -1e30
NT = (((1,), (1,)), ((), ()))
NN = (((1,), (0,)), ((), ()))
BF16 = jnp.bfloat16
ANY = pl.BlockSpec(memory_space=pl.ANY)
SMEM = pl.BlockSpec(memory_space=pltpu.SMEM)


def dot(a, b, dims):
    return lax.dot_general(a, b, dims, preferred_element_type=jnp.float32)


def clip_bias(lo, hi):
    return jnp.where(
        lax.broadcasted_iota(jnp.int32, (FRAME, NEAR), 1) < hi - lo, 0.0, FAR
    ).astype(jnp.float32)


def attend(blocks):
    scores = [dot(q(), k(), NT) * SCORE_SCALE + bias for q, k, _, bias, _ in blocks]
    peaks = [jnp.max(s, axis=-1, keepdims=True) for s in scores]
    weights = [jnp.exp2(s - m) for s, m in zip(scores, peaks)]
    totals = [jnp.sum(w, axis=-1, keepdims=True) for w in weights]
    mixed = [dot(w.astype(BF16), block[2](), NN) for w, block in zip(weights, blocks)]
    for block, mix, total in zip(blocks, mixed, totals):
        block[4]((mix * (1.0 / total)).astype(BF16))


def local_kernel(lo_ref, hi_ref, q_ref, k_ref, v_ref, o_ref):
    rows = q_ref.shape[0]
    base = lax.axis_index("seq") * rows
    blocks = []
    for row in range(FRAME, rows - FRAME, FRAME):
        lo, hi = lo_ref[row], hi_ref[row]
        keys = pl.ds(pl.multiple_of(lo - base, FRAME), NEAR)
        bias = clip_bias(lo, hi)
        for col in range(0, CHUNK, HD):
            part = slice(col, col + HD)

            def put(value, at=row - FRAME, part=part):
                o_ref[at : at + FRAME, part] = value

            blocks.append(
                (
                    lambda row=row, part=part: q_ref[row : row + FRAME, part],
                    lambda keys=keys, part=part: k_ref[keys, part],
                    lambda keys=keys, part=part: v_ref[keys, part],
                    bias,
                    put,
                )
            )
    attend(blocks)


def local_attention(lo, hi, q, k, v):
    rows, width = q.shape
    inner = rows - NEAR
    block = pl.BlockSpec((rows, CHUNK), lambda i: (0, i))
    return pl.pallas_call(
        local_kernel,
        grid=(width // CHUNK,),
        out_shape=jax.ShapeDtypeStruct((inner, width), BF16),
        in_specs=[SMEM, SMEM, block, block, block],
        out_specs=pl.BlockSpec((inner, CHUNK), lambda i: (0, i)),
        compiler_params=pltpu.CompilerParams(vmem_limit_bytes=16 << 20),
        cost_estimate=pl.CostEstimate(
            flops=4 * inner * NEAR * width,
            bytes_accessed=7 * rows * width,
            transcendentals=inner * NEAR * HEADS,
        ),
        name="local_attention",
    )(lo, hi, q, k, v)


def merge_kernel(layout, frozen, own_down, att, *rest):
    refs, rest = rest[: len(layout)], rest[len(layout) :]
    merged, attended, down, up, w, a, mixed, inner, sems, in_sems, out_sems = rest
    shard, width = frozen.shape
    me = lax.axis_index("seq")
    kind = lax.axis_index("group")
    loads = [
        pltpu.make_async_copy(own_down, a, in_sems.at[0]),
        pltpu.make_async_copy(att, mixed, in_sems.at[1]),
        pltpu.make_async_copy(frozen, w, in_sems.at[2]),
    ]
    pieces = []
    for ref, (swapped, masks) in zip(refs, layout):
        for i, mask in enumerate(masks):
            rows = pl.ds(pl.multiple_of((me ^ mask) * shard, shard), shard)
            pieces.append((swapped, ref.at[i], rows))
    for this, other, up_swapped in ((down, up, 1), (up, down, 0)):
        first_kind = 1 - up_swapped

        @pl.when(kind == first_kind)
        def _(this=this, other=other):
            for n, (swapped, source, rows) in enumerate(pieces):
                target = (other if swapped else this).at[rows]
                pltpu.make_async_copy(source, target, sems.at[n]).start()

    for copy in loads:
        copy.start()
    for n, (_, source, rows) in enumerate(pieces):
        pltpu.make_async_copy(source, down.at[rows], sems.at[n]).wait()
    for copy in loads:
        copy.wait()
    reduced = dot(mixed[...], down[...], NN).astype(BF16)
    stores = []
    for step in range(width // CHUNK):
        part = pl.ds(step * CHUNK, CHUNK)
        factor = up[part, :]
        delta = dot(reduced, factor, NT)
        inner[:, part] = (mixed[:, part].astype(jnp.float32) + ADAPTER_SCALE * delta).astype(BF16)
        product = dot(a[...], factor, NT)
        w[:, part] = (w[:, part].astype(jnp.float32) + ADAPTER_SCALE * product).astype(BF16)
        rows = pl.ds(FRAME, inner.shape[0])
        stores += [
            pltpu.make_async_copy(w.at[:, part], merged.at[:, part], out_sems.at[2 * step]),
            pltpu.make_async_copy(
                inner.at[:, part], attended.at[rows, part], out_sems.at[2 * step + 1]
            ),
        ]
        stores[-1].start()
        stores[-2].start()
    for store in stores:
        store.wait()


def merge(frozen, own_down, att, layout, pieces):
    shard, width = frozen.shape
    rank = own_down.shape[1]
    inner = att.shape[0]
    count = sum(len(masks) for _, masks in layout)
    whole = pl.BlockSpec(memory_space=pltpu.VMEM)
    factor = jax.ShapeDtypeStruct((width, rank), BF16)
    return pl.pallas_call(
        functools.partial(merge_kernel, layout),
        out_shape=(
            jax.ShapeDtypeStruct((shard, width), BF16),
            jax.ShapeDtypeStruct((inner + NEAR, width), BF16),
            factor,
            factor,
        ),
        in_specs=[ANY] * (3 + len(pieces)),
        out_specs=(ANY, ANY, whole, whole),
        scratch_shapes=[
            pltpu.VMEM((shard, width), BF16),
            pltpu.VMEM((shard, rank), BF16),
            pltpu.VMEM((inner, width), BF16),
            pltpu.VMEM((inner, width), BF16),
            pltpu.SemaphoreType.DMA((count,)),
            pltpu.SemaphoreType.DMA((3,)),
            pltpu.SemaphoreType.DMA((2 * (width // CHUNK),)),
        ],
        compiler_params=pltpu.CompilerParams(vmem_limit_bytes=20 << 20),
        cost_estimate=pl.CostEstimate(
            flops=2 * shard * width * rank + 4 * inner * width * rank,
            bytes_accessed=4 * shard * width + 4 * inner * width + 8 * width * rank,
            transcendentals=0,
        ),
        name="merge_and_inner_adapter",
    )(frozen, own_down, att, *pieces)


def edge_kernel(lo_ref, hi_ref, q, k, v, left, right, down, up, _, out, *scratch):
    q_edge, k_edge, v_edge, a, b, mixed, result, reduced, sems, b_sem, out_sems = scratch
    rows, width = q.shape
    span = width // sems.shape[0]
    base = lax.axis_index("seq") * rows
    loads = []
    for n in range(width // span):
        part = pl.ds(n * span, span)
        moves = [
            (q.at[pl.ds(0, FRAME), part], q_edge.at[0, :, part]),
            (q.at[pl.ds(rows - FRAME, FRAME), part], q_edge.at[1, :, part]),
            (left.at[0, :, part], k_edge.at[0, pl.ds(0, FRAME), part]),
            (k.at[pl.ds(0, NEAR), part], k_edge.at[0, pl.ds(FRAME, NEAR), part]),
            (k.at[pl.ds(rows - NEAR, NEAR), part], k_edge.at[1, pl.ds(0, NEAR), part]),
            (right.at[0, :, part], k_edge.at[1, pl.ds(NEAR, FRAME), part]),
            (left.at[1, :, part], v_edge.at[0, pl.ds(0, FRAME), part]),
            (v.at[pl.ds(0, NEAR), part], v_edge.at[0, pl.ds(FRAME, NEAR), part]),
            (v.at[pl.ds(rows - NEAR, NEAR), part], v_edge.at[1, pl.ds(0, NEAR), part]),
            (right.at[1, :, part], v_edge.at[1, pl.ds(NEAR, FRAME), part]),
            (down.at[part], a.at[part]),
        ]
        loads.append(
            [pltpu.make_async_copy(s, t, sems.at[n, i]) for i, (s, t) in enumerate(moves)]
        )
    for group in loads:
        for copy in group:
            copy.start()
    load_up = pltpu.make_async_copy(up, b, b_sem.at[0])
    load_up.start()
    keys, biases = [], []
    for row, first in ((0, base - FRAME), (rows - FRAME, base + rows - NEAR)):
        lo, hi = lo_ref[row], hi_ref[row]
        keys.append(pl.ds(pl.multiple_of(lo - first, FRAME), NEAR))
        biases.append(clip_bias(lo, hi))
    reduced[...] = jnp.zeros_like(reduced)
    for n, group in enumerate(loads):
        for copy in group:
            copy.wait()

        def step(i, _, first=n * span):
            start = first + i * CHUNK
            blocks = []
            for col in range(0, CHUNK, HD):
                part = pl.ds(pl.multiple_of(start + col, HD), HD)
                for e in range(2):

                    def put(value, e=e, part=part):
                        mixed[e * FRAME : (e + 1) * FRAME, part] = value

                    blocks.append(
                        (
                            lambda e=e, part=part: q_edge[e, :, part],
                            lambda e=e, part=part: k_edge[e, keys[e], part],
                            lambda e=e, part=part: v_edge[e, keys[e], part],
                            biases[e],
                            put,
                        )
                    )
            attend(blocks)
            wide = pl.ds(pl.multiple_of(start, CHUNK), CHUNK)
            reduced[...] += dot(mixed[:, wide], a[wide, :], NN)
            return 0

        lax.fori_loop(0, span // CHUNK, step, 0)
    load_up.wait()
    narrow = reduced[...].astype(BF16)
    stores = []
    for n in range(width // CHUNK):
        part = pl.ds(n * CHUNK, CHUNK)
        delta = dot(narrow, b[part, :], NT)
        result[:, part] = (mixed[:, part].astype(jnp.float32) + ADAPTER_SCALE * delta).astype(BF16)
        for e, row in ((0, 0), (1, rows - FRAME)):
            stores.append(
                pltpu.make_async_copy(
                    result.at[pl.ds(e * FRAME, FRAME), part],
                    out.at[pl.ds(row, FRAME), part],
                    out_sems.at[2 * n + e],
                )
            )
            stores[-1].start()
    for store in stores:
        store.wait()


def edge(lo, hi, q, k, v, left, right, down, up, attended):
    rows, width = q.shape
    rank = down.shape[1]
    return pl.pallas_call(
        edge_kernel,
        out_shape=jax.ShapeDtypeStruct((rows, width), BF16),
        in_specs=[SMEM, SMEM] + [ANY] * 8,
        out_specs=ANY,
        input_output_aliases={9: 0},
        scratch_shapes=[
            pltpu.VMEM((2, FRAME, width), BF16),
            pltpu.VMEM((2, WINDOW, width), BF16),
            pltpu.VMEM((2, WINDOW, width), BF16),
            pltpu.VMEM((width, rank), BF16),
            pltpu.VMEM((width, rank), BF16),
            pltpu.VMEM((NEAR, width), BF16),
            pltpu.VMEM((NEAR, width), BF16),
            pltpu.VMEM((NEAR, rank), jnp.float32),
            pltpu.SemaphoreType.DMA((width // (2 * CHUNK), 11)),
            pltpu.SemaphoreType.DMA((1,)),
            pltpu.SemaphoreType.DMA((2 * (width // CHUNK),)),
        ],
        compiler_params=pltpu.CompilerParams(vmem_limit_bytes=24 << 20),
        cost_estimate=pl.CostEstimate(
            flops=4 * NEAR * width * (NEAR + rank),
            bytes_accessed=24 * FRAME * width + 4 * rank * width,
            transcendentals=NEAR * NEAR * HEADS,
        ),
        name="edge_attention_adapter",
    )(lo, hi, q, k, v, left, right, down, up, attended)


def gather_factors(down, up):
    count = lax.axis_size("seq")
    if lax.axis_size("group") != 2 or down.shape[0] % 32:
        both = lax.all_gather(jnp.stack([down, up]), "seq", axis=1)
        kind = lax.axis_index("group")
        order = jnp.arange(count, dtype=jnp.int32) ^ lax.axis_index("seq")
        both = both[:, order]
        masks = list(range(count))
        return [(0, masks), (1, masks)], [both[kind], both[1 - kind]]

    def swap(cells, mask):
        return lax.ppermute(cells, "seq", [(i, i ^ mask) for i in range(count)])

    cells = jnp.where(lax.axis_index("group") == 0, down, up)[None]
    masks = [0]
    low = 2
    while low < count:
        bits = 1 if (count // low).bit_length() % 2 == 0 else 2
        steps = [low * j for j in range(1, 1 << bits)]
        cells = jnp.concatenate([cells] + [swap(cells, mask) for mask in steps])
        masks = masks + [have ^ mask for mask in steps for have in masks]
        low <<= bits
    other = lax.ppermute(cells, "group", [(0, 1), (1, 0)])
    across = [mask ^ 1 for mask in masks]
    return (
        [(0, masks), (0, across), (1, masks), (1, across)],
        [cells, swap(cells, 1), other, swap(other, 1)],
    )


def body(q, k, v, lo, hi, down, up, frozen):
    count = lax.axis_size("seq")
    rows = q.shape[0]
    layout, pieces = gather_factors(down, up.T)
    tails = jnp.stack([k[rows - FRAME :], v[rows - FRAME :]])
    heads = jnp.stack([k[:FRAME], v[:FRAME]])
    left = lax.ppermute(tails, "seq", [(i, i + 1) for i in range(count - 1)])
    right = lax.ppermute(heads, "seq", [(i + 1, i) for i in range(count - 1)])
    att = local_attention(lo, hi, q, k, v)
    merged, attended, down_full, up_full = merge(frozen, down, att, layout, pieces)
    attended = edge(lo, hi, q, k, v, left, right, down_full, up_full, attended)
    return (attended, merged)


def solution(mesh):
    rows = P(("group", "seq"), None)
    flat = P(("group", "seq"))
    return jax.shard_map(
        body,
        mesh=mesh,
        in_specs=(rows, rows, rows, flat, flat, P("seq", None), P(None, "seq"), P("seq", None)),
        out_specs=(rows, rows),
        check_vma=False,
    )
```

time: 241 us -> 78 us (0.32)
  waiting for transfers between devices: 114 us -> 7.99 us
  matrix products: 42.2 us -> 0 us
  other arithmetic: 43.4 us -> 1.22 us
  starting transfers between devices: 6.72 us -> 40.4 us
  Pallas kernels: 0 us -> 25 us
  local copies, waits for them, and re-layouts: 19.3 us -> 2.12 us
  between operations: 14.1 us -> 0.82 us
    all_gather x2 -> x0, waiting for transfers between devices: 72.3 us -> none  [the longest x1 72.3 us: body(): lax.all_gather(adapter_up_factor, 'seq', axis=1, tiled=True)]
    dot_general x4 -> x0, matrix products: 42.2 us -> none  [the longest x1 16.1 us: attend(): jnp.einsum('hts,shd->thd', weights_bf, value_heads, preferred_element_typ...]
    ppermute x2 -> x9, starting transfers between devices: 6.65 us -> 40.4 us  [the longest x6 27.3 us: swap(): return lax.ppermute(cells, 'seq', [(i, i ^ mask) for i in range(count)])]
    ppermute x2 -> x9, waiting for transfers between devices: 41.2 us -> 7.99 us  [the longest x6 7.98 us: swap(): return lax.ppermute(cells, 'seq', [(i, i ^ mask) for i in range(count)])]
    sub x1 -> x0, other arithmetic: 31.4 us -> none  [attend(): weights = jnp.exp(scores - highest)]
    pallas_call x0 -> x3, Pallas kernels: none -> 25 us  [the longest x1 10.6 us: edge(): pl.pallas_call(edge_kernel, out_shape=jax.ShapeDtypeStruct((rows, width),...]
    unnamed x16 -> x17, local copies, waits for them, and re-layouts: 8.99 us -> 0.1 us
    concatenate x1, other arithmetic: 6.39 us -> 0.02 us  [gather_factors(): cells = jnp.concatenate([cells] + [swap(cells, mask) for mask in steps])]
  transfers between devices with their start and end apart: 4 -> 9, of which waited for: 2 -> 2; matrix products, arithmetic and copies ran while one was open for 35% -> 3% of each run, Pallas kernels for 0% -> 19%
where the time goes in v2:
time: 78 us; the launch traced here: 77.5 us
  starting transfers between devices  40.4 us (52%)
  Pallas kernels  25 us (32%)
  waiting for transfers between devices  7.99 us (10%)
  local copies, waits for them, and re-layouts  2.12 us (3%)
  other arithmetic  1.22 us (2%)
  between operations  0.82 us (1%)
    ppermute x6, starting transfers between devices, swap(): return lax.ppermute(cells, 'seq', [(i, i ^ mask) for i in range(count)])  27.3 us
    pallas_call x1, Pallas kernels, edge(): pl.pallas_call(edge_kernel, out_shape=jax.ShapeDtypeStruct((rows, width),...  10.6 us
    ppermute x6, waiting for transfers between devices, swap(): return lax.ppermute(cells, 'seq', [(i, i ^ mask) for i in range(count)])  7.98 us
    pallas_call x1, Pallas kernels, merge(): pl.pallas_call(functools.partial(merge_kernel, layout), out_shape=(jax.Sh...  7.78 us
    ppermute x1, starting transfers between devices, body(): left = lax.ppermute(tails, 'seq', [(i, i + 1) for i in range(count - 1)])  7.71 us
    pallas_call x1, Pallas kernels, local_attention(): pl.pallas_call(local_kernel, grid=(width // CHUNK,), out_shape=jax.ShapeD...  6.59 us
    ppermute x1, starting transfers between devices, body(): right = lax.ppermute(heads, 'seq', [(i + 1, i) for i in range(count - 1)])  4.14 us
    another operation x1, local copies, waits for them, and re-layouts, body(): heads = jnp.stack([k[:FRAME], v[:FRAME]])  2 us
  transfers between devices with their start and end apart: 9, of which 2 were waited for; matrix products, arithmetic and copies ran while one was open for 3% of the time, Pallas kernels for 19%

profile of v2, /device:TPU:1, one launch (start us, length us, event | category | flops | bytes accessed | tf_op | source)
XLA Modules:
  0.0 77.5 jit_solution(12108272789725825959)
XLA Ops:
  0.6 1.0 %constant_dynamic-update-slice_fusion.4 = (bf16[8,320,128]{2,1,0:T(8,128)(2,1)S(1)}, bf16[1,320,128]{2,1,0:T(8,128)(2,1)S(1)}) fusion(bf16[320,128]{1,0:T(8,128)(2,1)} %own_down.1, bf16[128,320]{0,1:T(8,128)(2,1)} %param.14, pred[]{:T(512)S(6)} %eq.3), kind=kLoop, calls=%fused_computation.13 | loop fusion | flops 40959 | bytes 327681
  1.6 2.1 %collective-permute-start.2 = (bf16[1,320,128]{2,1,0:T(8,128)(2,1)S(1)}, bf16[1,320,128]{2,1,0:T(8,128)(2,1)S(1)}, u32[]{:S(2)}, u32[]{:S(2)}) collective-permute-start(bf16[1,320,128]{2,1,0:T(8,128)(2,1)S(1)} %get-tuple-element.11), channel_id=1, source_target_pairs={{0,2},{1,3},{2,0},{3,1},{4,6},{5,7},{6,4},{7,5},{8,10},{9,11},{10,... | collective-permute-start | bytes 245768 | tf_op jit(solution)/shard_map/ppermute | solution.py:309
  3.7 0.0 copy-start.2
  3.7 2.0 %slice_bitcast_fusion = (bf16[1,64,5120]{2,1,0:T(8,128)(2,1)S(1)}, bf16[1,64,5120]{2,1,0:T(8,128)(2,1)S(1)}, bf16[1,64,5120]{2,1,0:T(8,128)(2,1)S(1)}, bf16[1,64,5120]{2,1,0:T(8,128)(2,1)S(1)}) fusion(bf16[256,5120]{1,0:T(8,128)(2,1)} %v.1, bf16[256,5120]{1,0:T(8,128)(2,1)} %k.1), kind=kLoop, calls=%fused_computation.2 | loop fusion | bytes 5242880 | tf_op jit(solution)/shard_map/stack | solution.py:333
  5.7 0.2 collective-permute-done.2
  5.9 1.2 %collective-permute-start.3 = (bf16[2,320,128]{2,1,0:T(8,128)(2,1)S(1)}, bf16[2,320,128]{2,1,0:T(8,128)(2,1)S(1)}, u32[]{:S(2)}, u32[]{:S(2)}) collective-permute-start(bf16[2,320,128]{2,1,0:T(8,128)(2,1)S(1)} %pad_maximum_fusion.2), channel_id=1, source_target_pairs={{0,4},{1,5},{2,6},{3,7},{4,0},{5,1},{6,2},{7,3},{8,12},{9,13},{10,... | collective-permute-start | bytes 491528 | tf_op jit(solution)/shard_map/ppermute | solution.py:309
  7.2 0.0 copy-start.1
  7.2 0.1 pad_maximum_fusion.1
  7.3 4.1 %collective-permute-start.1 = (bf16[2,64,5120]{2,1,0:T(8,128)(2,1)S(1)}, bf16[2,64,5120]{2,1,0:T(8,128)(2,1)S(1)}, u32[]{:S(2)}, u32[]{:S(2)}) collective-permute-start(bf16[2,64,5120]{2,1,0:T(8,128)(2,1)S(1)} %pad_maximum_fusion.1), channel_id=1, source_target_pairs={{1,0},{2,1},{3,2},{4,3},{5,4},{6,5},{7,6},{8,7},{9,8},{10,9},{11,1... | collective-permute-start | bytes 3932168 | tf_op jit(solution)/shard_map/ppermute | solution.py:335
  11.4 2.4 %collective-permute-start.4 = (bf16[2,320,128]{2,1,0:T(8,128)(2,1)S(1)}, bf16[2,320,128]{2,1,0:T(8,128)(2,1)S(1)}, u32[]{:S(2)}, u32[]{:S(2)}) collective-permute-start(bf16[2,320,128]{2,1,0:T(8,128)(2,1)S(1)} %pad_maximum_fusion.2), channel_id=1, source_target_pairs={{0,8},{1,9},{2,10},{3,11},{4,12},{5,13},{6,14},{7,15},{8,0},{9,1},... | collective-permute-start | bytes 491528 | tf_op jit(solution)/shard_map/ppermute | solution.py:309
  13.8 0.0 collective-permute-start.5
  13.8 0.0 collective-permute-done.3
  13.9 7.8 %collective-permute-done.4 = bf16[2,320,128]{2,1,0:T(8,128)(2,1)S(1)} collective-permute-done((bf16[2,320,128]{2,1,0:T(8,128)(2,1)S(1)}, bf16[2,320,128]{2,1,0:T(8,128)(2,1)S(1)}, u32[]{:S(2)}, u32[]{:S(2)}) %collective-permute-start.4) | collective-permute-done | bytes 163872 | tf_op jit(solution)/shard_map/ppermute | solution.py:309
  21.7 0.0 collective-permute-done.5
  21.7 0.0 copy-start.5
  21.7 0.0 copy-start.6
  21.8 1.3 %collective-permute-start.7 = (bf16[8,320,128]{2,1,0:T(8,128)(2,1)S(1)}, bf16[8,320,128]{2,1,0:T(8,128)(2,1)S(1)}, u32[]{:S(2)}, u32[]{:S(2)}) collective-permute-start(bf16[8,320,128]{2,1,0:T(8,128)(2,1)S(1)} %constant_dynamic-update-slice_fusion.rest_0_), channel_id=1, source_target_pairs={{0,16},{16,0},{1,17},{17,1},{2,18},{18,2},{3,19},{19,3},{4,20},{20... | collective-permute-start | bytes 1966088 | tf_op jit(solution)/shard_map/ppermute | solution.py:320
  23.1 0.0 copy-start
  23.1 0.1 pad_maximum_fusion
  23.2 0.0 copy-start.4
  23.2 7.7 %collective-permute-start = (bf16[2,64,5120]{2,1,0:T(8,128)(2,1)S(1)}, bf16[2,64,5120]{2,1,0:T(8,128)(2,1)S(1)}, u32[]{:S(2)}, u32[]{:S(2)}) collective-permute-start(bf16[2,64,5120]{2,1,0:T(8,128)(2,1)S(1)} %pad_maximum_fusion), channel_id=1, source_target_pairs={{0,1},{1,2},{2,3},{3,4},{4,5},{5,6},{6,7},{7,8},{8,9},{9,10},{10,1... | collective-permute-start | bytes 3932168 | tf_op jit(solution)/shard_map/ppermute | solution.py:334
  30.9 14.2 %collective-permute-start.6 = (bf16[8,320,128]{2,1,0:T(8,128)(2,1)S(1)}, bf16[8,320,128]{2,1,0:T(8,128)(2,1)S(1)}, u32[]{:S(2)}, u32[]{:S(2)}) collective-permute-start(bf16[8,320,128]{2,1,0:T(8,128)(2,1)S(1)} %constant_dynamic-update-slice_fusion.rest_0_), channel_id=1, source_target_pairs={{0,1},{1,0},{2,3},{3,2},{4,5},{5,4},{6,7},{7,6},{8,9},{9,8},{10,11... | collective-permute-start | bytes 1966088 | tf_op jit(solution)/shard_map/ppermute | solution.py:309
  45.1 0.0 collective-permute-done.7.rest_2_
  45.1 7.4 %collective-permute-start.8 = (bf16[8,320,128]{2,1,0:T(8,128)(2,1)S(1)}, bf16[8,320,128]{2,1,0:T(8,128)(2,1)S(1)}, u32[]{:S(2)}, u32[]{:S(2)}) collective-permute-start(bf16[8,320,128]{2,1,0:T(8,128)(2,1)S(1)} %collective-permute-done.7.rest_2_), channel_id=1, source_target_pairs={{0,1},{1,0},{2,3},{3,2},{4,5},{5,4},{6,7},{7,6},{8,9},{9,8},{10,11... | collective-permute-start | bytes 1966088 | tf_op jit(solution)/shard_map/ppermute | solution.py:309
  52.5 0.0 copy-done.2
  52.5 0.0 copy-done.1
  52.5 0.0 copy-done.5
  52.5 0.0 copy-done.6
  52.5 0.0 copy-done
  52.5 0.0 copy-start.3
  52.5 6.6 %local_attention.1.att = bf16[128,5120]{1,0:T(8,128)(2,1)S(1)} custom-call(s32[256]{0:T(256)S(1)} %copy-done.5, s32[256]{0:T(256)S(1)} %copy-done.6, bf16[256,5120]{1,0:T(8,128)(2,1)S(1)} %copy-done.2, bf16[256,5120]{1,0:T(8,128)(2,1)S(1)} %copy-done, bf16[256,5120]{1,0:T(8,128)(2,1)S(1)} %copy-done.1), custom_call_target="tpu_custom_call" | custom-call | flops 335544320 | bytes 9175040 | tf_op jit(solution)/shard_map/local_attention/pallas_call | solution.py:77
  59.1 0.0 collective-permute-done.6.rest_1_
  59.1 0.0 collective-permute-done.8.rest_3_
  59.1 0.0 copy-done.4
  59.1 0.0 copy-done.3
  59.1 7.8 %merge_and_inner_adapter.1 = (bf16[320,5120]{1,0:T(8,128)(2,1)}, bf16[256,5120]{1,0:T(8,128)(2,1)}, bf16[5120,128]{1,0:T(8,128)(2,1)S(1)}, bf16[5120,128]{1,0:T(8,128)(2,1)S(1)}) custom-call(bf16[320,5120]{1,0:T(8,128)(2,1)S(1)} %copy-done.3, bf16[320,128]{1,0:T(8,128)(2,1)S(1)} %copy-done.4, bf16[128,5120]{1,0:T(8,128)(2,1)S(1)} %local_attention.1.att, ...), custom_call_target="tpu_custom_call" | custom-call | flops 754974720 | bytes 14417920 | tf_op jit(solution)/shard_map/merge_and_inner_adapter/pallas_call | solution.py:153
  66.9 0.0 collective-permute-done.1.right
  66.9 0.0 collective-permute-done.left
  67.0 10.6 %edge_attention_adapter.1 = bf16[256,5120]{1,0:T(8,128)(2,1)} custom-call(s32[256]{0:T(256)S(1)} %copy-done.5, s32[256]{0:T(256)S(1)} %copy-done.6, bf16[256,5120]{1,0:T(8,128)(2,1)S(1)} %copy-done.2, bf16[256,5120]{1,0:T(8,128)(2,1)S(1)} %copy-done, bf16[256,5120]{1,0:T(8,128)(2,1)S(1)} %copy-done.1, ...), custom_call_target="tpu_custom_call", output_to_operand_aliasing={{}: (9, {})} | custom-call | flops 671088640 | bytes 10485760 | tf_op jit(solution)/shard_map/edge_attention_adapter/pallas_call | solution.py:269
  (5 shorter events, 0.1 us)
Async XLA Ops:
  1.6 4.3 %collective-permute-start.2 = (bf16[1,320,128]{2,1,0:T(8,128)(2,1)S(1)}, bf16[1,320,128]{2,1,0:T(8,128)(2,1)S(1)}, u32[]{:S(2)}, u32[]{:S(2)}) collective-permute-start(bf16[1,320,128]{2,1,0:T(8,128)(2,1)S(1)} %get-tuple-element.11), channel_id=1, source_target_pairs={{0,2},{1,3},{2,0},{3,1},{4,6},{5,7},{6,4},{7,5},{8,10},{9,11},{10,... | collective-permute-start | bytes 245768 | tf_op jit(solution)/shard_map/ppermute | solution.py:309
  3.7 48.7 %copy-start.2 = (bf16[256,5120]{1,0:T(8,128)(2,1)S(1)}, bf16[256,5120]{1,0:T(8,128)(2,1)}, u32[]{:S(2)}) copy-start(bf16[256,5120]{1,0:T(8,128)(2,1)} %q.1) | copy-start | bytes 7864324
  5.9 7.9 %collective-permute-start.3 = (bf16[2,320,128]{2,1,0:T(8,128)(2,1)S(1)}, bf16[2,320,128]{2,1,0:T(8,128)(2,1)S(1)}, u32[]{:S(2)}, u32[]{:S(2)}) collective-permute-start(bf16[2,320,128]{2,1,0:T(8,128)(2,1)S(1)} %pad_maximum_fusion.2), channel_id=1, source_target_pairs={{0,4},{1,5},{2,6},{3,7},{4,0},{5,1},{6,2},{7,3},{8,12},{9,13},{10,... | collective-permute-start | bytes 491528 | tf_op jit(solution)/shard_map/ppermute | solution.py:309
  7.2 45.3 %copy-start.1 = (bf16[256,5120]{1,0:T(8,128)(2,1)S(1)}, bf16[256,5120]{1,0:T(8,128)(2,1)}, u32[]{:S(2)}) copy-start(bf16[256,5120]{1,0:T(8,128)(2,1)} %v.1) | copy-start | bytes 7864324
  7.3 59.6 %collective-permute-start.1 = (bf16[2,64,5120]{2,1,0:T(8,128)(2,1)S(1)}, bf16[2,64,5120]{2,1,0:T(8,128)(2,1)S(1)}, u32[]{:S(2)}, u32[]{:S(2)}) collective-permute-start(bf16[2,64,5120]{2,1,0:T(8,128)(2,1)S(1)} %pad_maximum_fusion.1), channel_id=1, source_target_pairs={{1,0},{2,1},{3,2},{4,3},{5,4},{6,5},{7,6},{8,7},{9,8},{10,9},{11,1... | collective-permute-start | bytes 3932168 | tf_op jit(solution)/shard_map/ppermute | solution.py:335
  11.4 10.2 %collective-permute-start.4 = (bf16[2,320,128]{2,1,0:T(8,128)(2,1)S(1)}, bf16[2,320,128]{2,1,0:T(8,128)(2,1)S(1)}, u32[]{:S(2)}, u32[]{:S(2)}) collective-permute-start(bf16[2,320,128]{2,1,0:T(8,128)(2,1)S(1)} %pad_maximum_fusion.2), channel_id=1, source_target_pairs={{0,8},{1,9},{2,10},{3,11},{4,12},{5,13},{6,14},{7,15},{8,0},{9,1},... | collective-permute-start | bytes 491528 | tf_op jit(solution)/shard_map/ppermute | solution.py:309
  13.8 7.9 %collective-permute-start.5 = (bf16[2,320,128]{2,1,0:T(8,128)(2,1)S(1)}, bf16[2,320,128]{2,1,0:T(8,128)(2,1)S(1)}, u32[]{:S(2)}, u32[]{:S(2)}) collective-permute-start(bf16[2,320,128]{2,1,0:T(8,128)(2,1)S(1)} %pad_maximum_fusion.2), channel_id=1, source_target_pairs={{0,12},{1,13},{2,14},{3,15},{4,8},{5,9},{6,10},{7,11},{8,4},{9,5},... | collective-permute-start | bytes 491528 | tf_op jit(solution)/shard_map/ppermute | solution.py:309
  21.7 30.8 %copy-start.5 = (s32[256]{0:T(256)S(1)}, s32[256]{0:T(256)}, u32[]{:S(2)}) copy-start(s32[256]{0:T(256)} %lo_ref.3) | copy-start | bytes 3076
  21.7 30.7 %copy-start.6 = (s32[256]{0:T(256)S(1)}, s32[256]{0:T(256)}, u32[]{:S(2)}) copy-start(s32[256]{0:T(256)} %hi_ref.3) | copy-start | bytes 3076
  21.8 23.3 %collective-permute-start.7 = (bf16[8,320,128]{2,1,0:T(8,128)(2,1)S(1)}, bf16[8,320,128]{2,1,0:T(8,128)(2,1)S(1)}, u32[]{:S(2)}, u32[]{:S(2)}) collective-permute-start(bf16[8,320,128]{2,1,0:T(8,128)(2,1)S(1)} %constant_dynamic-update-slice_fusion.rest_0_), channel_id=1, source_target_pairs={{0,16},{16,0},{1,17},{17,1},{2,18},{18,2},{3,19},{19,3},{4,20},{20... | collective-permute-start | bytes 1966088 | tf_op jit(solution)/shard_map/ppermute | solution.py:320
  23.1 29.4 %copy-start = (bf16[256,5120]{1,0:T(8,128)(2,1)S(1)}, bf16[256,5120]{1,0:T(8,128)(2,1)}, u32[]{:S(2)}) copy-start(bf16[256,5120]{1,0:T(8,128)(2,1)} %k.1) | copy-start | bytes 7864324
  23.2 35.9 %copy-start.4 = (bf16[320,128]{1,0:T(8,128)(2,1)S(1)}, bf16[320,128]{1,0:T(8,128)(2,1)}, u32[]{:S(2)}) copy-start(bf16[320,128]{1,0:T(8,128)(2,1)} %own_down.1) | copy-start | bytes 245764
  23.2 43.7 %collective-permute-start = (bf16[2,64,5120]{2,1,0:T(8,128)(2,1)S(1)}, bf16[2,64,5120]{2,1,0:T(8,128)(2,1)S(1)}, u32[]{:S(2)}, u32[]{:S(2)}) collective-permute-start(bf16[2,64,5120]{2,1,0:T(8,128)(2,1)S(1)} %pad_maximum_fusion), channel_id=1, source_target_pairs={{0,1},{1,2},{2,3},{3,4},{4,5},{5,6},{6,7},{7,8},{8,9},{9,10},{10,1... | collective-permute-start | bytes 3932168 | tf_op jit(solution)/shard_map/ppermute | solution.py:334
  30.9 28.2 %collective-permute-start.6 = (bf16[8,320,128]{2,1,0:T(8,128)(2,1)S(1)}, bf16[8,320,128]{2,1,0:T(8,128)(2,1)S(1)}, u32[]{:S(2)}, u32[]{:S(2)}) collective-permute-start(bf16[8,320,128]{2,1,0:T(8,128)(2,1)S(1)} %constant_dynamic-update-slice_fusion.rest_0_), channel_id=1, source_target_pairs={{0,1},{1,0},{2,3},{3,2},{4,5},{5,4},{6,7},{7,6},{8,9},{9,8},{10,11... | collective-permute-start | bytes 1966088 | tf_op jit(solution)/shard_map/ppermute | solution.py:309
  45.1 14.0 %collective-permute-start.8 = (bf16[8,320,128]{2,1,0:T(8,128)(2,1)S(1)}, bf16[8,320,128]{2,1,0:T(8,128)(2,1)S(1)}, u32[]{:S(2)}, u32[]{:S(2)}) collective-permute-start(bf16[8,320,128]{2,1,0:T(8,128)(2,1)S(1)} %collective-permute-done.7.rest_2_), channel_id=1, source_target_pairs={{0,1},{1,0},{2,3},{3,2},{4,5},{5,4},{6,7},{7,6},{8,9},{9,8},{10,11... | collective-permute-start | bytes 1966088 | tf_op jit(solution)/shard_map/ppermute | solution.py:309
  52.5 6.6 %copy-start.3 = (bf16[320,5120]{1,0:T(8,128)(2,1)S(1)}, bf16[320,5120]{1,0:T(8,128)(2,1)}, u32[]{:S(2)}) copy-start(bf16[320,5120]{1,0:T(8,128)(2,1)} %frozen.1) | copy-start | bytes 9830404

commit v3 on v0

v3 whole, which is shorter than its diff:
```python
import functools

import jax
import jax.numpy as jnp
from jax import lax
from jax.experimental import pallas as pl
from jax.experimental.pallas import tpu as pltpu
from jax.sharding import PartitionSpec as P

MODEL_WIDTH = 5120
HEADS = 40
HD = 128
FRAME = 64
NEAR = 2 * FRAME
CHUNK = 512
SCORE_SCALE = HD ** (-0.5) * 1.4426950408889634
ADAPTER_SCALE = MODEL_WIDTH ** (-0.5)
FAR = -1e30
NT = (((1,), (1,)), ((), ()))
NN = (((1,), (0,)), ((), ()))
BF16 = jnp.bfloat16
F32 = jnp.float32
ANY = pl.BlockSpec(memory_space=pl.ANY)
SMEM = pl.BlockSpec(memory_space=pltpu.SMEM)
VMEM = pl.BlockSpec(memory_space=pltpu.VMEM)


def dot(a, b, dims):
    return lax.dot_general(a, b, dims, preferred_element_type=F32)


def clip_bias(first, second):
    lengths = [hi - lo for lo, hi in (first, second)]
    position = lax.broadcasted_iota(jnp.int32, (FRAME, NEAR), 1)
    return jnp.concatenate([jnp.where(position < n, 0.0, FAR).astype(F32) for n in lengths])


def diagonal(top, bottom):
    zeros = jnp.zeros((FRAME, NEAR), BF16)
    return jnp.concatenate(
        [jnp.concatenate([top, zeros], axis=1), jnp.concatenate([zeros, bottom], axis=1)]
    )


def attend(loads, bias):
    ones = jnp.ones((NEAR, HD), BF16)
    scores = []
    for load_q, load_k, _ in loads:
        keys = jnp.concatenate(load_k(), axis=1)
        scores.append(dot(diagonal(*load_q()), keys, NT) * SCORE_SCALE + bias)
    weights = [jnp.exp2(s - jnp.max(s, axis=-1, keepdims=True)).astype(BF16) for s in scores]
    results = []
    for w, (_, _, load_v) in zip(weights, loads):
        values = jnp.concatenate([jnp.concatenate([v, ones], axis=1) for v in load_v()])
        mixed = dot(diagonal(w[:FRAME], w[FRAME:]), values, NN)
        results.append((mixed[:, :HD] * (1.0 / mixed[:, HD:])).astype(BF16))
    return results


def inner_kernel(lo_ref, hi_ref, q_ref, k_ref, v_ref, o_ref):
    rows = q_ref.shape[0]
    base = lax.axis_index("seq") * rows
    clips = [(lo_ref[row], hi_ref[row]) for row in (FRAME, NEAR)]
    keys = [pl.ds(pl.multiple_of(lo - base, FRAME), NEAR) for lo, _ in clips]
    loads, parts = [], []
    for col in range(0, CHUNK, HD):
        part = slice(col, col + HD)
        parts.append(part)
        loads.append(
            (
                lambda part=part: [q_ref[at : at + FRAME, part] for at in (FRAME, NEAR)],
                lambda part=part: [k_ref[at, part] for at in keys],
                lambda part=part: [v_ref[at, part] for at in keys],
            )
        )
    for part, result in zip(parts, attend(loads, clip_bias(*clips))):
        o_ref[:, part] = result


def inner_attention(lo, hi, q, k, v):
    rows, width = q.shape
    block = pl.BlockSpec((rows, CHUNK), lambda i: (0, i))
    return pl.pallas_call(
        inner_kernel,
        grid=(width // CHUNK,),
        out_shape=jax.ShapeDtypeStruct((NEAR, width), BF16),
        in_specs=[SMEM, SMEM, block, block, block],
        out_specs=pl.BlockSpec((NEAR, CHUNK), lambda i: (0, i)),
        compiler_params=pltpu.CompilerParams(vmem_limit_bytes=16 << 20),
        cost_estimate=pl.CostEstimate(
            flops=16 * NEAR * NEAR * width,
            bytes_accessed=7 * rows * width,
            transcendentals=NEAR * NEAR * HEADS,
        ),
        name="inner_attention",
    )(lo, hi, q, k, v)


def edge_kernel(lo_ref, hi_ref, q, k, v, far, near, out):
    rows, width = q.shape
    me = lax.axis_index("seq")
    base = me * rows
    even = lax.rem(me, 2) == 0
    clips = [(lo_ref[row], hi_ref[row]) for row in (0, rows - FRAME)]
    crosses = [clips[0][0] < base, clips[1][1] > base + rows]
    tail = rows - NEAR

    def window(ref, kind, part):
        away, close = far[kind, :, part], near[kind, :, part]
        first, second = ref[0:FRAME, part], ref[FRAME:NEAR, part]
        third, fourth = ref[tail : tail + FRAME, part], ref[tail + FRAME : rows, part]
        left, right = jnp.where(even, away, close), jnp.where(even, close, away)
        inside = clips[1][0] < base + rows - FRAME
        return [
            jnp.concatenate(
                [jnp.where(crosses[0], left, first), jnp.where(crosses[0], first, second)]
            ),
            jnp.concatenate(
                [jnp.where(inside, third, fourth), jnp.where(inside, fourth, right)]
            ),
        ]

    bias = clip_bias(*clips)

    def step(i, _):
        loads, parts = [], []
        for col in range(0, CHUNK, HD):
            part = pl.ds(pl.multiple_of(i * CHUNK + col, HD), HD)
            parts.append(part)
            loads.append(
                (
                    lambda part=part: [q[0:FRAME, part], q[rows - FRAME : rows, part]],
                    lambda part=part: window(k, 0, part),
                    lambda part=part: window(v, 1, part),
                )
            )
        for part, result in zip(parts, attend(loads, bias)):
            out[:, part] = result
        return 0

    lax.fori_loop(0, width // CHUNK, step, 0)


def edge_attention(lo, hi, q, k, v, far, near):
    rows, width = q.shape
    return pl.pallas_call(
        edge_kernel,
        out_shape=jax.ShapeDtypeStruct((NEAR, width), BF16),
        in_specs=[SMEM, SMEM] + [VMEM] * 5,
        out_specs=VMEM,
        compiler_params=pltpu.CompilerParams(vmem_limit_bytes=20 << 20),
        cost_estimate=pl.CostEstimate(
            flops=16 * NEAR * NEAR * width,
            bytes_accessed=7 * rows * width,
            transcendentals=NEAR * NEAR * HEADS,
        ),
        name="edge_attention",
    )(lo, hi, q, k, v, far, near)


def last_kernel(layout, frozen, own_down, inner, edges, *rest):
    refs, rest = rest[:-6], rest[-6:]
    merged, attended, factors, w, result, sems = rest
    shard, width = frozen.shape
    rows = result.shape[0]
    me = lax.axis_index("seq")
    kind = lax.axis_index("group")
    for ref, (swapped, masks) in zip(refs, layout):
        target = 1 - kind if swapped else kind
        for i, mask in enumerate(masks):
            at = pl.ds(pl.multiple_of((me ^ mask) * shard, shard), shard)
            factors[target, at, :] = ref[i]
    if not layout:
        factors = refs[0]
    down, up = factors.at[0], factors.at[1]
    parts = ((inner, FRAME), (edges, 0))
    reduced = [dot(att[...], down[...], NN).astype(BF16) for att, _ in parts]
    stores = []

    def store(source, target):
        stores.append(pltpu.make_async_copy(source, target, sems.at[len(stores)]))
        stores[-1].start()

    for first in range(0, width, CHUNK):
        part = pl.ds(first, CHUNK)
        factor = up[part, :]
        product = dot(own_down[...], factor, NT)
        w[:, part] = (frozen[:, part].astype(F32) + ADAPTER_SCALE * product).astype(BF16)
        store(w.at[:, part], merged.at[:, part])
        for narrow, (att, _) in zip(reduced, parts):
            value = att[:, part].astype(F32) + ADAPTER_SCALE * dot(narrow, factor, NT)
            value = value.astype(BF16)
            if att is inner:
                result[FRAME : rows - FRAME, part] = value
            else:
                result[0:FRAME, part] = value[:FRAME]
                result[rows - FRAME : rows, part] = value[FRAME:]
        store(result.at[:, part], attended.at[:, part])
    for copy in stores:
        copy.wait()


def last(frozen, own_down, inner, edges, layout, pieces):
    shard, width = frozen.shape
    rank = own_down.shape[1]
    rows = 2 * NEAR
    return pl.pallas_call(
        functools.partial(last_kernel, layout),
        out_shape=(
            jax.ShapeDtypeStruct((shard, width), BF16),
            jax.ShapeDtypeStruct((rows, width), BF16),
        ),
        in_specs=[VMEM] * (4 + len(pieces)),
        out_specs=(ANY, ANY),
        scratch_shapes=[
            pltpu.VMEM((2, width, rank), BF16),
            pltpu.VMEM((shard, width), BF16),
            pltpu.VMEM((rows, width), BF16),
            pltpu.SemaphoreType.DMA((2 * (width // CHUNK),)),
        ],
        compiler_params=pltpu.CompilerParams(vmem_limit_bytes=24 << 20),
        cost_estimate=pl.CostEstimate(
            flops=2 * (shard + 2 * rows) * width * rank,
            bytes_accessed=4 * (shard + rows) * width + 4 * width * rank,
            transcendentals=0,
        ),
        name="adapter_and_merge",
    )(frozen, own_down, inner, edges, *pieces)


def gather_factors(down, up, inner):
    count = lax.axis_size("seq")
    if lax.axis_size("group") != 2 or down.shape[0] % 32:
        both = lax.all_gather(jnp.stack([down, up]), "seq", axis=1, tiled=True)
        return [], [both], inner

    def swap(cells, mask):
        return lax.ppermute(cells, "seq", [(i, i ^ mask) for i in range(count)])

    def cross(cells):
        return lax.ppermute(cells, "group", [(0, 1), (1, 0)])

    cells = jnp.where(lax.axis_index("group") == 0, down, up)[None]
    masks = [0]
    steps = [2] + [count >> j for j in range(1, count.bit_length()) if count >> j > 2]
    for mask in steps[:-1]:
        cells = jnp.concatenate([cells, swap(cells, mask)])
        masks = masks + [have ^ mask for have in masks]
    cells, inner = lax.optimization_barrier((cells, inner))
    early = cross(cells)
    new = swap(cells, steps[-1])
    late = cross(new)
    cells = jnp.concatenate([cells, new])
    masks = masks + [have ^ steps[-1] for have in masks]
    other = jnp.concatenate([early, late])
    across = [mask ^ 1 for mask in masks]
    return (
        [(0, masks), (0, across), (1, masks), (1, across)],
        [cells, swap(cells, 1), other, swap(other, 1)],
        inner,
    )


def exchange_halos(k, v):
    count = lax.axis_size("seq")
    rows = k.shape[0]
    odd = lax.rem(lax.axis_index("seq"), 2)

    def rim(start):
        return jnp.stack([lax.dynamic_slice_in_dim(x, start, FRAME, 0) for x in (k, v)])

    links = [(i, i + 1) for i in range(1, count - 1, 2)]
    far = lax.ppermute(
        rim(odd * (rows - FRAME)), "seq", links + [(b, a) for a, b in links]
    )
    near = lax.ppermute(
        rim((1 - odd) * (rows - FRAME)), "seq", [(i, i ^ 1) for i in range(count)]
    )
    return far, near


def body(q, k, v, lo, hi, down, up, frozen):
    far, near = exchange_halos(k, v)
    inner = inner_attention(lo, hi, q, k, v)
    layout, pieces, inner = gather_factors(down, up.T, inner)
    edges = edge_attention(lo, hi, q, k, v, far, near)
    merged, attended = last(frozen, down, inner, edges, layout, pieces)
    return (attended, merged)


def solution(mesh):
    rows = P(("group", "seq"), None)
    flat = P(("group", "seq"))
    return jax.shard_map(
        body,
        mesh=mesh,
        in_specs=(rows, rows, rows, flat, flat, P("seq", None), P(None, "seq"), P("seq", None)),
        out_specs=(rows, rows),
        check_vma=False,
    )
```

time: 241 us -> 55.3 us (0.23)
  waiting for transfers between devices: 114 us -> 7.24 us
  matrix products: 42.2 us -> 0 us
  other arithmetic: 43.4 us -> 1.24 us
  starting transfers between devices: 6.72 us -> 27.8 us
  local copies, waits for them, and re-layouts: 19.3 us -> 2.16 us
  Pallas kernels: 0 us -> 15.8 us
  between operations: 14.1 us -> 0.82 us
    all_gather x2 -> x0, waiting for transfers between devices: 72.3 us -> none  [the longest x1 72.3 us: body(): lax.all_gather(adapter_up_factor, 'seq', axis=1, tiled=True)]
    dot_general x4 -> x0, matrix products: 42.2 us -> none  [the longest x1 16.1 us: attend(): jnp.einsum('hts,shd->thd', weights_bf, value_heads, preferred_element_typ...]
    ppermute x2 -> x9, waiting for transfers between devices: 41.2 us -> 7.24 us  [the longest x5 7.23 us: swap(): return lax.ppermute(cells, 'seq', [(i, i ^ mask) for i in range(count)])]
    sub x1 -> x0, other arithmetic: 31.4 us -> none  [attend(): weights = jnp.exp(scores - highest)]
    ppermute x2 -> x9, starting transfers between devices: 6.65 us -> 27.8 us  [the longest x5 20.1 us: swap(): return lax.ppermute(cells, 'seq', [(i, i ^ mask) for i in range(count)])]
    pallas_call x0 -> x3, Pallas kernels: none -> 15.8 us  [the longest x1 6.09 us: inner_attention(): pl.pallas_call(inner_kernel, grid=(width // CHUNK,), out_shape=jax.ShapeD...]
    unnamed x16, local copies, waits for them, and re-layouts: 8.99 us -> 0.07 us
    concatenate x1 -> x2, other arithmetic: 6.39 us -> 0.05 us  [gather_factors(): cells = jnp.concatenate([cells, swap(cells, mask)])]
  transfers between devices with their start and end apart: 4 -> 9, of which waited for: 2 -> 2; matrix products, arithmetic and copies ran while one was open for 35% -> 4% of each run, Pallas kernels for 0% -> 22%
where the time goes in v3:
time: 55.3 us; the launch traced here: 55.1 us
  starting transfers between devices  27.8 us (50%)
  Pallas kernels  15.8 us (29%)
  waiting for transfers between devices  7.24 us (13%)
  local copies, waits for them, and re-layouts  2.16 us (4%)
  other arithmetic  1.24 us (2%)
  between operations  0.82 us (1%)
    ppermute x5, starting transfers between devices, swap(): return lax.ppermute(cells, 'seq', [(i, i ^ mask) for i in range(count)])  20.1 us
    ppermute x5, waiting for transfers between devices, swap(): return lax.ppermute(cells, 'seq', [(i, i ^ mask) for i in range(count)])  7.23 us
    pallas_call x1, Pallas kernels, inner_attention(): pl.pallas_call(inner_kernel, grid=(width // CHUNK,), out_shape=jax.ShapeD...  6.09 us
    pallas_call x1, Pallas kernels, edge_attention(): pl.pallas_call(edge_kernel, out_shape=jax.ShapeDtypeStruct((NEAR, width),...  5.87 us
    ppermute x1, starting transfers between devices, exchange_halos(): lax.ppermute(rim(odd * (rows - FRAME)), 'seq', links + [(b, a) for a, b i...  5.27 us
    pallas_call x1, Pallas kernels, last(): pl.pallas_call(functools.partial(last_kernel, layout), out_shape=(jax.Sha...  3.83 us
    ppermute x2, starting transfers between devices, cross(): return lax.ppermute(cells, 'group', [(0, 1), (1, 0)])  2.41 us
    another operation x1, local copies, waits for them, and re-layouts, rim(): jnp.stack([lax.dynamic_slice_in_dim(x, start, FRAME, 0) for x in (k, v)])  2 us
  transfers between devices with their start and end apart: 9, of which 2 were waited for; matrix products, arithmetic and copies ran while one was open for 4% of the time, Pallas kernels for 22%

profile of v3, /device:TPU:1, one launch (start us, length us, event | category | flops | bytes accessed | tf_op | source)
XLA Modules:
  0.0 55.1 jit_solution(14198799104313200773)
XLA Ops:
  0.6 0.9 %fusion = bf16[1,320,128]{2,1,0:T(8,128)(2,1)S(1)} fusion(bf16[320,128]{1,0:T(8,128)(2,1)} %own_down.1, bf16[128,320]{0,1:T(8,128)(2,1)} %param.14, pred[]{:T(512)S(6)} %eq.3), kind=kLoop, calls=%fused_computation.9 | loop fusion | flops 40960 | bytes 245761 | tf_op jit(solution)/shard_map/broadcast_in_dim | solution.py:243
  1.6 2.1 %collective-permute-start = (bf16[1,320,128]{2,1,0:T(8,128)(2,1)S(1)}, bf16[1,320,128]{2,1,0:T(8,128)(2,1)S(1)}, u32[]{:S(2)}, u32[]{:S(2)}) collective-permute-start(bf16[1,320,128]{2,1,0:T(8,128)(2,1)S(1)} %fusion), channel_id=1, source_target_pairs={{0,2},{1,3},{2,0},{3,1},{4,6},{5,7},{6,4},{7,5},{8,10},{9,11},{10,... | collective-permute-start | bytes 245768 | tf_op jit(solution)/shard_map/ppermute | solution.py:238
  3.7 0.0 copy-start.1
  3.7 0.0 copy-start.2
  3.7 2.0 %dynamic-slice_bitcast_fusion = (bf16[1,64,5120]{2,1,0:T(8,128)(2,1)S(1)}, bf16[1,64,5120]{2,1,0:T(8,128)(2,1)S(1)}, bf16[1,64,5120]{2,1,0:T(8,128)(2,1)S(1)}, bf16[1,64,5120]{2,1,0:T(8,128)(2,1)S(1)}) fusion(bf16[256,5120]{1,0:T(8,128)(2,1)} %v.1, s32[]{:T(128)S(6)} %select_n.19, s32[]{:T(128)S(6)} %select_n.18, bf16[256,5120]{1,0:T(8,128)(2,1)} %k.1), kind=kLoop, calls=%fused_computation.2 | loop fusion | bytes 5242888 | tf_op jit(solution)/shard_map/stack | solution.py:270
  5.7 0.2 collective-permute-done
  5.9 0.0 copy-start.5
  5.9 0.0 copy-start.6
  5.9 2.3 %collective-permute-start.1 = (bf16[2,320,128]{2,1,0:T(8,128)(2,1)S(1)}, bf16[2,320,128]{2,1,0:T(8,128)(2,1)S(1)}, u32[]{:S(2)}, u32[]{:S(2)}) collective-permute-start(bf16[2,320,128]{2,1,0:T(8,128)(2,1)S(1)} %pad_maximum_fusion.3), channel_id=1, source_target_pairs={{0,8},{1,9},{2,10},{3,11},{4,12},{5,13},{6,14},{7,15},{8,0},{9,1},... | collective-permute-start | bytes 491528 | tf_op jit(solution)/shard_map/ppermute | solution.py:238
  8.2 0.0 copy-start
  8.2 0.1 pad_maximum_fusion
  8.3 5.3 %collective-permute-start.2 = (bf16[2,64,5120]{2,1,0:T(8,128)(2,1)S(1)}, bf16[2,64,5120]{2,1,0:T(8,128)(2,1)S(1)}, u32[]{:S(2)}, u32[]{:S(2)}) collective-permute-start(bf16[2,64,5120]{2,1,0:T(8,128)(2,1)S(1)} %pad_maximum_fusion), channel_id=1, source_target_pairs={{1,2},{3,4},{5,6},{7,8},{9,10},{11,12},{13,14},{2,1},{4,3},{6,5},{... | collective-permute-start | bytes 3932168 | tf_op jit(solution)/shard_map/ppermute | solution.py:273
  13.6 0.0 copy-done.1
  13.6 0.0 copy-done.2
  13.6 0.0 copy-done.5
  13.6 0.0 copy-done.6
  13.6 0.0 copy-done
  13.6 6.1 %inner_attention.1.inner = bf16[128,5120]{1,0:T(8,128)(2,1)S(1)} custom-call(s32[256]{0:T(256)S(1)} %copy-done.5, s32[256]{0:T(256)S(1)} %copy-done.6, bf16[256,5120]{1,0:T(8,128)(2,1)S(1)} %copy-done.2, bf16[256,5120]{1,0:T(8,128)(2,1)S(1)} %copy-done, bf16[256,5120]{1,0:T(8,128)(2,1)S(1)} %copy-done.1), custom_call_target="tpu_custom_call" | custom-call | flops 1342177280 | bytes 9175040 | tf_op jit(solution)/shard_map/inner_attention/pallas_call | solution.py:83
  19.7 0.0 collective-permute-done.1
  19.8 1.4 %collective-permute-start.4 = (bf16[4,320,128]{2,1,0:T(8,128)(2,1)S(1)}, bf16[4,320,128]{2,1,0:T(8,128)(2,1)S(1)}, u32[]{:S(2)}, u32[]{:S(2)}) collective-permute-start(bf16[4,320,128]{2,1,0:T(8,128)(2,1)S(1)} %pad_maximum_fusion.2), channel_id=1, source_target_pairs={{0,4},{1,5},{2,6},{3,7},{4,0},{5,1},{6,2},{7,3},{8,12},{9,13},{10,... | collective-permute-start | bytes 983048 | tf_op jit(solution)/shard_map/ppermute | solution.py:238
  21.1 0.1 pad_maximum_fusion.1
  21.3 0.1 collective-permute-start.3
  21.3 1.2 %collective-permute-start.6 = (bf16[4,320,128]{2,1,0:T(8,128)(2,1)S(1)}, bf16[4,320,128]{2,1,0:T(8,128)(2,1)S(1)}, u32[]{:S(2)}, u32[]{:S(2)}) collective-permute-start(bf16[4,320,128]{2,1,0:T(8,128)(2,1)S(1)} %pad_maximum_fusion.2), channel_id=1, source_target_pairs={{0,16},{16,0},{1,17},{17,1},{2,18},{18,2},{3,19},{19,3},{4,20},{20... | collective-permute-start | bytes 983048 | tf_op jit(solution)/shard_map/ppermute | solution.py:241
  22.6 7.1 %collective-permute-done.4 = bf16[4,320,128]{2,1,0:T(8,128)(2,1)S(1)} collective-permute-done((bf16[4,320,128]{2,1,0:T(8,128)(2,1)S(1)}, bf16[4,320,128]{2,1,0:T(8,128)(2,1)S(1)}, u32[]{:S(2)}, u32[]{:S(2)}) %collective-permute-start.4) | collective-permute-done | bytes 327712 | tf_op jit(solution)/shard_map/ppermute | solution.py:238
  29.6 1.2 %collective-permute-start.7 = (bf16[4,320,128]{2,1,0:T(8,128)(2,1)S(1)}, bf16[4,320,128]{2,1,0:T(8,128)(2,1)S(1)}, u32[]{:S(2)}, u32[]{:S(2)}) collective-permute-start(bf16[4,320,128]{2,1,0:T(8,128)(2,1)S(1)} %collective-permute-done.4), channel_id=1, source_target_pairs={{0,16},{16,0},{1,17},{17,1},{2,18},{18,2},{3,19},{19,3},{4,20},{20... | collective-permute-start | bytes 983048 | tf_op jit(solution)/shard_map/ppermute | solution.py:241
  30.9 8.7 %collective-permute-start.5 = (bf16[8,320,128]{2,1,0:T(8,128)(2,1)S(1)}, bf16[8,320,128]{2,1,0:T(8,128)(2,1)S(1)}, u32[]{:S(2)}, u32[]{:S(2)}) collective-permute-start(bf16[8,320,128]{2,1,0:T(8,128)(2,1)S(1)} %constant_dynamic-update-slice_fusion.rest_0_), channel_id=1, source_target_pairs={{0,1},{1,0},{2,3},{3,2},{4,5},{5,4},{6,7},{7,6},{8,9},{9,8},{10,11... | collective-permute-start | bytes 1966088 | tf_op jit(solution)/shard_map/ppermute | solution.py:238
  39.6 0.0 collective-permute-done.6
  39.6 0.0 collective-permute-done.7
  39.7 0.0 copy-start.4
  39.7 5.6 %collective-permute-start.8 = (bf16[8,320,128]{2,1,0:T(8,128)(2,1)S(1)}, bf16[8,320,128]{2,1,0:T(8,128)(2,1)S(1)}, u32[]{:S(2)}, u32[]{:S(2)}) collective-permute-start(bf16[8,320,128]{2,1,0:T(8,128)(2,1)S(1)} %constant_dynamic-update-slice_fusion.2.rest_2_), channel_id=1, source_target_pairs={{0,1},{1,0},{2,3},{3,2},{4,5},{5,4},{6,7},{7,6},{8,9},{9,8},{10,11... | collective-permute-start | bytes 1966088 | tf_op jit(solution)/shard_map/ppermute | solution.py:238
  45.3 0.0 collective-permute-done.2.far
  45.3 0.0 collective-permute-done.3.near
  45.3 0.0 copy-start.3
  45.3 5.9 %edge_attention.1.edges = bf16[128,5120]{1,0:T(8,128)(2,1)S(1)} custom-call(s32[256]{0:T(256)S(1)} %copy-done.5, s32[256]{0:T(256)S(1)} %copy-done.6, bf16[256,5120]{1,0:T(8,128)(2,1)S(1)} %copy-done.2, bf16[256,5120]{1,0:T(8,128)(2,1)S(1)} %copy-done, bf16[256,5120]{1,0:T(8,128)(2,1)S(1)} %copy-done.1, bf16[2,64,5120]{2,1,0:T(8,128)(2,1)S(1)} %collective-permute-done.2.far, ...), custom_call_target="tpu_custom_call" | custom-call | flops 1342177280 | bytes 9175040 | tf_op jit(solution)/shard_map/edge_attention/pallas_call | solution.py:146
  51.2 0.0 collective-permute-done.5.rest_1_
  51.2 0.0 collective-permute-done.8.rest_3_
  51.2 0.0 copy-done.4
  51.2 0.0 copy-done.3
  51.3 3.8 %adapter_and_merge.1 = (bf16[320,5120]{1,0:T(8,128)(2,1)}, bf16[256,5120]{1,0:T(8,128)(2,1)}) custom-call(bf16[320,5120]{1,0:T(8,128)(2,1)S(1)} %copy-done.3, bf16[320,128]{1,0:T(8,128)(2,1)S(1)} %copy-done.4, bf16[128,5120]{1,0:T(8,128)(2,1)S(1)} %inner_attention.1.inner, bf16[128,5120]{1,0:T(8,128)(2,1)S(1)} %edge_attention.1.edges, ...), custom_call_target="tpu_custom_call" | custom-call | flops 1090519040 | bytes 14417920 | tf_op jit(solution)/shard_map/adapter_and_merge/pallas_call | solution.py:207
  (6 shorter events, 0.2 us)
Async XLA Ops:
  1.6 4.3 %collective-permute-start = (bf16[1,320,128]{2,1,0:T(8,128)(2,1)S(1)}, bf16[1,320,128]{2,1,0:T(8,128)(2,1)S(1)}, u32[]{:S(2)}, u32[]{:S(2)}) collective-permute-start(bf16[1,320,128]{2,1,0:T(8,128)(2,1)S(1)} %fusion), channel_id=1, source_target_pairs={{0,2},{1,3},{2,0},{3,1},{4,6},{5,7},{6,4},{7,5},{8,10},{9,11},{10,... | collective-permute-start | bytes 245768 | tf_op jit(solution)/shard_map/ppermute | solution.py:238
  3.7 9.9 %copy-start.1 = (bf16[256,5120]{1,0:T(8,128)(2,1)S(1)}, bf16[256,5120]{1,0:T(8,128)(2,1)}, u32[]{:S(2)}) copy-start(bf16[256,5120]{1,0:T(8,128)(2,1)} %v.1) | copy-start | bytes 7864324
  3.7 9.9 %copy-start.2 = (bf16[256,5120]{1,0:T(8,128)(2,1)S(1)}, bf16[256,5120]{1,0:T(8,128)(2,1)}, u32[]{:S(2)}) copy-start(bf16[256,5120]{1,0:T(8,128)(2,1)} %q.1) | copy-start | bytes 7864324
  5.9 7.7 %copy-start.5 = (s32[256]{0:T(256)S(1)}, s32[256]{0:T(256)}, u32[]{:S(2)}) copy-start(s32[256]{0:T(256)} %lo_ref.3) | copy-start | bytes 3076
  5.9 7.7 %copy-start.6 = (s32[256]{0:T(256)S(1)}, s32[256]{0:T(256)}, u32[]{:S(2)}) copy-start(s32[256]{0:T(256)} %hi_ref.3) | copy-start | bytes 3076
  5.9 13.8 %collective-permute-start.1 = (bf16[2,320,128]{2,1,0:T(8,128)(2,1)S(1)}, bf16[2,320,128]{2,1,0:T(8,128)(2,1)S(1)}, u32[]{:S(2)}, u32[]{:S(2)}) collective-permute-start(bf16[2,320,128]{2,1,0:T(8,128)(2,1)S(1)} %pad_maximum_fusion.3), channel_id=1, source_target_pairs={{0,8},{1,9},{2,10},{3,11},{4,12},{5,13},{6,14},{7,15},{8,0},{9,1},... | collective-permute-start | bytes 491528 | tf_op jit(solution)/shard_map/ppermute | solution.py:238
  8.2 5.4 %copy-start = (bf16[256,5120]{1,0:T(8,128)(2,1)S(1)}, bf16[256,5120]{1,0:T(8,128)(2,1)}, u32[]{:S(2)}) copy-start(bf16[256,5120]{1,0:T(8,128)(2,1)} %k.1) | copy-start | bytes 7864324
  8.3 37.0 %collective-permute-start.2 = (bf16[2,64,5120]{2,1,0:T(8,128)(2,1)S(1)}, bf16[2,64,5120]{2,1,0:T(8,128)(2,1)S(1)}, u32[]{:S(2)}, u32[]{:S(2)}) collective-permute-start(bf16[2,64,5120]{2,1,0:T(8,128)(2,1)S(1)} %pad_maximum_fusion), channel_id=1, source_target_pairs={{1,2},{3,4},{5,6},{7,8},{9,10},{11,12},{13,14},{2,1},{4,3},{6,5},{... | collective-permute-start | bytes 3932168 | tf_op jit(solution)/shard_map/ppermute | solution.py:273
  19.8 9.9 %collective-permute-start.4 = (bf16[4,320,128]{2,1,0:T(8,128)(2,1)S(1)}, bf16[4,320,128]{2,1,0:T(8,128)(2,1)S(1)}, u32[]{:S(2)}, u32[]{:S(2)}) collective-permute-start(bf16[4,320,128]{2,1,0:T(8,128)(2,1)S(1)} %pad_maximum_fusion.2), channel_id=1, source_target_pairs={{0,4},{1,5},{2,6},{3,7},{4,0},{5,1},{6,2},{7,3},{8,12},{9,13},{10,... | collective-permute-start | bytes 983048 | tf_op jit(solution)/shard_map/ppermute | solution.py:238
  21.3 24.1 %collective-permute-start.3 = (bf16[2,64,5120]{2,1,0:T(8,128)(2,1)S(1)}, bf16[2,64,5120]{2,1,0:T(8,128)(2,1)S(1)}, u32[]{:S(2)}, u32[]{:S(2)}) collective-permute-start(bf16[2,64,5120]{2,1,0:T(8,128)(2,1)S(1)} %pad_maximum_fusion.1), channel_id=1, source_target_pairs={{0,1},{1,0},{2,3},{3,2},{4,5},{5,4},{6,7},{7,6},{8,9},{9,8},{10,11... | collective-permute-start | bytes 3932168 | tf_op jit(solution)/shard_map/ppermute | solution.py:276
  21.3 18.3 %collective-permute-start.6 = (bf16[4,320,128]{2,1,0:T(8,128)(2,1)S(1)}, bf16[4,320,128]{2,1,0:T(8,128)(2,1)S(1)}, u32[]{:S(2)}, u32[]{:S(2)}) collective-permute-start(bf16[4,320,128]{2,1,0:T(8,128)(2,1)S(1)} %pad_maximum_fusion.2), channel_id=1, source_target_pairs={{0,16},{16,0},{1,17},{17,1},{2,18},{18,2},{3,19},{19,3},{4,20},{20... | collective-permute-start | bytes 983048 | tf_op jit(solution)/shard_map/ppermute | solution.py:241
  29.6 10.0 %collective-permute-start.7 = (bf16[4,320,128]{2,1,0:T(8,128)(2,1)S(1)}, bf16[4,320,128]{2,1,0:T(8,128)(2,1)S(1)}, u32[]{:S(2)}, u32[]{:S(2)}) collective-permute-start(bf16[4,320,128]{2,1,0:T(8,128)(2,1)S(1)} %collective-permute-done.4), channel_id=1, source_target_pairs={{0,16},{16,0},{1,17},{17,1},{2,18},{18,2},{3,19},{19,3},{4,20},{20... | collective-permute-start | bytes 983048 | tf_op jit(solution)/shard_map/ppermute | solution.py:241
  30.9 20.3 %collective-permute-start.5 = (bf16[8,320,128]{2,1,0:T(8,128)(2,1)S(1)}, bf16[8,320,128]{2,1,0:T(8,128)(2,1)S(1)}, u32[]{:S(2)}, u32[]{:S(2)}) collective-permute-start(bf16[8,320,128]{2,1,0:T(8,128)(2,1)S(1)} %constant_dynamic-update-slice_fusion.rest_0_), channel_id=1, source_target_pairs={{0,1},{1,0},{2,3},{3,2},{4,5},{5,4},{6,7},{7,6},{8,9},{9,8},{10,11... | collective-permute-start | bytes 1966088 | tf_op jit(solution)/shard_map/ppermute | solution.py:238
  39.7 11.5 %copy-start.4 = (bf16[320,128]{1,0:T(8,128)(2,1)S(1)}, bf16[320,128]{1,0:T(8,128)(2,1)}, u32[]{:S(2)}) copy-start(bf16[320,128]{1,0:T(8,128)(2,1)} %own_down.1) | copy-start | bytes 245764
  39.7 11.5 %collective-permute-start.8 = (bf16[8,320,128]{2,1,0:T(8,128)(2,1)S(1)}, bf16[8,320,128]{2,1,0:T(8,128)(2,1)S(1)}, u32[]{:S(2)}, u32[]{:S(2)}) collective-permute-start(bf16[8,320,128]{2,1,0:T(8,128)(2,1)S(1)} %constant_dynamic-update-slice_fusion.2.rest_2_), channel_id=1, source_target_pairs={{0,1},{1,0},{2,3},{3,2},{4,5},{5,4},{6,7},{7,6},{8,9},{9,8},{10,11... | collective-permute-start | bytes 1966088 | tf_op jit(solution)/shard_map/ppermute | solution.py:238
  45.3 5.9 %copy-start.3 = (bf16[320,5120]{1,0:T(8,128)(2,1)S(1)}, bf16[320,5120]{1,0:T(8,128)(2,1)}, u32[]{:S(2)}) copy-start(bf16[320,5120]{1,0:T(8,128)(2,1)} %frozen.1) | copy-start | bytes 9830404

commit v4 on v3

v4 whole, which is shorter than its diff:
```python
import functools

import jax
import jax.numpy as jnp
from jax import lax
from jax.experimental import pallas as pl
from jax.experimental.pallas import tpu as pltpu
from jax.sharding import PartitionSpec as P

MODEL_WIDTH = 5120
HEADS = 40
HD = 128
FRAME = 64
NEAR = 2 * FRAME
CHUNK = 512
SCORE_SCALE = HD ** (-0.5) * 1.4426950408889634
ADAPTER_SCALE = MODEL_WIDTH ** (-0.5)
FAR = -1e30
NT = (((1,), (1,)), ((), ()))
NN = (((1,), (0,)), ((), ()))
BF16 = jnp.bfloat16
F32 = jnp.float32
ANY = pl.BlockSpec(memory_space=pl.ANY)
SMEM = pl.BlockSpec(memory_space=pltpu.SMEM)
VMEM = pl.BlockSpec(memory_space=pltpu.VMEM)


def dot(a, b, dims):
    return lax.dot_general(a, b, dims, preferred_element_type=F32)


def clip_bias(lo, hi):
    position = lax.broadcasted_iota(jnp.int32, (NEAR, NEAR), 1)
    return jnp.where(position < hi - lo, 0.0, FAR).astype(F32)


def diagonal(top, bottom):
    zeros = jnp.zeros((FRAME, NEAR), BF16)
    return jnp.concatenate(
        [jnp.concatenate([top, zeros], axis=1), jnp.concatenate([zeros, bottom], axis=1)]
    )


def attend(loads):
    ones = jnp.ones((NEAR, HD), BF16)
    scores = []
    for load_q, load_k, _, bias in loads:
        q = load_q()
        scores.append(dot(diagonal(q[:, :HD], q[:, HD:]), load_k(), NT) * SCORE_SCALE + bias)
    weights = [jnp.exp2(s - jnp.max(s, axis=-1, keepdims=True)).astype(BF16) for s in scores]
    results = []
    for w, (_, _, load_v, _) in zip(weights, loads):
        v = load_v()
        values = jnp.concatenate(
            [jnp.concatenate([v[:, at : at + HD], ones], axis=1) for at in (0, HD)]
        )
        mixed = dot(diagonal(w[:FRAME], w[FRAME:]), values, NN)
        mixed = (mixed[:, :HD] * (1.0 / mixed[:, HD:])).astype(BF16)
        results.append(jnp.concatenate([mixed[:FRAME], mixed[FRAME:]], axis=1))
    return results


def inner_kernel(lo_ref, hi_ref, q_ref, k_ref, v_ref, o_ref):
    rows = q_ref.shape[0]
    base = lax.axis_index("seq") * rows
    loads, targets = [], []
    for row in (FRAME, NEAR):
        lo, hi = lo_ref[row], hi_ref[row]
        keys = pl.ds(pl.multiple_of(lo - base, FRAME), NEAR)
        bias = clip_bias(lo, hi)
        for col in range(0, CHUNK, 2 * HD):
            part = slice(col, col + 2 * HD)
            targets.append((slice(row - FRAME, row), part))
            loads.append(
                (
                    lambda row=row, part=part: q_ref[row : row + FRAME, part],
                    lambda keys=keys, part=part: k_ref[keys, part],
                    lambda keys=keys, part=part: v_ref[keys, part],
                    bias,
                )
            )
    for target, result in zip(targets, attend(loads)):
        o_ref[target] = result


def inner_attention(lo, hi, q, k, v):
    rows, width = q.shape
    block = pl.BlockSpec((rows, CHUNK), lambda i: (0, i))
    return pl.pallas_call(
        inner_kernel,
        grid=(width // CHUNK,),
        out_shape=jax.ShapeDtypeStruct((NEAR, width), BF16),
        in_specs=[SMEM, SMEM, block, block, block],
        out_specs=pl.BlockSpec((NEAR, CHUNK), lambda i: (0, i)),
        compiler_params=pltpu.CompilerParams(vmem_limit_bytes=16 << 20),
        cost_estimate=pl.CostEstimate(
            flops=16 * NEAR * NEAR * width,
            bytes_accessed=7 * rows * width,
            transcendentals=NEAR * NEAR * HEADS,
        ),
        name="inner_attention",
    )(lo, hi, q, k, v)


def edge_kernel(is_near, lo_ref, hi_ref, q, k, v, *rest):
    halos, out = rest[:-1], rest[-1]
    rows, width = q.shape
    me = lax.axis_index("seq")
    base = me * rows
    right = lax.rem(me, 2) == (0 if is_near else 1)
    row = pl.multiple_of(jnp.where(right, rows - FRAME, 0), FRAME)
    first = pl.multiple_of(jnp.where(right, rows - NEAR, 0), NEAR)
    second = pl.multiple_of(first + FRAME, FRAME)
    lo, hi = lo_ref[row], hi_ref[row]
    before = lo < base
    after = jnp.logical_and(right, lo == base + rows - FRAME)
    direct = lax.rem(lax.div(me + 1, 2), 2) == 1

    def window(ref, kind, part):
        halo = halos[0][kind, :, part]
        if len(halos) == 2:
            halo = jnp.where(direct, halo, halos[1][kind, :, part])
        one, two = ref[pl.ds(first, FRAME), part], ref[pl.ds(second, FRAME), part]
        return jnp.concatenate(
            [
                jnp.where(before, halo, jnp.where(after, two, one)),
                jnp.where(before, one, jnp.where(after, halo, two)),
            ]
        )

    bias = clip_bias(lo, hi)

    def step(i, _):
        loads, parts = [], []
        for col in range(0, 2 * CHUNK, 2 * HD):
            part = pl.ds(pl.multiple_of(i * 2 * CHUNK + col, 2 * HD), 2 * HD)
            parts.append(part)
            loads.append(
                (
                    lambda part=part: q[pl.ds(row, FRAME), part],
                    lambda part=part: window(k, 0, part),
                    lambda part=part: window(v, 1, part),
                    bias,
                )
            )
        for part, result in zip(parts, attend(loads)):
            out[:, part] = result
        return 0

    lax.fori_loop(0, width // (2 * CHUNK), step, 0)


def edge_attention(lo, hi, q, k, v, *halos):
    rows, width = q.shape
    is_near = len(halos) == 1
    return pl.pallas_call(
        functools.partial(edge_kernel, is_near),
        out_shape=jax.ShapeDtypeStruct((FRAME, width), BF16),
        in_specs=[SMEM, SMEM] + [VMEM] * (3 + len(halos)),
        out_specs=VMEM,
        compiler_params=pltpu.CompilerParams(vmem_limit_bytes=20 << 20),
        cost_estimate=pl.CostEstimate(
            flops=8 * NEAR * NEAR * width,
            bytes_accessed=7 * rows * width,
            transcendentals=FRAME * NEAR * HEADS,
        ),
        name="near_edge_attention" if is_near else "far_edge_attention",
    )(lo, hi, q, k, v, *halos)


def last_kernel(layout, frozen, own_down, inner, near, far, *rest):
    refs, rest = rest[:-6], rest[-6:]
    merged, attended, factors, w, result, sems = rest
    shard, width = frozen.shape
    rows = result.shape[0]
    me = lax.axis_index("seq")
    kind = lax.axis_index("group")
    for ref, (swapped, masks) in zip(refs, layout):
        target = 1 - kind if swapped else kind
        for i, mask in enumerate(masks):
            at = pl.ds(pl.multiple_of((me ^ mask) * shard, shard), shard)
            factors[target, at, :] = ref[i]
    if not layout:
        factors = refs[0]
    down, up = factors.at[0], factors.at[1]
    right = lax.rem(me, 2) == 0
    near_row = pl.multiple_of(jnp.where(right, rows - FRAME, 0), FRAME)
    far_row = pl.multiple_of(jnp.where(right, 0, rows - FRAME), FRAME)
    parts = ((inner, FRAME), (near, near_row), (far, far_row))
    reduced = [dot(att[...], down[...], NN).astype(BF16) for att, _ in parts]
    stores = []

    def store(source, target):
        stores.append(pltpu.make_async_copy(source, target, sems.at[len(stores)]))
        stores[-1].start()

    for first in range(0, width, CHUNK):
        part = pl.ds(first, CHUNK)
        factor = up[part, :]
        product = dot(own_down[...], factor, NT)
        w[:, part] = (frozen[:, part].astype(F32) + ADAPTER_SCALE * product).astype(BF16)
        store(w.at[:, part], merged.at[:, part])
        for narrow, (att, row) in zip(reduced, parts):
            value = att[:, part].astype(F32) + ADAPTER_SCALE * dot(narrow, factor, NT)
            result[pl.ds(row, att.shape[0]), part] = value.astype(BF16)
        store(result.at[:, part], attended.at[:, part])
    for copy in stores:
        copy.wait()


def last(frozen, own_down, inner, near, far, layout, pieces):
    shard, width = frozen.shape
    rank = own_down.shape[1]
    rows = 2 * NEAR
    return pl.pallas_call(
        functools.partial(last_kernel, layout),
        out_shape=(
            jax.ShapeDtypeStruct((shard, width), BF16),
            jax.ShapeDtypeStruct((rows, width), BF16),
        ),
        in_specs=[VMEM] * (5 + len(pieces)),
        out_specs=(ANY, ANY),
        scratch_shapes=[
            pltpu.VMEM((2, width, rank), BF16),
            pltpu.VMEM((shard, width), BF16),
            pltpu.VMEM((rows, width), BF16),
            pltpu.SemaphoreType.DMA((2 * (width // CHUNK),)),
        ],
        compiler_params=pltpu.CompilerParams(vmem_limit_bytes=24 << 20),
        cost_estimate=pl.CostEstimate(
            flops=2 * (shard + 2 * rows) * width * rank,
            bytes_accessed=4 * (shard + rows) * width + 4 * width * rank,
            transcendentals=0,
        ),
        name="adapter_and_merge",
    )(frozen, own_down, inner, near, far, *pieces)


def body(q, k, v, lo, hi, down, up, frozen):
    count = lax.axis_size("seq")
    rows = k.shape[0]
    odd = lax.rem(lax.axis_index("seq"), 2)

    def rim(start):
        return jnp.stack([lax.dynamic_slice_in_dim(x, start, FRAME, 0) for x in (k, v)])

    def send(cells, pairs):
        return lax.ppermute(cells, "seq", pairs + [(b, a) for a, b in pairs])

    def swap(cells, mask):
        return send(cells, [(i, i ^ mask) for i in range(count) if not i & mask])

    def cross(cells):
        return lax.ppermute(cells, "group", [(0, 1), (1, 0)])

    far_rim = rim(odd * (rows - FRAME))
    direct = send(far_rim, [(i, i + 1) for i in range(1, count - 1, 4)])
    near = swap(rim((1 - odd) * (rows - FRAME)), 1)
    distant = [(i, i + 1) for i in range(3, count - 1, 4)]
    up = up.T
    if lax.axis_size("group") != 2 or down.shape[0] % 32:
        both = lax.all_gather(jnp.stack([down, up]), "seq", axis=1, tiled=True)
        layout, pieces = [], [both]
        inner = inner_attention(lo, hi, q, k, v)
        near_edge = edge_attention(lo, hi, q, k, v, near)
        diagonal_halo = send(far_rim, distant)
    else:
        cells = jnp.where(lax.axis_index("group") == 0, down, up)[None]
        masks = [0]
        steps = [2] + [count >> j for j in range(1, count.bit_length()) if count >> j > 2]
        for mask in steps[:-1]:
            cells = jnp.concatenate([cells, swap(cells, mask)])
            masks = masks + [have ^ mask for have in masks]
        cells, far_rim, lo_inner = lax.optimization_barrier((cells, far_rim, lo))
        new = swap(cells, steps[-1])
        diagonal_halo = send(far_rim, distant)
        early = cross(cells)
        inner = inner_attention(lo_inner, hi, q, k, v)
        new, inner, lo_near = lax.optimization_barrier((new, inner, lo))
        late = cross(new)
        cells = jnp.concatenate([cells, new])
        masks = masks + [have ^ steps[-1] for have in masks]
        near_edge = edge_attention(lo_near, hi, q, k, v, near)
        other = jnp.concatenate([early, late])
        other, near_edge = lax.optimization_barrier((other, near_edge))
        across = [mask ^ 1 for mask in masks]
        layout = [(0, masks), (0, across), (1, masks), (1, across)]
        pieces = [cells, swap(cells, 1), other, swap(other, 1)]
    far_edge = edge_attention(lo, hi, q, k, v, direct, diagonal_halo)
    merged, attended = last(frozen, down, inner, near_edge, far_edge, layout, pieces)
    return (attended, merged)


def solution(mesh):
    rows = P(("group", "seq"), None)
    flat = P(("group", "seq"))
    return jax.shard_map(
        body,
        mesh=mesh,
        in_specs=(rows, rows, rows, flat, flat, P("seq", None), P(None, "seq"), P("seq", None)),
        out_specs=(rows, rows),
        check_vma=False,
    )
```

time: 55.3 us -> 58.5 us (1.058)
  the two profiles are of different devices: /device:TPU:1 before, /device:TPU:17 now
where the time goes in v4:
time: 58.5 us; the launch traced here: 58.3 us
  waiting for transfers between devices  23.4 us (40%)
  Pallas kernels  16.4 us (28%)
  starting transfers between devices  14.3 us (24%)
  local copies, waits for them, and re-layouts  2.1 us (4%)
  other arithmetic  1.3 us (2%)
  between operations  0.8 us (1%)
    ppermute x8, waiting for transfers between devices, send(): return lax.ppermute(cells, 'seq', pairs + [(b, a) for a, b in pairs])  15.3 us
    ppermute x8, starting transfers between devices, send(): return lax.ppermute(cells, 'seq', pairs + [(b, a) for a, b in pairs])  12.7 us
    ppermute x2, waiting for transfers between devices, cross(): return lax.ppermute(cells, 'group', [(0, 1), (1, 0)])  8.11 us
    pallas_call x2, Pallas kernels, edge_attention(): pl.pallas_call(functools.partial(edge_kernel, is_near), out_shape=jax.Sha...  6.11 us
    pallas_call x1, Pallas kernels, inner_attention(): pl.pallas_call(inner_kernel, grid=(width // CHUNK,), out_shape=jax.ShapeD...  6.07 us
    pallas_call x1, Pallas kernels, last(): pl.pallas_call(functools.partial(last_kernel, layout), out_shape=(jax.Sha...  4.25 us
    another operation x1, local copies, waits for them, and re-layouts, rim(): jnp.stack([lax.dynamic_slice_in_dim(x, start, FRAME, 0) for x in (k, v)])  2 us
    ppermute x2, starting transfers between devices, cross(): return lax.ppermute(cells, 'group', [(0, 1), (1, 0)])  1.6 us
  transfers between devices with their start and end apart: 10, of which 4 were waited for; matrix products, arithmetic and copies ran while one was open for 4% of the time, Pallas kernels for 21%

profile of v4, /device:TPU:17, one launch (start us, length us, event | category | flops | bytes accessed | tf_op | source)
XLA Modules:
  0.0 58.3 jit_solution(898586671132510687)
XLA Ops:
  0.6 0.9 %fusion = bf16[1,320,128]{2,1,0:T(8,128)(2,1)S(1)} fusion(bf16[320,128]{1,0:T(8,128)(2,1)} %own_down.1, bf16[128,320]{0,1:T(8,128)(2,1)} %param.14, pred[]{:T(512)S(6)} %eq.3), kind=kLoop, calls=%fused_computation.10 | loop fusion | flops 40960 | bytes 245761 | tf_op jit(solution)/shard_map/broadcast_in_dim | solution.py:268
  1.6 1.3 %collective-permute-start = (bf16[1,320,128]{2,1,0:T(8,128)(2,1)S(1)}, bf16[1,320,128]{2,1,0:T(8,128)(2,1)S(1)}, u32[]{:S(2)}, u32[]{:S(2)}) collective-permute-start(bf16[1,320,128]{2,1,0:T(8,128)(2,1)S(1)} %fusion), channel_id=1, source_target_pairs={{0,2},{1,3},{4,6},{5,7},{8,10},{9,11},{12,14},{13,15},{2,0},{3,1},... | collective-permute-start | bytes 245768 | tf_op jit(solution)/shard_map/ppermute | solution.py:248
  2.9 0.0 copy-start.2
  2.9 2.0 %dynamic-slice_bitcast_fusion = (bf16[1,64,5120]{2,1,0:T(8,128)(2,1)S(1)}, bf16[1,64,5120]{2,1,0:T(8,128)(2,1)S(1)}, bf16[1,64,5120]{2,1,0:T(8,128)(2,1)S(1)}, bf16[1,64,5120]{2,1,0:T(8,128)(2,1)S(1)}) fusion(bf16[256,5120]{1,0:T(8,128)(2,1)} %v.3, s32[]{:T(128)S(6)} %select_n.19, s32[]{:T(128)S(6)} %select_n.18, bf16[256,5120]{1,0:T(8,128)(2,1)} %k.3), kind=kLoop, calls=%fused_computation.3 | loop fusion | bytes 5242888 | tf_op jit(solution)/shard_map/stack | solution.py:245
  4.9 0.0 copy-start.1
  4.9 0.1 pad_maximum_fusion.1
  5.0 1.0 %collective-permute-start.5 = (bf16[2,64,5120]{2,1,0:T(8,128)(2,1)S(1)}, bf16[2,64,5120]{2,1,0:T(8,128)(2,1)S(1)}, u32[]{:S(2)}, u32[]{:S(2)}) collective-permute-start(bf16[2,64,5120]{2,1,0:T(8,128)(2,1)S(1)} %pad_maximum_fusion.1), channel_id=1, source_target_pairs={{0,1},{2,3},{4,5},{6,7},{8,9},{10,11},{12,13},{14,15},{1,0},{3,2},... | collective-permute-start | bytes 3932168 | tf_op jit(solution)/shard_map/ppermute | solution.py:248
  6.1 0.0 collective-permute-done
  6.1 0.1 collective-permute-start.1
  6.2 0.0 copy-start
  6.2 0.0 copy-start.5
  6.2 0.0 copy-start.6
  6.2 0.1 pad_maximum_fusion
  6.3 6.6 %collective-permute-done.1 = bf16[2,320,128]{2,1,0:T(8,128)(2,1)S(1)} collective-permute-done((bf16[2,320,128]{2,1,0:T(8,128)(2,1)S(1)}, bf16[2,320,128]{2,1,0:T(8,128)(2,1)S(1)}, u32[]{:S(2)}, u32[]{:S(2)}) %collective-permute-start.1) | collective-permute-done | bytes 163872 | tf_op jit(solution)/shard_map/ppermute | solution.py:248
  13.0 5.0 %collective-permute-start.2 = (bf16[4,320,128]{2,1,0:T(8,128)(2,1)S(1)}, bf16[4,320,128]{2,1,0:T(8,128)(2,1)S(1)}, u32[]{:S(2)}, u32[]{:S(2)}) collective-permute-start(bf16[4,320,128]{2,1,0:T(8,128)(2,1)S(1)} %pad_maximum_fusion.3), channel_id=1, source_target_pairs={{0,4},{1,5},{2,6},{3,7},{8,12},{9,13},{10,14},{11,15},{4,0},{5,1},... | collective-permute-start | bytes 983048 | tf_op jit(solution)/shard_map/ppermute | solution.py:248
  18.0 2.8 %collective-permute-start.6 = (bf16[2,64,5120]{2,1,0:T(8,128)(2,1)S(1)}, bf16[2,64,5120]{2,1,0:T(8,128)(2,1)S(1)}, u32[]{:S(2)}, u32[]{:S(2)}) collective-permute-start(bf16[2,64,5120]{2,1,0:T(8,128)(2,1)S(1)} %pad_maximum_fusion), channel_id=1, source_target_pairs={{1,2},{5,6},{9,10},{13,14},{2,1},{6,5},{10,9},{14,13},{17,18},{21,... | collective-permute-start | bytes 3932168 | tf_op jit(solution)/shard_map/ppermute | solution.py:248
  20.8 0.7 %collective-permute-start.7 = (bf16[2,64,5120]{2,1,0:T(8,128)(2,1)S(1)}, bf16[2,64,5120]{2,1,0:T(8,128)(2,1)S(1)}, u32[]{:S(2)}, u32[]{:S(2)}) collective-permute-start(bf16[2,64,5120]{2,1,0:T(8,128)(2,1)S(1)} %pad_maximum_fusion), channel_id=1, source_target_pairs={{3,4},{7,8},{11,12},{4,3},{8,7},{12,11},{19,20},{23,24},{27,28},{2... | collective-permute-start | bytes 3932168 | tf_op jit(solution)/shard_map/ppermute | solution.py:248
  21.5 1.2 %collective-permute-start.3 = (bf16[4,320,128]{2,1,0:T(8,128)(2,1)S(1)}, bf16[4,320,128]{2,1,0:T(8,128)(2,1)S(1)}, u32[]{:S(2)}, u32[]{:S(2)}) collective-permute-start(bf16[4,320,128]{2,1,0:T(8,128)(2,1)S(1)} %pad_maximum_fusion.3), channel_id=1, source_target_pairs={{0,16},{16,0},{1,17},{17,1},{2,18},{18,2},{3,19},{19,3},{4,20},{20... | collective-permute-start | bytes 983048 | tf_op jit(solution)/shard_map/ppermute | solution.py:254
  22.7 0.0 copy-done.2
  22.7 0.0 copy-done.1
  22.8 0.0 copy-done
  22.8 0.0 copy-done.5
  22.8 0.0 copy-done.6
  22.8 6.1 %inner_attention.1.inner = bf16[128,5120]{1,0:T(8,128)(2,1)S(1)} custom-call(s32[256]{0:T(256)S(1)} %copy-done.5, s32[256]{0:T(256)S(1)} %copy-done.6, bf16[256,5120]{1,0:T(8,128)(2,1)S(1)} %copy-done.2, bf16[256,5120]{1,0:T(8,128)(2,1)S(1)} %copy-done, bf16[256,5120]{1,0:T(8,128)(2,1)S(1)} %copy-done.1), custom_call_target="tpu_custom_call" | custom-call | flops 1342177280 | bytes 9175040 | tf_op jit(solution)/shard_map/inner_attention/pallas_call | solution.py:89
  28.8 0.0 collective-permute-done.2
  28.9 0.4 collective-permute-start.4
  29.3 1.7 %collective-permute-done.3 = bf16[4,320,128]{2,1,0:T(8,128)(2,1)S(1)} collective-permute-done((bf16[4,320,128]{2,1,0:T(8,128)(2,1)S(1)}, bf16[4,320,128]{2,1,0:T(8,128)(2,1)S(1)}, u32[]{:S(2)}, u32[]{:S(2)}) %collective-permute-start.3) | collective-permute-done | bytes 327712 | tf_op jit(solution)/shard_map/ppermute | solution.py:254
  31.0 0.7 %collective-permute-start.8 = (bf16[8,320,128]{2,1,0:T(8,128)(2,1)S(1)}, bf16[8,320,128]{2,1,0:T(8,128)(2,1)S(1)}, u32[]{:S(2)}, u32[]{:S(2)}) collective-permute-start(bf16[8,320,128]{2,1,0:T(8,128)(2,1)S(1)} %constant_dynamic-update-slice_fusion.rest_0_), channel_id=1, source_target_pairs={{0,1},{2,3},{4,5},{6,7},{8,9},{10,11},{12,13},{14,15},{1,0},{3,2},... | collective-permute-start | bytes 1966088 | tf_op jit(solution)/shard_map/ppermute | solution.py:248
  31.7 6.4 %collective-permute-done.4 = bf16[4,320,128]{2,1,0:T(8,128)(2,1)S(1)} collective-permute-done((bf16[4,320,128]{2,1,0:T(8,128)(2,1)S(1)}, bf16[4,320,128]{2,1,0:T(8,128)(2,1)S(1)}, u32[]{:S(2)}, u32[]{:S(2)}) %collective-permute-start.4) | collective-permute-done | bytes 327712 | tf_op jit(solution)/shard_map/ppermute | solution.py:254
  38.1 0.1 pad_maximum_fusion.2.rest_2_
  38.1 0.0 collective-permute-done.5.rest_0_
  38.1 3.0 %near_edge_attention.1.near = bf16[64,5120]{1,0:T(8,128)(2,1)S(1)} custom-call(s32[256]{0:T(256)S(1)} %copy-done.5, s32[256]{0:T(256)S(1)} %copy-done.6, bf16[256,5120]{1,0:T(8,128)(2,1)S(1)} %copy-done.2, bf16[256,5120]{1,0:T(8,128)(2,1)S(1)} %copy-done, bf16[256,5120]{1,0:T(8,128)(2,1)S(1)} %copy-done.1, ...), custom_call_target="tpu_custom_call" | custom-call | flops 671088640 | bytes 9175040 | tf_op jit(solution)/shard_map/near_edge_attention/pallas_call | solution.py:156
  41.2 0.0 copy-start.4
  41.2 1.1 %collective-permute-start.9 = (bf16[8,320,128]{2,1,0:T(8,128)(2,1)S(1)}, bf16[8,320,128]{2,1,0:T(8,128)(2,1)S(1)}, u32[]{:S(2)}, u32[]{:S(2)}) collective-permute-start(bf16[8,320,128]{2,1,0:T(8,128)(2,1)S(1)} %pad_maximum_fusion.2.rest_2_), channel_id=1, source_target_pairs={{0,1},{2,3},{4,5},{6,7},{8,9},{10,11},{12,13},{14,15},{1,0},{3,2},... | collective-permute-start | bytes 1966088 | tf_op jit(solution)/shard_map/ppermute | solution.py:248
  42.2 8.7 %collective-permute-done.6.rest_0_ = bf16[2,64,5120]{2,1,0:T(8,128)(2,1)S(1)} collective-permute-done((bf16[2,64,5120]{2,1,0:T(8,128)(2,1)S(1)}, bf16[2,64,5120]{2,1,0:T(8,128)(2,1)S(1)}, u32[]{:S(2)}, u32[]{:S(2)}) %collective-permute-start.6) | collective-permute-done | bytes 1310752 | tf_op jit(solution)/shard_map/ppermute | solution.py:248
  50.9 0.0 collective-permute-done.7.rest_1_
  50.9 0.0 copy-start.3
  50.9 3.1 %far_edge_attention.1.far = bf16[64,5120]{1,0:T(8,128)(2,1)S(1)} custom-call(s32[256]{0:T(256)S(1)} %copy-done.5, s32[256]{0:T(256)S(1)} %copy-done.6, bf16[256,5120]{1,0:T(8,128)(2,1)S(1)} %copy-done.2, bf16[256,5120]{1,0:T(8,128)(2,1)S(1)} %copy-done, bf16[256,5120]{1,0:T(8,128)(2,1)S(1)} %copy-done.1, ...), custom_call_target="tpu_custom_call" | custom-call | flops 671088640 | bytes 9175040 | tf_op jit(solution)/shard_map/far_edge_attention/pallas_call | solution.py:156
  54.0 0.0 collective-permute-done.8.rest_1_
  54.1 0.0 collective-permute-done.9.rest_3_
  54.1 0.0 copy-done.4
  54.1 0.0 copy-done.3
  54.1 4.2 %adapter_and_merge.1 = (bf16[320,5120]{1,0:T(8,128)(2,1)}, bf16[256,5120]{1,0:T(8,128)(2,1)}) custom-call(bf16[320,5120]{1,0:T(8,128)(2,1)S(1)} %copy-done.3, bf16[320,128]{1,0:T(8,128)(2,1)S(1)} %copy-done.4, bf16[128,5120]{1,0:T(8,128)(2,1)S(1)} %inner_attention.1.inner, bf16[64,5120]{1,0:T(8,128)(2,1)S(1)} %near_edge_attention.1.near, ...), custom_call_target="tpu_custom_call" | custom-call | flops 1090519040 | bytes 14417920 | tf_op jit(solution)/shard_map/adapter_and_merge/pallas_call | solution.py:215
  (4 shorter events, 0.1 us)
Async XLA Ops:
  1.6 4.5 %collective-permute-start = (bf16[1,320,128]{2,1,0:T(8,128)(2,1)S(1)}, bf16[1,320,128]{2,1,0:T(8,128)(2,1)S(1)}, u32[]{:S(2)}, u32[]{:S(2)}) collective-permute-start(bf16[1,320,128]{2,1,0:T(8,128)(2,1)S(1)} %fusion), channel_id=1, source_target_pairs={{0,2},{1,3},{4,6},{5,7},{8,10},{9,11},{12,14},{13,15},{2,0},{3,1},... | collective-permute-start | bytes 245768 | tf_op jit(solution)/shard_map/ppermute | solution.py:248
  2.9 19.9 %copy-start.2 = (bf16[256,5120]{1,0:T(8,128)(2,1)S(1)}, bf16[256,5120]{1,0:T(8,128)(2,1)}, u32[]{:S(2)}) copy-start(bf16[256,5120]{1,0:T(8,128)(2,1)} %q.3) | copy-start | bytes 7864324
  4.9 17.9 %copy-start.1 = (bf16[256,5120]{1,0:T(8,128)(2,1)S(1)}, bf16[256,5120]{1,0:T(8,128)(2,1)}, u32[]{:S(2)}) copy-start(bf16[256,5120]{1,0:T(8,128)(2,1)} %v.3) | copy-start | bytes 7864324
  5.0 33.1 %collective-permute-start.5 = (bf16[2,64,5120]{2,1,0:T(8,128)(2,1)S(1)}, bf16[2,64,5120]{2,1,0:T(8,128)(2,1)S(1)}, u32[]{:S(2)}, u32[]{:S(2)}) collective-permute-start(bf16[2,64,5120]{2,1,0:T(8,128)(2,1)S(1)} %pad_maximum_fusion.1), channel_id=1, source_target_pairs={{0,1},{2,3},{4,5},{6,7},{8,9},{10,11},{12,13},{14,15},{1,0},{3,2},... | collective-permute-start | bytes 3932168 | tf_op jit(solution)/shard_map/ppermute | solution.py:248
  6.1 6.8 %collective-permute-start.1 = (bf16[2,320,128]{2,1,0:T(8,128)(2,1)S(1)}, bf16[2,320,128]{2,1,0:T(8,128)(2,1)S(1)}, u32[]{:S(2)}, u32[]{:S(2)}) collective-permute-start(bf16[2,320,128]{2,1,0:T(8,128)(2,1)S(1)} %pad_maximum_fusion.4), channel_id=1, source_target_pairs={{0,8},{1,9},{2,10},{3,11},{4,12},{5,13},{6,14},{7,15},{8,0},{9,1},... | collective-permute-start | bytes 491528 | tf_op jit(solution)/shard_map/ppermute | solution.py:248
  6.2 16.6 %copy-start = (bf16[256,5120]{1,0:T(8,128)(2,1)S(1)}, bf16[256,5120]{1,0:T(8,128)(2,1)}, u32[]{:S(2)}) copy-start(bf16[256,5120]{1,0:T(8,128)(2,1)} %k.3) | copy-start | bytes 7864324
  6.2 16.6 %copy-start.5 = (s32[256]{0:T(256)S(1)}, s32[256]{0:T(256)}, u32[]{:S(2)}) copy-start(s32[256]{0:T(256)} %lo_ref.3) | copy-start | bytes 3076
  6.2 16.6 %copy-start.6 = (s32[256]{0:T(256)S(1)}, s32[256]{0:T(256)}, u32[]{:S(2)}) copy-start(s32[256]{0:T(256)} %hi_ref.5) | copy-start | bytes 3076
  13.0 15.9 %collective-permute-start.2 = (bf16[4,320,128]{2,1,0:T(8,128)(2,1)S(1)}, bf16[4,320,128]{2,1,0:T(8,128)(2,1)S(1)}, u32[]{:S(2)}, u32[]{:S(2)}) collective-permute-start(bf16[4,320,128]{2,1,0:T(8,128)(2,1)S(1)} %pad_maximum_fusion.3), channel_id=1, source_target_pairs={{0,4},{1,5},{2,6},{3,7},{8,12},{9,13},{10,14},{11,15},{4,0},{5,1},... | collective-permute-start | bytes 983048 | tf_op jit(solution)/shard_map/ppermute | solution.py:248
  18.0 33.0 %collective-permute-start.6 = (bf16[2,64,5120]{2,1,0:T(8,128)(2,1)S(1)}, bf16[2,64,5120]{2,1,0:T(8,128)(2,1)S(1)}, u32[]{:S(2)}, u32[]{:S(2)}) collective-permute-start(bf16[2,64,5120]{2,1,0:T(8,128)(2,1)S(1)} %pad_maximum_fusion), channel_id=1, source_target_pairs={{1,2},{5,6},{9,10},{13,14},{2,1},{6,5},{10,9},{14,13},{17,18},{21,... | collective-permute-start | bytes 3932168 | tf_op jit(solution)/shard_map/ppermute | solution.py:248
  20.8 30.2 %collective-permute-start.7 = (bf16[2,64,5120]{2,1,0:T(8,128)(2,1)S(1)}, bf16[2,64,5120]{2,1,0:T(8,128)(2,1)S(1)}, u32[]{:S(2)}, u32[]{:S(2)}) collective-permute-start(bf16[2,64,5120]{2,1,0:T(8,128)(2,1)S(1)} %pad_maximum_fusion), channel_id=1, source_target_pairs={{3,4},{7,8},{11,12},{4,3},{8,7},{12,11},{19,20},{23,24},{27,28},{2... | collective-permute-start | bytes 3932168 | tf_op jit(solution)/shard_map/ppermute | solution.py:248
  21.5 9.5 %collective-permute-start.3 = (bf16[4,320,128]{2,1,0:T(8,128)(2,1)S(1)}, bf16[4,320,128]{2,1,0:T(8,128)(2,1)S(1)}, u32[]{:S(2)}, u32[]{:S(2)}) collective-permute-start(bf16[4,320,128]{2,1,0:T(8,128)(2,1)S(1)} %pad_maximum_fusion.3), channel_id=1, source_target_pairs={{0,16},{16,0},{1,17},{17,1},{2,18},{18,2},{3,19},{19,3},{4,20},{20... | collective-permute-start | bytes 983048 | tf_op jit(solution)/shard_map/ppermute | solution.py:254
  28.9 9.2 %collective-permute-start.4 = (bf16[4,320,128]{2,1,0:T(8,128)(2,1)S(1)}, bf16[4,320,128]{2,1,0:T(8,128)(2,1)S(1)}, u32[]{:S(2)}, u32[]{:S(2)}) collective-permute-start(bf16[4,320,128]{2,1,0:T(8,128)(2,1)S(1)} %collective-permute-done.2), channel_id=1, source_target_pairs={{0,16},{16,0},{1,17},{17,1},{2,18},{18,2},{3,19},{19,3},{4,20},{20... | collective-permute-start | bytes 983048 | tf_op jit(solution)/shard_map/ppermute | solution.py:254
  31.0 23.0 %collective-permute-start.8 = (bf16[8,320,128]{2,1,0:T(8,128)(2,1)S(1)}, bf16[8,320,128]{2,1,0:T(8,128)(2,1)S(1)}, u32[]{:S(2)}, u32[]{:S(2)}) collective-permute-start(bf16[8,320,128]{2,1,0:T(8,128)(2,1)S(1)} %constant_dynamic-update-slice_fusion.rest_0_), channel_id=1, source_target_pairs={{0,1},{2,3},{4,5},{6,7},{8,9},{10,11},{12,13},{14,15},{1,0},{3,2},... | collective-permute-start | bytes 1966088 | tf_op jit(solution)/shard_map/ppermute | solution.py:248
  41.2 12.9 %copy-start.4 = (bf16[320,128]{1,0:T(8,128)(2,1)S(1)}, bf16[320,128]{1,0:T(8,128)(2,1)}, u32[]{:S(2)}) copy-start(bf16[320,128]{1,0:T(8,128)(2,1)} %own_down.1) | copy-start | bytes 245764
  41.2 12.9 %collective-permute-start.9 = (bf16[8,320,128]{2,1,0:T(8,128)(2,1)S(1)}, bf16[8,320,128]{2,1,0:T(8,128)(2,1)S(1)}, u32[]{:S(2)}, u32[]{:S(2)}) collective-permute-start(bf16[8,320,128]{2,1,0:T(8,128)(2,1)S(1)} %pad_maximum_fusion.2.rest_2_), channel_id=1, source_target_pairs={{0,1},{2,3},{4,5},{6,7},{8,9},{10,11},{12,13},{14,15},{1,0},{3,2},... | collective-permute-start | bytes 1966088 | tf_op jit(solution)/shard_map/ppermute | solution.py:248
  50.9 3.1 %copy-start.3 = (bf16[320,5120]{1,0:T(8,128)(2,1)S(1)}, bf16[320,5120]{1,0:T(8,128)(2,1)}, u32[]{:S(2)}) copy-start(bf16[320,5120]{1,0:T(8,128)(2,1)} %frozen.1) | copy-start | bytes 9830404

commit v5 on v4

--- a/solution.py
+++ b/solution.py
@@ -13,6 +13,8 @@
 FRAME = 64
 NEAR = 2 * FRAME
 CHUNK = 512
+WIDE = 2 * CHUNK
+FAR_CUTS = (0, 2048, MODEL_WIDTH)
 SCORE_SCALE = HD ** (-0.5) * 1.4426950408889634
 ADAPTER_SCALE = MODEL_WIDTH ** (-0.5)
 FAR = -1e30
@@ -68,7 +70,7 @@
         lo, hi = lo_ref[row], hi_ref[row]
         keys = pl.ds(pl.multiple_of(lo - base, FRAME), NEAR)
         bias = clip_bias(lo, hi)
-        for col in range(0, CHUNK, 2 * HD):
+        for col in range(0, WIDE, 2 * HD):
             part = slice(col, col + 2 * HD)
             targets.append((slice(row - FRAME, row), part))
             loads.append(
@@ -85,13 +87,13 @@
 
 def inner_attention(lo, hi, q, k, v):
     rows, width = q.shape
-    block = pl.BlockSpec((rows, CHUNK), lambda i: (0, i))
+    block = pl.BlockSpec((rows, WIDE), lambda i: (0, i))
     return pl.pallas_call(
         inner_kernel,
-        grid=(width // CHUNK,),
+        grid=(width // WIDE,),
         out_shape=jax.ShapeDtypeStruct((NEAR, width), BF16),
         in_specs=[SMEM, SMEM, block, block, block],
-        out_specs=pl.BlockSpec((NEAR, CHUNK), lambda i: (0, i)),
+        out_specs=pl.BlockSpec((NEAR, WIDE), lambda i: (0, i)),
         compiler_params=pltpu.CompilerParams(vmem_limit_bytes=16 << 20),
         cost_estimate=pl.CostEstimate(
             flops=16 * NEAR * NEAR * width,
@@ -102,9 +104,11 @@
     )(lo, hi, q, k, v)
 
 
-def edge_kernel(is_near, lo_ref, hi_ref, q, k, v, *rest):
+def edge_kernel(is_near, start, lo_ref, hi_ref, q, k, v, *rest):
     halos, out = rest[:-1], rest[-1]
-    rows, width = q.shape
+    rows, width = q.shape[0], out.shape[1]
+    pairs = width // (2 * HD)
+    unroll = next(n for n in (8, 6, 5, 4, 2, 1) if pairs % n == 0)
     me = lax.axis_index("seq")
     base = me * rows
     right = lax.rem(me, 2) == (0 if is_near else 1)
@@ -116,10 +120,10 @@
     after = jnp.logical_and(right, lo == base + rows - FRAME)
     direct = lax.rem(lax.div(me + 1, 2), 2) == 1
 
-    def window(ref, kind, part):
-        halo = halos[0][kind, :, part]
+    def window(ref, kind, part, here):
+        halo = halos[0][kind, :, here]
         if len(halos) == 2:
-            halo = jnp.where(direct, halo, halos[1][kind, :, part])
+            halo = jnp.where(direct, halo, halos[1][kind, :, here])
         one, two = ref[pl.ds(first, FRAME), part], ref[pl.ds(second, FRAME), part]
         return jnp.concatenate(
             [
@@ -132,29 +136,31 @@
 
     def step(i, _):
         loads, parts = [], []
-        for col in range(0, 2 * CHUNK, 2 * HD):
-            part = pl.ds(pl.multiple_of(i * 2 * CHUNK + col, 2 * HD), 2 * HD)
-            parts.append(part)
+        for pair in range(unroll):
+            col = pl.multiple_of((i * unroll + pair) * 2 * HD, 2 * HD)
+            here = pl.ds(col, 2 * HD)
+            part = pl.ds(pl.multiple_of(col + start, 2 * HD), 2 * HD)
+            parts.append(here)
             loads.append(
                 (
                     lambda part=part: q[pl.ds(row, FRAME), part],
-                    lambda part=part: window(k, 0, part),
-                    lambda part=part: window(v, 1, part),
+                    lambda part=part, here=here: window(k, 0, part, here),
+                    lambda part=part, here=here: window(v, 1, part, here),
                     bias,
                 )
             )
-        for part, result in zip(parts, attend(loads)):
-            out[:, part] = result
+        for here, result in zip(parts, attend(loads)):
+            out[:, here] = result
         return 0
 
-    lax.fori_loop(0, width // (2 * CHUNK), step, 0)
-
-
-def edge_attention(lo, hi, q, k, v, *halos):
-    rows, width = q.shape
-    is_near = len(halos) == 1
+    lax.fori_loop(0, pairs // unroll, step, 0)
+
+
+def edge_attention(name, start, lo, hi, q, k, v, *halos):
+    rows = q.shape[0]
+    width = halos[0].shape[2]
     return pl.pallas_call(
-        functools.partial(edge_kernel, is_near),
+        functools.partial(edge_kernel, name == "near_edge", start),
         out_shape=jax.ShapeDtypeStruct((FRAME, width), BF16),
         in_specs=[SMEM, SMEM] + [VMEM] * (3 + len(halos)),
         out_specs=VMEM,
@@ -164,11 +170,12 @@
             bytes_accessed=7 * rows * width,
             transcendentals=FRAME * NEAR * HEADS,
         ),
-        name="near_edge_attention" if is_near else "far_edge_attention",
+        name=name,
     )(lo, hi, q, k, v, *halos)
 
 
-def last_kernel(layout, frozen, own_down, inner, near, far, *rest):
+def last_kernel(layout, frozen, own_down, inner, near, *rest):
+    fars, rest = rest[: len(FAR_CUTS) - 1], rest[len(FAR_CUTS) - 1 :]
     refs, rest = rest[:-6], rest[-6:]
     merged, attended, factors, w, result, sems = rest
     shard, width = frozen.shape
@@ -186,8 +193,13 @@
     right = lax.rem(me, 2) == 0
     near_row = pl.multiple_of(jnp.where(right, rows - FRAME, 0), FRAME)
     far_row = pl.multiple_of(jnp.where(right, 0, rows - FRAME), FRAME)
-    parts = ((inner, FRAME), (near, near_row), (far, far_row))
-    reduced = [dot(att[...], down[...], NN).astype(BF16) for att, _ in parts]
+    parts = ((inner, FRAME), (near, near_row), (None, far_row))
+    reduced = [dot(att[...], down[...], NN).astype(BF16) for att in (inner, near)]
+    pieces = [
+        dot(att[...], down[start : start + att.shape[1]], NN)
+        for att, start in zip(fars, FAR_CUTS)
+    ]
+    reduced.append(sum(pieces[1:], pieces[0]).astype(BF16))
     stores = []
 
     def store(source, target):
@@ -201,14 +213,19 @@
         w[:, part] = (frozen[:, part].astype(F32) + ADAPTER_SCALE * product).astype(BF16)
         store(w.at[:, part], merged.at[:, part])
         for narrow, (att, row) in zip(reduced, parts):
-            value = att[:, part].astype(F32) + ADAPTER_SCALE * dot(narrow, factor, NT)
-            result[pl.ds(row, att.shape[0]), part] = value.astype(BF16)
+            if att is None:
+                at = max(i for i, start in enumerate(FAR_CUTS) if start <= first)
+                value = fars[at][:, pl.ds(first - FAR_CUTS[at], CHUNK)]
+            else:
+                value = att[:, part]
+            value = value.astype(F32) + ADAPTER_SCALE * dot(narrow, factor, NT)
+            result[pl.ds(row, value.shape[0]), part] = value.astype(BF16)
         store(result.at[:, part], attended.at[:, part])
     for copy in stores:
         copy.wait()
 
 
-def last(frozen, own_down, inner, near, far, layout, pieces):
+def last(frozen, own_down, attention, layout, pieces):
     shard, width = frozen.shape
     rank = own_down.shape[1]
     rows = 2 * NEAR
@@ -218,7 +235,7 @@
             jax.ShapeDtypeStruct((shard, width), BF16),
             jax.ShapeDtypeStruct((rows, width), BF16),
         ),
-        in_specs=[VMEM] * (5 + len(pieces)),
+        in_specs=[VMEM] * (2 + len(attention) + len(pieces)),
         out_specs=(ANY, ANY),
         scratch_shapes=[
             pltpu.VMEM((2, width, rank), BF16),
@@ -233,7 +250,7 @@
             transcendentals=0,
         ),
         name="adapter_and_merge",
-    )(frozen, own_down, inner, near, far, *pieces)
+    )(frozen, own_down, *attention, *pieces)
 
 
 def body(q, k, v, lo, hi, down, up, frozen):
@@ -241,53 +258,70 @@
     rows = k.shape[0]
     odd = lax.rem(lax.axis_index("seq"), 2)
 
-    def rim(start):
-        return jnp.stack([lax.dynamic_slice_in_dim(x, start, FRAME, 0) for x in (k, v)])
-
-    def send(cells, pairs):
-        return lax.ppermute(cells, "seq", pairs + [(b, a) for a, b in pairs])
+    def rim(start, columns):
+        return jnp.stack([lax.dynamic_slice_in_dim(x, start, FRAME, 0)[:, columns] for x in (k, v)])
 
     def swap(cells, mask):
-        return send(cells, [(i, i ^ mask) for i in range(count) if not i & mask])
+        return lax.ppermute(cells, "seq", [(i, i ^ mask) for i in range(count)])
 
     def cross(cells):
         return lax.ppermute(cells, "group", [(0, 1), (1, 0)])
 
-    far_rim = rim(odd * (rows - FRAME))
-    direct = send(far_rim, [(i, i + 1) for i in range(1, count - 1, 4)])
-    near = swap(rim((1 - odd) * (rows - FRAME)), 1)
-    distant = [(i, i + 1) for i in range(3, count - 1, 4)]
+    close, distant = (
+        [(i + a, i + 1 - a) for i in range(first, count - 1, 4) for a in (0, 1)]
+        for first in (1, 3)
+    )
+
+    def far_rim(at):
+        return rim(odd * (rows - FRAME), slice(FAR_CUTS[at], FAR_CUTS[at + 1]))
+
+    def near_halo(odd):
+        return swap(rim((1 - odd) * (rows - FRAME), slice(None)), 1)
+
+    def far_edge(at, *halos):
+        return edge_attention("far_edge", FAR_CUTS[at], lo, hi, q, k, v, *halos)
+
     up = up.T
     if lax.axis_size("group") != 2 or down.shape[0] % 32:
         both = lax.all_gather(jnp.stack([down, up]), "seq", axis=1, tiled=True)
         layout, pieces = [], [both]
         inner = inner_attention(lo, hi, q, k, v)
-        near_edge = edge_attention(lo, hi, q, k, v, near)
-        diagonal_halo = send(far_rim, distant)
+        near = edge_attention("near_edge", 0, lo, hi, q, k, v, near_halo(odd))
+        fars = [
+            far_edge(at, lax.ppermute(far_rim(at), "seq", close + distant)) for at in range(2)
+        ]
     else:
+        barrier = lax.optimization_barrier
+        inner = inner_attention(lo, hi, q, k, v)
+        early_halo = lax.ppermute(far_rim(0), "seq", close + distant)
         cells = jnp.where(lax.axis_index("group") == 0, down, up)[None]
         masks = [0]
         steps = [2] + [count >> j for j in range(1, count.bit_length()) if count >> j > 2]
         for mask in steps[:-1]:
             cells = jnp.concatenate([cells, swap(cells, mask)])
             masks = masks + [have ^ mask for have in masks]
-        cells, far_rim, lo_inner = lax.optimization_barrier((cells, far_rim, lo))
+            if mask == 2:
+                cells, later = barrier((cells, odd))
+        near = near_halo(later)
+        late_rim = far_rim(1)
+        late_halos = [lax.ppermute(late_rim, "seq", close)]
+        cells, inner, early_halo, late_rim = barrier((cells, inner, early_halo, late_rim))
         new = swap(cells, steps[-1])
-        diagonal_halo = send(far_rim, distant)
+        late_halos.append(lax.ppermute(late_rim, "seq", distant))
         early = cross(cells)
-        inner = inner_attention(lo_inner, hi, q, k, v)
-        new, inner, lo_near = lax.optimization_barrier((new, inner, lo))
+        new, lo_edge = barrier((new, lo))
         late = cross(new)
         cells = jnp.concatenate([cells, new])
         masks = masks + [have ^ steps[-1] for have in masks]
-        near_edge = edge_attention(lo_near, hi, q, k, v, near)
+        near = edge_attention("near_edge", 0, lo_edge, hi, q, k, v, near)
+        fars = [far_edge(0, early_halo)]
         other = jnp.concatenate([early, late])
-        other, near_edge = lax.optimization_barrier((other, near_edge))
+        other, near, fars, late_halos = barrier((other, near, fars, late_halos))
+        fars.append(far_edge(1, *late_halos))
         across = [mask ^ 1 for mask in masks]
         layout = [(0, masks), (0, across), (1, masks), (1, across)]
         pieces = [cells, swap(cells, 1), other, swap(other, 1)]
-    far_edge = edge_attention(lo, hi, q, k, v, direct, diagonal_halo)
-    merged, attended = last(frozen, down, inner, near_edge, far_edge, layout, pieces)
+    merged, attended = last(frozen, down, (inner, near, *fars), layout, pieces)
     return (attended, merged)
 
 

time: 58.5 us -> 55.5 us (0.949)
  the two profiles are of different devices: /device:TPU:17 before, /device:TPU:1 now
where the time goes in v5:
time: 55.5 us; the launch traced here: 55 us
  starting transfers between devices  15.6 us (28%)
  waiting for transfers between devices  13.7 us (25%)
  Pallas kernels  13.7 us (25%)
  local copies, waits for them, and re-layouts  5.85 us (11%)
  other arithmetic  5.36 us (10%)
  between operations  0.83 us (1%)
    ppermute x2, waiting for transfers between devices, cross(): return lax.ppermute(cells, 'group', [(0, 1), (1, 0)])  12.4 us
    ppermute x6, starting transfers between devices, swap(): return lax.ppermute(cells, 'seq', [(i, i ^ mask) for i in range(count)])  6.13 us
    pallas_call x3, Pallas kernels, edge_attention(): pl.pallas_call(functools.partial(edge_kernel, name == 'near_edge', start)...  5.53 us
    another operation x3, local copies, waits for them, and re-layouts, rim(): jnp.stack([lax.dynamic_slice_in_dim(x, start, FRAME, 0)[:, columns] for x...  4.31 us
    pallas_call x1, Pallas kernels, last(): pl.pallas_call(functools.partial(last_kernel, layout), out_shape=(jax.Sha...  4.26 us
    pallas_call x1, Pallas kernels, inner_attention(): pl.pallas_call(inner_kernel, grid=(width // WIDE,), out_shape=jax.ShapeDt...  3.92 us
    ppermute x1, starting transfers between devices, body(): late_halos = [lax.ppermute(late_rim, 'seq', close)]  3.9 us
    concatenate x2, other arithmetic, body(): cells = jnp.concatenate([cells, swap(cells, mask)])  2.54 us
  transfers between devices with their start and end apart: 11, of which 4 were waited for; matrix products, arithmetic and copies ran while one was open for 15% of the time, Pallas kernels for 17%

profile of v5, /device:TPU:1, one launch (start us, length us, event | category | flops | bytes accessed | tf_op | source)
XLA Modules:
  0.0 55.0 jit_solution(8049125790669098213)
XLA Ops:
  0.6 0.0 copy-start
  0.6 1.7 %fusion = bf16[1,320,128]{2,1,0:T(8,128)(2,1)} fusion(bf16[320,128]{1,0:T(8,128)(2,1)} %own_down.1, bf16[128,320]{0,1:T(8,128)(2,1)} %param.14, pred[]{:T(512)S(6)} %eq.3), kind=kLoop, calls=%fused_computation.13 | loop fusion | flops 40960 | bytes 245761 | tf_op jit(solution)/shard_map/broadcast_in_dim | solution.py:297
  2.4 2.1 %collective-permute-start = (bf16[1,320,128]{2,1,0:T(8,128)(2,1)}, bf16[1,320,128]{2,1,0:T(8,128)(2,1)}, u32[]{:S(2)}, u32[]{:S(2)}) collective-permute-start(bf16[1,320,128]{2,1,0:T(8,128)(2,1)} %fusion), channel_id=1, source_target_pairs={{0,2},{1,3},{2,0},{3,1},{4,6},{5,7},{6,4},{7,5},{8,10},{9,11},{10,... | collective-permute-start | bytes 245768 | tf_op jit(solution)/shard_map/ppermute | solution.py:265
  4.4 1.1 %dynamic-slice_bitcast_fusion.4 = (bf16[1,64,2048]{2,1,0:T(8,128)(2,1)S(1)}, bf16[1,64,2048]{2,1,0:T(8,128)(2,1)S(1)}) fusion(bf16[256,5120]{1,0:T(8,128)(2,1)} %v.5, s32[]{:T(128)S(6)} %select_n.20, bf16[256,5120]{1,0:T(8,128)(2,1)} %k.5), kind=kLoop, calls=%fused_computation.9 | loop fusion | bytes 1048580 | tf_op jit(solution)/shard_map/stack | solution.py:262
  5.5 0.8 %pad_maximum_fusion.3 = bf16[2,64,2048]{2,1,0:T(8,128)(2,1)} fusion(bf16[1,64,2048]{2,1,0:T(8,128)(2,1)S(1)} %get-tuple-element.34, bf16[1,64,2048]{2,1,0:T(8,128)(2,1)S(1)} %get-tuple-element.35), kind=kLoop, calls=%fused_computation.5 | loop fusion | flops 262144 | bytes 1048576 | tf_op jit(solution)/shard_map/stack | solution.py:262
  6.3 2.5 %collective-permute-start.2 = (bf16[2,64,2048]{2,1,0:T(8,128)(2,1)}, bf16[2,64,2048]{2,1,0:T(8,128)(2,1)S(1)}, u32[]{:S(2)}, u32[]{:S(2)}) collective-permute-start(bf16[2,64,2048]{2,1,0:T(8,128)(2,1)} %pad_maximum_fusion.3), channel_id=1, source_target_pairs={{1,2},{2,1},{5,6},{6,5},{9,10},{10,9},{13,14},{14,13},{3,4},{4,3},... | collective-permute-start | bytes 1572872 | tf_op jit(solution)/shard_map/ppermute | solution.py:296
  8.8 1.9 %dynamic-slice_bitcast_fusion.2 = (bf16[1,64,3072]{2,1,0:T(8,128)(2,1)S(1)}, bf16[1,64,3072]{2,1,0:T(8,128)(2,1)}) fusion(bf16[256,5120]{1,0:T(8,128)(2,1)} %v.5, s32[]{:T(128)S(6)} %select_n.20, s32[]{:T(128)S(6)} %add.12, bf16[256,5120]{1,0:T(8,128)(2,1)} %k.5), kind=kLoop, calls=%fused_computation.6 | loop fusion | bytes 1572872 | tf_op jit(solution)/shard_map/stack | solution.py:262
  10.7 0.0 collective-permute-done
  10.7 1.6 %pad_maximum_fusion.5 = bf16[2,320,128]{2,1,0:T(8,128)(2,1)} fusion(bf16[1,320,128]{2,1,0:T(8,128)(2,1)} %collective-permute-done, bf16[1,320,128]{2,1,0:T(8,128)(2,1)} %fusion), kind=kLoop, calls=%fused_computation.11 | loop fusion | flops 81920 | bytes 327680 | tf_op jit(solution)/shard_map/concatenate | solution.py:301
  12.3 2.8 %collective-permute-start.1 = (bf16[2,320,128]{2,1,0:T(8,128)(2,1)}, bf16[2,320,128]{2,1,0:T(8,128)(2,1)}, u32[]{:S(2)}, u32[]{:S(2)}) collective-permute-start(bf16[2,320,128]{2,1,0:T(8,128)(2,1)} %pad_maximum_fusion.5), channel_id=1, source_target_pairs={{0,8},{1,9},{2,10},{3,11},{4,12},{5,13},{6,14},{7,15},{8,0},{9,1},... | collective-permute-start | bytes 491528 | tf_op jit(solution)/shard_map/ppermute | solution.py:265
  15.1 0.0 copy-done
  15.2 1.3 %dynamic-slice_bitcast_fusion = (bf16[1,64,5120]{2,1,0:T(8,128)(2,1)S(1)}, bf16[1,64,5120]{2,1,0:T(8,128)(2,1)S(1)}) fusion(bf16[256,5120]{1,0:T(8,128)(2,1)} %v.5, s32[]{:T(128)S(6)} %select_n.21, bf16[256,5120]{1,0:T(8,128)(2,1)S(1)} %copy-done), kind=kLoop, calls=%fused_computation.3 | loop fusion | bytes 2621444 | tf_op jit(solution)/shard_map/stack | solution.py:262
  16.5 0.0 copy-start.1
  16.5 0.0 copy-start.5
  16.5 0.0 copy-start.6
  16.5 0.1 pad_maximum_fusion
  16.6 0.2 collective-permute-start.6
  16.9 0.1 pad_maximum_fusion.1
  17.0 0.3 copy-done.2
  17.2 1.2 %copy-done.1 = bf16[256,5120]{1,0:T(8,128)(2,1)S(1)} copy-done((bf16[256,5120]{1,0:T(8,128)(2,1)S(1)}, bf16[256,5120]{1,0:T(8,128)(2,1)}, u32[]{:S(2)}) %copy-start.1) | copy-done | bytes 2621464
  18.4 3.9 %inner_attention.1.inner = bf16[128,5120]{1,0:T(8,128)(2,1)S(1)} custom-call(s32[256]{0:T(256)S(1)} %copy-done.5, s32[256]{0:T(256)S(1)} %copy-done.6, bf16[256,5120]{1,0:T(8,128)(2,1)S(1)} %copy-done.2, bf16[256,5120]{1,0:T(8,128)(2,1)S(1)} %copy-done, bf16[256,5120]{1,0:T(8,128)(2,1)S(1)} %copy-done.1), custom_call_target="tpu_custom_call" | custom-call | flops 1342177280 | bytes 9175040 | tf_op jit(solution)/shard_map/inner_attention/pallas_call | solution.py:91
  22.3 1.2 %collective-permute-done.1 = bf16[2,320,128]{2,1,0:T(8,128)(2,1)} collective-permute-done((bf16[2,320,128]{2,1,0:T(8,128)(2,1)}, bf16[2,320,128]{2,1,0:T(8,128)(2,1)}, u32[]{:S(2)}, u32[]{:S(2)}) %collective-permute-start.1) | collective-permute-done | bytes 163872 | tf_op jit(solution)/shard_map/ppermute | solution.py:265
  23.5 0.0 copy-done.8
  23.5 0.9 %pad_maximum_fusion.4 = bf16[4,320,128]{2,1,0:T(8,128)(2,1)S(1)} fusion(bf16[2,320,128]{2,1,0:T(8,128)(2,1)} %collective-permute-done.1, bf16[2,320,128]{2,1,0:T(8,128)(2,1)S(1)} %copy-done.8), kind=kLoop, calls=%fused_computation.8 | loop fusion | flops 163840 | bytes 655360 | tf_op jit(solution)/shard_map/concatenate | solution.py:301
  24.5 0.0 collective-permute-done.2.rest_0_
  24.5 0.7 %collective-permute-start.4 = (bf16[4,320,128]{2,1,0:T(8,128)(2,1)S(1)}, bf16[4,320,128]{2,1,0:T(8,128)(2,1)S(1)}, u32[]{:S(2)}, u32[]{:S(2)}) collective-permute-start(bf16[4,320,128]{2,1,0:T(8,128)(2,1)S(1)} %pad_maximum_fusion.4), channel_id=1, source_target_pairs={{0,4},{1,5},{2,6},{3,7},{4,0},{5,1},{6,2},{7,3},{8,12},{9,13},{10,... | collective-permute-start | bytes 983048 | tf_op jit(solution)/shard_map/ppermute | solution.py:265
  25.2 3.9 %collective-permute-start.7 = (bf16[2,64,3072]{2,1,0:T(8,128)(2,1)S(1)}, bf16[2,64,3072]{2,1,0:T(8,128)(2,1)S(1)}, u32[]{:S(2)}, u32[]{:S(2)}) collective-permute-start(bf16[2,64,3072]{2,1,0:T(8,128)(2,1)S(1)} %pad_maximum_fusion.1), channel_id=1, source_target_pairs={{1,2},{2,1},{5,6},{6,5},{9,10},{10,9},{13,14},{14,13},{17,18},{18,... | collective-permute-start | bytes 2359304 | tf_op jit(solution)/shard_map/ppermute | solution.py:307
  29.1 0.7 %collective-permute-start.8 = (bf16[2,64,3072]{2,1,0:T(8,128)(2,1)S(1)}, bf16[2,64,3072]{2,1,0:T(8,128)(2,1)S(1)}, u32[]{:S(2)}, u32[]{:S(2)}) collective-permute-start(bf16[2,64,3072]{2,1,0:T(8,128)(2,1)S(1)} %pad_maximum_fusion.1), channel_id=1, source_target_pairs={{3,4},{4,3},{7,8},{8,7},{11,12},{12,11},{19,20},{20,19},{23,24},{2... | collective-permute-start | bytes 2359304 | tf_op jit(solution)/shard_map/ppermute | solution.py:310
  29.8 1.2 %collective-permute-start.3 = (bf16[4,320,128]{2,1,0:T(8,128)(2,1)S(1)}, bf16[4,320,128]{2,1,0:T(8,128)(2,1)S(1)}, u32[]{:S(2)}, u32[]{:S(2)}) collective-permute-start(bf16[4,320,128]{2,1,0:T(8,128)(2,1)S(1)} %pad_maximum_fusion.4), channel_id=1, source_target_pairs={{0,16},{16,0},{1,17},{17,1},{2,18},{18,2},{3,19},{19,3},{4,20},{20... | collective-permute-start | bytes 983048 | tf_op jit(solution)/shard_map/ppermute | solution.py:268
  31.0 0.0 collective-permute-done.4
  31.0 1.1 %collective-permute-start.5 = (bf16[4,320,128]{2,1,0:T(8,128)(2,1)S(1)}, bf16[4,320,128]{2,1,0:T(8,128)(2,1)S(1)}, u32[]{:S(2)}, u32[]{:S(2)}) collective-permute-start(bf16[4,320,128]{2,1,0:T(8,128)(2,1)S(1)} %collective-permute-done.4), channel_id=1, source_target_pairs={{0,16},{16,0},{1,17},{17,1},{2,18},{18,2},{3,19},{19,3},{4,20},{20... | collective-permute-start | bytes 983048 | tf_op jit(solution)/shard_map/ppermute | solution.py:268
  32.2 1.1 %far_edge.2.rest_0_ = bf16[64,2048]{1,0:T(8,128)(2,1)S(1)} custom-call(s32[256]{0:T(256)S(1)} %copy-done.5, s32[256]{0:T(256)S(1)} %copy-done.6, bf16[256,5120]{1,0:T(8,128)(2,1)S(1)} %copy-done.2, bf16[256,5120]{1,0:T(8,128)(2,1)S(1)} %copy-done, bf16[256,5120]{1,0:T(8,128)(2,1)S(1)} %copy-done.1, bf16[2,64,2048]{2,1,0:T(8,128)(2,1)S(1)} %collective-permute-done.2.rest_0_), custom_call_target="tpu_custom_call" | custom-call | flops 268435456 | bytes 3670016 | tf_op jit(solution)/shard_map/far_edge/pallas_call | solution.py:162
  33.4 6.1 %collective-permute-done.3 = bf16[4,320,128]{2,1,0:T(8,128)(2,1)S(1)} collective-permute-done((bf16[4,320,128]{2,1,0:T(8,128)(2,1)S(1)}, bf16[4,320,128]{2,1,0:T(8,128)(2,1)S(1)}, u32[]{:S(2)}, u32[]{:S(2)}) %collective-permute-start.3) | collective-permute-done | bytes 327712 | tf_op jit(solution)/shard_map/ppermute | solution.py:268
  39.5 0.0 collective-permute-start.9
  39.5 6.3 %collective-permute-done.5 = bf16[4,320,128]{2,1,0:T(8,128)(2,1)S(1)} collective-permute-done((bf16[4,320,128]{2,1,0:T(8,128)(2,1)S(1)}, bf16[4,320,128]{2,1,0:T(8,128)(2,1)S(1)}, u32[]{:S(2)}, u32[]{:S(2)}) %collective-permute-start.5) | collective-permute-done | bytes 327712 | tf_op jit(solution)/shard_map/ppermute | solution.py:268
  45.8 0.1 pad_maximum_fusion.2.rest_4_
  45.9 0.0 collective-permute-done.6.rest_0_
  45.9 2.7 %near_edge.1.near = bf16[64,5120]{1,0:T(8,128)(2,1)S(1)} custom-call(s32[256]{0:T(256)S(1)} %copy-done.5, s32[256]{0:T(256)S(1)} %copy-done.6, bf16[256,5120]{1,0:T(8,128)(2,1)S(1)} %copy-done.2, bf16[256,5120]{1,0:T(8,128)(2,1)S(1)} %copy-done, bf16[256,5120]{1,0:T(8,128)(2,1)S(1)} %copy-done.1, bf16[2,64,5120]{2,1,0:T(8,128)(2,1)S(1)} %collective-permute-done.6.rest_0_), custom_call_target="tpu_custom_call" | custom-call | flops 671088640 | bytes 9175040 | tf_op jit(solution)/shard_map/near_edge/pallas_call | solution.py:162
  48.5 0.0 copy-start.3
  48.5 0.0 copy-start.4
  48.6 0.0 collective-permute-done.7.rest_0_
  48.6 0.0 collective-permute-done.8.rest_1_
  48.6 0.3 collective-permute-start.10
  48.9 1.7 %far_edge.3.rest_1_ = bf16[64,3072]{1,0:T(8,128)(2,1)S(1)} custom-call(s32[256]{0:T(256)S(1)} %copy-done.5, s32[256]{0:T(256)S(1)} %copy-done.6, bf16[256,5120]{1,0:T(8,128)(2,1)S(1)} %copy-done.2, bf16[256,5120]{1,0:T(8,128)(2,1)S(1)} %copy-done, bf16[256,5120]{1,0:T(8,128)(2,1)S(1)} %copy-done.1, bf16[2,64,3072]{2,1,0:T(8,128)(2,1)S(1)} %collective-permute-done.7.rest_0_, ...), custom_call_target="tpu_custom_call" | custom-call | flops 402653184 | bytes 5505024 | tf_op jit(solution)/shard_map/far_edge/pallas_call | solution.py:162
  50.6 0.0 collective-permute-done.9.rest_3_
  50.6 0.1 collective-permute-done.10.rest_5_
  50.7 0.0 copy-done.4
  50.7 4.3 %adapter_and_merge.1 = (bf16[320,5120]{1,0:T(8,128)(2,1)}, bf16[256,5120]{1,0:T(8,128)(2,1)}) custom-call(bf16[320,5120]{1,0:T(8,128)(2,1)S(1)} %copy-done.3, bf16[320,128]{1,0:T(8,128)(2,1)S(1)} %copy-done.4, bf16[128,5120]{1,0:T(8,128)(2,1)S(1)} %inner_attention.1.inner, bf16[64,5120]{1,0:T(8,128)(2,1)S(1)} %near_edge.1.near, ...), custom_call_target="tpu_custom_call" | custom-call | flops 1090519040 | bytes 14417920 | tf_op jit(solution)/shard_map/adapter_and_merge/pallas_call | solution.py:232
  (9 shorter events, 0.1 us)
Async XLA Ops:
  0.6 14.5 %copy-start = (bf16[256,5120]{1,0:T(8,128)(2,1)S(1)}, bf16[256,5120]{1,0:T(8,128)(2,1)}, u32[]{:S(2)}) copy-start(bf16[256,5120]{1,0:T(8,128)(2,1)} %k.5) | copy-start | bytes 7864324
  2.4 8.4 %collective-permute-start = (bf16[1,320,128]{2,1,0:T(8,128)(2,1)}, bf16[1,320,128]{2,1,0:T(8,128)(2,1)}, u32[]{:S(2)}, u32[]{:S(2)}) collective-permute-start(bf16[1,320,128]{2,1,0:T(8,128)(2,1)} %fusion), channel_id=1, source_target_pairs={{0,2},{1,3},{2,0},{3,1},{4,6},{5,7},{6,4},{7,5},{8,10},{9,11},{10,... | collective-permute-start | bytes 245768 | tf_op jit(solution)/shard_map/ppermute | solution.py:265
  6.3 18.1 %collective-permute-start.2 = (bf16[2,64,2048]{2,1,0:T(8,128)(2,1)}, bf16[2,64,2048]{2,1,0:T(8,128)(2,1)S(1)}, u32[]{:S(2)}, u32[]{:S(2)}) collective-permute-start(bf16[2,64,2048]{2,1,0:T(8,128)(2,1)} %pad_maximum_fusion.3), channel_id=1, source_target_pairs={{1,2},{2,1},{5,6},{6,5},{9,10},{10,9},{13,14},{14,13},{3,4},{4,3},... | collective-permute-start | bytes 1572872 | tf_op jit(solution)/shard_map/ppermute | solution.py:296
  12.3 11.2 %collective-permute-start.1 = (bf16[2,320,128]{2,1,0:T(8,128)(2,1)}, bf16[2,320,128]{2,1,0:T(8,128)(2,1)}, u32[]{:S(2)}, u32[]{:S(2)}) collective-permute-start(bf16[2,320,128]{2,1,0:T(8,128)(2,1)} %pad_maximum_fusion.5), channel_id=1, source_target_pairs={{0,8},{1,9},{2,10},{3,11},{4,12},{5,13},{6,14},{7,15},{8,0},{9,1},... | collective-permute-start | bytes 491528 | tf_op jit(solution)/shard_map/ppermute | solution.py:265
  15.2 1.7 %copy-start.7 = (bf16[1,64,3072]{2,1,0:T(8,128)(2,1)S(1)}, bf16[1,64,3072]{2,1,0:T(8,128)(2,1)}, u32[]{:S(2)}) copy-start(bf16[1,64,3072]{2,1,0:T(8,128)(2,1)} %get-tuple-element.33) | copy-start | bytes 1179652
  15.2 2.1 %copy-start.2 = (bf16[256,5120]{1,0:T(8,128)(2,1)S(1)}, bf16[256,5120]{1,0:T(8,128)(2,1)}, u32[]{:S(2)}) copy-start(bf16[256,5120]{1,0:T(8,128)(2,1)} %q.5) | copy-start | bytes 7864324
  16.5 1.9 %copy-start.1 = (bf16[256,5120]{1,0:T(8,128)(2,1)S(1)}, bf16[256,5120]{1,0:T(8,128)(2,1)}, u32[]{:S(2)}) copy-start(bf16[256,5120]{1,0:T(8,128)(2,1)} %v.5) | copy-start | bytes 7864324
  16.5 1.9 %copy-start.5 = (s32[256]{0:T(256)S(1)}, s32[256]{0:T(256)}, u32[]{:S(2)}) copy-start(s32[256]{0:T(256)} %lo_ref.6) | copy-start | bytes 3076
  16.5 1.9 %copy-start.6 = (s32[256]{0:T(256)S(1)}, s32[256]{0:T(256)}, u32[]{:S(2)}) copy-start(s32[256]{0:T(256)} %hi_ref.7) | copy-start | bytes 3076
  16.6 29.2 %collective-permute-start.6 = (bf16[2,64,5120]{2,1,0:T(8,128)(2,1)S(1)}, bf16[2,64,5120]{2,1,0:T(8,128)(2,1)S(1)}, u32[]{:S(2)}, u32[]{:S(2)}) collective-permute-start(bf16[2,64,5120]{2,1,0:T(8,128)(2,1)S(1)} %pad_maximum_fusion), channel_id=1, source_target_pairs={{0,1},{1,0},{2,3},{3,2},{4,5},{5,4},{6,7},{7,6},{8,9},{9,8},{10,11... | collective-permute-start | bytes 3932168 | tf_op jit(solution)/shard_map/ppermute | solution.py:265
  18.4 5.1 %copy-start.8 = (bf16[2,320,128]{2,1,0:T(8,128)(2,1)S(1)}, bf16[2,320,128]{2,1,0:T(8,128)(2,1)}, u32[]{:S(2)}) copy-start(bf16[2,320,128]{2,1,0:T(8,128)(2,1)} %pad_maximum_fusion.5) | copy-start | bytes 491524
  24.5 6.6 %collective-permute-start.4 = (bf16[4,320,128]{2,1,0:T(8,128)(2,1)S(1)}, bf16[4,320,128]{2,1,0:T(8,128)(2,1)S(1)}, u32[]{:S(2)}, u32[]{:S(2)}) collective-permute-start(bf16[4,320,128]{2,1,0:T(8,128)(2,1)S(1)} %pad_maximum_fusion.4), channel_id=1, source_target_pairs={{0,4},{1,5},{2,6},{3,7},{4,0},{5,1},{6,2},{7,3},{8,12},{9,13},{10,... | collective-permute-start | bytes 983048 | tf_op jit(solution)/shard_map/ppermute | solution.py:265
  25.2 23.4 %collective-permute-start.7 = (bf16[2,64,3072]{2,1,0:T(8,128)(2,1)S(1)}, bf16[2,64,3072]{2,1,0:T(8,128)(2,1)S(1)}, u32[]{:S(2)}, u32[]{:S(2)}) collective-permute-start(bf16[2,64,3072]{2,1,0:T(8,128)(2,1)S(1)} %pad_maximum_fusion.1), channel_id=1, source_target_pairs={{1,2},{2,1},{5,6},{6,5},{9,10},{10,9},{13,14},{14,13},{17,18},{18,... | collective-permute-start | bytes 2359304 | tf_op jit(solution)/shard_map/ppermute | solution.py:307
  29.1 19.5 %collective-permute-start.8 = (bf16[2,64,3072]{2,1,0:T(8,128)(2,1)S(1)}, bf16[2,64,3072]{2,1,0:T(8,128)(2,1)S(1)}, u32[]{:S(2)}, u32[]{:S(2)}) collective-permute-start(bf16[2,64,3072]{2,1,0:T(8,128)(2,1)S(1)} %pad_maximum_fusion.1), channel_id=1, source_target_pairs={{3,4},{4,3},{7,8},{8,7},{11,12},{12,11},{19,20},{20,19},{23,24},{2... | collective-permute-start | bytes 2359304 | tf_op jit(solution)/shard_map/ppermute | solution.py:310
  29.8 9.7 %collective-permute-start.3 = (bf16[4,320,128]{2,1,0:T(8,128)(2,1)S(1)}, bf16[4,320,128]{2,1,0:T(8,128)(2,1)S(1)}, u32[]{:S(2)}, u32[]{:S(2)}) collective-permute-start(bf16[4,320,128]{2,1,0:T(8,128)(2,1)S(1)} %pad_maximum_fusion.4), channel_id=1, source_target_pairs={{0,16},{16,0},{1,17},{17,1},{2,18},{18,2},{3,19},{19,3},{4,20},{20... | collective-permute-start | bytes 983048 | tf_op jit(solution)/shard_map/ppermute | solution.py:268
  31.0 14.8 %collective-permute-start.5 = (bf16[4,320,128]{2,1,0:T(8,128)(2,1)S(1)}, bf16[4,320,128]{2,1,0:T(8,128)(2,1)S(1)}, u32[]{:S(2)}, u32[]{:S(2)}) collective-permute-start(bf16[4,320,128]{2,1,0:T(8,128)(2,1)S(1)} %collective-permute-done.4), channel_id=1, source_target_pairs={{0,16},{16,0},{1,17},{17,1},{2,18},{18,2},{3,19},{19,3},{4,20},{20... | collective-permute-start | bytes 983048 | tf_op jit(solution)/shard_map/ppermute | solution.py:268
  39.5 11.1 %collective-permute-start.9 = (bf16[8,320,128]{2,1,0:T(8,128)(2,1)S(1)}, bf16[8,320,128]{2,1,0:T(8,128)(2,1)S(1)}, u32[]{:S(2)}, u32[]{:S(2)}) collective-permute-start(bf16[8,320,128]{2,1,0:T(8,128)(2,1)S(1)} %constant_dynamic-update-slice_fusion.rest_2_), channel_id=1, source_target_pairs={{0,1},{1,0},{2,3},{3,2},{4,5},{5,4},{6,7},{7,6},{8,9},{9,8},{10,11... | collective-permute-start | bytes 1966088 | tf_op jit(solution)/shard_map/ppermute | solution.py:265
  48.5 2.2 %copy-start.3 = (bf16[320,5120]{1,0:T(8,128)(2,1)S(1)}, bf16[320,5120]{1,0:T(8,128)(2,1)}, u32[]{:S(2)}) copy-start(bf16[320,5120]{1,0:T(8,128)(2,1)} %frozen.1) | copy-start | bytes 9830404
  48.5 2.2 %copy-start.4 = (bf16[320,128]{1,0:T(8,128)(2,1)S(1)}, bf16[320,128]{1,0:T(8,128)(2,1)}, u32[]{:S(2)}) copy-start(bf16[320,128]{1,0:T(8,128)(2,1)} %own_down.1) | copy-start | bytes 245764
  48.6 2.2 %collective-permute-start.10 = (bf16[8,320,128]{2,1,0:T(8,128)(2,1)S(1)}, bf16[8,320,128]{2,1,0:T(8,128)(2,1)S(1)}, u32[]{:S(2)}, u32[]{:S(2)}) collective-permute-start(bf16[8,320,128]{2,1,0:T(8,128)(2,1)S(1)} %pad_maximum_fusion.2.rest_4_), channel_id=1, source_target_pairs={{0,1},{1,0},{2,3},{3,2},{4,5},{5,4},{6,7},{7,6},{8,9},{9,8},{10,11... | collective-permute-start | bytes 1966088 | tf_op jit(solution)/shard_map/ppermute | solution.py:265

commit v6 on v4

--- a/solution.py
+++ b/solution.py
@@ -13,6 +13,7 @@
 FRAME = 64
 NEAR = 2 * FRAME
 CHUNK = 512
+WIDE = 2 * CHUNK
 SCORE_SCALE = HD ** (-0.5) * 1.4426950408889634
 ADAPTER_SCALE = MODEL_WIDTH ** (-0.5)
 FAR = -1e30
@@ -68,7 +69,7 @@
         lo, hi = lo_ref[row], hi_ref[row]
         keys = pl.ds(pl.multiple_of(lo - base, FRAME), NEAR)
         bias = clip_bias(lo, hi)
-        for col in range(0, CHUNK, 2 * HD):
+        for col in range(0, WIDE, 2 * HD):
             part = slice(col, col + 2 * HD)
             targets.append((slice(row - FRAME, row), part))
             loads.append(
@@ -85,13 +86,13 @@
 
 def inner_attention(lo, hi, q, k, v):
     rows, width = q.shape
-    block = pl.BlockSpec((rows, CHUNK), lambda i: (0, i))
+    block = pl.BlockSpec((rows, WIDE), lambda i: (0, i))
     return pl.pallas_call(
         inner_kernel,
-        grid=(width // CHUNK,),
+        grid=(width // WIDE,),
         out_shape=jax.ShapeDtypeStruct((NEAR, width), BF16),
         in_specs=[SMEM, SMEM, block, block, block],
-        out_specs=pl.BlockSpec((NEAR, CHUNK), lambda i: (0, i)),
+        out_specs=pl.BlockSpec((NEAR, WIDE), lambda i: (0, i)),
         compiler_params=pltpu.CompilerParams(vmem_limit_bytes=16 << 20),
         cost_estimate=pl.CostEstimate(
             flops=16 * NEAR * NEAR * width,
@@ -102,13 +103,18 @@
     )(lo, hi, q, k, v)
 
 
-def edge_kernel(is_near, lo_ref, hi_ref, q, k, v, *rest):
-    halos, out = rest[:-1], rest[-1]
-    rows, width = q.shape
+def edge_side(is_near, rows):
+    right = lax.rem(lax.axis_index("seq"), 2) == (0 if is_near else 1)
+    return right, pl.multiple_of(jnp.where(right, rows - FRAME, 0), FRAME)
+
+
+def attend_edge(is_near, lo_ref, hi_ref, q, k, v, halos, out):
+    rows, width = q.shape
+    pairs = width // (2 * HD)
+    unroll = next(n for n in (10, 8, 6, 5, 4, 2, 1) if pairs % n == 0)
     me = lax.axis_index("seq")
     base = me * rows
-    right = lax.rem(me, 2) == (0 if is_near else 1)
-    row = pl.multiple_of(jnp.where(right, rows - FRAME, 0), FRAME)
+    right, row = edge_side(is_near, rows)
     first = pl.multiple_of(jnp.where(right, rows - NEAR, 0), NEAR)
     second = pl.multiple_of(first + FRAME, FRAME)
     lo, hi = lo_ref[row], hi_ref[row]
@@ -132,8 +138,8 @@
 
     def step(i, _):
         loads, parts = [], []
-        for col in range(0, 2 * CHUNK, 2 * HD):
-            part = pl.ds(pl.multiple_of(i * 2 * CHUNK + col, 2 * HD), 2 * HD)
+        for pair in range(unroll):
+            part = pl.ds(pl.multiple_of((i * unroll + pair) * 2 * HD, 2 * HD), 2 * HD)
             parts.append(part)
             loads.append(
                 (
@@ -147,28 +153,39 @@
             out[:, part] = result
         return 0
 
-    lax.fori_loop(0, width // (2 * CHUNK), step, 0)
-
-
-def edge_attention(lo, hi, q, k, v, *halos):
-    rows, width = q.shape
-    is_near = len(halos) == 1
+    lax.fori_loop(0, pairs // unroll, step, 0)
+
+
+def near_kernel(lo_ref, hi_ref, q, k, v, halo, out):
+    attend_edge(True, lo_ref, hi_ref, q, k, v, (halo,), out)
+
+
+def edge_cost(rows, width):
+    return pl.CostEstimate(
+        flops=8 * NEAR * NEAR * width,
+        bytes_accessed=7 * rows * width,
+        transcendentals=FRAME * NEAR * HEADS,
+    )
+
+
+def near_attention(lo, hi, q, k, v, halo):
+    rows, width = q.shape
     return pl.pallas_call(
-        functools.partial(edge_kernel, is_near),
+        near_kernel,
         out_shape=jax.ShapeDtypeStruct((FRAME, width), BF16),
-        in_specs=[SMEM, SMEM] + [VMEM] * (3 + len(halos)),
+        in_specs=[SMEM, SMEM] + [VMEM] * 4,
         out_specs=VMEM,
         compiler_params=pltpu.CompilerParams(vmem_limit_bytes=20 << 20),
-        cost_estimate=pl.CostEstimate(
-            flops=8 * NEAR * NEAR * width,
-            bytes_accessed=7 * rows * width,
-            transcendentals=FRAME * NEAR * HEADS,
-        ),
-        name="near_edge_attention" if is_near else "far_edge_attention",
-    )(lo, hi, q, k, v, *halos)
-
-
-def last_kernel(layout, frozen, own_down, inner, near, far, *rest):
+        cost_estimate=edge_cost(rows, width),
+        name="near_edge_attention",
+    )(lo, hi, q, k, v, halo)
+
+
+def adapt(value, narrow, factor):
+    return (value.astype(F32) + ADAPTER_SCALE * dot(narrow, factor, NT)).astype(BF16)
+
+
+def merge_kernel(layout, frozen, own_down, inner, near, *rest):
     refs, rest = rest[:-6], rest[-6:]
     merged, attended, factors, w, result, sems = rest
     shard, width = frozen.shape
@@ -181,12 +198,10 @@
             at = pl.ds(pl.multiple_of((me ^ mask) * shard, shard), shard)
             factors[target, at, :] = ref[i]
     if not layout:
-        factors = refs[0]
+        factors[...] = refs[0][...]
     down, up = factors.at[0], factors.at[1]
-    right = lax.rem(me, 2) == 0
-    near_row = pl.multiple_of(jnp.where(right, rows - FRAME, 0), FRAME)
-    far_row = pl.multiple_of(jnp.where(right, 0, rows - FRAME), FRAME)
-    parts = ((inner, FRAME), (near, near_row), (far, far_row))
+    _, near_row = edge_side(True, rows)
+    parts = ((inner, FRAME), (near, near_row))
     reduced = [dot(att[...], down[...], NN).astype(BF16) for att, _ in parts]
     stores = []
 
@@ -197,34 +212,33 @@
     for first in range(0, width, CHUNK):
         part = pl.ds(first, CHUNK)
         factor = up[part, :]
-        product = dot(own_down[...], factor, NT)
-        w[:, part] = (frozen[:, part].astype(F32) + ADAPTER_SCALE * product).astype(BF16)
+        w[:, part] = adapt(frozen[:, part], own_down[...], factor)
         store(w.at[:, part], merged.at[:, part])
         for narrow, (att, row) in zip(reduced, parts):
-            value = att[:, part].astype(F32) + ADAPTER_SCALE * dot(narrow, factor, NT)
-            result[pl.ds(row, att.shape[0]), part] = value.astype(BF16)
-        store(result.at[:, part], attended.at[:, part])
+            result[pl.ds(row, att.shape[0]), part] = adapt(att[:, part], narrow, factor)
+            at = (pl.ds(row, att.shape[0]), part)
+            store(result.at[at], attended.at[at])
     for copy in stores:
         copy.wait()
 
 
-def last(frozen, own_down, inner, near, far, layout, pieces):
+def merge(frozen, own_down, inner, near, layout, pieces):
     shard, width = frozen.shape
     rank = own_down.shape[1]
     rows = 2 * NEAR
     return pl.pallas_call(
-        functools.partial(last_kernel, layout),
+        functools.partial(merge_kernel, layout),
         out_shape=(
             jax.ShapeDtypeStruct((shard, width), BF16),
             jax.ShapeDtypeStruct((rows, width), BF16),
+            jax.ShapeDtypeStruct((2, width, rank), BF16),
         ),
-        in_specs=[VMEM] * (5 + len(pieces)),
-        out_specs=(ANY, ANY),
+        in_specs=[VMEM] * (4 + len(pieces)),
+        out_specs=(ANY, ANY, VMEM),
         scratch_shapes=[
-            pltpu.VMEM((2, width, rank), BF16),
             pltpu.VMEM((shard, width), BF16),
             pltpu.VMEM((rows, width), BF16),
-            pltpu.SemaphoreType.DMA((2 * (width // CHUNK),)),
+            pltpu.SemaphoreType.DMA((3 * (width // CHUNK),)),
         ],
         compiler_params=pltpu.CompilerParams(vmem_limit_bytes=24 << 20),
         cost_estimate=pl.CostEstimate(
@@ -232,8 +246,46 @@
             bytes_accessed=4 * (shard + rows) * width + 4 * width * rank,
             transcendentals=0,
         ),
-        name="adapter_and_merge",
-    )(frozen, own_down, inner, near, far, *pieces)
+        name="merge_and_adapter",
+    )(frozen, own_down, inner, near, *pieces)
+
+
+def far_kernel(lo_ref, hi_ref, q, k, v, direct, distant, factors, _, out, mixed, result, sems):
+    rows, width = q.shape
+    attend_edge(False, lo_ref, hi_ref, q, k, v, (direct, distant), mixed)
+    narrow = dot(mixed[...], factors[0], NN).astype(BF16)
+    _, row = edge_side(False, rows)
+    stores = []
+    for first in range(0, width, WIDE):
+        part = pl.ds(first, WIDE)
+        result[:, part] = adapt(mixed[:, part], narrow, factors[1, part, :])
+        stores.append(
+            pltpu.make_async_copy(
+                result.at[:, part], out.at[pl.ds(row, FRAME), part], sems.at[len(stores)]
+            )
+        )
+        stores[-1].start()
+    for copy in stores:
+        copy.wait()
+
+
+def far_rows(lo, hi, q, k, v, direct, distant, factors, attended):
+    rows, width = q.shape
+    return pl.pallas_call(
+        far_kernel,
+        out_shape=jax.ShapeDtypeStruct((rows, width), BF16),
+        in_specs=[SMEM, SMEM] + [VMEM] * 6 + [ANY],
+        out_specs=ANY,
+        input_output_aliases={8: 0},
+        scratch_shapes=[
+            pltpu.VMEM((FRAME, width), BF16),
+            pltpu.VMEM((FRAME, width), BF16),
+            pltpu.SemaphoreType.DMA((width // WIDE,)),
+        ],
+        compiler_params=pltpu.CompilerParams(vmem_limit_bytes=24 << 20),
+        cost_estimate=edge_cost(rows, width),
+        name="far_edge_rows",
+    )(lo, hi, q, k, v, direct, distant, factors, attended)
 
 
 def body(q, k, v, lo, hi, down, up, frozen):
@@ -244,50 +296,57 @@
     def rim(start):
         return jnp.stack([lax.dynamic_slice_in_dim(x, start, FRAME, 0) for x in (k, v)])
 
-    def send(cells, pairs):
-        return lax.ppermute(cells, "seq", pairs + [(b, a) for a, b in pairs])
-
     def swap(cells, mask):
-        return send(cells, [(i, i ^ mask) for i in range(count) if not i & mask])
+        return lax.ppermute(cells, "seq", [(i, i ^ mask) for i in range(count)])
 
     def cross(cells):
         return lax.ppermute(cells, "group", [(0, 1), (1, 0)])
 
+    def near_halo(odd):
+        return swap(rim((1 - odd) * (rows - FRAME)), 1)
+
+    direct_pairs, distant_pairs = (
+        [(i + a, i + 1 - a) for i in range(first, count - 1, 4) for a in (0, 1)]
+        for first in (1, 3)
+    )
     far_rim = rim(odd * (rows - FRAME))
-    direct = send(far_rim, [(i, i + 1) for i in range(1, count - 1, 4)])
-    near = swap(rim((1 - odd) * (rows - FRAME)), 1)
-    distant = [(i, i + 1) for i in range(3, count - 1, 4)]
     up = up.T
     if lax.axis_size("group") != 2 or down.shape[0] % 32:
         both = lax.all_gather(jnp.stack([down, up]), "seq", axis=1, tiled=True)
         layout, pieces = [], [both]
+        direct = lax.ppermute(far_rim, "seq", direct_pairs)
+        distant = lax.ppermute(far_rim, "seq", distant_pairs)
         inner = inner_attention(lo, hi, q, k, v)
-        near_edge = edge_attention(lo, hi, q, k, v, near)
-        diagonal_halo = send(far_rim, distant)
+        near = near_attention(lo, hi, q, k, v, near_halo(odd))
     else:
+        barrier = lax.optimization_barrier
+        inner = inner_attention(lo, hi, q, k, v)
         cells = jnp.where(lax.axis_index("group") == 0, down, up)[None]
         masks = [0]
         steps = [2] + [count >> j for j in range(1, count.bit_length()) if count >> j > 2]
         for mask in steps[:-1]:
             cells = jnp.concatenate([cells, swap(cells, mask)])
             masks = masks + [have ^ mask for have in masks]
-        cells, far_rim, lo_inner = lax.optimization_barrier((cells, far_rim, lo))
+            if mask == 2:
+                cells, far_rim = barrier((cells, far_rim))
+                direct = lax.ppermute(far_rim, "seq", direct_pairs)
+        halo = near_halo(odd)
+        cells, inner, far_rim = barrier((cells, inner, far_rim))
         new = swap(cells, steps[-1])
-        diagonal_halo = send(far_rim, distant)
+        distant = lax.ppermute(far_rim, "seq", distant_pairs)
         early = cross(cells)
-        inner = inner_attention(lo_inner, hi, q, k, v)
-        new, inner, lo_near = lax.optimization_barrier((new, inner, lo))
+        near = near_attention(lo, hi, q, k, v, halo)
+        new, near = barrier((new, near))
         late = cross(new)
         cells = jnp.concatenate([cells, new])
         masks = masks + [have ^ steps[-1] for have in masks]
-        near_edge = edge_attention(lo_near, hi, q, k, v, near)
         other = jnp.concatenate([early, late])
-        other, near_edge = lax.optimization_barrier((other, near_edge))
+        other, direct = barrier((other, direct))
         across = [mask ^ 1 for mask in masks]
         layout = [(0, masks), (0, across), (1, masks), (1, across)]
         pieces = [cells, swap(cells, 1), other, swap(other, 1)]
-    far_edge = edge_attention(lo, hi, q, k, v, direct, diagonal_halo)
-    merged, attended = last(frozen, down, inner, near_edge, far_edge, layout, pieces)
+    merged, attended, factors = merge(frozen, down, inner, near, layout, pieces)
+    attended = far_rows(lo, hi, q, k, v, direct, distant, factors, attended)
     return (attended, merged)
 
 

time: 58.5 us -> 49 us (0.84)
  the two profiles are of different devices: /device:TPU:17 before, /device:TPU:1 now
where the time goes in v6:
time: 49 us; the launch traced here: 48.3 us
  starting transfers between devices  15.7 us (32%)
  waiting for transfers between devices  15.1 us (31%)
  Pallas kernels  13.3 us (27%)
  local copies, waits for them, and re-layouts  2.1 us (4%)
  other arithmetic  1.3 us (3%)
  between operations  0.78 us (2%)
    ppermute x6, starting transfers between devices, swap(): return lax.ppermute(cells, 'seq', [(i, i ^ mask) for i in range(count)])  8.63 us
    ppermute x6, waiting for transfers between devices, swap(): return lax.ppermute(cells, 'seq', [(i, i ^ mask) for i in range(count)])  8.4 us
    ppermute x2, waiting for transfers between devices, cross(): return lax.ppermute(cells, 'group', [(0, 1), (1, 0)])  6.72 us
    pallas_call x1, Pallas kernels, inner_attention(): pl.pallas_call(inner_kernel, grid=(width // WIDE,), out_shape=jax.ShapeDt...  3.93 us
    pallas_call x1, Pallas kernels, far_rows(): pl.pallas_call(far_kernel, out_shape=jax.ShapeDtypeStruct((rows, width),...  3.69 us
    pallas_call x1, Pallas kernels, merge(): pl.pallas_call(functools.partial(merge_kernel, layout), out_shape=(jax.Sh...  3.68 us
    ppermute x1, starting transfers between devices, body(): direct = lax.ppermute(far_rim, 'seq', direct_pairs)  3.59 us
    ppermute x2, starting transfers between devices, cross(): return lax.ppermute(cells, 'group', [(0, 1), (1, 0)])  2.77 us
  transfers between devices with their start and end apart: 10, of which 4 were waited for; matrix products, arithmetic and copies ran while one was open for 5% of the time, Pallas kernels for 20%

profile of v6, /device:TPU:1, one launch (start us, length us, event | category | flops | bytes accessed | tf_op | source)
XLA Modules:
  0.0 48.3 jit_solution(7490456463124479724)
XLA Ops:
  0.6 0.9 %fusion = bf16[1,320,128]{2,1,0:T(8,128)(2,1)S(1)} fusion(bf16[320,128]{1,0:T(8,128)(2,1)} %own_down.1, bf16[128,320]{0,1:T(8,128)(2,1)} %param.14, pred[]{:T(512)S(6)} %eq.3), kind=kLoop, calls=%fused_computation.10 | loop fusion | flops 40960 | bytes 245761 | tf_op jit(solution)/shard_map/broadcast_in_dim | solution.py:324
  1.6 2.1 %collective-permute-start = (bf16[1,320,128]{2,1,0:T(8,128)(2,1)S(1)}, bf16[1,320,128]{2,1,0:T(8,128)(2,1)S(1)}, u32[]{:S(2)}, u32[]{:S(2)}) collective-permute-start(bf16[1,320,128]{2,1,0:T(8,128)(2,1)S(1)} %fusion), channel_id=1, source_target_pairs={{0,2},{1,3},{2,0},{3,1},{4,6},{5,7},{6,4},{7,5},{8,10},{9,11},{10,... | collective-permute-start | bytes 245768 | tf_op jit(solution)/shard_map/ppermute | solution.py:300
  3.7 0.0 copy-start.2
  3.7 2.0 %dynamic-slice_bitcast_fusion = (bf16[1,64,5120]{2,1,0:T(8,128)(2,1)S(1)}, bf16[1,64,5120]{2,1,0:T(8,128)(2,1)S(1)}, bf16[1,64,5120]{2,1,0:T(8,128)(2,1)S(1)}, bf16[1,64,5120]{2,1,0:T(8,128)(2,1)S(1)}) fusion(bf16[256,5120]{1,0:T(8,128)(2,1)} %v.3, s32[]{:T(128)S(6)} %select_n.19, s32[]{:T(128)S(6)} %select_n.18, bf16[256,5120]{1,0:T(8,128)(2,1)} %k.3), kind=kLoop, calls=%fused_computation.3 | loop fusion | bytes 5242888 | tf_op jit(solution)/shard_map/stack | solution.py:297
  5.7 0.0 copy-start.1
  5.7 0.1 pad_maximum_fusion.1
  5.9 1.0 %collective-permute-start.4 = (bf16[2,64,5120]{2,1,0:T(8,128)(2,1)S(1)}, bf16[2,64,5120]{2,1,0:T(8,128)(2,1)S(1)}, u32[]{:S(2)}, u32[]{:S(2)}) collective-permute-start(bf16[2,64,5120]{2,1,0:T(8,128)(2,1)S(1)} %pad_maximum_fusion.1), channel_id=1, source_target_pairs={{0,1},{1,0},{2,3},{3,2},{4,5},{5,4},{6,7},{7,6},{8,9},{9,8},{10,11... | collective-permute-start | bytes 3932168 | tf_op jit(solution)/shard_map/ppermute | solution.py:300
  6.9 0.0 copy-start
  6.9 0.0 copy-start.5
  6.9 0.0 copy-start.6
  6.9 0.1 pad_maximum_fusion
  7.0 0.0 collective-permute-done
  7.1 3.6 %collective-permute-start.6 = (bf16[2,64,5120]{2,1,0:T(8,128)(2,1)S(1)}, bf16[2,64,5120]{2,1,0:T(8,128)(2,1)S(1)}, u32[]{:S(2)}, u32[]{:S(2)}) collective-permute-start(bf16[2,64,5120]{2,1,0:T(8,128)(2,1)S(1)} %pad_maximum_fusion), channel_id=1, source_target_pairs={{1,2},{2,1},{5,6},{6,5},{9,10},{10,9},{13,14},{14,13},{17,18},{18,... | collective-permute-start | bytes 3932168 | tf_op jit(solution)/shard_map/ppermute | solution.py:332
  10.7 2.4 %collective-permute-start.1 = (bf16[2,320,128]{2,1,0:T(8,128)(2,1)S(1)}, bf16[2,320,128]{2,1,0:T(8,128)(2,1)S(1)}, u32[]{:S(2)}, u32[]{:S(2)}) collective-permute-start(bf16[2,320,128]{2,1,0:T(8,128)(2,1)S(1)} %pad_maximum_fusion.4), channel_id=1, source_target_pairs={{0,8},{1,9},{2,10},{3,11},{4,12},{5,13},{6,14},{7,15},{8,0},{9,1},... | collective-permute-start | bytes 491528 | tf_op jit(solution)/shard_map/ppermute | solution.py:300
  13.0 0.0 copy-done.2
  13.0 0.0 copy-done.1
  13.0 0.0 copy-done
  13.0 0.0 copy-done.5
  13.0 0.0 copy-done.6
  13.1 3.9 %inner_attention.1.inner = bf16[128,5120]{1,0:T(8,128)(2,1)S(1)} custom-call(s32[256]{0:T(256)S(1)} %copy-done.5, s32[256]{0:T(256)S(1)} %copy-done.6, bf16[256,5120]{1,0:T(8,128)(2,1)S(1)} %copy-done.2, bf16[256,5120]{1,0:T(8,128)(2,1)S(1)} %copy-done, bf16[256,5120]{1,0:T(8,128)(2,1)S(1)} %copy-done.1), custom_call_target="tpu_custom_call" | custom-call | flops 1342177280 | bytes 9175040 | tf_op jit(solution)/shard_map/inner_attention/pallas_call | solution.py:90
  17.0 2.0 %collective-permute-done.1 = bf16[2,320,128]{2,1,0:T(8,128)(2,1)S(1)} collective-permute-done((bf16[2,320,128]{2,1,0:T(8,128)(2,1)S(1)}, bf16[2,320,128]{2,1,0:T(8,128)(2,1)S(1)}, u32[]{:S(2)}, u32[]{:S(2)}) %collective-permute-start.1) | collective-permute-done | bytes 163872 | tf_op jit(solution)/shard_map/ppermute | solution.py:300
  19.1 1.2 %collective-permute-start.3 = (bf16[4,320,128]{2,1,0:T(8,128)(2,1)S(1)}, bf16[4,320,128]{2,1,0:T(8,128)(2,1)S(1)}, u32[]{:S(2)}, u32[]{:S(2)}) collective-permute-start(bf16[4,320,128]{2,1,0:T(8,128)(2,1)S(1)} %pad_maximum_fusion.3), channel_id=1, source_target_pairs={{0,4},{1,5},{2,6},{3,7},{4,0},{5,1},{6,2},{7,3},{8,12},{9,13},{10,... | collective-permute-start | bytes 983048 | tf_op jit(solution)/shard_map/ppermute | solution.py:300
  20.2 0.7 %collective-permute-start.7 = (bf16[2,64,5120]{2,1,0:T(8,128)(2,1)S(1)}, bf16[2,64,5120]{2,1,0:T(8,128)(2,1)S(1)}, u32[]{:S(2)}, u32[]{:S(2)}) collective-permute-start(bf16[2,64,5120]{2,1,0:T(8,128)(2,1)S(1)} %pad_maximum_fusion), channel_id=1, source_target_pairs={{3,4},{4,3},{7,8},{8,7},{11,12},{12,11},{19,20},{20,19},{23,24},{2... | collective-permute-start | bytes 3932168 | tf_op jit(solution)/shard_map/ppermute | solution.py:336
  21.0 1.2 %collective-permute-start.2 = (bf16[4,320,128]{2,1,0:T(8,128)(2,1)S(1)}, bf16[4,320,128]{2,1,0:T(8,128)(2,1)S(1)}, u32[]{:S(2)}, u32[]{:S(2)}) collective-permute-start(bf16[4,320,128]{2,1,0:T(8,128)(2,1)S(1)} %pad_maximum_fusion.3), channel_id=1, source_target_pairs={{0,16},{16,0},{1,17},{17,1},{2,18},{18,2},{3,19},{19,3},{4,20},{20... | collective-permute-start | bytes 983048 | tf_op jit(solution)/shard_map/ppermute | solution.py:303
  22.2 0.0 collective-permute-done.4.halo
  22.2 0.0 copy-start.3
  22.2 2.0 %near_edge_attention.1.near = bf16[64,5120]{1,0:T(8,128)(2,1)S(1)} custom-call(s32[256]{0:T(256)S(1)} %copy-done.5, s32[256]{0:T(256)S(1)} %copy-done.6, bf16[256,5120]{1,0:T(8,128)(2,1)S(1)} %copy-done.2, bf16[256,5120]{1,0:T(8,128)(2,1)S(1)} %copy-done, bf16[256,5120]{1,0:T(8,128)(2,1)S(1)} %copy-done.1, bf16[2,64,5120]{2,1,0:T(8,128)(2,1)S(1)} %collective-permute-done.4.halo), custom_call_target="tpu_custom_call" | custom-call | flops 671088640 | bytes 9175040 | tf_op jit(solution)/shard_map/near_edge_attention/pallas_call | solution.py:173
  24.2 0.0 copy-start.4
  24.2 4.6 %collective-permute-done.3 = bf16[4,320,128]{2,1,0:T(8,128)(2,1)S(1)} collective-permute-done((bf16[4,320,128]{2,1,0:T(8,128)(2,1)S(1)}, bf16[4,320,128]{2,1,0:T(8,128)(2,1)S(1)}, u32[]{:S(2)}, u32[]{:S(2)}) %collective-permute-start.3) | collective-permute-done | bytes 327712 | tf_op jit(solution)/shard_map/ppermute | solution.py:300
  28.8 1.5 %collective-permute-start.5 = (bf16[4,320,128]{2,1,0:T(8,128)(2,1)S(1)}, bf16[4,320,128]{2,1,0:T(8,128)(2,1)S(1)}, u32[]{:S(2)}, u32[]{:S(2)}) collective-permute-start(bf16[4,320,128]{2,1,0:T(8,128)(2,1)S(1)} %collective-permute-done.3), channel_id=1, source_target_pairs={{0,16},{16,0},{1,17},{17,1},{2,18},{18,2},{3,19},{19,3},{4,20},{20... | collective-permute-start | bytes 983048 | tf_op jit(solution)/shard_map/ppermute | solution.py:303
  30.4 0.7 %collective-permute-start.8 = (bf16[8,320,128]{2,1,0:T(8,128)(2,1)S(1)}, bf16[8,320,128]{2,1,0:T(8,128)(2,1)S(1)}, u32[]{:S(2)}, u32[]{:S(2)}) collective-permute-start(bf16[8,320,128]{2,1,0:T(8,128)(2,1)S(1)} %constant_dynamic-update-slice_fusion.rest_0_), channel_id=1, source_target_pairs={{0,1},{1,0},{2,3},{3,2},{4,5},{5,4},{6,7},{7,6},{8,9},{9,8},{10,11... | collective-permute-start | bytes 1966088 | tf_op jit(solution)/shard_map/ppermute | solution.py:300
  31.1 0.0 collective-permute-done.2
  31.1 6.7 %collective-permute-done.5 = bf16[4,320,128]{2,1,0:T(8,128)(2,1)S(1)} collective-permute-done((bf16[4,320,128]{2,1,0:T(8,128)(2,1)S(1)}, bf16[4,320,128]{2,1,0:T(8,128)(2,1)S(1)}, u32[]{:S(2)}, u32[]{:S(2)}) %collective-permute-start.5) | collective-permute-done | bytes 327712 | tf_op jit(solution)/shard_map/ppermute | solution.py:303
  37.8 0.1 pad_maximum_fusion.2.rest_2_
  37.9 0.0 collective-permute-done.6.direct
  37.9 1.2 %collective-permute-start.9 = (bf16[8,320,128]{2,1,0:T(8,128)(2,1)S(1)}, bf16[8,320,128]{2,1,0:T(8,128)(2,1)S(1)}, u32[]{:S(2)}, u32[]{:S(2)}) collective-permute-start(bf16[8,320,128]{2,1,0:T(8,128)(2,1)S(1)} %pad_maximum_fusion.2.rest_2_), channel_id=1, source_target_pairs={{0,1},{1,0},{2,3},{3,2},{4,5},{5,4},{6,7},{7,6},{8,9},{9,8},{10,11... | collective-permute-start | bytes 1966088 | tf_op jit(solution)/shard_map/ppermute | solution.py:300
  39.2 0.0 collective-permute-done.8.rest_1_
  39.2 1.7 %collective-permute-done.9.rest_3_ = bf16[8,320,128]{2,1,0:T(8,128)(2,1)S(1)} collective-permute-done((bf16[8,320,128]{2,1,0:T(8,128)(2,1)S(1)}, bf16[8,320,128]{2,1,0:T(8,128)(2,1)S(1)}, u32[]{:S(2)}, u32[]{:S(2)}) %collective-permute-start.9) | collective-permute-done | bytes 655392 | tf_op jit(solution)/shard_map/ppermute | solution.py:300
  40.9 0.0 copy-done.3
  40.9 0.0 copy-done.4
  40.9 3.7 %merge_and_adapter.1 = (bf16[320,5120]{1,0:T(8,128)(2,1)}, bf16[256,5120]{1,0:T(8,128)(2,1)}, bf16[2,5120,128]{2,1,0:T(8,128)(2,1)S(1)}) custom-call(bf16[320,5120]{1,0:T(8,128)(2,1)S(1)} %copy-done.3, bf16[320,128]{1,0:T(8,128)(2,1)S(1)} %copy-done.4, bf16[128,5120]{1,0:T(8,128)(2,1)S(1)} %inner_attention.1.inner, ...), custom_call_target="tpu_custom_call" | custom-call | flops 1090519040 | bytes 14417920 | tf_op jit(solution)/shard_map/merge_and_adapter/pallas_call | solution.py:229
  44.6 0.0 collective-permute-done.7.distant
  44.6 3.7 %far_edge_rows.1 = bf16[256,5120]{1,0:T(8,128)(2,1)} custom-call(s32[256]{0:T(256)S(1)} %copy-done.5, s32[256]{0:T(256)S(1)} %copy-done.6, bf16[256,5120]{1,0:T(8,128)(2,1)S(1)} %copy-done.2, bf16[256,5120]{1,0:T(8,128)(2,1)S(1)} %copy-done, bf16[256,5120]{1,0:T(8,128)(2,1)S(1)} %copy-done.1, ...), custom_call_target="tpu_custom_call", output_to_operand_aliasing={{}: (8, {})} | custom-call | flops 671088640 | bytes 9175040 | tf_op jit(solution)/shard_map/far_edge_rows/pallas_call | solution.py:274
  (4 shorter events, 0.1 us)
Async XLA Ops:
  1.6 5.4 %collective-permute-start = (bf16[1,320,128]{2,1,0:T(8,128)(2,1)S(1)}, bf16[1,320,128]{2,1,0:T(8,128)(2,1)S(1)}, u32[]{:S(2)}, u32[]{:S(2)}) collective-permute-start(bf16[1,320,128]{2,1,0:T(8,128)(2,1)S(1)} %fusion), channel_id=1, source_target_pairs={{0,2},{1,3},{2,0},{3,1},{4,6},{5,7},{6,4},{7,5},{8,10},{9,11},{10,... | collective-permute-start | bytes 245768 | tf_op jit(solution)/shard_map/ppermute | solution.py:300
  3.7 9.3 %copy-start.2 = (bf16[256,5120]{1,0:T(8,128)(2,1)S(1)}, bf16[256,5120]{1,0:T(8,128)(2,1)}, u32[]{:S(2)}) copy-start(bf16[256,5120]{1,0:T(8,128)(2,1)} %q.3) | copy-start | bytes 7864324
  5.7 7.3 %copy-start.1 = (bf16[256,5120]{1,0:T(8,128)(2,1)S(1)}, bf16[256,5120]{1,0:T(8,128)(2,1)}, u32[]{:S(2)}) copy-start(bf16[256,5120]{1,0:T(8,128)(2,1)} %v.3) | copy-start | bytes 7864324
  5.9 16.4 %collective-permute-start.4 = (bf16[2,64,5120]{2,1,0:T(8,128)(2,1)S(1)}, bf16[2,64,5120]{2,1,0:T(8,128)(2,1)S(1)}, u32[]{:S(2)}, u32[]{:S(2)}) collective-permute-start(bf16[2,64,5120]{2,1,0:T(8,128)(2,1)S(1)} %pad_maximum_fusion.1), channel_id=1, source_target_pairs={{0,1},{1,0},{2,3},{3,2},{4,5},{5,4},{6,7},{7,6},{8,9},{9,8},{10,11... | collective-permute-start | bytes 3932168 | tf_op jit(solution)/shard_map/ppermute | solution.py:300
  6.9 6.2 %copy-start = (bf16[256,5120]{1,0:T(8,128)(2,1)S(1)}, bf16[256,5120]{1,0:T(8,128)(2,1)}, u32[]{:S(2)}) copy-start(bf16[256,5120]{1,0:T(8,128)(2,1)} %k.3) | copy-start | bytes 7864324
  6.9 6.2 %copy-start.5 = (s32[256]{0:T(256)S(1)}, s32[256]{0:T(256)}, u32[]{:S(2)}) copy-start(s32[256]{0:T(256)} %lo_ref.5) | copy-start | bytes 3076
  6.9 6.2 %copy-start.6 = (s32[256]{0:T(256)S(1)}, s32[256]{0:T(256)}, u32[]{:S(2)}) copy-start(s32[256]{0:T(256)} %hi_ref.5) | copy-start | bytes 3076
  7.1 30.9 %collective-permute-start.6 = (bf16[2,64,5120]{2,1,0:T(8,128)(2,1)S(1)}, bf16[2,64,5120]{2,1,0:T(8,128)(2,1)S(1)}, u32[]{:S(2)}, u32[]{:S(2)}) collective-permute-start(bf16[2,64,5120]{2,1,0:T(8,128)(2,1)S(1)} %pad_maximum_fusion), channel_id=1, source_target_pairs={{1,2},{2,1},{5,6},{6,5},{9,10},{10,9},{13,14},{14,13},{17,18},{18,... | collective-permute-start | bytes 3932168 | tf_op jit(solution)/shard_map/ppermute | solution.py:332
  10.7 8.4 %collective-permute-start.1 = (bf16[2,320,128]{2,1,0:T(8,128)(2,1)S(1)}, bf16[2,320,128]{2,1,0:T(8,128)(2,1)S(1)}, u32[]{:S(2)}, u32[]{:S(2)}) collective-permute-start(bf16[2,320,128]{2,1,0:T(8,128)(2,1)S(1)} %pad_maximum_fusion.4), channel_id=1, source_target_pairs={{0,8},{1,9},{2,10},{3,11},{4,12},{5,13},{6,14},{7,15},{8,0},{9,1},... | collective-permute-start | bytes 491528 | tf_op jit(solution)/shard_map/ppermute | solution.py:300
  19.1 9.8 %collective-permute-start.3 = (bf16[4,320,128]{2,1,0:T(8,128)(2,1)S(1)}, bf16[4,320,128]{2,1,0:T(8,128)(2,1)S(1)}, u32[]{:S(2)}, u32[]{:S(2)}) collective-permute-start(bf16[4,320,128]{2,1,0:T(8,128)(2,1)S(1)} %pad_maximum_fusion.3), channel_id=1, source_target_pairs={{0,4},{1,5},{2,6},{3,7},{4,0},{5,1},{6,2},{7,3},{8,12},{9,13},{10,... | collective-permute-start | bytes 983048 | tf_op jit(solution)/shard_map/ppermute | solution.py:300
  20.2 24.3 %collective-permute-start.7 = (bf16[2,64,5120]{2,1,0:T(8,128)(2,1)S(1)}, bf16[2,64,5120]{2,1,0:T(8,128)(2,1)S(1)}, u32[]{:S(2)}, u32[]{:S(2)}) collective-permute-start(bf16[2,64,5120]{2,1,0:T(8,128)(2,1)S(1)} %pad_maximum_fusion), channel_id=1, source_target_pairs={{3,4},{4,3},{7,8},{8,7},{11,12},{12,11},{19,20},{20,19},{23,24},{2... | collective-permute-start | bytes 3932168 | tf_op jit(solution)/shard_map/ppermute | solution.py:336
  21.0 10.1 %collective-permute-start.2 = (bf16[4,320,128]{2,1,0:T(8,128)(2,1)S(1)}, bf16[4,320,128]{2,1,0:T(8,128)(2,1)S(1)}, u32[]{:S(2)}, u32[]{:S(2)}) collective-permute-start(bf16[4,320,128]{2,1,0:T(8,128)(2,1)S(1)} %pad_maximum_fusion.3), channel_id=1, source_target_pairs={{0,16},{16,0},{1,17},{17,1},{2,18},{18,2},{3,19},{19,3},{4,20},{20... | collective-permute-start | bytes 983048 | tf_op jit(solution)/shard_map/ppermute | solution.py:303
  22.2 18.7 %copy-start.3 = (bf16[320,5120]{1,0:T(8,128)(2,1)S(1)}, bf16[320,5120]{1,0:T(8,128)(2,1)}, u32[]{:S(2)}) copy-start(bf16[320,5120]{1,0:T(8,128)(2,1)} %frozen.1) | copy-start | bytes 9830404
  24.2 16.7 %copy-start.4 = (bf16[320,128]{1,0:T(8,128)(2,1)S(1)}, bf16[320,128]{1,0:T(8,128)(2,1)}, u32[]{:S(2)}) copy-start(bf16[320,128]{1,0:T(8,128)(2,1)} %own_down.1) | copy-start | bytes 245764
  28.8 9.0 %collective-permute-start.5 = (bf16[4,320,128]{2,1,0:T(8,128)(2,1)S(1)}, bf16[4,320,128]{2,1,0:T(8,128)(2,1)S(1)}, u32[]{:S(2)}, u32[]{:S(2)}) collective-permute-start(bf16[4,320,128]{2,1,0:T(8,128)(2,1)S(1)} %collective-permute-done.3), channel_id=1, source_target_pairs={{0,16},{16,0},{1,17},{17,1},{2,18},{18,2},{3,19},{19,3},{4,20},{20... | collective-permute-start | bytes 983048 | tf_op jit(solution)/shard_map/ppermute | solution.py:303
  30.4 8.7 %collective-permute-start.8 = (bf16[8,320,128]{2,1,0:T(8,128)(2,1)S(1)}, bf16[8,320,128]{2,1,0:T(8,128)(2,1)S(1)}, u32[]{:S(2)}, u32[]{:S(2)}) collective-permute-start(bf16[8,320,128]{2,1,0:T(8,128)(2,1)S(1)} %constant_dynamic-update-slice_fusion.rest_0_), channel_id=1, source_target_pairs={{0,1},{1,0},{2,3},{3,2},{4,5},{5,4},{6,7},{7,6},{8,9},{9,8},{10,11... | collective-permute-start | bytes 1966088 | tf_op jit(solution)/shard_map/ppermute | solution.py:300
  37.9 3.0 %collective-permute-start.9 = (bf16[8,320,128]{2,1,0:T(8,128)(2,1)S(1)}, bf16[8,320,128]{2,1,0:T(8,128)(2,1)S(1)}, u32[]{:S(2)}, u32[]{:S(2)}) collective-permute-start(bf16[8,320,128]{2,1,0:T(8,128)(2,1)S(1)} %pad_maximum_fusion.2.rest_2_), channel_id=1, source_target_pairs={{0,1},{1,0},{2,3},{3,2},{4,5},{5,4},{6,7},{7,6},{8,9},{9,8},{10,11... | collective-permute-start | bytes 1966088 | tf_op jit(solution)/shard_map/ppermute | solution.py:300

commit v7 on v6

--- a/solution.py
+++ b/solution.py
@@ -311,7 +311,8 @@
     )
     far_rim = rim(odd * (rows - FRAME))
     up = up.T
-    if lax.axis_size("group") != 2 or down.shape[0] % 32:
+    steps = [1 << bit for bit in range(1, count.bit_length() - 1)]
+    if lax.axis_size("group") != 2 or len(steps) != 3 or down.shape[0] % 32:
         both = lax.all_gather(jnp.stack([down, up]), "seq", axis=1, tiled=True)
         layout, pieces = [], [both]
         direct = lax.ppermute(far_rim, "seq", direct_pairs)
@@ -320,30 +321,31 @@
         near = near_attention(lo, hi, q, k, v, near_halo(odd))
     else:
         barrier = lax.optimization_barrier
+        join = jnp.concatenate
         inner = inner_attention(lo, hi, q, k, v)
-        cells = jnp.where(lax.axis_index("group") == 0, down, up)[None]
-        masks = [0]
-        steps = [2] + [count >> j for j in range(1, count.bit_length()) if count >> j > 2]
-        for mask in steps[:-1]:
-            cells = jnp.concatenate([cells, swap(cells, mask)])
-            masks = masks + [have ^ mask for have in masks]
-            if mask == 2:
-                cells, far_rim = barrier((cells, far_rim))
-                direct = lax.ppermute(far_rim, "seq", direct_pairs)
         halo = near_halo(odd)
-        cells, inner, far_rim = barrier((cells, inner, far_rim))
-        new = swap(cells, steps[-1])
+        side, short, long = steps
+        own = jnp.where(lax.axis_index("group") == 0, down, up)[None]
+        plane = join([own, swap(own, side)])
+        plane, far_rim = barrier((plane, far_rim))
+        direct = lax.ppermute(far_rim, "seq", direct_pairs)
+        beyond = swap(plane, long)
+        beside = swap(plane, short)
+        crossed = [cross(plane)]
+        beyond, beside, crossed, inner, far_rim = barrier(
+            (beyond, beside, crossed, inner, far_rim)
+        )
+        last = swap(beyond, short)
         distant = lax.ppermute(far_rim, "seq", distant_pairs)
-        early = cross(cells)
+        crossed.append(cross(join([beside, beyond])))
         near = near_attention(lo, hi, q, k, v, halo)
-        new, near = barrier((new, near))
-        late = cross(new)
-        cells = jnp.concatenate([cells, new])
-        masks = masks + [have ^ steps[-1] for have in masks]
-        other = jnp.concatenate([early, late])
-        other, direct = barrier((other, direct))
+        last, near = barrier((last, near))
+        crossed.append(cross(last))
+        cells, other = join([plane, beside, beyond, last]), join(crossed)
+        masks = [a ^ b for a in (0, short, long, short ^ long) for b in (0, side)]
         across = [mask ^ 1 for mask in masks]
         layout = [(0, masks), (0, across), (1, masks), (1, across)]
+        other, direct = barrier((other, direct))
         pieces = [cells, swap(cells, 1), other, swap(other, 1)]
     merged, attended, factors = merge(frozen, down, inner, near, layout, pieces)
     attended = far_rows(lo, hi, q, k, v, direct, distant, factors, attended)

time: 49 us -> 49 us (level)
  the two profiles are of different devices: /device:TPU:1 before, /device:TPU:7 now
where the time goes in v7:
time: 49 us; the launch traced here: 48.8 us
  starting transfers between devices  21.3 us (43%)
  Pallas kernels  13.3 us (27%)
  waiting for transfers between devices  10 us (20%)
  local copies, waits for them, and re-layouts  2.11 us (4%)
  other arithmetic  1.28 us (3%)
  between operations  0.84 us (2%)
    ppermute x7, starting transfers between devices, swap(): return lax.ppermute(cells, 'seq', [(i, i ^ mask) for i in range(count)])  12 us
    ppermute x3, waiting for transfers between devices, cross(): return lax.ppermute(cells, 'group', [(0, 1), (1, 0)])  7.79 us
    ppermute x1, starting transfers between devices, body(): distant = lax.ppermute(far_rim, 'seq', distant_pairs)  6.77 us
    pallas_call x1, Pallas kernels, inner_attention(): pl.pallas_call(inner_kernel, grid=(width // WIDE,), out_shape=jax.ShapeDt...  3.94 us
    pallas_call x1, Pallas kernels, far_rows(): pl.pallas_call(far_kernel, out_shape=jax.ShapeDtypeStruct((rows, width),...  3.69 us
    pallas_call x1, Pallas kernels, merge(): pl.pallas_call(functools.partial(merge_kernel, layout), out_shape=(jax.Sh...  3.69 us
    ppermute x7, waiting for transfers between devices, swap(): return lax.ppermute(cells, 'seq', [(i, i ^ mask) for i in range(count)])  2.24 us
    another operation x1, local copies, waits for them, and re-layouts, rim(): jnp.stack([lax.dynamic_slice_in_dim(x, start, FRAME, 0) for x in (k, v)])  2 us
  transfers between devices with their start and end apart: 12, of which 4 were waited for; matrix products, arithmetic and copies ran while one was open for 5% of the time, Pallas kernels for 20%

profile of v7, /device:TPU:7, one launch (start us, length us, event | category | flops | bytes accessed | tf_op | source)
XLA Modules:
  0.0 48.8 jit_solution(11512933940055316972)
XLA Ops:
  0.6 0.9 %fusion = bf16[1,320,128]{2,1,0:T(8,128)(2,1)S(1)} fusion(bf16[320,128]{1,0:T(8,128)(2,1)} %own_down.1, bf16[128,320]{0,1:T(8,128)(2,1)} %param.14, pred[]{:T(512)S(6)} %eq.3), kind=kLoop, calls=%fused_computation.10 | loop fusion | flops 40960 | bytes 245761 | tf_op jit(solution)/shard_map/broadcast_in_dim | solution.py:328
  1.5 0.3 collective-permute-start
  1.8 0.0 copy-start.2
  1.8 2.0 %dynamic-slice_bitcast_fusion = (bf16[1,64,5120]{2,1,0:T(8,128)(2,1)S(1)}, bf16[1,64,5120]{2,1,0:T(8,128)(2,1)S(1)}, bf16[1,64,5120]{2,1,0:T(8,128)(2,1)S(1)}, bf16[1,64,5120]{2,1,0:T(8,128)(2,1)S(1)}) fusion(bf16[256,5120]{1,0:T(8,128)(2,1)} %v.3, s32[]{:T(128)S(6)} %select_n.19, s32[]{:T(128)S(6)} %select_n.18, bf16[256,5120]{1,0:T(8,128)(2,1)} %k.3), kind=kLoop, calls=%fused_computation.3 | loop fusion | bytes 5242888 | tf_op jit(solution)/shard_map/stack | solution.py:297
  3.8 0.0 copy-start.1
  3.9 0.1 pad_maximum_fusion.1
  4.0 1.0 %collective-permute-start.6 = (bf16[2,64,5120]{2,1,0:T(8,128)(2,1)S(1)}, bf16[2,64,5120]{2,1,0:T(8,128)(2,1)S(1)}, u32[]{:S(2)}, u32[]{:S(2)}) collective-permute-start(bf16[2,64,5120]{2,1,0:T(8,128)(2,1)S(1)} %pad_maximum_fusion.1), channel_id=1, source_target_pairs={{0,1},{1,0},{2,3},{3,2},{4,5},{5,4},{6,7},{7,6},{8,9},{9,8},{10,11... | collective-permute-start | bytes 3932168 | tf_op jit(solution)/shard_map/ppermute | solution.py:300
  5.0 0.0 copy-start
  5.0 0.0 copy-start.5
  5.0 0.0 copy-start.6
  5.0 0.1 pad_maximum_fusion
  5.1 0.0 collective-permute-done
  5.2 0.9 %collective-permute-start.8 = (bf16[2,64,5120]{2,1,0:T(8,128)(2,1)S(1)}, bf16[2,64,5120]{2,1,0:T(8,128)(2,1)S(1)}, u32[]{:S(2)}, u32[]{:S(2)}) collective-permute-start(bf16[2,64,5120]{2,1,0:T(8,128)(2,1)S(1)} %pad_maximum_fusion), channel_id=1, source_target_pairs={{1,2},{2,1},{5,6},{6,5},{9,10},{10,9},{13,14},{14,13},{17,18},{18,... | collective-permute-start | bytes 3932168 | tf_op jit(solution)/shard_map/ppermute | solution.py:331
  6.1 0.1 collective-permute-start.3
  6.2 1.5 %collective-permute-start.2 = (bf16[2,320,128]{2,1,0:T(8,128)(2,1)S(1)}, bf16[2,320,128]{2,1,0:T(8,128)(2,1)S(1)}, u32[]{:S(2)}, u32[]{:S(2)}) collective-permute-start(bf16[2,320,128]{2,1,0:T(8,128)(2,1)S(1)} %pad_maximum_fusion.4), channel_id=1, source_target_pairs={{0,4},{1,5},{2,6},{3,7},{4,0},{5,1},{6,2},{7,3},{8,12},{9,13},{10,... | collective-permute-start | bytes 491528 | tf_op jit(solution)/shard_map/ppermute | solution.py:300
  7.7 2.3 %collective-permute-start.1 = (bf16[2,320,128]{2,1,0:T(8,128)(2,1)S(1)}, bf16[2,320,128]{2,1,0:T(8,128)(2,1)S(1)}, u32[]{:S(2)}, u32[]{:S(2)}) collective-permute-start(bf16[2,320,128]{2,1,0:T(8,128)(2,1)S(1)} %pad_maximum_fusion.4), channel_id=1, source_target_pairs={{0,8},{1,9},{2,10},{3,11},{4,12},{5,13},{6,14},{7,15},{8,0},{9,1},... | collective-permute-start | bytes 491528 | tf_op jit(solution)/shard_map/ppermute | solution.py:300
  10.0 0.0 copy-done.2
  10.0 0.0 copy-done.1
  10.0 0.0 copy-done
  10.0 0.0 copy-done.5
  10.0 0.0 copy-done.6
  10.0 3.9 %inner_attention.1.inner = bf16[128,5120]{1,0:T(8,128)(2,1)S(1)} custom-call(s32[256]{0:T(256)S(1)} %copy-done.5, s32[256]{0:T(256)S(1)} %copy-done.6, bf16[256,5120]{1,0:T(8,128)(2,1)S(1)} %copy-done.2, bf16[256,5120]{1,0:T(8,128)(2,1)S(1)} %copy-done, bf16[256,5120]{1,0:T(8,128)(2,1)S(1)} %copy-done.1), custom_call_target="tpu_custom_call" | custom-call | flops 1342177280 | bytes 9175040 | tf_op jit(solution)/shard_map/inner_attention/pallas_call | solution.py:90
  14.0 0.0 collective-permute-done.3
  14.0 0.0 collective-permute-done.2
  14.0 0.5 %collective-permute-done.1 = bf16[2,320,128]{2,1,0:T(8,128)(2,1)S(1)} collective-permute-done((bf16[2,320,128]{2,1,0:T(8,128)(2,1)S(1)}, bf16[2,320,128]{2,1,0:T(8,128)(2,1)S(1)}, u32[]{:S(2)}, u32[]{:S(2)}) %collective-permute-start.1) | collective-permute-done | bytes 163872 | tf_op jit(solution)/shard_map/ppermute | solution.py:300
  14.5 0.2 collective-permute-start.5
  14.8 6.8 %collective-permute-start.9 = (bf16[2,64,5120]{2,1,0:T(8,128)(2,1)S(1)}, bf16[2,64,5120]{2,1,0:T(8,128)(2,1)S(1)}, u32[]{:S(2)}, u32[]{:S(2)}) collective-permute-start(bf16[2,64,5120]{2,1,0:T(8,128)(2,1)S(1)} %pad_maximum_fusion), channel_id=1, source_target_pairs={{3,4},{4,3},{7,8},{8,7},{11,12},{12,11},{19,20},{20,19},{23,24},{2... | collective-permute-start | bytes 3932168 | tf_op jit(solution)/shard_map/ppermute | solution.py:339
  21.6 1.2 %collective-permute-start.4 = (bf16[4,320,128]{2,1,0:T(8,128)(2,1)S(1)}, bf16[4,320,128]{2,1,0:T(8,128)(2,1)S(1)}, u32[]{:S(2)}, u32[]{:S(2)}) collective-permute-start(bf16[4,320,128]{2,1,0:T(8,128)(2,1)S(1)} %pad_maximum_fusion.3), channel_id=1, source_target_pairs={{0,16},{16,0},{1,17},{17,1},{2,18},{18,2},{3,19},{19,3},{4,20},{20... | collective-permute-start | bytes 983048 | tf_op jit(solution)/shard_map/ppermute | solution.py:303
  22.8 0.0 collective-permute-done.6.halo
  22.8 0.0 copy-start.3
  22.9 2.0 %near_edge_attention.1.near = bf16[64,5120]{1,0:T(8,128)(2,1)S(1)} custom-call(s32[256]{0:T(256)S(1)} %copy-done.5, s32[256]{0:T(256)S(1)} %copy-done.6, bf16[256,5120]{1,0:T(8,128)(2,1)S(1)} %copy-done.2, bf16[256,5120]{1,0:T(8,128)(2,1)S(1)} %copy-done, bf16[256,5120]{1,0:T(8,128)(2,1)S(1)} %copy-done.1, bf16[2,64,5120]{2,1,0:T(8,128)(2,1)S(1)} %collective-permute-done.6.halo), custom_call_target="tpu_custom_call" | custom-call | flops 671088640 | bytes 9175040 | tf_op jit(solution)/shard_map/near_edge_attention/pallas_call | solution.py:173
  24.8 0.0 copy-start.4
  24.8 0.0 collective-permute-done.5
  24.8 0.4 collective-permute-start.7
  25.3 0.8 %collective-permute-start.10 = (bf16[8,320,128]{2,1,0:T(8,128)(2,1)S(1)}, bf16[8,320,128]{2,1,0:T(8,128)(2,1)S(1)}, u32[]{:S(2)}, u32[]{:S(2)}) collective-permute-start(bf16[8,320,128]{2,1,0:T(8,128)(2,1)S(1)} %constant_dynamic-update-slice_fusion.rest_0_), channel_id=1, source_target_pairs={{0,1},{1,0},{2,3},{3,2},{4,5},{5,4},{6,7},{7,6},{8,9},{9,8},{10,11... | collective-permute-start | bytes 1966088 | tf_op jit(solution)/shard_map/ppermute | solution.py:300
  26.0 5.3 %collective-permute-done.4 = bf16[4,320,128]{2,1,0:T(8,128)(2,1)S(1)} collective-permute-done((bf16[4,320,128]{2,1,0:T(8,128)(2,1)S(1)}, bf16[4,320,128]{2,1,0:T(8,128)(2,1)S(1)}, u32[]{:S(2)}, u32[]{:S(2)}) %collective-permute-start.4) | collective-permute-done | bytes 327712 | tf_op jit(solution)/shard_map/ppermute | solution.py:303
  31.4 2.5 %collective-permute-done.7 = bf16[2,320,128]{2,1,0:T(8,128)(2,1)S(1)} collective-permute-done((bf16[2,320,128]{2,1,0:T(8,128)(2,1)S(1)}, bf16[2,320,128]{2,1,0:T(8,128)(2,1)S(1)}, u32[]{:S(2)}, u32[]{:S(2)}) %collective-permute-start.7) | collective-permute-done | bytes 163872 | tf_op jit(solution)/shard_map/ppermute | solution.py:303
  33.8 0.1 pad_maximum_fusion.2.rest_2_
  33.9 0.0 collective-permute-done.8.direct
  33.9 5.8 %collective-permute-start.11 = (bf16[8,320,128]{2,1,0:T(8,128)(2,1)S(1)}, bf16[8,320,128]{2,1,0:T(8,128)(2,1)S(1)}, u32[]{:S(2)}, u32[]{:S(2)}) collective-permute-start(bf16[8,320,128]{2,1,0:T(8,128)(2,1)S(1)} %pad_maximum_fusion.2.rest_2_), channel_id=1, source_target_pairs={{0,1},{1,0},{2,3},{3,2},{4,5},{5,4},{6,7},{7,6},{8,9},{9,8},{10,11... | collective-permute-start | bytes 1966088 | tf_op jit(solution)/shard_map/ppermute | solution.py:300
  39.7 0.0 collective-permute-done.10.rest_1_
  39.7 1.7 %collective-permute-done.11.rest_3_ = bf16[8,320,128]{2,1,0:T(8,128)(2,1)S(1)} collective-permute-done((bf16[8,320,128]{2,1,0:T(8,128)(2,1)S(1)}, bf16[8,320,128]{2,1,0:T(8,128)(2,1)S(1)}, u32[]{:S(2)}, u32[]{:S(2)}) %collective-permute-start.11) | collective-permute-done | bytes 655392 | tf_op jit(solution)/shard_map/ppermute | solution.py:300
  41.4 0.0 copy-done.3
  41.4 0.0 copy-done.4
  41.5 3.7 %merge_and_adapter.1 = (bf16[320,5120]{1,0:T(8,128)(2,1)}, bf16[256,5120]{1,0:T(8,128)(2,1)}, bf16[2,5120,128]{2,1,0:T(8,128)(2,1)S(1)}) custom-call(bf16[320,5120]{1,0:T(8,128)(2,1)S(1)} %copy-done.3, bf16[320,128]{1,0:T(8,128)(2,1)S(1)} %copy-done.4, bf16[128,5120]{1,0:T(8,128)(2,1)S(1)} %inner_attention.1.inner, ...), custom_call_target="tpu_custom_call" | custom-call | flops 1090519040 | bytes 14417920 | tf_op jit(solution)/shard_map/merge_and_adapter/pallas_call | solution.py:229
  45.1 0.0 collective-permute-done.9.distant
  45.2 3.7 %far_edge_rows.1 = bf16[256,5120]{1,0:T(8,128)(2,1)} custom-call(s32[256]{0:T(256)S(1)} %copy-done.5, s32[256]{0:T(256)S(1)} %copy-done.6, bf16[256,5120]{1,0:T(8,128)(2,1)S(1)} %copy-done.2, bf16[256,5120]{1,0:T(8,128)(2,1)S(1)} %copy-done, bf16[256,5120]{1,0:T(8,128)(2,1)S(1)} %copy-done.1, ...), custom_call_target="tpu_custom_call", output_to_operand_aliasing={{}: (8, {})} | custom-call | flops 671088640 | bytes 9175040 | tf_op jit(solution)/shard_map/far_edge_rows/pallas_call | solution.py:274
  (6 shorter events, 0.1 us)
Async XLA Ops:
  1.5 3.6 %collective-permute-start = (bf16[1,320,128]{2,1,0:T(8,128)(2,1)S(1)}, bf16[1,320,128]{2,1,0:T(8,128)(2,1)S(1)}, u32[]{:S(2)}, u32[]{:S(2)}) collective-permute-start(bf16[1,320,128]{2,1,0:T(8,128)(2,1)S(1)} %fusion), channel_id=1, source_target_pairs={{0,2},{1,3},{2,0},{3,1},{4,6},{5,7},{6,4},{7,5},{8,10},{9,11},{10,... | collective-permute-start | bytes 245768 | tf_op jit(solution)/shard_map/ppermute | solution.py:300
  1.8 8.2 %copy-start.2 = (bf16[256,5120]{1,0:T(8,128)(2,1)S(1)}, bf16[256,5120]{1,0:T(8,128)(2,1)}, u32[]{:S(2)}) copy-start(bf16[256,5120]{1,0:T(8,128)(2,1)} %q.3) | copy-start | bytes 7864324
  3.8 6.2 %copy-start.1 = (bf16[256,5120]{1,0:T(8,128)(2,1)S(1)}, bf16[256,5120]{1,0:T(8,128)(2,1)}, u32[]{:S(2)}) copy-start(bf16[256,5120]{1,0:T(8,128)(2,1)} %v.3) | copy-start | bytes 7864324
  4.0 18.9 %collective-permute-start.6 = (bf16[2,64,5120]{2,1,0:T(8,128)(2,1)S(1)}, bf16[2,64,5120]{2,1,0:T(8,128)(2,1)S(1)}, u32[]{:S(2)}, u32[]{:S(2)}) collective-permute-start(bf16[2,64,5120]{2,1,0:T(8,128)(2,1)S(1)} %pad_maximum_fusion.1), channel_id=1, source_target_pairs={{0,1},{1,0},{2,3},{3,2},{4,5},{5,4},{6,7},{7,6},{8,9},{9,8},{10,11... | collective-permute-start | bytes 3932168 | tf_op jit(solution)/shard_map/ppermute | solution.py:300
  5.0 5.0 %copy-start = (bf16[256,5120]{1,0:T(8,128)(2,1)S(1)}, bf16[256,5120]{1,0:T(8,128)(2,1)}, u32[]{:S(2)}) copy-start(bf16[256,5120]{1,0:T(8,128)(2,1)} %k.3) | copy-start | bytes 7864324
  5.0 5.0 %copy-start.5 = (s32[256]{0:T(256)S(1)}, s32[256]{0:T(256)}, u32[]{:S(2)}) copy-start(s32[256]{0:T(256)} %lo_ref.5) | copy-start | bytes 3076
  5.0 5.0 %copy-start.6 = (s32[256]{0:T(256)S(1)}, s32[256]{0:T(256)}, u32[]{:S(2)}) copy-start(s32[256]{0:T(256)} %hi_ref.5) | copy-start | bytes 3076
  5.2 28.7 %collective-permute-start.8 = (bf16[2,64,5120]{2,1,0:T(8,128)(2,1)S(1)}, bf16[2,64,5120]{2,1,0:T(8,128)(2,1)S(1)}, u32[]{:S(2)}, u32[]{:S(2)}) collective-permute-start(bf16[2,64,5120]{2,1,0:T(8,128)(2,1)S(1)} %pad_maximum_fusion), channel_id=1, source_target_pairs={{1,2},{2,1},{5,6},{6,5},{9,10},{10,9},{13,14},{14,13},{17,18},{18,... | collective-permute-start | bytes 3932168 | tf_op jit(solution)/shard_map/ppermute | solution.py:331
  6.1 8.0 %collective-permute-start.3 = (bf16[2,320,128]{2,1,0:T(8,128)(2,1)S(1)}, bf16[2,320,128]{2,1,0:T(8,128)(2,1)S(1)}, u32[]{:S(2)}, u32[]{:S(2)}) collective-permute-start(bf16[2,320,128]{2,1,0:T(8,128)(2,1)S(1)} %pad_maximum_fusion.4), channel_id=1, source_target_pairs={{0,16},{16,0},{1,17},{17,1},{2,18},{18,2},{3,19},{19,3},{4,20},{20... | collective-permute-start | bytes 491528 | tf_op jit(solution)/shard_map/ppermute | solution.py:303
  6.2 7.9 %collective-permute-start.2 = (bf16[2,320,128]{2,1,0:T(8,128)(2,1)S(1)}, bf16[2,320,128]{2,1,0:T(8,128)(2,1)S(1)}, u32[]{:S(2)}, u32[]{:S(2)}) collective-permute-start(bf16[2,320,128]{2,1,0:T(8,128)(2,1)S(1)} %pad_maximum_fusion.4), channel_id=1, source_target_pairs={{0,4},{1,5},{2,6},{3,7},{4,0},{5,1},{6,2},{7,3},{8,12},{9,13},{10,... | collective-permute-start | bytes 491528 | tf_op jit(solution)/shard_map/ppermute | solution.py:300
  7.7 6.8 %collective-permute-start.1 = (bf16[2,320,128]{2,1,0:T(8,128)(2,1)S(1)}, bf16[2,320,128]{2,1,0:T(8,128)(2,1)S(1)}, u32[]{:S(2)}, u32[]{:S(2)}) collective-permute-start(bf16[2,320,128]{2,1,0:T(8,128)(2,1)S(1)} %pad_maximum_fusion.4), channel_id=1, source_target_pairs={{0,8},{1,9},{2,10},{3,11},{4,12},{5,13},{6,14},{7,15},{8,0},{9,1},... | collective-permute-start | bytes 491528 | tf_op jit(solution)/shard_map/ppermute | solution.py:300
  14.5 10.3 %collective-permute-start.5 = (bf16[2,320,128]{2,1,0:T(8,128)(2,1)S(1)}, bf16[2,320,128]{2,1,0:T(8,128)(2,1)S(1)}, u32[]{:S(2)}, u32[]{:S(2)}) collective-permute-start(bf16[2,320,128]{2,1,0:T(8,128)(2,1)S(1)} %collective-permute-done.1), channel_id=1, source_target_pairs={{0,4},{1,5},{2,6},{3,7},{4,0},{5,1},{6,2},{7,3},{8,12},{9,13},{10,... | collective-permute-start | bytes 491528 | tf_op jit(solution)/shard_map/ppermute | solution.py:300
  14.8 30.4 %collective-permute-start.9 = (bf16[2,64,5120]{2,1,0:T(8,128)(2,1)S(1)}, bf16[2,64,5120]{2,1,0:T(8,128)(2,1)S(1)}, u32[]{:S(2)}, u32[]{:S(2)}) collective-permute-start(bf16[2,64,5120]{2,1,0:T(8,128)(2,1)S(1)} %pad_maximum_fusion), channel_id=1, source_target_pairs={{3,4},{4,3},{7,8},{8,7},{11,12},{12,11},{19,20},{20,19},{23,24},{2... | collective-permute-start | bytes 3932168 | tf_op jit(solution)/shard_map/ppermute | solution.py:339
  21.6 9.8 %collective-permute-start.4 = (bf16[4,320,128]{2,1,0:T(8,128)(2,1)S(1)}, bf16[4,320,128]{2,1,0:T(8,128)(2,1)S(1)}, u32[]{:S(2)}, u32[]{:S(2)}) collective-permute-start(bf16[4,320,128]{2,1,0:T(8,128)(2,1)S(1)} %pad_maximum_fusion.3), channel_id=1, source_target_pairs={{0,16},{16,0},{1,17},{17,1},{2,18},{18,2},{3,19},{19,3},{4,20},{20... | collective-permute-start | bytes 983048 | tf_op jit(solution)/shard_map/ppermute | solution.py:303
  22.8 18.6 %copy-start.3 = (bf16[320,5120]{1,0:T(8,128)(2,1)S(1)}, bf16[320,5120]{1,0:T(8,128)(2,1)}, u32[]{:S(2)}) copy-start(bf16[320,5120]{1,0:T(8,128)(2,1)} %frozen.1) | copy-start | bytes 9830404
  24.8 16.6 %copy-start.4 = (bf16[320,128]{1,0:T(8,128)(2,1)S(1)}, bf16[320,128]{1,0:T(8,128)(2,1)}, u32[]{:S(2)}) copy-start(bf16[320,128]{1,0:T(8,128)(2,1)} %own_down.1) | copy-start | bytes 245764
  24.8 9.0 %collective-permute-start.7 = (bf16[2,320,128]{2,1,0:T(8,128)(2,1)S(1)}, bf16[2,320,128]{2,1,0:T(8,128)(2,1)S(1)}, u32[]{:S(2)}, u32[]{:S(2)}) collective-permute-start(bf16[2,320,128]{2,1,0:T(8,128)(2,1)S(1)} %collective-permute-done.5), channel_id=1, source_target_pairs={{0,16},{16,0},{1,17},{17,1},{2,18},{18,2},{3,19},{19,3},{4,20},{20... | collective-permute-start | bytes 491528 | tf_op jit(solution)/shard_map/ppermute | solution.py:303
  25.3 14.5 %collective-permute-start.10 = (bf16[8,320,128]{2,1,0:T(8,128)(2,1)S(1)}, bf16[8,320,128]{2,1,0:T(8,128)(2,1)S(1)}, u32[]{:S(2)}, u32[]{:S(2)}) collective-permute-start(bf16[8,320,128]{2,1,0:T(8,128)(2,1)S(1)} %constant_dynamic-update-slice_fusion.rest_0_), channel_id=1, source_target_pairs={{0,1},{1,0},{2,3},{3,2},{4,5},{5,4},{6,7},{7,6},{8,9},{9,8},{10,11... | collective-permute-start | bytes 1966088 | tf_op jit(solution)/shard_map/ppermute | solution.py:300
  33.9 7.5 %collective-permute-start.11 = (bf16[8,320,128]{2,1,0:T(8,128)(2,1)S(1)}, bf16[8,320,128]{2,1,0:T(8,128)(2,1)S(1)}, u32[]{:S(2)}, u32[]{:S(2)}) collective-permute-start(bf16[8,320,128]{2,1,0:T(8,128)(2,1)S(1)} %pad_maximum_fusion.2.rest_2_), channel_id=1, source_target_pairs={{0,1},{1,0},{2,3},{3,2},{4,5},{5,4},{6,7},{7,6},{8,9},{9,8},{10,11... | collective-permute-start | bytes 1966088 | tf_op jit(solution)/shard_map/ppermute | solution.py:300

commit v8 on v7

--- a/solution.py
+++ b/solution.py
@@ -123,9 +123,9 @@
     direct = lax.rem(lax.div(me + 1, 2), 2) == 1
 
     def window(ref, kind, part):
-        halo = halos[0][kind, :, part]
-        if len(halos) == 2:
-            halo = jnp.where(direct, halo, halos[1][kind, :, part])
+        halo = halos[kind][:, part]
+        if len(halos) == 4:
+            halo = jnp.where(direct, halo, halos[2 + kind][:, part])
         one, two = ref[pl.ds(first, FRAME), part], ref[pl.ds(second, FRAME), part]
         return jnp.concatenate(
             [
@@ -157,7 +157,7 @@
 
 
 def near_kernel(lo_ref, hi_ref, q, k, v, halo, out):
-    attend_edge(True, lo_ref, hi_ref, q, k, v, (halo,), out)
+    attend_edge(True, lo_ref, hi_ref, q, k, v, (halo.at[0], halo.at[1]), out)
 
 
 def edge_cost(rows, width):
@@ -250,9 +250,11 @@
     )(frozen, own_down, inner, near, *pieces)
 
 
-def far_kernel(lo_ref, hi_ref, q, k, v, direct, distant, factors, _, out, mixed, result, sems):
-    rows, width = q.shape
-    attend_edge(False, lo_ref, hi_ref, q, k, v, (direct, distant), mixed)
+def far_kernel(lo_ref, hi_ref, q, k, v, *rest):
+    halos, (factors, _, out, mixed, result, sems) = rest[:3], rest[3:]
+    rows, width = q.shape
+    halos = (*halos[:2], halos[2].at[0], halos[2].at[1])
+    attend_edge(False, lo_ref, hi_ref, q, k, v, halos, mixed)
     narrow = dot(mixed[...], factors[0], NN).astype(BF16)
     _, row = edge_side(False, rows)
     stores = []
@@ -274,9 +276,9 @@
     return pl.pallas_call(
         far_kernel,
         out_shape=jax.ShapeDtypeStruct((rows, width), BF16),
-        in_specs=[SMEM, SMEM] + [VMEM] * 6 + [ANY],
+        in_specs=[SMEM, SMEM] + [VMEM] * 7 + [ANY],
         out_specs=ANY,
-        input_output_aliases={8: 0},
+        input_output_aliases={9: 0},
         scratch_shapes=[
             pltpu.VMEM((FRAME, width), BF16),
             pltpu.VMEM((FRAME, width), BF16),
@@ -285,7 +287,7 @@
         compiler_params=pltpu.CompilerParams(vmem_limit_bytes=24 << 20),
         cost_estimate=edge_cost(rows, width),
         name="far_edge_rows",
-    )(lo, hi, q, k, v, direct, distant, factors, attended)
+    )(lo, hi, q, k, v, *direct, distant, factors, attended)
 
 
 def body(q, k, v, lo, hi, down, up, frozen):
@@ -294,58 +296,59 @@
     odd = lax.rem(lax.axis_index("seq"), 2)
 
     def rim(start):
-        return jnp.stack([lax.dynamic_slice_in_dim(x, start, FRAME, 0) for x in (k, v)])
+        return [lax.dynamic_slice_in_dim(x, start, FRAME, 0) for x in (k, v)]
+
+    def send(cells, pairs):
+        return [lax.ppermute(x, "seq", pairs) for x in cells]
 
     def swap(cells, mask):
         return lax.ppermute(cells, "seq", [(i, i ^ mask) for i in range(count)])
 
     def cross(cells):
         return lax.ppermute(cells, "group", [(0, 1), (1, 0)])
-
-    def near_halo(odd):
-        return swap(rim((1 - odd) * (rows - FRAME)), 1)
 
     direct_pairs, distant_pairs = (
         [(i + a, i + 1 - a) for i in range(first, count - 1, 4) for a in (0, 1)]
         for first in (1, 3)
     )
     far_rim = rim(odd * (rows - FRAME))
+    near_rim = jnp.stack(rim((1 - odd) * (rows - FRAME)))
     up = up.T
     steps = [1 << bit for bit in range(1, count.bit_length() - 1)]
     if lax.axis_size("group") != 2 or len(steps) != 3 or down.shape[0] % 32:
         both = lax.all_gather(jnp.stack([down, up]), "seq", axis=1, tiled=True)
         layout, pieces = [], [both]
-        direct = lax.ppermute(far_rim, "seq", direct_pairs)
-        distant = lax.ppermute(far_rim, "seq", distant_pairs)
+        direct = send(far_rim, direct_pairs)
+        distant = lax.ppermute(jnp.stack(far_rim), "seq", distant_pairs)
         inner = inner_attention(lo, hi, q, k, v)
-        near = near_attention(lo, hi, q, k, v, near_halo(odd))
+        near = near_attention(lo, hi, q, k, v, swap(near_rim, 1))
     else:
         barrier = lax.optimization_barrier
         join = jnp.concatenate
-        inner = inner_attention(lo, hi, q, k, v)
-        halo = near_halo(odd)
         side, short, long = steps
         own = jnp.where(lax.axis_index("group") == 0, down, up)[None]
         plane = join([own, swap(own, side)])
-        plane, far_rim = barrier((plane, far_rim))
-        direct = lax.ppermute(far_rim, "seq", direct_pairs)
+        plane, far_rim, near_rim = barrier((plane, far_rim, near_rim))
+        halo = swap(near_rim, 1)
+        direct = send(far_rim, direct_pairs)
         beyond = swap(plane, long)
         beside = swap(plane, short)
         crossed = [cross(plane)]
-        beyond, beside, crossed, inner, far_rim = barrier(
-            (beyond, beside, crossed, inner, far_rim)
+        beyond, beside, crossed, far_rim = barrier(
+            (beyond, beside, crossed, far_rim)
         )
         last = swap(beyond, short)
-        distant = lax.ppermute(far_rim, "seq", distant_pairs)
+        distant = lax.ppermute(jnp.stack(far_rim), "seq", distant_pairs)
         crossed.append(cross(join([beside, beyond])))
-        near = near_attention(lo, hi, q, k, v, halo)
-        last, near = barrier((last, near))
+        last, direct, crossed[1], lo_later = barrier((last, direct, crossed[1], lo))
+        inner = inner_attention(lo_later, hi, q, k, v)
+        near = near_attention(lo_later, hi, q, k, v, halo)
         crossed.append(cross(last))
         cells, other = join([plane, beside, beyond, last]), join(crossed)
+        other, inner = barrier((other, inner))
         masks = [a ^ b for a in (0, short, long, short ^ long) for b in (0, side)]
         across = [mask ^ 1 for mask in masks]
         layout = [(0, masks), (0, across), (1, masks), (1, across)]
-        other, direct = barrier((other, direct))
         pieces = [cells, swap(cells, 1), other, swap(other, 1)]
     merged, attended, factors = merge(frozen, down, inner, near, layout, pieces)
     attended = far_rows(lo, hi, q, k, v, direct, distant, factors, attended)

time: 49 us -> 60.5 us (1.23)
  the two profiles are of different devices: /device:TPU:7 before, /device:TPU:1 now
where the time goes in v8:
time: 60.5 us; the launch traced here: 59.3 us
  waiting for transfers between devices  25 us (41%)
  starting transfers between devices  16.8 us (28%)
  Pallas kernels  13.3 us (22%)
  local copies, waits for them, and re-layouts  2.11 us (3%)
  other arithmetic  1.31 us (2%)
  between operations  0.89 us (1%)
    ppermute x2, waiting for transfers between devices, send(): return [lax.ppermute(x, 'seq', pairs) for x in cells]  18.3 us
    ppermute x2, starting transfers between devices, send(): return [lax.ppermute(x, 'seq', pairs) for x in cells]  7.49 us
    ppermute x7, starting transfers between devices, swap(): return lax.ppermute(cells, 'seq', [(i, i ^ mask) for i in range(count)])  6.65 us
    ppermute x7, waiting for transfers between devices, swap(): return lax.ppermute(cells, 'seq', [(i, i ^ mask) for i in range(count)])  4 us
    pallas_call x1, Pallas kernels, inner_attention(): pl.pallas_call(inner_kernel, grid=(width // WIDE,), out_shape=jax.ShapeDt...  3.93 us
    pallas_call x1, Pallas kernels, far_rows(): pl.pallas_call(far_kernel, out_shape=jax.ShapeDtypeStruct((rows, width),...  3.69 us
    pallas_call x1, Pallas kernels, merge(): pl.pallas_call(functools.partial(merge_kernel, layout), out_shape=(jax.Sh...  3.69 us
    ppermute x3, waiting for transfers between devices, cross(): return lax.ppermute(cells, 'group', [(0, 1), (1, 0)])  2.68 us
  transfers between devices with their start and end apart: 13, of which 3 were waited for; matrix products, arithmetic and copies ran while one was open for 4% of the time, Pallas kernels for 16%

profile of v8, /device:TPU:1, one launch (start us, length us, event | category | flops | bytes accessed | tf_op | source)
XLA Modules:
  0.0 59.3 jit_solution(13589187274580771685)
XLA Ops:
  0.6 0.9 %fusion = bf16[1,320,128]{2,1,0:T(8,128)(2,1)S(1)} fusion(bf16[320,128]{1,0:T(8,128)(2,1)} %own_down.1, bf16[128,320]{0,1:T(8,128)(2,1)} %param.14, pred[]{:T(512)S(6)} %eq.3), kind=kLoop, calls=%fused_computation.8 | loop fusion | flops 40960 | bytes 245761 | tf_op jit(solution)/shard_map/broadcast_in_dim | solution.py:329
  1.6 2.1 %collective-permute-start = (bf16[1,320,128]{2,1,0:T(8,128)(2,1)S(1)}, bf16[1,320,128]{2,1,0:T(8,128)(2,1)S(1)}, u32[]{:S(2)}, u32[]{:S(2)}) collective-permute-start(bf16[1,320,128]{2,1,0:T(8,128)(2,1)S(1)} %fusion), channel_id=1, source_target_pairs={{0,2},{1,3},{2,0},{3,1},{4,6},{5,7},{6,4},{7,5},{8,10},{9,11},{10,... | collective-permute-start | bytes 245768 | tf_op jit(solution)/shard_map/ppermute | solution.py:305
  3.7 0.0 copy-start.2
  3.7 2.0 %dynamic-slice_bitcast_fusion = (bf16[1,64,5120]{2,1,0:T(8,128)(2,1)S(1)}, bf16[64,5120]{1,0:T(8,128)(2,1)S(1)}, bf16[64,5120]{1,0:T(8,128)(2,1)S(1)}, bf16[1,64,5120]{2,1,0:T(8,128)(2,1)S(1)}) fusion(bf16[256,5120]{1,0:T(8,128)(2,1)} %v.3, s32[]{:T(128)S(6)} %select_n.19, s32[]{:T(128)S(6)} %select_n.18, bf16[256,5120]{1,0:T(8,128)(2,1)} %k.3), kind=kLoop, calls=%fused_computation.3 | loop fusion | bytes 5242888 | tf_op jit(solution)/shard_map/stack | solution.py:315
  5.7 0.0 copy-start.1
  5.7 0.1 pad_maximum_fusion
  5.9 0.0 collective-permute-done
  5.9 1.2 %collective-permute-start.3 = (bf16[2,320,128]{2,1,0:T(8,128)(2,1)S(1)}, bf16[2,320,128]{2,1,0:T(8,128)(2,1)S(1)}, u32[]{:S(2)}, u32[]{:S(2)}) collective-permute-start(bf16[2,320,128]{2,1,0:T(8,128)(2,1)S(1)} %pad_maximum_fusion.4), channel_id=1, source_target_pairs={{0,16},{16,0},{1,17},{17,1},{2,18},{18,2},{3,19},{19,3},{4,20},{20... | collective-permute-start | bytes 491528 | tf_op jit(solution)/shard_map/ppermute | solution.py:308
  7.1 1.3 %collective-permute-start.2 = (bf16[2,320,128]{2,1,0:T(8,128)(2,1)S(1)}, bf16[2,320,128]{2,1,0:T(8,128)(2,1)S(1)}, u32[]{:S(2)}, u32[]{:S(2)}) collective-permute-start(bf16[2,320,128]{2,1,0:T(8,128)(2,1)S(1)} %pad_maximum_fusion.4), channel_id=1, source_target_pairs={{0,4},{1,5},{2,6},{3,7},{4,0},{5,1},{6,2},{7,3},{8,12},{9,13},{10,... | collective-permute-start | bytes 491528 | tf_op jit(solution)/shard_map/ppermute | solution.py:305
  8.4 2.3 %collective-permute-start.1 = (bf16[2,320,128]{2,1,0:T(8,128)(2,1)S(1)}, bf16[2,320,128]{2,1,0:T(8,128)(2,1)S(1)}, u32[]{:S(2)}, u32[]{:S(2)}) collective-permute-start(bf16[2,320,128]{2,1,0:T(8,128)(2,1)S(1)} %pad_maximum_fusion.4), channel_id=1, source_target_pairs={{0,8},{1,9},{2,10},{3,11},{4,12},{5,13},{6,14},{7,15},{8,0},{9,1},... | collective-permute-start | bytes 491528 | tf_op jit(solution)/shard_map/ppermute | solution.py:305
  10.7 5.6 %collective-permute-start.5 = (bf16[64,5120]{1,0:T(8,128)(2,1)S(1)}, bf16[64,5120]{1,0:T(8,128)(2,1)S(1)}, u32[]{:S(2)}, u32[]{:S(2)}) collective-permute-start(bf16[64,5120]{1,0:T(8,128)(2,1)S(1)} %get-tuple-element.28), channel_id=1, source_target_pairs={{1,2},{2,1},{5,6},{6,5},{9,10},{10,9},{13,14},{14,13},{17,18},{18,... | collective-permute-start | bytes 1966088 | tf_op jit(solution)/shard_map/ppermute | solution.py:302
  16.3 1.9 %collective-permute-start.6 = (bf16[64,5120]{1,0:T(8,128)(2,1)S(1)}, bf16[64,5120]{1,0:T(8,128)(2,1)S(1)}, u32[]{:S(2)}, u32[]{:S(2)}) collective-permute-start(bf16[64,5120]{1,0:T(8,128)(2,1)S(1)} %get-tuple-element.29), channel_id=1, source_target_pairs={{1,2},{2,1},{5,6},{6,5},{9,10},{10,9},{13,14},{14,13},{17,18},{18,... | collective-permute-start | bytes 1966088 | tf_op jit(solution)/shard_map/ppermute | solution.py:302
  18.3 0.0 collective-permute-done.3
  18.3 0.1 collective-permute-start.10
  18.4 0.0 collective-permute-done.2
  18.4 0.0 collective-permute-done.1
  18.4 0.2 collective-permute-start.4
  18.7 0.4 collective-permute-start.7
  19.0 0.0 copy-start.5
  19.0 0.0 copy-start.6
  19.0 0.1 pad_maximum_fusion.1
  19.1 4.0 %collective-permute-done.4 = bf16[2,320,128]{2,1,0:T(8,128)(2,1)S(1)} collective-permute-done((bf16[2,320,128]{2,1,0:T(8,128)(2,1)S(1)}, bf16[2,320,128]{2,1,0:T(8,128)(2,1)S(1)}, u32[]{:S(2)}, u32[]{:S(2)}) %collective-permute-start.4) | collective-permute-done | bytes 163872 | tf_op jit(solution)/shard_map/ppermute | solution.py:305
  23.1 0.7 %collective-permute-start.8 = (bf16[2,64,5120]{2,1,0:T(8,128)(2,1)S(1)}, bf16[2,64,5120]{2,1,0:T(8,128)(2,1)S(1)}, u32[]{:S(2)}, u32[]{:S(2)}) collective-permute-start(bf16[2,64,5120]{2,1,0:T(8,128)(2,1)S(1)} %pad_maximum_fusion.1), channel_id=1, source_target_pairs={{3,4},{4,3},{7,8},{8,7},{11,12},{12,11},{19,20},{20,19},{23,24},{2... | collective-permute-start | bytes 3932168 | tf_op jit(solution)/shard_map/ppermute | solution.py:341
  23.9 2.7 %collective-permute-done.7 = bf16[4,320,128]{2,1,0:T(8,128)(2,1)S(1)} collective-permute-done((bf16[4,320,128]{2,1,0:T(8,128)(2,1)S(1)}, bf16[4,320,128]{2,1,0:T(8,128)(2,1)S(1)}, u32[]{:S(2)}, u32[]{:S(2)}) %collective-permute-start.7) | collective-permute-done | bytes 327712 | tf_op jit(solution)/shard_map/ppermute | solution.py:308
  26.6 0.0 collective-permute-done.5.rest_0_
  26.6 18.3 %collective-permute-done.6.rest_1_ = bf16[64,5120]{1,0:T(8,128)(2,1)S(1)} collective-permute-done((bf16[64,5120]{1,0:T(8,128)(2,1)S(1)}, bf16[64,5120]{1,0:T(8,128)(2,1)S(1)}, u32[]{:S(2)}, u32[]{:S(2)}) %collective-permute-start.6) | collective-permute-done | bytes 655392 | tf_op jit(solution)/shard_map/ppermute | solution.py:302
  44.9 0.3 collective-permute-start.9
  45.2 0.1 collective-permute-start.11
  45.3 0.0 copy-done.2
  45.3 0.0 copy-done.1
  45.3 0.0 copy-done
  45.3 0.0 copy-done.5
  45.3 0.0 copy-done.6
  45.4 3.9 %inner_attention.1.inner = bf16[128,5120]{1,0:T(8,128)(2,1)S(1)} custom-call(s32[256]{0:T(256)S(1)} %copy-done.5, s32[256]{0:T(256)S(1)} %copy-done.6, bf16[256,5120]{1,0:T(8,128)(2,1)S(1)} %copy-done.2, bf16[256,5120]{1,0:T(8,128)(2,1)S(1)} %copy-done, bf16[256,5120]{1,0:T(8,128)(2,1)S(1)} %copy-done.1), custom_call_target="tpu_custom_call" | custom-call | flops 1342177280 | bytes 9175040 | tf_op jit(solution)/shard_map/inner_attention/pallas_call | solution.py:90
  49.3 0.0 collective-permute-done.9
  49.3 0.1 pad_maximum_fusion.2.rest_2_
  49.4 0.0 copy-start.4
  49.4 0.5 collective-permute-start.12
  49.9 0.0 collective-permute-done.10.halo
  49.9 0.0 copy-start.3
  49.9 2.0 %near_edge_attention.1.near = bf16[64,5120]{1,0:T(8,128)(2,1)S(1)} custom-call(s32[256]{0:T(256)S(1)} %copy-done.5, s32[256]{0:T(256)S(1)} %copy-done.6, bf16[256,5120]{1,0:T(8,128)(2,1)S(1)} %copy-done.2, bf16[256,5120]{1,0:T(8,128)(2,1)S(1)} %copy-done, bf16[256,5120]{1,0:T(8,128)(2,1)S(1)} %copy-done.1, bf16[2,64,5120]{2,1,0:T(8,128)(2,1)S(1)} %collective-permute-done.10.halo), custom_call_target="tpu_custom_call" | custom-call | flops 671088640 | bytes 9175040 | tf_op jit(solution)/shard_map/near_edge_attention/pallas_call | solution.py:173
  51.9 0.0 collective-permute-done.11.rest_1_
  51.9 0.0 collective-permute-done.12.rest_3_
  51.9 0.0 copy-done.4
  51.9 0.0 copy-done.3
  51.9 3.7 %merge_and_adapter.1 = (bf16[320,5120]{1,0:T(8,128)(2,1)}, bf16[256,5120]{1,0:T(8,128)(2,1)}, bf16[2,5120,128]{2,1,0:T(8,128)(2,1)S(1)}) custom-call(bf16[320,5120]{1,0:T(8,128)(2,1)S(1)} %copy-done.3, bf16[320,128]{1,0:T(8,128)(2,1)S(1)} %copy-done.4, bf16[128,5120]{1,0:T(8,128)(2,1)S(1)} %inner_attention.1.inner, ...), custom_call_target="tpu_custom_call" | custom-call | flops 1090519040 | bytes 14417920 | tf_op jit(solution)/shard_map/merge_and_adapter/pallas_call | solution.py:229
  55.6 0.0 collective-permute-done.8.rest_2_
  55.7 3.7 %far_edge_rows.1 = bf16[256,5120]{1,0:T(8,128)(2,1)} custom-call(s32[256]{0:T(256)S(1)} %copy-done.5, s32[256]{0:T(256)S(1)} %copy-done.6, bf16[256,5120]{1,0:T(8,128)(2,1)S(1)} %copy-done.2, bf16[256,5120]{1,0:T(8,128)(2,1)S(1)} %copy-done, bf16[256,5120]{1,0:T(8,128)(2,1)S(1)} %copy-done.1, ...), custom_call_target="tpu_custom_call", output_to_operand_aliasing={{}: (9, {})} | custom-call | flops 671088640 | bytes 9175040 | tf_op jit(solution)/shard_map/far_edge_rows/pallas_call | solution.py:276
  (7 shorter events, 0.1 us)
Async XLA Ops:
  1.6 4.3 %collective-permute-start = (bf16[1,320,128]{2,1,0:T(8,128)(2,1)S(1)}, bf16[1,320,128]{2,1,0:T(8,128)(2,1)S(1)}, u32[]{:S(2)}, u32[]{:S(2)}) collective-permute-start(bf16[1,320,128]{2,1,0:T(8,128)(2,1)S(1)} %fusion), channel_id=1, source_target_pairs={{0,2},{1,3},{2,0},{3,1},{4,6},{5,7},{6,4},{7,5},{8,10},{9,11},{10,... | collective-permute-start | bytes 245768 | tf_op jit(solution)/shard_map/ppermute | solution.py:305
  3.7 41.6 %copy-start.2 = (bf16[256,5120]{1,0:T(8,128)(2,1)S(1)}, bf16[256,5120]{1,0:T(8,128)(2,1)}, u32[]{:S(2)}) copy-start(bf16[256,5120]{1,0:T(8,128)(2,1)} %q.3) | copy-start | bytes 7864324
  5.7 39.6 %copy-start.1 = (bf16[256,5120]{1,0:T(8,128)(2,1)S(1)}, bf16[256,5120]{1,0:T(8,128)(2,1)}, u32[]{:S(2)}) copy-start(bf16[256,5120]{1,0:T(8,128)(2,1)} %v.3) | copy-start | bytes 7864324
  5.9 12.4 %collective-permute-start.3 = (bf16[2,320,128]{2,1,0:T(8,128)(2,1)S(1)}, bf16[2,320,128]{2,1,0:T(8,128)(2,1)S(1)}, u32[]{:S(2)}, u32[]{:S(2)}) collective-permute-start(bf16[2,320,128]{2,1,0:T(8,128)(2,1)S(1)} %pad_maximum_fusion.4), channel_id=1, source_target_pairs={{0,16},{16,0},{1,17},{17,1},{2,18},{18,2},{3,19},{19,3},{4,20},{20... | collective-permute-start | bytes 491528 | tf_op jit(solution)/shard_map/ppermute | solution.py:308
  7.1 11.2 %collective-permute-start.2 = (bf16[2,320,128]{2,1,0:T(8,128)(2,1)S(1)}, bf16[2,320,128]{2,1,0:T(8,128)(2,1)S(1)}, u32[]{:S(2)}, u32[]{:S(2)}) collective-permute-start(bf16[2,320,128]{2,1,0:T(8,128)(2,1)S(1)} %pad_maximum_fusion.4), channel_id=1, source_target_pairs={{0,4},{1,5},{2,6},{3,7},{4,0},{5,1},{6,2},{7,3},{8,12},{9,13},{10,... | collective-permute-start | bytes 491528 | tf_op jit(solution)/shard_map/ppermute | solution.py:305
  8.4 9.9 %collective-permute-start.1 = (bf16[2,320,128]{2,1,0:T(8,128)(2,1)S(1)}, bf16[2,320,128]{2,1,0:T(8,128)(2,1)S(1)}, u32[]{:S(2)}, u32[]{:S(2)}) collective-permute-start(bf16[2,320,128]{2,1,0:T(8,128)(2,1)S(1)} %pad_maximum_fusion.4), channel_id=1, source_target_pairs={{0,8},{1,9},{2,10},{3,11},{4,12},{5,13},{6,14},{7,15},{8,0},{9,1},... | collective-permute-start | bytes 491528 | tf_op jit(solution)/shard_map/ppermute | solution.py:305
  10.7 15.8 %collective-permute-start.5 = (bf16[64,5120]{1,0:T(8,128)(2,1)S(1)}, bf16[64,5120]{1,0:T(8,128)(2,1)S(1)}, u32[]{:S(2)}, u32[]{:S(2)}) collective-permute-start(bf16[64,5120]{1,0:T(8,128)(2,1)S(1)} %get-tuple-element.28), channel_id=1, source_target_pairs={{1,2},{2,1},{5,6},{6,5},{9,10},{10,9},{13,14},{14,13},{17,18},{18,... | collective-permute-start | bytes 1966088 | tf_op jit(solution)/shard_map/ppermute | solution.py:302
  16.3 28.6 %collective-permute-start.6 = (bf16[64,5120]{1,0:T(8,128)(2,1)S(1)}, bf16[64,5120]{1,0:T(8,128)(2,1)S(1)}, u32[]{:S(2)}, u32[]{:S(2)}) collective-permute-start(bf16[64,5120]{1,0:T(8,128)(2,1)S(1)} %get-tuple-element.29), channel_id=1, source_target_pairs={{1,2},{2,1},{5,6},{6,5},{9,10},{10,9},{13,14},{14,13},{17,18},{18,... | collective-permute-start | bytes 1966088 | tf_op jit(solution)/shard_map/ppermute | solution.py:302
  18.3 31.6 %collective-permute-start.10 = (bf16[2,64,5120]{2,1,0:T(8,128)(2,1)S(1)}, bf16[2,64,5120]{2,1,0:T(8,128)(2,1)S(1)}, u32[]{:S(2)}, u32[]{:S(2)}) collective-permute-start(bf16[2,64,5120]{2,1,0:T(8,128)(2,1)S(1)} %pad_maximum_fusion), channel_id=1, source_target_pairs={{0,1},{1,0},{2,3},{3,2},{4,5},{5,4},{6,7},{7,6},{8,9},{9,8},{10,11... | collective-permute-start | bytes 3932168 | tf_op jit(solution)/shard_map/ppermute | solution.py:305
  18.4 4.7 %collective-permute-start.4 = (bf16[2,320,128]{2,1,0:T(8,128)(2,1)S(1)}, bf16[2,320,128]{2,1,0:T(8,128)(2,1)S(1)}, u32[]{:S(2)}, u32[]{:S(2)}) collective-permute-start(bf16[2,320,128]{2,1,0:T(8,128)(2,1)S(1)} %collective-permute-done.1), channel_id=1, source_target_pairs={{0,4},{1,5},{2,6},{3,7},{4,0},{5,1},{6,2},{7,3},{8,12},{9,13},{10,... | collective-permute-start | bytes 491528 | tf_op jit(solution)/shard_map/ppermute | solution.py:305
  18.7 7.9 %collective-permute-start.7 = (bf16[4,320,128]{2,1,0:T(8,128)(2,1)S(1)}, bf16[4,320,128]{2,1,0:T(8,128)(2,1)S(1)}, u32[]{:S(2)}, u32[]{:S(2)}) collective-permute-start(bf16[4,320,128]{2,1,0:T(8,128)(2,1)S(1)} %pad_maximum_fusion.3), channel_id=1, source_target_pairs={{0,16},{16,0},{1,17},{17,1},{2,18},{18,2},{3,19},{19,3},{4,20},{20... | collective-permute-start | bytes 983048 | tf_op jit(solution)/shard_map/ppermute | solution.py:308
  19.0 26.3 %copy-start = (bf16[256,5120]{1,0:T(8,128)(2,1)S(1)}, bf16[256,5120]{1,0:T(8,128)(2,1)}, u32[]{:S(2)}) copy-start(bf16[256,5120]{1,0:T(8,128)(2,1)} %k.3) | copy-start | bytes 7864324
  19.0 26.3 %copy-start.5 = (s32[256]{0:T(256)S(1)}, s32[256]{0:T(256)}, u32[]{:S(2)}) copy-start(s32[256]{0:T(256)} %lo_ref.3) | copy-start | bytes 3076
  19.0 26.3 %copy-start.6 = (s32[256]{0:T(256)S(1)}, s32[256]{0:T(256)}, u32[]{:S(2)}) copy-start(s32[256]{0:T(256)} %hi_ref.5) | copy-start | bytes 3076
  23.1 32.5 %collective-permute-start.8 = (bf16[2,64,5120]{2,1,0:T(8,128)(2,1)S(1)}, bf16[2,64,5120]{2,1,0:T(8,128)(2,1)S(1)}, u32[]{:S(2)}, u32[]{:S(2)}) collective-permute-start(bf16[2,64,5120]{2,1,0:T(8,128)(2,1)S(1)} %pad_maximum_fusion.1), channel_id=1, source_target_pairs={{3,4},{4,3},{7,8},{8,7},{11,12},{12,11},{19,20},{20,19},{23,24},{2... | collective-permute-start | bytes 3932168 | tf_op jit(solution)/shard_map/ppermute | solution.py:341
  44.9 4.4 %collective-permute-start.9 = (bf16[2,320,128]{2,1,0:T(8,128)(2,1)S(1)}, bf16[2,320,128]{2,1,0:T(8,128)(2,1)S(1)}, u32[]{:S(2)}, u32[]{:S(2)}) collective-permute-start(bf16[2,320,128]{2,1,0:T(8,128)(2,1)S(1)} %collective-permute-done.4), channel_id=1, source_target_pairs={{0,16},{16,0},{1,17},{17,1},{2,18},{18,2},{3,19},{19,3},{4,20},{20... | collective-permute-start | bytes 491528 | tf_op jit(solution)/shard_map/ppermute | solution.py:308
  45.2 6.7 %collective-permute-start.11 = (bf16[8,320,128]{2,1,0:T(8,128)(2,1)S(1)}, bf16[8,320,128]{2,1,0:T(8,128)(2,1)S(1)}, u32[]{:S(2)}, u32[]{:S(2)}) collective-permute-start(bf16[8,320,128]{2,1,0:T(8,128)(2,1)S(1)} %constant_dynamic-update-slice_fusion.rest_0_), channel_id=1, source_target_pairs={{0,1},{1,0},{2,3},{3,2},{4,5},{5,4},{6,7},{7,6},{8,9},{9,8},{10,11... | collective-permute-start | bytes 1966088 | tf_op jit(solution)/shard_map/ppermute | solution.py:305
  49.4 2.5 %copy-start.4 = (bf16[320,128]{1,0:T(8,128)(2,1)S(1)}, bf16[320,128]{1,0:T(8,128)(2,1)}, u32[]{:S(2)}) copy-start(bf16[320,128]{1,0:T(8,128)(2,1)} %own_down.1) | copy-start | bytes 245764
  49.4 2.5 %collective-permute-start.12 = (bf16[8,320,128]{2,1,0:T(8,128)(2,1)S(1)}, bf16[8,320,128]{2,1,0:T(8,128)(2,1)S(1)}, u32[]{:S(2)}, u32[]{:S(2)}) collective-permute-start(bf16[8,320,128]{2,1,0:T(8,128)(2,1)S(1)} %pad_maximum_fusion.2.rest_2_), channel_id=1, source_target_pairs={{0,1},{1,0},{2,3},{3,2},{4,5},{5,4},{6,7},{7,6},{8,9},{9,8},{10,11... | collective-permute-start | bytes 1966088 | tf_op jit(solution)/shard_map/ppermute | solution.py:305
  49.9 2.0 %copy-start.3 = (bf16[320,5120]{1,0:T(8,128)(2,1)S(1)}, bf16[320,5120]{1,0:T(8,128)(2,1)}, u32[]{:S(2)}) copy-start(bf16[320,5120]{1,0:T(8,128)(2,1)} %frozen.1) | copy-start | bytes 9830404

commit v9 on v8

--- a/solution.py
+++ b/solution.py
@@ -328,19 +328,18 @@
         side, short, long = steps
         own = jnp.where(lax.axis_index("group") == 0, down, up)[None]
         plane = join([own, swap(own, side)])
-        plane, far_rim, near_rim = barrier((plane, far_rim, near_rim))
+        direct = send(far_rim, direct_pairs)
+        plane, near_rim = barrier((plane, near_rim))
         halo = swap(near_rim, 1)
-        direct = send(far_rim, direct_pairs)
         beyond = swap(plane, long)
         beside = swap(plane, short)
         crossed = [cross(plane)]
-        beyond, beside, crossed, far_rim = barrier(
-            (beyond, beside, crossed, far_rim)
-        )
+        beyond, beside, crossed = barrier((beyond, beside, crossed))
+        far_rim, direct = barrier((far_rim, direct))
         last = swap(beyond, short)
         distant = lax.ppermute(jnp.stack(far_rim), "seq", distant_pairs)
         crossed.append(cross(join([beside, beyond])))
-        last, direct, crossed[1], lo_later = barrier((last, direct, crossed[1], lo))
+        last, crossed[1], lo_later = barrier((last, crossed[1], lo))
         inner = inner_attention(lo_later, hi, q, k, v)
         near = near_attention(lo_later, hi, q, k, v, halo)
         crossed.append(cross(last))

time: 60.5 us -> 46.2 us (0.76); the launches traced: 59.3 us -> 45.9 us
  waiting for transfers between devices: 25 us -> 10.5 us
  starting transfers between devices: 16.8 us -> 18.2 us
    ppermute x2, waiting for transfers between devices: 18.3 us -> 2.94 us  [send(): return [lax.ppermute(x, 'seq', pairs) for x in cells]]
    ppermute x2, starting transfers between devices: 7.49 us -> 5.56 us  [send(): return [lax.ppermute(x, 'seq', pairs) for x in cells]]
    ppermute x3, starting transfers between devices: 1.88 us -> 3.59 us  [cross(): return lax.ppermute(cells, 'group', [(0, 1), (1, 0)])]
    ppermute x7, starting transfers between devices: 6.65 us -> 8.21 us  [swap(): return lax.ppermute(cells, 'seq', [(i, i ^ mask) for i in range(count)])]
    ppermute x3, waiting for transfers between devices: 2.68 us -> 4.13 us  [cross(): return lax.ppermute(cells, 'group', [(0, 1), (1, 0)])]
    ppermute x7, waiting for transfers between devices: 4 us -> 3.38 us  [swap(): return lax.ppermute(cells, 'seq', [(i, i ^ mask) for i in range(count)])]
    another operation x1 -> x2, local copies, waits for them, and re-layouts: 2 us -> 1.61 us  [body(): near_rim = jnp.stack(rim((1 - odd) * (rows - FRAME)))]
  transfers between devices with their start and end apart: 13 -> 13, of which waited for: 3 -> 4; matrix products, arithmetic and copies ran while one was open for 4% -> 5% of each run, Pallas kernels for 16% -> 21%
where the time goes in v9:
time: 46.2 us; the launch traced here: 45.9 us
  starting transfers between devices  18.2 us (39%)
  Pallas kernels  13.3 us (29%)
  waiting for transfers between devices  10.5 us (23%)
  local copies, waits for them, and re-layouts  1.73 us (4%)
  other arithmetic  1.32 us (3%)
  between operations  0.85 us (2%)
    ppermute x7, starting transfers between devices, swap(): return lax.ppermute(cells, 'seq', [(i, i ^ mask) for i in range(count)])  8.21 us
    ppermute x2, starting transfers between devices, send(): return [lax.ppermute(x, 'seq', pairs) for x in cells]  5.56 us
    ppermute x3, waiting for transfers between devices, cross(): return lax.ppermute(cells, 'group', [(0, 1), (1, 0)])  4.13 us
    pallas_call x1, Pallas kernels, inner_attention(): pl.pallas_call(inner_kernel, grid=(width // WIDE,), out_shape=jax.ShapeDt...  3.94 us
    pallas_call x1, Pallas kernels, far_rows(): pl.pallas_call(far_kernel, out_shape=jax.ShapeDtypeStruct((rows, width),...  3.69 us
    pallas_call x1, Pallas kernels, merge(): pl.pallas_call(functools.partial(merge_kernel, layout), out_shape=(jax.Sh...  3.68 us
    ppermute x3, starting transfers between devices, cross(): return lax.ppermute(cells, 'group', [(0, 1), (1, 0)])  3.59 us
    ppermute x7, waiting for transfers between devices, swap(): return lax.ppermute(cells, 'seq', [(i, i ^ mask) for i in range(count)])  3.38 us
  transfers between devices with their start and end apart: 13, of which 4 were waited for; matrix products, arithmetic and copies ran while one was open for 5% of the time, Pallas kernels for 21%

profile of v9, /device:TPU:1, one launch (start us, length us, event | category | flops | bytes accessed | tf_op | source)
XLA Modules:
  0.0 45.9 jit_solution(9677781897282762522)
XLA Ops:
  0.6 0.9 %fusion = bf16[1,320,128]{2,1,0:T(8,128)(2,1)S(1)} fusion(bf16[320,128]{1,0:T(8,128)(2,1)} %own_down.1, bf16[128,320]{0,1:T(8,128)(2,1)} %param.14, pred[]{:T(512)S(6)} %eq.3), kind=kLoop, calls=%fused_computation.8 | loop fusion | flops 40960 | bytes 245761 | tf_op jit(solution)/shard_map/broadcast_in_dim | solution.py:329
  1.6 2.1 %collective-permute-start.3 = (bf16[1,320,128]{2,1,0:T(8,128)(2,1)S(1)}, bf16[1,320,128]{2,1,0:T(8,128)(2,1)S(1)}, u32[]{:S(2)}, u32[]{:S(2)}) collective-permute-start(bf16[1,320,128]{2,1,0:T(8,128)(2,1)S(1)} %fusion), channel_id=1, source_target_pairs={{0,2},{1,3},{2,0},{3,1},{4,6},{5,7},{6,4},{7,5},{8,10},{9,11},{10,... | collective-permute-start | bytes 245768 | tf_op jit(solution)/shard_map/ppermute | solution.py:305
  3.7 0.0 copy-start
  3.7 1.5 %dynamic-slice_bitcast_fusion = (bf16[1,64,5120]{2,1,0:T(8,128)(2,1)S(1)}, bf16[64,5120]{1,0:T(8,128)(2,1)S(1)}) fusion(bf16[256,5120]{1,0:T(8,128)(2,1)} %v.3, s32[]{:T(128)S(6)} %select_n.19, s32[]{:T(128)S(6)} %select_n.16), kind=kLoop, calls=%fused_computation.3 | loop fusion | bytes 2621448 | tf_op jit(solution)/shard_map/stack | solution.py:315
  5.2 2.5 %collective-permute-start.1 = (bf16[64,5120]{1,0:T(8,128)(2,1)S(1)}, bf16[64,5120]{1,0:T(8,128)(2,1)S(1)}, u32[]{:S(2)}, u32[]{:S(2)}) collective-permute-start(bf16[64,5120]{1,0:T(8,128)(2,1)S(1)} %get-tuple-element.22), channel_id=1, source_target_pairs={{1,2},{2,1},{5,6},{6,5},{9,10},{10,9},{13,14},{14,13},{17,18},{18,... | collective-permute-start | bytes 1966088 | tf_op jit(solution)/shard_map/ppermute | solution.py:302
  7.8 0.0 copy-done
  7.8 0.1 dynamic-slice_bitcast_fusion.1
  7.9 3.0 %collective-permute-start = (bf16[64,5120]{1,0:T(8,128)(2,1)S(1)}, bf16[64,5120]{1,0:T(8,128)(2,1)S(1)}, u32[]{:S(2)}, u32[]{:S(2)}) collective-permute-start(bf16[64,5120]{1,0:T(8,128)(2,1)S(1)} %get-tuple-element.21), channel_id=1, source_target_pairs={{1,2},{2,1},{5,6},{6,5},{9,10},{10,9},{13,14},{14,13},{17,18},{18,... | collective-permute-start | bytes 1966088 | tf_op jit(solution)/shard_map/ppermute | solution.py:302
  10.9 0.0 copy-start.2
  10.9 0.1 pad_maximum_fusion.1
  11.1 0.0 collective-permute-done.3
  11.1 2.4 %collective-permute-start.4 = (bf16[2,320,128]{2,1,0:T(8,128)(2,1)S(1)}, bf16[2,320,128]{2,1,0:T(8,128)(2,1)S(1)}, u32[]{:S(2)}, u32[]{:S(2)}) collective-permute-start(bf16[2,320,128]{2,1,0:T(8,128)(2,1)S(1)} %pad_maximum_fusion.4), channel_id=1, source_target_pairs={{0,8},{1,9},{2,10},{3,11},{4,12},{5,13},{6,14},{7,15},{8,0},{9,1},... | collective-permute-start | bytes 491528 | tf_op jit(solution)/shard_map/ppermute | solution.py:305
  13.5 1.3 %collective-permute-start.5 = (bf16[2,320,128]{2,1,0:T(8,128)(2,1)S(1)}, bf16[2,320,128]{2,1,0:T(8,128)(2,1)S(1)}, u32[]{:S(2)}, u32[]{:S(2)}) collective-permute-start(bf16[2,320,128]{2,1,0:T(8,128)(2,1)S(1)} %pad_maximum_fusion.4), channel_id=1, source_target_pairs={{0,4},{1,5},{2,6},{3,7},{4,0},{5,1},{6,2},{7,3},{8,12},{9,13},{10,... | collective-permute-start | bytes 491528 | tf_op jit(solution)/shard_map/ppermute | solution.py:305
  14.8 1.2 %collective-permute-start.6 = (bf16[2,320,128]{2,1,0:T(8,128)(2,1)S(1)}, bf16[2,320,128]{2,1,0:T(8,128)(2,1)S(1)}, u32[]{:S(2)}, u32[]{:S(2)}) collective-permute-start(bf16[2,320,128]{2,1,0:T(8,128)(2,1)S(1)} %pad_maximum_fusion.4), channel_id=1, source_target_pairs={{0,16},{16,0},{1,17},{17,1},{2,18},{18,2},{3,19},{19,3},{4,20},{20... | collective-permute-start | bytes 491528 | tf_op jit(solution)/shard_map/ppermute | solution.py:308
  16.0 2.9 %collective-permute-done.4 = bf16[2,320,128]{2,1,0:T(8,128)(2,1)S(1)} collective-permute-done((bf16[2,320,128]{2,1,0:T(8,128)(2,1)S(1)}, bf16[2,320,128]{2,1,0:T(8,128)(2,1)S(1)}, u32[]{:S(2)}, u32[]{:S(2)}) %collective-permute-start.4) | collective-permute-done | bytes 163872 | tf_op jit(solution)/shard_map/ppermute | solution.py:305
  18.9 0.0 collective-permute-start.10
  18.9 0.5 collective-permute-done.5
  19.3 0.0 collective-permute-done.6
  19.4 0.9 %collective-permute-start.7 = (bf16[2,320,128]{2,1,0:T(8,128)(2,1)S(1)}, bf16[2,320,128]{2,1,0:T(8,128)(2,1)S(1)}, u32[]{:S(2)}, u32[]{:S(2)}) collective-permute-start(bf16[2,320,128]{2,1,0:T(8,128)(2,1)S(1)} %collective-permute-done.4), channel_id=1, source_target_pairs={{0,4},{1,5},{2,6},{3,7},{4,0},{5,1},{6,2},{7,3},{8,12},{9,13},{10,... | collective-permute-start | bytes 491528 | tf_op jit(solution)/shard_map/ppermute | solution.py:305
  20.3 1.2 %collective-permute-start.8 = (bf16[4,320,128]{2,1,0:T(8,128)(2,1)S(1)}, bf16[4,320,128]{2,1,0:T(8,128)(2,1)S(1)}, u32[]{:S(2)}, u32[]{:S(2)}) collective-permute-start(bf16[4,320,128]{2,1,0:T(8,128)(2,1)S(1)} %pad_maximum_fusion.3), channel_id=1, source_target_pairs={{0,16},{16,0},{1,17},{17,1},{2,18},{18,2},{3,19},{19,3},{4,20},{20... | collective-permute-start | bytes 983048 | tf_op jit(solution)/shard_map/ppermute | solution.py:308
  21.5 0.0 collective-permute-done.1.rest_1_
  21.5 2.9 %collective-permute-done.rest_0_ = bf16[64,5120]{1,0:T(8,128)(2,1)S(1)} collective-permute-done((bf16[64,5120]{1,0:T(8,128)(2,1)S(1)}, bf16[64,5120]{1,0:T(8,128)(2,1)S(1)}, u32[]{:S(2)}, u32[]{:S(2)}) %collective-permute-start) | collective-permute-done | bytes 655392 | tf_op jit(solution)/shard_map/ppermute | solution.py:302
  24.5 0.0 copy-start.1
  24.5 0.0 copy-start.5
  24.5 0.1 pad_maximum_fusion
  24.6 0.9 %collective-permute-start.2 = (bf16[2,64,5120]{2,1,0:T(8,128)(2,1)S(1)}, bf16[2,64,5120]{2,1,0:T(8,128)(2,1)S(1)}, u32[]{:S(2)}, u32[]{:S(2)}) collective-permute-start(bf16[2,64,5120]{2,1,0:T(8,128)(2,1)S(1)} %pad_maximum_fusion), channel_id=1, source_target_pairs={{3,4},{4,3},{7,8},{8,7},{11,12},{12,11},{19,20},{20,19},{23,24},{2... | collective-permute-start | bytes 3932168 | tf_op jit(solution)/shard_map/ppermute | solution.py:340
  25.5 0.0 collective-permute-done.7
  25.6 4.1 %collective-permute-done.8 = bf16[4,320,128]{2,1,0:T(8,128)(2,1)S(1)} collective-permute-done((bf16[4,320,128]{2,1,0:T(8,128)(2,1)S(1)}, bf16[4,320,128]{2,1,0:T(8,128)(2,1)S(1)}, u32[]{:S(2)}, u32[]{:S(2)}) %collective-permute-start.8) | collective-permute-done | bytes 327712 | tf_op jit(solution)/shard_map/ppermute | solution.py:308
  29.7 1.2 %collective-permute-start.9 = (bf16[2,320,128]{2,1,0:T(8,128)(2,1)S(1)}, bf16[2,320,128]{2,1,0:T(8,128)(2,1)S(1)}, u32[]{:S(2)}, u32[]{:S(2)}) collective-permute-start(bf16[2,320,128]{2,1,0:T(8,128)(2,1)S(1)} %collective-permute-done.7), channel_id=1, source_target_pairs={{0,16},{16,0},{1,17},{17,1},{2,18},{18,2},{3,19},{19,3},{4,20},{20... | collective-permute-start | bytes 491528 | tf_op jit(solution)/shard_map/ppermute | solution.py:308
  30.9 1.1 %collective-permute-start.11 = (bf16[8,320,128]{2,1,0:T(8,128)(2,1)S(1)}, bf16[8,320,128]{2,1,0:T(8,128)(2,1)S(1)}, u32[]{:S(2)}, u32[]{:S(2)}) collective-permute-start(bf16[8,320,128]{2,1,0:T(8,128)(2,1)S(1)} %constant_dynamic-update-slice_fusion.rest_0_), channel_id=1, source_target_pairs={{0,1},{1,0},{2,3},{3,2},{4,5},{5,4},{6,7},{7,6},{8,9},{9,8},{10,11... | collective-permute-start | bytes 1966088 | tf_op jit(solution)/shard_map/ppermute | solution.py:305
  32.0 0.0 copy-done.2
  32.0 0.0 copy-done.1
  32.0 0.0 copy-done.5
  32.0 0.0 copy-done.6
  32.0 3.9 %inner_attention.1.inner = bf16[128,5120]{1,0:T(8,128)(2,1)S(1)} custom-call(s32[256]{0:T(256)S(1)} %copy-done.5, s32[256]{0:T(256)S(1)} %copy-done.6, bf16[256,5120]{1,0:T(8,128)(2,1)S(1)} %copy-done.2, bf16[256,5120]{1,0:T(8,128)(2,1)S(1)} %copy-done, bf16[256,5120]{1,0:T(8,128)(2,1)S(1)} %copy-done.1), custom_call_target="tpu_custom_call" | custom-call | flops 1342177280 | bytes 9175040 | tf_op jit(solution)/shard_map/inner_attention/pallas_call | solution.py:90
  36.0 0.0 collective-permute-done.9
  36.0 0.1 pad_maximum_fusion.2.rest_2_
  36.1 0.0 copy-start.4
  36.1 0.4 collective-permute-start.12
  36.4 0.0 collective-permute-done.10.halo
  36.5 2.0 %near_edge_attention.1.near = bf16[64,5120]{1,0:T(8,128)(2,1)S(1)} custom-call(s32[256]{0:T(256)S(1)} %copy-done.5, s32[256]{0:T(256)S(1)} %copy-done.6, bf16[256,5120]{1,0:T(8,128)(2,1)S(1)} %copy-done.2, bf16[256,5120]{1,0:T(8,128)(2,1)S(1)} %copy-done, bf16[256,5120]{1,0:T(8,128)(2,1)S(1)} %copy-done.1, bf16[2,64,5120]{2,1,0:T(8,128)(2,1)S(1)} %collective-permute-done.10.halo), custom_call_target="tpu_custom_call" | custom-call | flops 671088640 | bytes 9175040 | tf_op jit(solution)/shard_map/near_edge_attention/pallas_call | solution.py:173
  38.4 0.0 collective-permute-done.11.rest_1_
  38.4 0.0 collective-permute-done.12.rest_3_
  38.4 0.0 copy-done.4
  38.5 0.0 copy-done.3
  38.5 3.7 %merge_and_adapter.1 = (bf16[320,5120]{1,0:T(8,128)(2,1)}, bf16[256,5120]{1,0:T(8,128)(2,1)}, bf16[2,5120,128]{2,1,0:T(8,128)(2,1)S(1)}) custom-call(bf16[320,5120]{1,0:T(8,128)(2,1)S(1)} %copy-done.3, bf16[320,128]{1,0:T(8,128)(2,1)S(1)} %copy-done.4, bf16[128,5120]{1,0:T(8,128)(2,1)S(1)} %inner_attention.1.inner, ...), custom_call_target="tpu_custom_call" | custom-call | flops 1090519040 | bytes 14417920 | tf_op jit(solution)/shard_map/merge_and_adapter/pallas_call | solution.py:229
  42.2 0.0 collective-permute-done.2.rest_2_
  42.2 3.7 %far_edge_rows.1 = bf16[256,5120]{1,0:T(8,128)(2,1)} custom-call(s32[256]{0:T(256)S(1)} %copy-done.5, s32[256]{0:T(256)S(1)} %copy-done.6, bf16[256,5120]{1,0:T(8,128)(2,1)S(1)} %copy-done.2, bf16[256,5120]{1,0:T(8,128)(2,1)S(1)} %copy-done, bf16[256,5120]{1,0:T(8,128)(2,1)S(1)} %copy-done.1, ...), custom_call_target="tpu_custom_call", output_to_operand_aliasing={{}: (9, {})} | custom-call | flops 671088640 | bytes 9175040 | tf_op jit(solution)/shard_map/far_edge_rows/pallas_call | solution.py:276
  (8 shorter events, 0.1 us)
Async XLA Ops:
  1.6 9.5 %collective-permute-start.3 = (bf16[1,320,128]{2,1,0:T(8,128)(2,1)S(1)}, bf16[1,320,128]{2,1,0:T(8,128)(2,1)S(1)}, u32[]{:S(2)}, u32[]{:S(2)}) collective-permute-start(bf16[1,320,128]{2,1,0:T(8,128)(2,1)S(1)} %fusion), channel_id=1, source_target_pairs={{0,2},{1,3},{2,0},{3,1},{4,6},{5,7},{6,4},{7,5},{8,10},{9,11},{10,... | collective-permute-start | bytes 245768 | tf_op jit(solution)/shard_map/ppermute | solution.py:305
  3.7 4.0 %copy-start = (bf16[256,5120]{1,0:T(8,128)(2,1)S(1)}, bf16[256,5120]{1,0:T(8,128)(2,1)}, u32[]{:S(2)}) copy-start(bf16[256,5120]{1,0:T(8,128)(2,1)} %k.3) | copy-start | bytes 7864324
  5.2 16.3 %collective-permute-start.1 = (bf16[64,5120]{1,0:T(8,128)(2,1)S(1)}, bf16[64,5120]{1,0:T(8,128)(2,1)S(1)}, u32[]{:S(2)}, u32[]{:S(2)}) collective-permute-start(bf16[64,5120]{1,0:T(8,128)(2,1)S(1)} %get-tuple-element.22), channel_id=1, source_target_pairs={{1,2},{2,1},{5,6},{6,5},{9,10},{10,9},{13,14},{14,13},{17,18},{18,... | collective-permute-start | bytes 1966088 | tf_op jit(solution)/shard_map/ppermute | solution.py:302
  7.9 16.6 %collective-permute-start = (bf16[64,5120]{1,0:T(8,128)(2,1)S(1)}, bf16[64,5120]{1,0:T(8,128)(2,1)S(1)}, u32[]{:S(2)}, u32[]{:S(2)}) collective-permute-start(bf16[64,5120]{1,0:T(8,128)(2,1)S(1)} %get-tuple-element.21), channel_id=1, source_target_pairs={{1,2},{2,1},{5,6},{6,5},{9,10},{10,9},{13,14},{14,13},{17,18},{18,... | collective-permute-start | bytes 1966088 | tf_op jit(solution)/shard_map/ppermute | solution.py:302
  10.9 21.1 %copy-start.2 = (bf16[256,5120]{1,0:T(8,128)(2,1)S(1)}, bf16[256,5120]{1,0:T(8,128)(2,1)}, u32[]{:S(2)}) copy-start(bf16[256,5120]{1,0:T(8,128)(2,1)} %q.3) | copy-start | bytes 7864324
  11.1 7.8 %collective-permute-start.4 = (bf16[2,320,128]{2,1,0:T(8,128)(2,1)S(1)}, bf16[2,320,128]{2,1,0:T(8,128)(2,1)S(1)}, u32[]{:S(2)}, u32[]{:S(2)}) collective-permute-start(bf16[2,320,128]{2,1,0:T(8,128)(2,1)S(1)} %pad_maximum_fusion.4), channel_id=1, source_target_pairs={{0,8},{1,9},{2,10},{3,11},{4,12},{5,13},{6,14},{7,15},{8,0},{9,1},... | collective-permute-start | bytes 491528 | tf_op jit(solution)/shard_map/ppermute | solution.py:305
  13.5 5.9 %collective-permute-start.5 = (bf16[2,320,128]{2,1,0:T(8,128)(2,1)S(1)}, bf16[2,320,128]{2,1,0:T(8,128)(2,1)S(1)}, u32[]{:S(2)}, u32[]{:S(2)}) collective-permute-start(bf16[2,320,128]{2,1,0:T(8,128)(2,1)S(1)} %pad_maximum_fusion.4), channel_id=1, source_target_pairs={{0,4},{1,5},{2,6},{3,7},{4,0},{5,1},{6,2},{7,3},{8,12},{9,13},{10,... | collective-permute-start | bytes 491528 | tf_op jit(solution)/shard_map/ppermute | solution.py:305
  14.8 4.6 %collective-permute-start.6 = (bf16[2,320,128]{2,1,0:T(8,128)(2,1)S(1)}, bf16[2,320,128]{2,1,0:T(8,128)(2,1)S(1)}, u32[]{:S(2)}, u32[]{:S(2)}) collective-permute-start(bf16[2,320,128]{2,1,0:T(8,128)(2,1)S(1)} %pad_maximum_fusion.4), channel_id=1, source_target_pairs={{0,16},{16,0},{1,17},{17,1},{2,18},{18,2},{3,19},{19,3},{4,20},{20... | collective-permute-start | bytes 491528 | tf_op jit(solution)/shard_map/ppermute | solution.py:308
  18.9 17.6 %collective-permute-start.10 = (bf16[2,64,5120]{2,1,0:T(8,128)(2,1)S(1)}, bf16[2,64,5120]{2,1,0:T(8,128)(2,1)S(1)}, u32[]{:S(2)}, u32[]{:S(2)}) collective-permute-start(bf16[2,64,5120]{2,1,0:T(8,128)(2,1)S(1)} %pad_maximum_fusion.1), channel_id=1, source_target_pairs={{0,1},{1,0},{2,3},{3,2},{4,5},{5,4},{6,7},{7,6},{8,9},{9,8},{10,11... | collective-permute-start | bytes 3932168 | tf_op jit(solution)/shard_map/ppermute | solution.py:305
  19.4 6.2 %collective-permute-start.7 = (bf16[2,320,128]{2,1,0:T(8,128)(2,1)S(1)}, bf16[2,320,128]{2,1,0:T(8,128)(2,1)S(1)}, u32[]{:S(2)}, u32[]{:S(2)}) collective-permute-start(bf16[2,320,128]{2,1,0:T(8,128)(2,1)S(1)} %collective-permute-done.4), channel_id=1, source_target_pairs={{0,4},{1,5},{2,6},{3,7},{4,0},{5,1},{6,2},{7,3},{8,12},{9,13},{10,... | collective-permute-start | bytes 491528 | tf_op jit(solution)/shard_map/ppermute | solution.py:305
  20.3 9.4 %collective-permute-start.8 = (bf16[4,320,128]{2,1,0:T(8,128)(2,1)S(1)}, bf16[4,320,128]{2,1,0:T(8,128)(2,1)S(1)}, u32[]{:S(2)}, u32[]{:S(2)}) collective-permute-start(bf16[4,320,128]{2,1,0:T(8,128)(2,1)S(1)} %pad_maximum_fusion.3), channel_id=1, source_target_pairs={{0,16},{16,0},{1,17},{17,1},{2,18},{18,2},{3,19},{19,3},{4,20},{20... | collective-permute-start | bytes 983048 | tf_op jit(solution)/shard_map/ppermute | solution.py:308
  24.5 7.6 %copy-start.1 = (bf16[256,5120]{1,0:T(8,128)(2,1)S(1)}, bf16[256,5120]{1,0:T(8,128)(2,1)}, u32[]{:S(2)}) copy-start(bf16[256,5120]{1,0:T(8,128)(2,1)} %v.3) | copy-start | bytes 7864324
  24.5 7.6 %copy-start.5 = (s32[256]{0:T(256)S(1)}, s32[256]{0:T(256)}, u32[]{:S(2)}) copy-start(s32[256]{0:T(256)} %lo_ref.3) | copy-start | bytes 3076
  24.5 7.6 %copy-start.6 = (s32[256]{0:T(256)S(1)}, s32[256]{0:T(256)}, u32[]{:S(2)}) copy-start(s32[256]{0:T(256)} %hi_ref.5) | copy-start | bytes 3076
  24.6 17.6 %collective-permute-start.2 = (bf16[2,64,5120]{2,1,0:T(8,128)(2,1)S(1)}, bf16[2,64,5120]{2,1,0:T(8,128)(2,1)S(1)}, u32[]{:S(2)}, u32[]{:S(2)}) collective-permute-start(bf16[2,64,5120]{2,1,0:T(8,128)(2,1)S(1)} %pad_maximum_fusion), channel_id=1, source_target_pairs={{3,4},{4,3},{7,8},{8,7},{11,12},{12,11},{19,20},{20,19},{23,24},{2... | collective-permute-start | bytes 3932168 | tf_op jit(solution)/shard_map/ppermute | solution.py:340
  29.7 6.3 %collective-permute-start.9 = (bf16[2,320,128]{2,1,0:T(8,128)(2,1)S(1)}, bf16[2,320,128]{2,1,0:T(8,128)(2,1)S(1)}, u32[]{:S(2)}, u32[]{:S(2)}) collective-permute-start(bf16[2,320,128]{2,1,0:T(8,128)(2,1)S(1)} %collective-permute-done.7), channel_id=1, source_target_pairs={{0,16},{16,0},{1,17},{17,1},{2,18},{18,2},{3,19},{19,3},{4,20},{20... | collective-permute-start | bytes 491528 | tf_op jit(solution)/shard_map/ppermute | solution.py:308
  30.9 7.5 %collective-permute-start.11 = (bf16[8,320,128]{2,1,0:T(8,128)(2,1)S(1)}, bf16[8,320,128]{2,1,0:T(8,128)(2,1)S(1)}, u32[]{:S(2)}, u32[]{:S(2)}) collective-permute-start(bf16[8,320,128]{2,1,0:T(8,128)(2,1)S(1)} %constant_dynamic-update-slice_fusion.rest_0_), channel_id=1, source_target_pairs={{0,1},{1,0},{2,3},{3,2},{4,5},{5,4},{6,7},{7,6},{8,9},{9,8},{10,11... | collective-permute-start | bytes 1966088 | tf_op jit(solution)/shard_map/ppermute | solution.py:305
  36.1 2.4 %copy-start.4 = (bf16[320,128]{1,0:T(8,128)(2,1)S(1)}, bf16[320,128]{1,0:T(8,128)(2,1)}, u32[]{:S(2)}) copy-start(bf16[320,128]{1,0:T(8,128)(2,1)} %own_down.1) | copy-start | bytes 245764
  36.1 2.3 %collective-permute-start.12 = (bf16[8,320,128]{2,1,0:T(8,128)(2,1)S(1)}, bf16[8,320,128]{2,1,0:T(8,128)(2,1)S(1)}, u32[]{:S(2)}, u32[]{:S(2)}) collective-permute-start(bf16[8,320,128]{2,1,0:T(8,128)(2,1)S(1)} %pad_maximum_fusion.2.rest_2_), channel_id=1, source_target_pairs={{0,1},{1,0},{2,3},{3,2},{4,5},{5,4},{6,7},{7,6},{8,9},{9,8},{10,11... | collective-permute-start | bytes 1966088 | tf_op jit(solution)/shard_map/ppermute | solution.py:305
  36.5 2.0 %copy-start.3 = (bf16[320,5120]{1,0:T(8,128)(2,1)S(1)}, bf16[320,5120]{1,0:T(8,128)(2,1)}, u32[]{:S(2)}) copy-start(bf16[320,5120]{1,0:T(8,128)(2,1)} %frozen.1) | copy-start | bytes 9830404

commit v10 on v9

--- a/solution.py
+++ b/solution.py
@@ -335,16 +335,15 @@
         beside = swap(plane, short)
         crossed = [cross(plane)]
         beyond, beside, crossed = barrier((beyond, beside, crossed))
-        far_rim, direct = barrier((far_rim, direct))
+        far_rim, direct, lo_later = barrier((far_rim, direct, lo))
         last = swap(beyond, short)
         distant = lax.ppermute(jnp.stack(far_rim), "seq", distant_pairs)
         crossed.append(cross(join([beside, beyond])))
-        last, crossed[1], lo_later = barrier((last, crossed[1], lo))
         inner = inner_attention(lo_later, hi, q, k, v)
         near = near_attention(lo_later, hi, q, k, v, halo)
+        last, inner, near = barrier((last, inner, near))
         crossed.append(cross(last))
         cells, other = join([plane, beside, beyond, last]), join(crossed)
-        other, inner = barrier((other, inner))
         masks = [a ^ b for a in (0, short, long, short ^ long) for b in (0, side)]
         across = [mask ^ 1 for mask in masks]
         layout = [(0, masks), (0, across), (1, masks), (1, across)]

time: 46.2 us -> 46.3 us (level)
  starting transfers between devices: 18.2 us -> 15.2 us
  waiting for transfers between devices: 10.5 us -> 13 us
  local copies, waits for them, and re-layouts: 1.73 us -> 2.49 us
    ppermute x7, waiting for transfers between devices: 3.38 us -> 7.95 us  [swap(): return lax.ppermute(cells, 'seq', [(i, i ^ mask) for i in range(count)])]
    ppermute x7, starting transfers between devices: 8.21 us -> 5.89 us  [swap(): return lax.ppermute(cells, 'seq', [(i, i ^ mask) for i in range(count)])]
    ppermute x3, waiting for transfers between devices: 4.13 us -> 2.85 us  [cross(): return lax.ppermute(cells, 'group', [(0, 1), (1, 0)])]
    ppermute x2, waiting for transfers between devices: 2.94 us -> 2.16 us  [send(): return [lax.ppermute(x, 'seq', pairs) for x in cells]]
    ppermute x3, starting transfers between devices: 3.59 us -> 2.83 us  [cross(): return lax.ppermute(cells, 'group', [(0, 1), (1, 0)])]
    unnamed x17 -> x19, local copies, waits for them, and re-layouts: 0.09 us -> 0.83 us
  transfers between devices with their start and end apart: 13 -> 13, of which waited for: 4 -> 5; matrix products, arithmetic and copies ran while one was open for 5% -> 4% of each run, Pallas kernels for 21% -> 21%
where the time goes in v10:
time: 46.3 us; the launch traced here: 46 us
  starting transfers between devices  15.2 us (33%)
  Pallas kernels  13.3 us (29%)
  waiting for transfers between devices  13 us (28%)
  local copies, waits for them, and re-layouts  2.49 us (5%)
  other arithmetic  1.24 us (3%)
  between operations  0.87 us (2%)
    ppermute x7, waiting for transfers between devices, swap(): return lax.ppermute(cells, 'seq', [(i, i ^ mask) for i in range(count)])  7.95 us
    ppermute x7, starting transfers between devices, swap(): return lax.ppermute(cells, 'seq', [(i, i ^ mask) for i in range(count)])  5.89 us
    ppermute x2, starting transfers between devices, send(): return [lax.ppermute(x, 'seq', pairs) for x in cells]  5.56 us
    pallas_call x1, Pallas kernels, inner_attention(): pl.pallas_call(inner_kernel, grid=(width // WIDE,), out_shape=jax.ShapeDt...  3.92 us
    pallas_call x1, Pallas kernels, far_rows(): pl.pallas_call(far_kernel, out_shape=jax.ShapeDtypeStruct((rows, width),...  3.69 us
    pallas_call x1, Pallas kernels, merge(): pl.pallas_call(functools.partial(merge_kernel, layout), out_shape=(jax.Sh...  3.68 us
    ppermute x3, waiting for transfers between devices, cross(): return lax.ppermute(cells, 'group', [(0, 1), (1, 0)])  2.85 us
    ppermute x3, starting transfers between devices, cross(): return lax.ppermute(cells, 'group', [(0, 1), (1, 0)])  2.83 us
  transfers between devices with their start and end apart: 13, of which 5 were waited for; matrix products, arithmetic and copies ran while one was open for 4% of the time, Pallas kernels for 21%

profile of v10, /device:TPU:1, one launch (start us, length us, event | category | flops | bytes accessed | tf_op | source)
XLA Modules:
  0.0 46.0 jit_solution(1312398405887340060)
XLA Ops:
  0.6 0.9 %fusion = bf16[1,320,128]{2,1,0:T(8,128)(2,1)S(1)} fusion(bf16[320,128]{1,0:T(8,128)(2,1)} %own_down.1, bf16[128,320]{0,1:T(8,128)(2,1)} %param.14, pred[]{:T(512)S(6)} %eq.3), kind=kLoop, calls=%fused_computation.7 | loop fusion | flops 40960 | bytes 245761 | tf_op jit(solution)/shard_map/broadcast_in_dim | solution.py:329
  1.6 2.1 %collective-permute-start.3 = (bf16[1,320,128]{2,1,0:T(8,128)(2,1)S(1)}, bf16[1,320,128]{2,1,0:T(8,128)(2,1)S(1)}, u32[]{:S(2)}, u32[]{:S(2)}) collective-permute-start(bf16[1,320,128]{2,1,0:T(8,128)(2,1)S(1)} %fusion), channel_id=1, source_target_pairs={{0,2},{1,3},{2,0},{3,1},{4,6},{5,7},{6,4},{7,5},{8,10},{9,11},{10,... | collective-permute-start | bytes 245768 | tf_op jit(solution)/shard_map/ppermute | solution.py:305
  3.7 0.0 copy-start.1
  3.7 1.5 %dynamic-slice_bitcast_fusion.1 = (bf16[1,64,5120]{2,1,0:T(8,128)(2,1)S(1)}, bf16[64,5120]{1,0:T(8,128)(2,1)S(1)}) fusion(bf16[256,5120]{1,0:T(8,128)(2,1)} %k.3, s32[]{:T(128)S(6)} %select_n.19, s32[]{:T(128)S(6)} %select_n.16), kind=kLoop, calls=%fused_computation.3 | loop fusion | bytes 2621448 | tf_op jit(solution)/shard_map/stack | solution.py:315
  5.2 2.5 %collective-permute-start = (bf16[64,5120]{1,0:T(8,128)(2,1)S(1)}, bf16[64,5120]{1,0:T(8,128)(2,1)S(1)}, u32[]{:S(2)}, u32[]{:S(2)}) collective-permute-start(bf16[64,5120]{1,0:T(8,128)(2,1)S(1)} %get-tuple-element.20), channel_id=1, source_target_pairs={{1,2},{2,1},{5,6},{6,5},{9,10},{10,9},{13,14},{14,13},{17,18},{18,... | collective-permute-start | bytes 1966088 | tf_op jit(solution)/shard_map/ppermute | solution.py:302
  7.8 0.0 copy-done.1
  7.8 0.1 dynamic-slice_bitcast_fusion
  7.9 3.1 %collective-permute-start.1 = (bf16[64,5120]{1,0:T(8,128)(2,1)S(1)}, bf16[64,5120]{1,0:T(8,128)(2,1)S(1)}, u32[]{:S(2)}, u32[]{:S(2)}) collective-permute-start(bf16[64,5120]{1,0:T(8,128)(2,1)S(1)} %get-tuple-element.21), channel_id=1, source_target_pairs={{1,2},{2,1},{5,6},{6,5},{9,10},{10,9},{13,14},{14,13},{17,18},{18,... | collective-permute-start | bytes 1966088 | tf_op jit(solution)/shard_map/ppermute | solution.py:302
  10.9 0.0 copy-start.2
  10.9 0.1 pad_maximum_fusion.1
  11.1 0.0 collective-permute-done.3
  11.1 1.2 %collective-permute-start.6 = (bf16[2,320,128]{2,1,0:T(8,128)(2,1)S(1)}, bf16[2,320,128]{2,1,0:T(8,128)(2,1)S(1)}, u32[]{:S(2)}, u32[]{:S(2)}) collective-permute-start(bf16[2,320,128]{2,1,0:T(8,128)(2,1)S(1)} %pad_maximum_fusion.3), channel_id=1, source_target_pairs={{0,16},{16,0},{1,17},{17,1},{2,18},{18,2},{3,19},{19,3},{4,20},{20... | collective-permute-start | bytes 491528 | tf_op jit(solution)/shard_map/ppermute | solution.py:308
  12.4 1.3 %collective-permute-start.5 = (bf16[2,320,128]{2,1,0:T(8,128)(2,1)S(1)}, bf16[2,320,128]{2,1,0:T(8,128)(2,1)S(1)}, u32[]{:S(2)}, u32[]{:S(2)}) collective-permute-start(bf16[2,320,128]{2,1,0:T(8,128)(2,1)S(1)} %pad_maximum_fusion.3), channel_id=1, source_target_pairs={{0,4},{1,5},{2,6},{3,7},{4,0},{5,1},{6,2},{7,3},{8,12},{9,13},{10,... | collective-permute-start | bytes 491528 | tf_op jit(solution)/shard_map/ppermute | solution.py:305
  13.6 2.3 %collective-permute-start.4 = (bf16[2,320,128]{2,1,0:T(8,128)(2,1)S(1)}, bf16[2,320,128]{2,1,0:T(8,128)(2,1)S(1)}, u32[]{:S(2)}, u32[]{:S(2)}) collective-permute-start(bf16[2,320,128]{2,1,0:T(8,128)(2,1)S(1)} %pad_maximum_fusion.3), channel_id=1, source_target_pairs={{0,8},{1,9},{2,10},{3,11},{4,12},{5,13},{6,14},{7,15},{8,0},{9,1},... | collective-permute-start | bytes 491528 | tf_op jit(solution)/shard_map/ppermute | solution.py:305
  16.0 0.0 collective-permute-done.6
  16.0 0.0 collective-permute-start.8
  16.0 2.8 %collective-permute-done.5 = bf16[2,320,128]{2,1,0:T(8,128)(2,1)S(1)} collective-permute-done((bf16[2,320,128]{2,1,0:T(8,128)(2,1)S(1)}, bf16[2,320,128]{2,1,0:T(8,128)(2,1)S(1)}, u32[]{:S(2)}, u32[]{:S(2)}) %collective-permute-start.5) | collective-permute-done | bytes 163872 | tf_op jit(solution)/shard_map/ppermute | solution.py:305
  18.8 3.1 %collective-permute-done.4 = bf16[2,320,128]{2,1,0:T(8,128)(2,1)S(1)} collective-permute-done((bf16[2,320,128]{2,1,0:T(8,128)(2,1)S(1)}, bf16[2,320,128]{2,1,0:T(8,128)(2,1)S(1)}, u32[]{:S(2)}, u32[]{:S(2)}) %collective-permute-start.4) | collective-permute-done | bytes 163872 | tf_op jit(solution)/shard_map/ppermute | solution.py:305
  21.8 0.0 collective-permute-start.7
  21.9 0.4 collective-permute-start.10
  22.3 0.0 collective-permute-done.rest_0_
  22.3 2.2 %collective-permute-done.1.rest_1_ = bf16[64,5120]{1,0:T(8,128)(2,1)S(1)} collective-permute-done((bf16[64,5120]{1,0:T(8,128)(2,1)S(1)}, bf16[64,5120]{1,0:T(8,128)(2,1)S(1)}, u32[]{:S(2)}, u32[]{:S(2)}) %collective-permute-start.1) | collective-permute-done | bytes 655392 | tf_op jit(solution)/shard_map/ppermute | solution.py:302
  24.5 0.0 copy-start
  24.5 0.0 copy-start.5
  24.5 0.1 pad_maximum_fusion
  24.6 0.9 %collective-permute-start.2 = (bf16[2,64,5120]{2,1,0:T(8,128)(2,1)S(1)}, bf16[2,64,5120]{2,1,0:T(8,128)(2,1)S(1)}, u32[]{:S(2)}, u32[]{:S(2)}) collective-permute-start(bf16[2,64,5120]{2,1,0:T(8,128)(2,1)S(1)} %pad_maximum_fusion), channel_id=1, source_target_pairs={{3,4},{4,3},{7,8},{8,7},{11,12},{12,11},{19,20},{20,19},{23,24},{2... | collective-permute-start | bytes 3932168 | tf_op jit(solution)/shard_map/ppermute | solution.py:340
  25.5 0.0 copy-done.2
  25.5 0.7 %copy-done = bf16[256,5120]{1,0:T(8,128)(2,1)S(1)} copy-done((bf16[256,5120]{1,0:T(8,128)(2,1)S(1)}, bf16[256,5120]{1,0:T(8,128)(2,1)}, u32[]{:S(2)}) %copy-start) | copy-done | bytes 2621464
  26.2 0.0 copy-done.5
  26.2 0.0 copy-done.6
  26.2 3.9 %inner_attention.1.inner = bf16[128,5120]{1,0:T(8,128)(2,1)S(1)} custom-call(s32[256]{0:T(256)S(1)} %copy-done.5, s32[256]{0:T(256)S(1)} %copy-done.6, bf16[256,5120]{1,0:T(8,128)(2,1)S(1)} %copy-done.2, bf16[256,5120]{1,0:T(8,128)(2,1)S(1)} %copy-done, bf16[256,5120]{1,0:T(8,128)(2,1)S(1)} %copy-done.1), custom_call_target="tpu_custom_call" | custom-call | flops 1342177280 | bytes 9175040 | tf_op jit(solution)/shard_map/inner_attention/pallas_call | solution.py:90
  30.1 0.0 collective-permute-done.8.halo
  30.2 0.0 copy-start.3
  30.2 2.0 %near_edge_attention.1.near = bf16[64,5120]{1,0:T(8,128)(2,1)S(1)} custom-call(s32[256]{0:T(256)S(1)} %copy-done.5, s32[256]{0:T(256)S(1)} %copy-done.6, bf16[256,5120]{1,0:T(8,128)(2,1)S(1)} %copy-done.2, bf16[256,5120]{1,0:T(8,128)(2,1)S(1)} %copy-done, bf16[256,5120]{1,0:T(8,128)(2,1)S(1)} %copy-done.1, bf16[2,64,5120]{2,1,0:T(8,128)(2,1)S(1)} %collective-permute-done.8.halo), custom_call_target="tpu_custom_call" | custom-call | flops 671088640 | bytes 9175040 | tf_op jit(solution)/shard_map/near_edge_attention/pallas_call | solution.py:173
  32.1 0.0 copy-start.4
  32.1 0.0 collective-permute-done.7
  32.2 1.2 %collective-permute-start.11 = (bf16[2,320,128]{2,1,0:T(8,128)(2,1)S(1)}, bf16[2,320,128]{2,1,0:T(8,128)(2,1)S(1)}, u32[]{:S(2)}, u32[]{:S(2)}) collective-permute-start(bf16[2,320,128]{2,1,0:T(8,128)(2,1)S(1)} %collective-permute-done.7), channel_id=1, source_target_pairs={{0,16},{16,0},{1,17},{17,1},{2,18},{18,2},{3,19},{19,3},{4,20},{20... | collective-permute-start | bytes 491528 | tf_op jit(solution)/shard_map/ppermute | solution.py:308
  33.4 0.0 collective-permute-done.10
  33.5 0.1 collective-permute-start.9
  33.5 2.8 %collective-permute-done.11 = bf16[2,320,128]{2,1,0:T(8,128)(2,1)S(1)} collective-permute-done((bf16[2,320,128]{2,1,0:T(8,128)(2,1)S(1)}, bf16[2,320,128]{2,1,0:T(8,128)(2,1)S(1)}, u32[]{:S(2)}, u32[]{:S(2)}) %collective-permute-start.11) | collective-permute-done | bytes 163872 | tf_op jit(solution)/shard_map/ppermute | solution.py:308
  36.4 0.1 collective-permute-start.12
  36.5 0.0 collective-permute-done.9.rest_1_
  36.5 2.1 %collective-permute-done.12.rest_3_ = bf16[8,320,128]{2,1,0:T(8,128)(2,1)S(1)} collective-permute-done((bf16[8,320,128]{2,1,0:T(8,128)(2,1)S(1)}, bf16[8,320,128]{2,1,0:T(8,128)(2,1)S(1)}, u32[]{:S(2)}, u32[]{:S(2)}) %collective-permute-start.12) | collective-permute-done | bytes 655392 | tf_op jit(solution)/shard_map/ppermute | solution.py:305
  38.6 0.0 copy-done.3
  38.6 0.0 copy-done.4
  38.6 3.7 %merge_and_adapter.1 = (bf16[320,5120]{1,0:T(8,128)(2,1)}, bf16[256,5120]{1,0:T(8,128)(2,1)}, bf16[2,5120,128]{2,1,0:T(8,128)(2,1)S(1)}) custom-call(bf16[320,5120]{1,0:T(8,128)(2,1)S(1)} %copy-done.3, bf16[320,128]{1,0:T(8,128)(2,1)S(1)} %copy-done.4, bf16[128,5120]{1,0:T(8,128)(2,1)S(1)} %inner_attention.1.inner, ...), custom_call_target="tpu_custom_call" | custom-call | flops 1090519040 | bytes 14417920 | tf_op jit(solution)/shard_map/merge_and_adapter/pallas_call | solution.py:229
  42.3 0.0 collective-permute-done.2.rest_2_
  42.3 3.7 %far_edge_rows.1 = bf16[256,5120]{1,0:T(8,128)(2,1)} custom-call(s32[256]{0:T(256)S(1)} %copy-done.5, s32[256]{0:T(256)S(1)} %copy-done.6, bf16[256,5120]{1,0:T(8,128)(2,1)S(1)} %copy-done.2, bf16[256,5120]{1,0:T(8,128)(2,1)S(1)} %copy-done, bf16[256,5120]{1,0:T(8,128)(2,1)S(1)} %copy-done.1, ...), custom_call_target="tpu_custom_call", output_to_operand_aliasing={{}: (9, {})} | custom-call | flops 671088640 | bytes 9175040 | tf_op jit(solution)/shard_map/far_edge_rows/pallas_call | solution.py:276
  (10 shorter events, 0.2 us)
Async XLA Ops:
  1.6 9.5 %collective-permute-start.3 = (bf16[1,320,128]{2,1,0:T(8,128)(2,1)S(1)}, bf16[1,320,128]{2,1,0:T(8,128)(2,1)S(1)}, u32[]{:S(2)}, u32[]{:S(2)}) collective-permute-start(bf16[1,320,128]{2,1,0:T(8,128)(2,1)S(1)} %fusion), channel_id=1, source_target_pairs={{0,2},{1,3},{2,0},{3,1},{4,6},{5,7},{6,4},{7,5},{8,10},{9,11},{10,... | collective-permute-start | bytes 245768 | tf_op jit(solution)/shard_map/ppermute | solution.py:305
  3.7 4.0 %copy-start.1 = (bf16[256,5120]{1,0:T(8,128)(2,1)S(1)}, bf16[256,5120]{1,0:T(8,128)(2,1)}, u32[]{:S(2)}) copy-start(bf16[256,5120]{1,0:T(8,128)(2,1)} %v.3) | copy-start | bytes 7864324
  5.2 17.1 %collective-permute-start = (bf16[64,5120]{1,0:T(8,128)(2,1)S(1)}, bf16[64,5120]{1,0:T(8,128)(2,1)S(1)}, u32[]{:S(2)}, u32[]{:S(2)}) collective-permute-start(bf16[64,5120]{1,0:T(8,128)(2,1)S(1)} %get-tuple-element.20), channel_id=1, source_target_pairs={{1,2},{2,1},{5,6},{6,5},{9,10},{10,9},{13,14},{14,13},{17,18},{18,... | collective-permute-start | bytes 1966088 | tf_op jit(solution)/shard_map/ppermute | solution.py:302
  7.9 16.6 %collective-permute-start.1 = (bf16[64,5120]{1,0:T(8,128)(2,1)S(1)}, bf16[64,5120]{1,0:T(8,128)(2,1)S(1)}, u32[]{:S(2)}, u32[]{:S(2)}) collective-permute-start(bf16[64,5120]{1,0:T(8,128)(2,1)S(1)} %get-tuple-element.21), channel_id=1, source_target_pairs={{1,2},{2,1},{5,6},{6,5},{9,10},{10,9},{13,14},{14,13},{17,18},{18,... | collective-permute-start | bytes 1966088 | tf_op jit(solution)/shard_map/ppermute | solution.py:302
  10.9 14.6 %copy-start.2 = (bf16[256,5120]{1,0:T(8,128)(2,1)S(1)}, bf16[256,5120]{1,0:T(8,128)(2,1)}, u32[]{:S(2)}) copy-start(bf16[256,5120]{1,0:T(8,128)(2,1)} %q.3) | copy-start | bytes 7864324
  11.1 4.8 %collective-permute-start.6 = (bf16[2,320,128]{2,1,0:T(8,128)(2,1)S(1)}, bf16[2,320,128]{2,1,0:T(8,128)(2,1)S(1)}, u32[]{:S(2)}, u32[]{:S(2)}) collective-permute-start(bf16[2,320,128]{2,1,0:T(8,128)(2,1)S(1)} %pad_maximum_fusion.3), channel_id=1, source_target_pairs={{0,16},{16,0},{1,17},{17,1},{2,18},{18,2},{3,19},{19,3},{4,20},{20... | collective-permute-start | bytes 491528 | tf_op jit(solution)/shard_map/ppermute | solution.py:308
  12.4 6.4 %collective-permute-start.5 = (bf16[2,320,128]{2,1,0:T(8,128)(2,1)S(1)}, bf16[2,320,128]{2,1,0:T(8,128)(2,1)S(1)}, u32[]{:S(2)}, u32[]{:S(2)}) collective-permute-start(bf16[2,320,128]{2,1,0:T(8,128)(2,1)S(1)} %pad_maximum_fusion.3), channel_id=1, source_target_pairs={{0,4},{1,5},{2,6},{3,7},{4,0},{5,1},{6,2},{7,3},{8,12},{9,13},{10,... | collective-permute-start | bytes 491528 | tf_op jit(solution)/shard_map/ppermute | solution.py:305
  13.6 8.2 %collective-permute-start.4 = (bf16[2,320,128]{2,1,0:T(8,128)(2,1)S(1)}, bf16[2,320,128]{2,1,0:T(8,128)(2,1)S(1)}, u32[]{:S(2)}, u32[]{:S(2)}) collective-permute-start(bf16[2,320,128]{2,1,0:T(8,128)(2,1)S(1)} %pad_maximum_fusion.3), channel_id=1, source_target_pairs={{0,8},{1,9},{2,10},{3,11},{4,12},{5,13},{6,14},{7,15},{8,0},{9,1},... | collective-permute-start | bytes 491528 | tf_op jit(solution)/shard_map/ppermute | solution.py:305
  16.0 14.2 %collective-permute-start.8 = (bf16[2,64,5120]{2,1,0:T(8,128)(2,1)S(1)}, bf16[2,64,5120]{2,1,0:T(8,128)(2,1)S(1)}, u32[]{:S(2)}, u32[]{:S(2)}) collective-permute-start(bf16[2,64,5120]{2,1,0:T(8,128)(2,1)S(1)} %pad_maximum_fusion.1), channel_id=1, source_target_pairs={{0,1},{1,0},{2,3},{3,2},{4,5},{5,4},{6,7},{7,6},{8,9},{9,8},{10,11... | collective-permute-start | bytes 3932168 | tf_op jit(solution)/shard_map/ppermute | solution.py:305
  21.8 10.3 %collective-permute-start.7 = (bf16[2,320,128]{2,1,0:T(8,128)(2,1)S(1)}, bf16[2,320,128]{2,1,0:T(8,128)(2,1)S(1)}, u32[]{:S(2)}, u32[]{:S(2)}) collective-permute-start(bf16[2,320,128]{2,1,0:T(8,128)(2,1)S(1)} %collective-permute-done.4), channel_id=1, source_target_pairs={{0,4},{1,5},{2,6},{3,7},{4,0},{5,1},{6,2},{7,3},{8,12},{9,13},{10,... | collective-permute-start | bytes 491528 | tf_op jit(solution)/shard_map/ppermute | solution.py:305
  21.9 11.5 %collective-permute-start.10 = (bf16[4,320,128]{2,1,0:T(8,128)(2,1)S(1)}, bf16[4,320,128]{2,1,0:T(8,128)(2,1)S(1)}, u32[]{:S(2)}, u32[]{:S(2)}) collective-permute-start(bf16[4,320,128]{2,1,0:T(8,128)(2,1)S(1)} %pad_maximum_fusion.2), channel_id=1, source_target_pairs={{0,16},{16,0},{1,17},{17,1},{2,18},{18,2},{3,19},{19,3},{4,20},{20... | collective-permute-start | bytes 983048 | tf_op jit(solution)/shard_map/ppermute | solution.py:308
  24.5 1.7 %copy-start = (bf16[256,5120]{1,0:T(8,128)(2,1)S(1)}, bf16[256,5120]{1,0:T(8,128)(2,1)}, u32[]{:S(2)}) copy-start(bf16[256,5120]{1,0:T(8,128)(2,1)} %k.3) | copy-start | bytes 7864324
  24.5 1.7 %copy-start.5 = (s32[256]{0:T(256)S(1)}, s32[256]{0:T(256)}, u32[]{:S(2)}) copy-start(s32[256]{0:T(256)} %lo_ref.3) | copy-start | bytes 3076
  24.5 1.7 %copy-start.6 = (s32[256]{0:T(256)S(1)}, s32[256]{0:T(256)}, u32[]{:S(2)}) copy-start(s32[256]{0:T(256)} %hi_ref.5) | copy-start | bytes 3076
  24.6 17.7 %collective-permute-start.2 = (bf16[2,64,5120]{2,1,0:T(8,128)(2,1)S(1)}, bf16[2,64,5120]{2,1,0:T(8,128)(2,1)S(1)}, u32[]{:S(2)}, u32[]{:S(2)}) collective-permute-start(bf16[2,64,5120]{2,1,0:T(8,128)(2,1)S(1)} %pad_maximum_fusion), channel_id=1, source_target_pairs={{3,4},{4,3},{7,8},{8,7},{11,12},{12,11},{19,20},{20,19},{23,24},{2... | collective-permute-start | bytes 3932168 | tf_op jit(solution)/shard_map/ppermute | solution.py:340
  30.2 8.4 %copy-start.3 = (bf16[320,5120]{1,0:T(8,128)(2,1)S(1)}, bf16[320,5120]{1,0:T(8,128)(2,1)}, u32[]{:S(2)}) copy-start(bf16[320,5120]{1,0:T(8,128)(2,1)} %frozen.1) | copy-start | bytes 9830404
  32.1 6.5 %copy-start.4 = (bf16[320,128]{1,0:T(8,128)(2,1)S(1)}, bf16[320,128]{1,0:T(8,128)(2,1)}, u32[]{:S(2)}) copy-start(bf16[320,128]{1,0:T(8,128)(2,1)} %own_down.1) | copy-start | bytes 245764
  32.2 4.2 %collective-permute-start.11 = (bf16[2,320,128]{2,1,0:T(8,128)(2,1)S(1)}, bf16[2,320,128]{2,1,0:T(8,128)(2,1)S(1)}, u32[]{:S(2)}, u32[]{:S(2)}) collective-permute-start(bf16[2,320,128]{2,1,0:T(8,128)(2,1)S(1)} %collective-permute-done.7), channel_id=1, source_target_pairs={{0,16},{16,0},{1,17},{17,1},{2,18},{18,2},{3,19},{19,3},{4,20},{20... | collective-permute-start | bytes 491528 | tf_op jit(solution)/shard_map/ppermute | solution.py:308
  33.5 3.0 %collective-permute-start.9 = (bf16[8,320,128]{2,1,0:T(8,128)(2,1)S(1)}, bf16[8,320,128]{2,1,0:T(8,128)(2,1)S(1)}, u32[]{:S(2)}, u32[]{:S(2)}) collective-permute-start(bf16[8,320,128]{2,1,0:T(8,128)(2,1)S(1)} %constant_dynamic-update-slice_fusion.rest_0_), channel_id=1, source_target_pairs={{0,1},{1,0},{2,3},{3,2},{4,5},{5,4},{6,7},{7,6},{8,9},{9,8},{10,11... | collective-permute-start | bytes 1966088 | tf_op jit(solution)/shard_map/ppermute | solution.py:305
  36.4 2.2 %collective-permute-start.12 = (bf16[8,320,128]{2,1,0:T(8,128)(2,1)S(1)}, bf16[8,320,128]{2,1,0:T(8,128)(2,1)S(1)}, u32[]{:S(2)}, u32[]{:S(2)}) collective-permute-start(bf16[8,320,128]{2,1,0:T(8,128)(2,1)S(1)} %constant_dynamic-update-slice_fusion.4.rest_2_), channel_id=1, source_target_pairs={{0,1},{1,0},{2,3},{3,2},{4,5},{5,4},{6,7},{7,6},{8,9},{9,8},{10,11... | collective-permute-start | bytes 1966088 | tf_op jit(solution)/shard_map/ppermute | solution.py:305

commit v11 on v10

--- a/solution.py
+++ b/solution.py
@@ -192,11 +192,10 @@
     rows = result.shape[0]
     me = lax.axis_index("seq")
     kind = lax.axis_index("group")
-    for ref, (swapped, masks) in zip(refs, layout):
-        target = 1 - kind if swapped else kind
-        for i, mask in enumerate(masks):
+    for ref, cells in zip(refs, layout):
+        for i, (swapped, mask) in enumerate(cells):
             at = pl.ds(pl.multiple_of((me ^ mask) * shard, shard), shard)
-            factors[target, at, :] = ref[i]
+            factors[1 - kind if swapped else kind, at, :] = ref[i]
     if not layout:
         factors[...] = refs[0][...]
     down, up = factors.at[0], factors.at[1]
@@ -326,28 +325,37 @@
         barrier = lax.optimization_barrier
         join = jnp.concatenate
         side, short, long = steps
-        own = jnp.where(lax.axis_index("group") == 0, down, up)[None]
+        own = join([down, up])[None]
+        first = lax.axis_index("group") == 0
+        shard = down.shape[0]
+        direct = send(far_rim, direct_pairs)
         plane = join([own, swap(own, side)])
-        direct = send(far_rim, direct_pairs)
         plane, near_rim = barrier((plane, near_rim))
         halo = swap(near_rim, 1)
+        halves = plane[:, :shard], plane[:, shard:]
+        plane = jnp.where(first, *halves)
+        crossed = [jnp.where(first, *halves[::-1])]
         beyond = swap(plane, long)
         beside = swap(plane, short)
-        crossed = [cross(plane)]
-        beyond, beside, crossed = barrier((beyond, beside, crossed))
-        far_rim, direct, lo_later = barrier((far_rim, direct, lo))
+        inner = inner_attention(lo, hi, q, k, v)
+        beyond, beside, inner = barrier((beyond, beside, inner))
+        far_rim, direct, lo_near = barrier((far_rim, direct, lo))
         last = swap(beyond, short)
         distant = lax.ppermute(jnp.stack(far_rim), "seq", distant_pairs)
         crossed.append(cross(join([beside, beyond])))
-        inner = inner_attention(lo_later, hi, q, k, v)
-        near = near_attention(lo_later, hi, q, k, v, halo)
-        last, inner, near = barrier((last, inner, near))
+        near = near_attention(lo, hi, q, k, v, halo)
+        last, crossed[1], near = barrier((last, crossed[1], near))
         crossed.append(cross(last))
-        cells, other = join([plane, beside, beyond, last]), join(crossed)
-        masks = [a ^ b for a in (0, short, long, short ^ long) for b in (0, side)]
-        across = [mask ^ 1 for mask in masks]
-        layout = [(0, masks), (0, across), (1, masks), (1, across)]
-        pieces = [cells, swap(cells, 1), other, swap(other, 1)]
+        masks = [a ^ b for a in (0, short, long) for b in (0, side)]
+        late_masks = [short ^ long ^ b for b in (0, side)]
+        early = join([plane, beside, beyond, *crossed[:2]])
+        late = join([last, crossed[2]])
+        pieces = [early, swap(early, 1), late, swap(late, 1)]
+        layout = [
+            [(kind, mask ^ core) for kind in (0, 1) for mask in group]
+            for group in (masks, late_masks)
+            for core in (0, 1)
+        ]
     merged, attended, factors = merge(frozen, down, inner, near, layout, pieces)
     attended = far_rows(lo, hi, q, k, v, direct, distant, factors, attended)
     return (attended, merged)

time: 46.3 us -> 53.2 us (1.15)
  local copies, waits for them, and re-layouts: 2.49 us -> 6.95 us
  waiting for transfers between devices: 13 us -> 8.55 us
  other arithmetic: 1.24 us -> 4.87 us
  starting transfers between devices: 15.2 us -> 17.5 us
    ppermute x7, waiting for transfers between devices: 7.95 us -> 1.27 us  [swap(): return lax.ppermute(cells, 'seq', [(i, i ^ mask) for i in range(count)])]
    ppermute x3 -> x2, waiting for transfers between devices: 2.85 us -> 7.27 us  [cross(): return lax.ppermute(cells, 'group', [(0, 1), (1, 0)])]
    ppermute x7, starting transfers between devices: 5.89 us -> 8.69 us  [swap(): return lax.ppermute(cells, 'seq', [(i, i ^ mask) for i in range(count)])]
    unnamed x19 -> x23, local copies, waits for them, and re-layouts: 0.83 us -> 3.57 us
    ppermute x2, waiting for transfers between devices: 2.16 us -> 0.01 us  [send(): return [lax.ppermute(x, 'seq', pairs) for x in cells]]
    another operation x2, local copies, waits for them, and re-layouts: 1.61 us -> 3.31 us  [body(): near_rim = jnp.stack(rim((1 - odd) * (rows - FRAME)))]
    another operation x1, other arithmetic: 0.12 us -> 1.56 us  [body(): distant = lax.ppermute(jnp.stack(far_rim), 'seq', distant_pairs)]
    another operation x1, other arithmetic: 0.12 us -> 1.17 us  [body(): near_rim = jnp.stack(rim((1 - odd) * (rows - FRAME)))]
  transfers between devices with their start and end apart: 13 -> 12, of which waited for: 5 -> 3; matrix products, arithmetic and copies ran while one was open for 4% -> 14% of each run, Pallas kernels for 21% -> 18%
where the time goes in v11:
time: 53.2 us; the launch traced here: 52.4 us
  starting transfers between devices  17.5 us (33%)
  Pallas kernels  13.7 us (26%)
  waiting for transfers between devices  8.55 us (16%)
  local copies, waits for them, and re-layouts  6.95 us (13%)
  other arithmetic  4.87 us (9%)
  between operations  0.86 us (2%)
    ppermute x7, starting transfers between devices, swap(): return lax.ppermute(cells, 'seq', [(i, i ^ mask) for i in range(count)])  8.69 us
    ppermute x2, waiting for transfers between devices, cross(): return lax.ppermute(cells, 'group', [(0, 1), (1, 0)])  7.27 us
    ppermute x2, starting transfers between devices, send(): return [lax.ppermute(x, 'seq', pairs) for x in cells]  5.54 us
    pallas_call x1, Pallas kernels, far_rows(): pl.pallas_call(far_kernel, out_shape=jax.ShapeDtypeStruct((rows, width),...  4.22 us
    pallas_call x1, Pallas kernels, inner_attention(): pl.pallas_call(inner_kernel, grid=(width // WIDE,), out_shape=jax.ShapeDt...  3.92 us
    pallas_call x1, Pallas kernels, merge(): pl.pallas_call(functools.partial(merge_kernel, layout), out_shape=(jax.Sh...  3.63 us
    unnamed x23, local copies, waits for them, and re-layouts  3.57 us
    another operation x2, local copies, waits for them, and re-layouts, body(): near_rim = jnp.stack(rim((1 - odd) * (rows - FRAME)))  3.31 us
  transfers between devices with their start and end apart: 12, of which 3 were waited for; matrix products, arithmetic and copies ran while one was open for 14% of the time, Pallas kernels for 18%

profile of v11, /device:TPU:1, one launch (start us, length us, event | category | flops | bytes accessed | tf_op | source)
XLA Modules:
  0.0 52.4 jit_solution(7232647204217348316)
XLA Ops:
  0.6 0.9 %maximum_bitcast_fusion = bf16[1,640,128]{2,1,0:T(8,128)(2,1)S(1)} fusion(bf16[320,128]{1,0:T(8,128)(2,1)} %bitcast.9, bf16[320,128]{1,0:T(8,128)(2,1)} %own_down.1), kind=kLoop, calls=%fused_computation.6 | loop fusion | flops 327680 | bytes 327680 | tf_op jit(solution)/shard_map/broadcast_in_dim | solution.py:328
  1.6 2.1 %collective-permute-start.3 = (bf16[1,640,128]{2,1,0:T(8,128)(2,1)S(1)}, bf16[1,640,128]{2,1,0:T(8,128)(2,1)}, u32[]{:S(2)}, u32[]{:S(2)}) collective-permute-start(bf16[1,640,128]{2,1,0:T(8,128)(2,1)S(1)} %maximum_bitcast_fusion), channel_id=1, source_target_pairs={{0,2},{1,3},{2,0},{3,1},{4,6},{5,7},{6,4},{7,5},{8,10},{9,11},{10,... | collective-permute-start | bytes 491528 | tf_op jit(solution)/shard_map/ppermute | solution.py:304
  3.7 2.4 %dynamic-slice_bitcast_fusion = (bf16[1,64,5120]{2,1,0:T(8,128)(2,1)S(1)}, bf16[64,5120]{1,0:T(8,128)(2,1)}) fusion(bf16[256,5120]{1,0:T(8,128)(2,1)} %v.3, s32[]{:T(128)S(6)} %select_n.22, s32[]{:T(128)S(6)} %select_n.20), kind=kLoop, calls=%fused_computation.2 | loop fusion | bytes 2621448 | tf_op jit(solution)/shard_map/stack | solution.py:314
  6.1 2.5 %collective-permute-start.1 = (bf16[64,5120]{1,0:T(8,128)(2,1)}, bf16[64,5120]{1,0:T(8,128)(2,1)S(1)}, u32[]{:S(2)}, u32[]{:S(2)}) collective-permute-start(bf16[64,5120]{1,0:T(8,128)(2,1)} %get-tuple-element.20), channel_id=1, source_target_pairs={{1,2},{2,1},{5,6},{6,5},{9,10},{10,9},{13,14},{14,13},{17,18},{18,... | collective-permute-start | bytes 1966088 | tf_op jit(solution)/shard_map/ppermute | solution.py:301
  8.6 0.0 copy-done
  8.6 0.9 %dynamic-slice_bitcast_fusion.1 = (bf16[1,64,5120]{2,1,0:T(8,128)(2,1)S(1)}, bf16[64,5120]{1,0:T(8,128)(2,1)}) fusion(bf16[256,5120]{1,0:T(8,128)(2,1)S(1)} %copy-done, s32[]{:T(128)S(6)} %select_n.22, s32[]{:T(128)S(6)} %select_n.20), kind=kLoop, calls=%fused_computation.3 | loop fusion | bytes 2621448 | tf_op jit(solution)/shard_map/stack | solution.py:314
  9.5 3.0 %collective-permute-start = (bf16[64,5120]{1,0:T(8,128)(2,1)}, bf16[64,5120]{1,0:T(8,128)(2,1)}, u32[]{:S(2)}, u32[]{:S(2)}) collective-permute-start(bf16[64,5120]{1,0:T(8,128)(2,1)} %get-tuple-element.19), channel_id=1, source_target_pairs={{1,2},{2,1},{5,6},{6,5},{9,10},{10,9},{13,14},{14,13},{17,18},{18,... | collective-permute-start | bytes 1966088 | tf_op jit(solution)/shard_map/ppermute | solution.py:301
  12.6 1.2 %pad_maximum_fusion.1 = bf16[2,64,5120]{2,1,0:T(8,128)(2,1)} fusion(bf16[1,64,5120]{2,1,0:T(8,128)(2,1)S(1)} %get-tuple-element.36, bf16[1,64,5120]{2,1,0:T(8,128)(2,1)S(1)} %get-tuple-element.34), kind=kLoop, calls=%fused_computation.1 | loop fusion | flops 655360 | bytes 2621440 | tf_op jit(solution)/shard_map/stack | solution.py:314
  13.8 0.0 collective-permute-done.3
  13.8 1.1 %pad_maximum_fusion.2 = bf16[2,640,128]{2,1,0:T(8,128)(2,1)S(1)} fusion(bf16[1,640,128]{2,1,0:T(8,128)(2,1)} %collective-permute-done.3, bf16[1,640,128]{2,1,0:T(8,128)(2,1)S(1)} %maximum_bitcast_fusion), kind=kLoop, calls=%fused_computation.4 | loop fusion | flops 163840 | bytes 655360 | tf_op jit(solution)/shard_map/concatenate | solution.py:332
  14.9 2.4 %collective-permute-start.4 = (bf16[2,320,128]{2,1,0:T(8,128)(2,1)S(1)}, bf16[2,320,128]{2,1,0:T(8,128)(2,1)S(1)}, u32[]{:S(2)}, u32[]{:S(2)}) collective-permute-start(bf16[2,320,128]{2,1,0:T(8,128)(2,1)S(1)} %get-tuple-element.33), channel_id=1, source_target_pairs={{0,8},{1,9},{2,10},{3,11},{4,12},{5,13},{6,14},{7,15},{8,0},{9,1},... | collective-permute-start | bytes 491528 | tf_op jit(solution)/shard_map/ppermute | solution.py:304
  17.3 1.3 %collective-permute-start.5 = (bf16[2,320,128]{2,1,0:T(8,128)(2,1)S(1)}, bf16[2,320,128]{2,1,0:T(8,128)(2,1)S(1)}, u32[]{:S(2)}, u32[]{:S(2)}) collective-permute-start(bf16[2,320,128]{2,1,0:T(8,128)(2,1)S(1)} %get-tuple-element.33), channel_id=1, source_target_pairs={{0,4},{1,5},{2,6},{3,7},{4,0},{5,1},{6,2},{7,3},{8,12},{9,13},{10,... | collective-permute-start | bytes 491528 | tf_op jit(solution)/shard_map/ppermute | solution.py:304
  18.6 0.0 copy-done.9
  18.6 0.0 collective-permute-start.8
  18.6 0.0 copy-done.7
  18.6 0.0 copy-done.8
  18.6 0.0 copy-start.1
  18.6 1.7 %copy-done.1 = bf16[256,5120]{1,0:T(8,128)(2,1)S(1)} copy-done((bf16[256,5120]{1,0:T(8,128)(2,1)S(1)}, bf16[256,5120]{1,0:T(8,128)(2,1)}, u32[]{:S(2)}) %copy-start.1) | copy-done | bytes 2621464
  20.3 1.7 %copy-done.3 = bf16[256,5120]{1,0:T(8,128)(2,1)S(1)} copy-done((bf16[256,5120]{1,0:T(8,128)(2,1)S(1)}, bf16[256,5120]{1,0:T(8,128)(2,1)}, u32[]{:S(2)}) %copy-start.3) | copy-done | bytes 2621464
  22.1 3.9 %inner_attention.1.inner = bf16[128,5120]{1,0:T(8,128)(2,1)S(1)} custom-call(s32[256]{0:T(256)S(1)} %copy-done.7, s32[256]{0:T(256)S(1)} %copy-done.8, bf16[256,5120]{1,0:T(8,128)(2,1)S(1)} %copy-done.3, bf16[256,5120]{1,0:T(8,128)(2,1)S(1)} %copy-done, bf16[256,5120]{1,0:T(8,128)(2,1)S(1)} %copy-done.1), custom_call_target="tpu_custom_call" | custom-call | flops 1342177280 | bytes 9175040 | tf_op jit(solution)/shard_map/inner_attention/pallas_call | solution.py:90
  26.0 0.0 collective-permute-done.4
  26.0 0.0 collective-permute-done.5
  26.0 0.2 collective-permute-start.6
  26.3 1.3 %collective-permute-start.7 = (bf16[4,320,128]{2,1,0:T(8,128)(2,1)S(1)}, bf16[4,320,128]{2,1,0:T(8,128)(2,1)S(1)}, u32[]{:S(2)}, u32[]{:S(2)}) collective-permute-start(bf16[4,320,128]{2,1,0:T(8,128)(2,1)S(1)} %pad_maximum_fusion.3), channel_id=1, source_target_pairs={{0,16},{16,0},{1,17},{17,1},{2,18},{18,2},{3,19},{19,3},{4,20},{20... | collective-permute-start | bytes 983048 | tf_op jit(solution)/shard_map/ppermute | solution.py:307
  27.6 0.0 collective-permute-done.1.rest_1_
  27.6 0.0 collective-permute-done.rest_0_
  27.6 0.0 copy-start.2
  27.6 1.6 %pad_maximum_fusion = bf16[2,64,5120]{2,1,0:T(8,128)(2,1)S(1)} fusion(bf16[1,64,5120]{2,1,0:T(8,128)(2,1)} %bitcast.1, bf16[1,64,5120]{2,1,0:T(8,128)(2,1)} %bitcast), kind=kLoop, calls=%fused_computation | loop fusion | flops 655360 | bytes 2621440 | tf_op jit(solution)/shard_map/stack | solution.py:344
  29.2 0.7 %collective-permute-start.2 = (bf16[2,64,5120]{2,1,0:T(8,128)(2,1)S(1)}, bf16[2,64,5120]{2,1,0:T(8,128)(2,1)S(1)}, u32[]{:S(2)}, u32[]{:S(2)}) collective-permute-start(bf16[2,64,5120]{2,1,0:T(8,128)(2,1)S(1)} %pad_maximum_fusion), channel_id=1, source_target_pairs={{3,4},{4,3},{7,8},{8,7},{11,12},{12,11},{19,20},{20,19},{23,24},{2... | collective-permute-start | bytes 3932168 | tf_op jit(solution)/shard_map/ppermute | solution.py:344
  29.9 0.1 select_dynamic-update-slice_fusion
  30.0 0.0 collective-permute-done.8.halo
  30.0 0.0 copy-done.4
  30.0 0.0 copy-done.2
  30.1 0.0 copy-start.5
  30.1 2.0 %near_edge_attention.1.near = bf16[64,5120]{1,0:T(8,128)(2,1)S(1)} custom-call(s32[256]{0:T(256)S(1)} %copy-done.7, s32[256]{0:T(256)S(1)} %copy-done.8, bf16[256,5120]{1,0:T(8,128)(2,1)S(1)} %copy-done.4, bf16[256,5120]{1,0:T(8,128)(2,1)S(1)} %copy-done, bf16[256,5120]{1,0:T(8,128)(2,1)S(1)} %copy-done.2, bf16[2,64,5120]{2,1,0:T(8,128)(2,1)S(1)} %collective-permute-done.8.halo), custom_call_target="tpu_custom_call" | custom-call | flops 671088640 | bytes 9175040 | tf_op jit(solution)/shard_map/near_edge_attention/pallas_call | solution.py:173
  32.0 0.0 copy-start.6
  32.0 0.0 collective-permute-done.6
  32.1 2.7 %collective-permute-done.7 = bf16[4,320,128]{2,1,0:T(8,128)(2,1)S(1)} collective-permute-done((bf16[4,320,128]{2,1,0:T(8,128)(2,1)S(1)}, bf16[4,320,128]{2,1,0:T(8,128)(2,1)S(1)}, u32[]{:S(2)}, u32[]{:S(2)}) %collective-permute-start.7) | collective-permute-done | bytes 327712 | tf_op jit(solution)/shard_map/ppermute | solution.py:307
  34.8 1.7 %collective-permute-start.9 = (bf16[12,320,128]{2,1,0:T(8,128)(2,1)S(1)}, bf16[12,320,128]{2,1,0:T(8,128)(2,1)S(1)}, u32[]{:S(2)}, u32[]{:S(2)}) collective-permute-start(bf16[12,320,128]{2,1,0:T(8,128)(2,1)S(1)} %constant_dynamic-update-slice_fusion.rest_0_), channel_id=1, source_target_pairs={{0,1},{1,0},{2,3},{3,2},{4,5},{5,4},{6,7},{7,6},{8,9},{9,8},{10,11... | collective-permute-start | bytes 2949128 | tf_op jit(solution)/shard_map/ppermute | solution.py:304
  36.6 1.2 %collective-permute-start.10 = (bf16[2,320,128]{2,1,0:T(8,128)(2,1)S(1)}, bf16[2,320,128]{2,1,0:T(8,128)(2,1)S(1)}, u32[]{:S(2)}, u32[]{:S(2)}) collective-permute-start(bf16[2,320,128]{2,1,0:T(8,128)(2,1)S(1)} %collective-permute-done.6), channel_id=1, source_target_pairs={{0,16},{16,0},{1,17},{17,1},{2,18},{18,2},{3,19},{19,3},{4,20},{20... | collective-permute-start | bytes 491528 | tf_op jit(solution)/shard_map/ppermute | solution.py:307
  37.8 4.5 %collective-permute-done.10 = bf16[2,320,128]{2,1,0:T(8,128)(2,1)S(1)} collective-permute-done((bf16[2,320,128]{2,1,0:T(8,128)(2,1)S(1)}, bf16[2,320,128]{2,1,0:T(8,128)(2,1)S(1)}, u32[]{:S(2)}, u32[]{:S(2)}) %collective-permute-start.10) | collective-permute-done | bytes 163872 | tf_op jit(solution)/shard_map/ppermute | solution.py:307
  42.4 0.9 %collective-permute-start.11 = (bf16[4,320,128]{2,1,0:T(8,128)(2,1)S(1)}, bf16[4,320,128]{2,1,0:T(8,128)(2,1)S(1)}, u32[]{:S(2)}, u32[]{:S(2)}) collective-permute-start(bf16[4,320,128]{2,1,0:T(8,128)(2,1)S(1)} %constant_dynamic-update-slice_fusion.4.rest_2_), channel_id=1, source_target_pairs={{0,1},{1,0},{2,3},{3,2},{4,5},{5,4},{6,7},{7,6},{8,9},{9,8},{10,11... | collective-permute-start | bytes 983048 | tf_op jit(solution)/shard_map/ppermute | solution.py:304
  43.3 1.3 %collective-permute-done.11.rest_3_ = bf16[4,320,128]{2,1,0:T(8,128)(2,1)S(1)} collective-permute-done((bf16[4,320,128]{2,1,0:T(8,128)(2,1)S(1)}, bf16[4,320,128]{2,1,0:T(8,128)(2,1)S(1)}, u32[]{:S(2)}, u32[]{:S(2)}) %collective-permute-start.11) | collective-permute-done | bytes 327712 | tf_op jit(solution)/shard_map/ppermute | solution.py:304
  44.6 0.0 collective-permute-done.9.rest_1_
  44.6 0.0 copy-done.6
  44.6 3.6 %merge_and_adapter.1 = (bf16[320,5120]{1,0:T(8,128)(2,1)}, bf16[256,5120]{1,0:T(8,128)(2,1)}, bf16[2,5120,128]{2,1,0:T(8,128)(2,1)S(1)}) custom-call(bf16[320,5120]{1,0:T(8,128)(2,1)S(1)} %copy-done.5, bf16[320,128]{1,0:T(8,128)(2,1)S(1)} %copy-done.6, bf16[128,5120]{1,0:T(8,128)(2,1)S(1)} %inner_attention.1.inner, ...), custom_call_target="tpu_custom_call" | custom-call | flops 1090519040 | bytes 14417920 | tf_op jit(solution)/shard_map/merge_and_adapter/pallas_call | solution.py:228
  48.2 0.0 collective-permute-done.2.rest_2_
  48.2 4.2 %far_edge_rows.1 = bf16[256,5120]{1,0:T(8,128)(2,1)} custom-call(s32[256]{0:T(256)S(1)} %copy-done.7, s32[256]{0:T(256)S(1)} %copy-done.8, bf16[256,5120]{1,0:T(8,128)(2,1)S(1)} %copy-done.4, bf16[256,5120]{1,0:T(8,128)(2,1)S(1)} %copy-done, bf16[256,5120]{1,0:T(8,128)(2,1)S(1)} %copy-done.2, ...), custom_call_target="tpu_custom_call", output_to_operand_aliasing={{}: (9, {})} | custom-call | flops 671088640 | bytes 9175040 | tf_op jit(solution)/shard_map/far_edge_rows/pallas_call | solution.py:275
  (14 shorter events, 0.2 us)
Async XLA Ops:
  1.6 12.2 %collective-permute-start.3 = (bf16[1,640,128]{2,1,0:T(8,128)(2,1)S(1)}, bf16[1,640,128]{2,1,0:T(8,128)(2,1)}, u32[]{:S(2)}, u32[]{:S(2)}) collective-permute-start(bf16[1,640,128]{2,1,0:T(8,128)(2,1)S(1)} %maximum_bitcast_fusion), channel_id=1, source_target_pairs={{0,2},{1,3},{2,0},{3,1},{4,6},{5,7},{6,4},{7,5},{8,10},{9,11},{10,... | collective-permute-start | bytes 491528 | tf_op jit(solution)/shard_map/ppermute | solution.py:304
  3.7 4.9 %copy-start = (bf16[256,5120]{1,0:T(8,128)(2,1)S(1)}, bf16[256,5120]{1,0:T(8,128)(2,1)}, u32[]{:S(2)}) copy-start(bf16[256,5120]{1,0:T(8,128)(2,1)} %k.3) | copy-start | bytes 7864324
  6.1 21.5 %collective-permute-start.1 = (bf16[64,5120]{1,0:T(8,128)(2,1)}, bf16[64,5120]{1,0:T(8,128)(2,1)S(1)}, u32[]{:S(2)}, u32[]{:S(2)}) collective-permute-start(bf16[64,5120]{1,0:T(8,128)(2,1)} %get-tuple-element.20), channel_id=1, source_target_pairs={{1,2},{2,1},{5,6},{6,5},{9,10},{10,9},{13,14},{14,13},{17,18},{18,... | collective-permute-start | bytes 1966088 | tf_op jit(solution)/shard_map/ppermute | solution.py:301
  9.5 18.1 %collective-permute-start = (bf16[64,5120]{1,0:T(8,128)(2,1)}, bf16[64,5120]{1,0:T(8,128)(2,1)}, u32[]{:S(2)}, u32[]{:S(2)}) collective-permute-start(bf16[64,5120]{1,0:T(8,128)(2,1)} %get-tuple-element.19), channel_id=1, source_target_pairs={{1,2},{2,1},{5,6},{6,5},{9,10},{10,9},{13,14},{14,13},{17,18},{18,... | collective-permute-start | bytes 1966088 | tf_op jit(solution)/shard_map/ppermute | solution.py:301
  13.8 4.8 %copy-start.7 = (s32[256]{0:T(256)S(1)}, s32[256]{0:T(256)}, u32[]{:S(2)}) copy-start(s32[256]{0:T(256)} %lo_ref.5) | copy-start | bytes 3076
  13.8 4.8 %copy-start.8 = (s32[256]{0:T(256)S(1)}, s32[256]{0:T(256)}, u32[]{:S(2)}) copy-start(s32[256]{0:T(256)} %hi_ref.5) | copy-start | bytes 3076
  13.8 4.8 %copy-start.9 = (bf16[2,64,5120]{2,1,0:T(8,128)(2,1)S(1)}, bf16[2,64,5120]{2,1,0:T(8,128)(2,1)}, u32[]{:S(2)}) copy-start(bf16[2,64,5120]{2,1,0:T(8,128)(2,1)} %pad_maximum_fusion.1) | copy-start | bytes 3932164
  14.9 11.1 %collective-permute-start.4 = (bf16[2,320,128]{2,1,0:T(8,128)(2,1)S(1)}, bf16[2,320,128]{2,1,0:T(8,128)(2,1)S(1)}, u32[]{:S(2)}, u32[]{:S(2)}) collective-permute-start(bf16[2,320,128]{2,1,0:T(8,128)(2,1)S(1)} %get-tuple-element.33), channel_id=1, source_target_pairs={{0,8},{1,9},{2,10},{3,11},{4,12},{5,13},{6,14},{7,15},{8,0},{9,1},... | collective-permute-start | bytes 491528 | tf_op jit(solution)/shard_map/ppermute | solution.py:304
  17.3 8.7 %collective-permute-start.5 = (bf16[2,320,128]{2,1,0:T(8,128)(2,1)S(1)}, bf16[2,320,128]{2,1,0:T(8,128)(2,1)S(1)}, u32[]{:S(2)}, u32[]{:S(2)}) collective-permute-start(bf16[2,320,128]{2,1,0:T(8,128)(2,1)S(1)} %get-tuple-element.33), channel_id=1, source_target_pairs={{0,4},{1,5},{2,6},{3,7},{4,0},{5,1},{6,2},{7,3},{8,12},{9,13},{10,... | collective-permute-start | bytes 491528 | tf_op jit(solution)/shard_map/ppermute | solution.py:304
  18.6 11.5 %collective-permute-start.8 = (bf16[2,64,5120]{2,1,0:T(8,128)(2,1)S(1)}, bf16[2,64,5120]{2,1,0:T(8,128)(2,1)S(1)}, u32[]{:S(2)}, u32[]{:S(2)}) collective-permute-start(bf16[2,64,5120]{2,1,0:T(8,128)(2,1)S(1)} %copy-done.9), channel_id=1, source_target_pairs={{0,1},{1,0},{2,3},{3,2},{4,5},{5,4},{6,7},{7,6},{8,9},{9,8},{10,11... | collective-permute-start | bytes 3932168 | tf_op jit(solution)/shard_map/ppermute | solution.py:304
  18.6 1.7 %copy-start.1 = (bf16[256,5120]{1,0:T(8,128)(2,1)S(1)}, bf16[256,5120]{1,0:T(8,128)(2,1)}, u32[]{:S(2)}) copy-start(bf16[256,5120]{1,0:T(8,128)(2,1)} %v.3) | copy-start | bytes 7864324
  20.3 1.7 %copy-start.3 = (bf16[256,5120]{1,0:T(8,128)(2,1)S(1)}, bf16[256,5120]{1,0:T(8,128)(2,1)}, u32[]{:S(2)}) copy-start(bf16[256,5120]{1,0:T(8,128)(2,1)} %q.3) | copy-start | bytes 7864324
  22.1 8.0 %copy-start.4 = (bf16[256,5120]{1,0:T(8,128)(2,1)S(1)}, bf16[256,5120]{1,0:T(8,128)(2,1)}, u32[]{:S(2)}) copy-start(bf16[256,5120]{1,0:T(8,128)(2,1)} %q.3) | copy-start | bytes 7864324
  26.0 6.0 %collective-permute-start.6 = (bf16[2,320,128]{2,1,0:T(8,128)(2,1)S(1)}, bf16[2,320,128]{2,1,0:T(8,128)(2,1)S(1)}, u32[]{:S(2)}, u32[]{:S(2)}) collective-permute-start(bf16[2,320,128]{2,1,0:T(8,128)(2,1)S(1)} %collective-permute-done.4), channel_id=1, source_target_pairs={{0,4},{1,5},{2,6},{3,7},{4,0},{5,1},{6,2},{7,3},{8,12},{9,13},{10,... | collective-permute-start | bytes 491528 | tf_op jit(solution)/shard_map/ppermute | solution.py:304
  26.3 8.5 %collective-permute-start.7 = (bf16[4,320,128]{2,1,0:T(8,128)(2,1)S(1)}, bf16[4,320,128]{2,1,0:T(8,128)(2,1)S(1)}, u32[]{:S(2)}, u32[]{:S(2)}) collective-permute-start(bf16[4,320,128]{2,1,0:T(8,128)(2,1)S(1)} %pad_maximum_fusion.3), channel_id=1, source_target_pairs={{0,16},{16,0},{1,17},{17,1},{2,18},{18,2},{3,19},{19,3},{4,20},{20... | collective-permute-start | bytes 983048 | tf_op jit(solution)/shard_map/ppermute | solution.py:307
  27.6 2.4 %copy-start.2 = (bf16[256,5120]{1,0:T(8,128)(2,1)S(1)}, bf16[256,5120]{1,0:T(8,128)(2,1)}, u32[]{:S(2)}) copy-start(bf16[256,5120]{1,0:T(8,128)(2,1)} %v.3) | copy-start | bytes 7864324
  29.2 19.0 %collective-permute-start.2 = (bf16[2,64,5120]{2,1,0:T(8,128)(2,1)S(1)}, bf16[2,64,5120]{2,1,0:T(8,128)(2,1)S(1)}, u32[]{:S(2)}, u32[]{:S(2)}) collective-permute-start(bf16[2,64,5120]{2,1,0:T(8,128)(2,1)S(1)} %pad_maximum_fusion), channel_id=1, source_target_pairs={{3,4},{4,3},{7,8},{8,7},{11,12},{12,11},{19,20},{20,19},{23,24},{2... | collective-permute-start | bytes 3932168 | tf_op jit(solution)/shard_map/ppermute | solution.py:344
  30.1 14.5 %copy-start.5 = (bf16[320,5120]{1,0:T(8,128)(2,1)S(1)}, bf16[320,5120]{1,0:T(8,128)(2,1)}, u32[]{:S(2)}) copy-start(bf16[320,5120]{1,0:T(8,128)(2,1)} %frozen.1) | copy-start | bytes 9830404
  32.0 12.5 %copy-start.6 = (bf16[320,128]{1,0:T(8,128)(2,1)S(1)}, bf16[320,128]{1,0:T(8,128)(2,1)}, u32[]{:S(2)}) copy-start(bf16[320,128]{1,0:T(8,128)(2,1)} %own_down.1) | copy-start | bytes 245764
  34.8 9.7 %collective-permute-start.9 = (bf16[12,320,128]{2,1,0:T(8,128)(2,1)S(1)}, bf16[12,320,128]{2,1,0:T(8,128)(2,1)S(1)}, u32[]{:S(2)}, u32[]{:S(2)}) collective-permute-start(bf16[12,320,128]{2,1,0:T(8,128)(2,1)S(1)} %constant_dynamic-update-slice_fusion.rest_0_), channel_id=1, source_target_pairs={{0,1},{1,0},{2,3},{3,2},{4,5},{5,4},{6,7},{7,6},{8,9},{9,8},{10,11... | collective-permute-start | bytes 2949128 | tf_op jit(solution)/shard_map/ppermute | solution.py:304
  36.6 5.8 %collective-permute-start.10 = (bf16[2,320,128]{2,1,0:T(8,128)(2,1)S(1)}, bf16[2,320,128]{2,1,0:T(8,128)(2,1)S(1)}, u32[]{:S(2)}, u32[]{:S(2)}) collective-permute-start(bf16[2,320,128]{2,1,0:T(8,128)(2,1)S(1)} %collective-permute-done.6), channel_id=1, source_target_pairs={{0,16},{16,0},{1,17},{17,1},{2,18},{18,2},{3,19},{19,3},{4,20},{20... | collective-permute-start | bytes 491528 | tf_op jit(solution)/shard_map/ppermute | solution.py:307
  42.4 2.2 %collective-permute-start.11 = (bf16[4,320,128]{2,1,0:T(8,128)(2,1)S(1)}, bf16[4,320,128]{2,1,0:T(8,128)(2,1)S(1)}, u32[]{:S(2)}, u32[]{:S(2)}) collective-permute-start(bf16[4,320,128]{2,1,0:T(8,128)(2,1)S(1)} %constant_dynamic-update-slice_fusion.4.rest_2_), channel_id=1, source_target_pairs={{0,1},{1,0},{2,3},{3,2},{4,5},{5,4},{6,7},{7,6},{8,9},{9,8},{10,11... | collective-permute-start | bytes 983048 | tf_op jit(solution)/shard_map/ppermute | solution.py:304

commit v12 on v11

--- a/solution.py
+++ b/solution.py
@@ -93,7 +93,7 @@
         out_shape=jax.ShapeDtypeStruct((NEAR, width), BF16),
         in_specs=[SMEM, SMEM, block, block, block],
         out_specs=pl.BlockSpec((NEAR, WIDE), lambda i: (0, i)),
-        compiler_params=pltpu.CompilerParams(vmem_limit_bytes=16 << 20),
+        compiler_params=pltpu.CompilerParams(vmem_limit_bytes=6 << 20),
         cost_estimate=pl.CostEstimate(
             flops=16 * NEAR * NEAR * width,
             bytes_accessed=7 * rows * width,
@@ -175,7 +175,7 @@
         out_shape=jax.ShapeDtypeStruct((FRAME, width), BF16),
         in_specs=[SMEM, SMEM] + [VMEM] * 4,
         out_specs=VMEM,
-        compiler_params=pltpu.CompilerParams(vmem_limit_bytes=20 << 20),
+        compiler_params=pltpu.CompilerParams(vmem_limit_bytes=13 << 20),
         cost_estimate=edge_cost(rows, width),
         name="near_edge_attention",
     )(lo, hi, q, k, v, halo)
@@ -239,7 +239,7 @@
             pltpu.VMEM((rows, width), BF16),
             pltpu.SemaphoreType.DMA((3 * (width // CHUNK),)),
         ],
-        compiler_params=pltpu.CompilerParams(vmem_limit_bytes=24 << 20),
+        compiler_params=pltpu.CompilerParams(vmem_limit_bytes=18 << 20),
         cost_estimate=pl.CostEstimate(
             flops=2 * (shard + 2 * rows) * width * rank,
             bytes_accessed=4 * (shard + rows) * width + 4 * width * rank,
@@ -283,7 +283,7 @@
             pltpu.VMEM((FRAME, width), BF16),
             pltpu.SemaphoreType.DMA((width // WIDE,)),
         ],
-        compiler_params=pltpu.CompilerParams(vmem_limit_bytes=24 << 20),
+        compiler_params=pltpu.CompilerParams(vmem_limit_bytes=18 << 20),
         cost_estimate=edge_cost(rows, width),
         name="far_edge_rows",
     )(lo, hi, q, k, v, *direct, distant, factors, attended)

time: 53.2 us -> 53.2 us (level)
  no operation moved by 1% of the time
where the time goes in v12:
time: 53.2 us; the launch traced here: 52.4 us
  starting transfers between devices  17.5 us (33%)
  Pallas kernels  13.7 us (26%)
  waiting for transfers between devices  8.56 us (16%)
  local copies, waits for them, and re-layouts  6.95 us (13%)
  other arithmetic  4.87 us (9%)
  between operations  0.86 us (2%)
    ppermute x7, starting transfers between devices, swap(): return lax.ppermute(cells, 'seq', [(i, i ^ mask) for i in range(count)])  8.69 us
    ppermute x2, waiting for transfers between devices, cross(): return lax.ppermute(cells, 'group', [(0, 1), (1, 0)])  7.28 us
    ppermute x2, starting transfers between devices, send(): return [lax.ppermute(x, 'seq', pairs) for x in cells]  5.54 us
    pallas_call x1, Pallas kernels, far_rows(): pl.pallas_call(far_kernel, out_shape=jax.ShapeDtypeStruct((rows, width),...  4.22 us
    pallas_call x1, Pallas kernels, inner_attention(): pl.pallas_call(inner_kernel, grid=(width // WIDE,), out_shape=jax.ShapeDt...  3.92 us
    pallas_call x1, Pallas kernels, merge(): pl.pallas_call(functools.partial(merge_kernel, layout), out_shape=(jax.Sh...  3.63 us
    unnamed x23, local copies, waits for them, and re-layouts  3.57 us
    another operation x2, local copies, waits for them, and re-layouts, body(): near_rim = jnp.stack(rim((1 - odd) * (rows - FRAME)))  3.31 us
  transfers between devices with their start and end apart: 12, of which 3 were waited for; matrix products, arithmetic and copies ran while one was open for 14% of the time, Pallas kernels for 18%

profile of v12, /device:TPU:1, one launch (start us, length us, event | category | flops | bytes accessed | tf_op | source)
XLA Modules:
  0.0 52.4 jit_solution(16661087309945735467)
XLA Ops:
  0.6 0.9 %maximum_bitcast_fusion = bf16[1,640,128]{2,1,0:T(8,128)(2,1)S(1)} fusion(bf16[320,128]{1,0:T(8,128)(2,1)} %bitcast.9, bf16[320,128]{1,0:T(8,128)(2,1)} %own_down.1), kind=kLoop, calls=%fused_computation.6 | loop fusion | flops 327680 | bytes 327680 | tf_op jit(solution)/shard_map/broadcast_in_dim | solution.py:328
  1.6 2.1 %collective-permute-start.3 = (bf16[1,640,128]{2,1,0:T(8,128)(2,1)S(1)}, bf16[1,640,128]{2,1,0:T(8,128)(2,1)}, u32[]{:S(2)}, u32[]{:S(2)}) collective-permute-start(bf16[1,640,128]{2,1,0:T(8,128)(2,1)S(1)} %maximum_bitcast_fusion), channel_id=1, source_target_pairs={{0,2},{1,3},{2,0},{3,1},{4,6},{5,7},{6,4},{7,5},{8,10},{9,11},{10,... | collective-permute-start | bytes 491528 | tf_op jit(solution)/shard_map/ppermute | solution.py:304
  3.7 2.4 %dynamic-slice_bitcast_fusion = (bf16[1,64,5120]{2,1,0:T(8,128)(2,1)S(1)}, bf16[64,5120]{1,0:T(8,128)(2,1)}) fusion(bf16[256,5120]{1,0:T(8,128)(2,1)} %v.3, s32[]{:T(128)S(6)} %select_n.22, s32[]{:T(128)S(6)} %select_n.20), kind=kLoop, calls=%fused_computation.2 | loop fusion | bytes 2621448 | tf_op jit(solution)/shard_map/stack | solution.py:314
  6.1 2.5 %collective-permute-start.1 = (bf16[64,5120]{1,0:T(8,128)(2,1)}, bf16[64,5120]{1,0:T(8,128)(2,1)S(1)}, u32[]{:S(2)}, u32[]{:S(2)}) collective-permute-start(bf16[64,5120]{1,0:T(8,128)(2,1)} %get-tuple-element.20), channel_id=1, source_target_pairs={{1,2},{2,1},{5,6},{6,5},{9,10},{10,9},{13,14},{14,13},{17,18},{18,... | collective-permute-start | bytes 1966088 | tf_op jit(solution)/shard_map/ppermute | solution.py:301
  8.6 0.0 copy-done
  8.6 0.9 %dynamic-slice_bitcast_fusion.1 = (bf16[1,64,5120]{2,1,0:T(8,128)(2,1)S(1)}, bf16[64,5120]{1,0:T(8,128)(2,1)}) fusion(bf16[256,5120]{1,0:T(8,128)(2,1)S(1)} %copy-done, s32[]{:T(128)S(6)} %select_n.22, s32[]{:T(128)S(6)} %select_n.20), kind=kLoop, calls=%fused_computation.3 | loop fusion | bytes 2621448 | tf_op jit(solution)/shard_map/stack | solution.py:314
  9.5 3.0 %collective-permute-start = (bf16[64,5120]{1,0:T(8,128)(2,1)}, bf16[64,5120]{1,0:T(8,128)(2,1)}, u32[]{:S(2)}, u32[]{:S(2)}) collective-permute-start(bf16[64,5120]{1,0:T(8,128)(2,1)} %get-tuple-element.19), channel_id=1, source_target_pairs={{1,2},{2,1},{5,6},{6,5},{9,10},{10,9},{13,14},{14,13},{17,18},{18,... | collective-permute-start | bytes 1966088 | tf_op jit(solution)/shard_map/ppermute | solution.py:301
  12.6 1.2 %pad_maximum_fusion.1 = bf16[2,64,5120]{2,1,0:T(8,128)(2,1)} fusion(bf16[1,64,5120]{2,1,0:T(8,128)(2,1)S(1)} %get-tuple-element.36, bf16[1,64,5120]{2,1,0:T(8,128)(2,1)S(1)} %get-tuple-element.34), kind=kLoop, calls=%fused_computation.1 | loop fusion | flops 655360 | bytes 2621440 | tf_op jit(solution)/shard_map/stack | solution.py:314
  13.8 0.0 collective-permute-done.3
  13.8 1.1 %pad_maximum_fusion.2 = bf16[2,640,128]{2,1,0:T(8,128)(2,1)S(1)} fusion(bf16[1,640,128]{2,1,0:T(8,128)(2,1)} %collective-permute-done.3, bf16[1,640,128]{2,1,0:T(8,128)(2,1)S(1)} %maximum_bitcast_fusion), kind=kLoop, calls=%fused_computation.4 | loop fusion | flops 163840 | bytes 655360 | tf_op jit(solution)/shard_map/concatenate | solution.py:332
  14.9 2.4 %collective-permute-start.4 = (bf16[2,320,128]{2,1,0:T(8,128)(2,1)S(1)}, bf16[2,320,128]{2,1,0:T(8,128)(2,1)S(1)}, u32[]{:S(2)}, u32[]{:S(2)}) collective-permute-start(bf16[2,320,128]{2,1,0:T(8,128)(2,1)S(1)} %get-tuple-element.33), channel_id=1, source_target_pairs={{0,8},{1,9},{2,10},{3,11},{4,12},{5,13},{6,14},{7,15},{8,0},{9,1},... | collective-permute-start | bytes 491528 | tf_op jit(solution)/shard_map/ppermute | solution.py:304
  17.3 1.3 %collective-permute-start.5 = (bf16[2,320,128]{2,1,0:T(8,128)(2,1)S(1)}, bf16[2,320,128]{2,1,0:T(8,128)(2,1)S(1)}, u32[]{:S(2)}, u32[]{:S(2)}) collective-permute-start(bf16[2,320,128]{2,1,0:T(8,128)(2,1)S(1)} %get-tuple-element.33), channel_id=1, source_target_pairs={{0,4},{1,5},{2,6},{3,7},{4,0},{5,1},{6,2},{7,3},{8,12},{9,13},{10,... | collective-permute-start | bytes 491528 | tf_op jit(solution)/shard_map/ppermute | solution.py:304
  18.6 0.0 copy-done.9
  18.6 0.0 collective-permute-start.8
  18.6 0.0 copy-done.7
  18.6 0.0 copy-done.8
  18.6 0.0 copy-start.1
  18.6 1.7 %copy-done.1 = bf16[256,5120]{1,0:T(8,128)(2,1)S(1)} copy-done((bf16[256,5120]{1,0:T(8,128)(2,1)S(1)}, bf16[256,5120]{1,0:T(8,128)(2,1)}, u32[]{:S(2)}) %copy-start.1) | copy-done | bytes 2621464
  20.3 1.7 %copy-done.3 = bf16[256,5120]{1,0:T(8,128)(2,1)S(1)} copy-done((bf16[256,5120]{1,0:T(8,128)(2,1)S(1)}, bf16[256,5120]{1,0:T(8,128)(2,1)}, u32[]{:S(2)}) %copy-start.3) | copy-done | bytes 2621464
  22.1 3.9 %inner_attention.1.inner = bf16[128,5120]{1,0:T(8,128)(2,1)S(1)} custom-call(s32[256]{0:T(256)S(1)} %copy-done.7, s32[256]{0:T(256)S(1)} %copy-done.8, bf16[256,5120]{1,0:T(8,128)(2,1)S(1)} %copy-done.3, bf16[256,5120]{1,0:T(8,128)(2,1)S(1)} %copy-done, bf16[256,5120]{1,0:T(8,128)(2,1)S(1)} %copy-done.1), custom_call_target="tpu_custom_call" | custom-call | flops 1342177280 | bytes 9175040 | tf_op jit(solution)/shard_map/inner_attention/pallas_call | solution.py:90
  26.0 0.0 collective-permute-done.4
  26.0 0.0 collective-permute-done.5
  26.0 0.2 collective-permute-start.6
  26.3 1.3 %collective-permute-start.7 = (bf16[4,320,128]{2,1,0:T(8,128)(2,1)S(1)}, bf16[4,320,128]{2,1,0:T(8,128)(2,1)S(1)}, u32[]{:S(2)}, u32[]{:S(2)}) collective-permute-start(bf16[4,320,128]{2,1,0:T(8,128)(2,1)S(1)} %pad_maximum_fusion.3), channel_id=1, source_target_pairs={{0,16},{16,0},{1,17},{17,1},{2,18},{18,2},{3,19},{19,3},{4,20},{20... | collective-permute-start | bytes 983048 | tf_op jit(solution)/shard_map/ppermute | solution.py:307
  27.6 0.0 collective-permute-done.1.rest_1_
  27.6 0.0 collective-permute-done.rest_0_
  27.6 0.0 copy-start.2
  27.6 1.6 %pad_maximum_fusion = bf16[2,64,5120]{2,1,0:T(8,128)(2,1)S(1)} fusion(bf16[1,64,5120]{2,1,0:T(8,128)(2,1)} %bitcast.1, bf16[1,64,5120]{2,1,0:T(8,128)(2,1)} %bitcast), kind=kLoop, calls=%fused_computation | loop fusion | flops 655360 | bytes 2621440 | tf_op jit(solution)/shard_map/stack | solution.py:344
  29.2 0.7 %collective-permute-start.2 = (bf16[2,64,5120]{2,1,0:T(8,128)(2,1)S(1)}, bf16[2,64,5120]{2,1,0:T(8,128)(2,1)S(1)}, u32[]{:S(2)}, u32[]{:S(2)}) collective-permute-start(bf16[2,64,5120]{2,1,0:T(8,128)(2,1)S(1)} %pad_maximum_fusion), channel_id=1, source_target_pairs={{3,4},{4,3},{7,8},{8,7},{11,12},{12,11},{19,20},{20,19},{23,24},{2... | collective-permute-start | bytes 3932168 | tf_op jit(solution)/shard_map/ppermute | solution.py:344
  29.9 0.1 select_dynamic-update-slice_fusion
  30.0 0.0 collective-permute-done.8.halo
  30.0 0.0 copy-done.4
  30.0 0.0 copy-done.2
  30.0 0.0 copy-start.5
  30.1 2.0 %near_edge_attention.1.near = bf16[64,5120]{1,0:T(8,128)(2,1)S(1)} custom-call(s32[256]{0:T(256)S(1)} %copy-done.7, s32[256]{0:T(256)S(1)} %copy-done.8, bf16[256,5120]{1,0:T(8,128)(2,1)S(1)} %copy-done.4, bf16[256,5120]{1,0:T(8,128)(2,1)S(1)} %copy-done, bf16[256,5120]{1,0:T(8,128)(2,1)S(1)} %copy-done.2, bf16[2,64,5120]{2,1,0:T(8,128)(2,1)S(1)} %collective-permute-done.8.halo), custom_call_target="tpu_custom_call" | custom-call | flops 671088640 | bytes 9175040 | tf_op jit(solution)/shard_map/near_edge_attention/pallas_call | solution.py:173
  32.0 0.0 copy-start.6
  32.0 0.0 collective-permute-done.6
  32.0 2.7 %collective-permute-done.7 = bf16[4,320,128]{2,1,0:T(8,128)(2,1)S(1)} collective-permute-done((bf16[4,320,128]{2,1,0:T(8,128)(2,1)S(1)}, bf16[4,320,128]{2,1,0:T(8,128)(2,1)S(1)}, u32[]{:S(2)}, u32[]{:S(2)}) %collective-permute-start.7) | collective-permute-done | bytes 327712 | tf_op jit(solution)/shard_map/ppermute | solution.py:307
  34.8 1.7 %collective-permute-start.9 = (bf16[12,320,128]{2,1,0:T(8,128)(2,1)S(1)}, bf16[12,320,128]{2,1,0:T(8,128)(2,1)S(1)}, u32[]{:S(2)}, u32[]{:S(2)}) collective-permute-start(bf16[12,320,128]{2,1,0:T(8,128)(2,1)S(1)} %constant_dynamic-update-slice_fusion.rest_0_), channel_id=1, source_target_pairs={{0,1},{1,0},{2,3},{3,2},{4,5},{5,4},{6,7},{7,6},{8,9},{9,8},{10,11... | collective-permute-start | bytes 2949128 | tf_op jit(solution)/shard_map/ppermute | solution.py:304
  36.6 1.2 %collective-permute-start.10 = (bf16[2,320,128]{2,1,0:T(8,128)(2,1)S(1)}, bf16[2,320,128]{2,1,0:T(8,128)(2,1)S(1)}, u32[]{:S(2)}, u32[]{:S(2)}) collective-permute-start(bf16[2,320,128]{2,1,0:T(8,128)(2,1)S(1)} %collective-permute-done.6), channel_id=1, source_target_pairs={{0,16},{16,0},{1,17},{17,1},{2,18},{18,2},{3,19},{19,3},{4,20},{20... | collective-permute-start | bytes 491528 | tf_op jit(solution)/shard_map/ppermute | solution.py:307
  37.8 4.5 %collective-permute-done.10 = bf16[2,320,128]{2,1,0:T(8,128)(2,1)S(1)} collective-permute-done((bf16[2,320,128]{2,1,0:T(8,128)(2,1)S(1)}, bf16[2,320,128]{2,1,0:T(8,128)(2,1)S(1)}, u32[]{:S(2)}, u32[]{:S(2)}) %collective-permute-start.10) | collective-permute-done | bytes 163872 | tf_op jit(solution)/shard_map/ppermute | solution.py:307
  42.4 0.9 %collective-permute-start.11 = (bf16[4,320,128]{2,1,0:T(8,128)(2,1)S(1)}, bf16[4,320,128]{2,1,0:T(8,128)(2,1)S(1)}, u32[]{:S(2)}, u32[]{:S(2)}) collective-permute-start(bf16[4,320,128]{2,1,0:T(8,128)(2,1)S(1)} %constant_dynamic-update-slice_fusion.4.rest_2_), channel_id=1, source_target_pairs={{0,1},{1,0},{2,3},{3,2},{4,5},{5,4},{6,7},{7,6},{8,9},{9,8},{10,11... | collective-permute-start | bytes 983048 | tf_op jit(solution)/shard_map/ppermute | solution.py:304
  43.3 1.3 %collective-permute-done.11.rest_3_ = bf16[4,320,128]{2,1,0:T(8,128)(2,1)S(1)} collective-permute-done((bf16[4,320,128]{2,1,0:T(8,128)(2,1)S(1)}, bf16[4,320,128]{2,1,0:T(8,128)(2,1)S(1)}, u32[]{:S(2)}, u32[]{:S(2)}) %collective-permute-start.11) | collective-permute-done | bytes 327712 | tf_op jit(solution)/shard_map/ppermute | solution.py:304
  44.6 0.0 collective-permute-done.9.rest_1_
  44.6 0.0 copy-done.6
  44.6 3.6 %merge_and_adapter.1 = (bf16[320,5120]{1,0:T(8,128)(2,1)}, bf16[256,5120]{1,0:T(8,128)(2,1)}, bf16[2,5120,128]{2,1,0:T(8,128)(2,1)S(1)}) custom-call(bf16[320,5120]{1,0:T(8,128)(2,1)S(1)} %copy-done.5, bf16[320,128]{1,0:T(8,128)(2,1)S(1)} %copy-done.6, bf16[128,5120]{1,0:T(8,128)(2,1)S(1)} %inner_attention.1.inner, ...), custom_call_target="tpu_custom_call" | custom-call | flops 1090519040 | bytes 14417920 | tf_op jit(solution)/shard_map/merge_and_adapter/pallas_call | solution.py:228
  48.2 0.0 collective-permute-done.2.rest_2_
  48.2 4.2 %far_edge_rows.1 = bf16[256,5120]{1,0:T(8,128)(2,1)} custom-call(s32[256]{0:T(256)S(1)} %copy-done.7, s32[256]{0:T(256)S(1)} %copy-done.8, bf16[256,5120]{1,0:T(8,128)(2,1)S(1)} %copy-done.4, bf16[256,5120]{1,0:T(8,128)(2,1)S(1)} %copy-done, bf16[256,5120]{1,0:T(8,128)(2,1)S(1)} %copy-done.2, ...), custom_call_target="tpu_custom_call", output_to_operand_aliasing={{}: (9, {})} | custom-call | flops 671088640 | bytes 9175040 | tf_op jit(solution)/shard_map/far_edge_rows/pallas_call | solution.py:275
  (14 shorter events, 0.2 us)
Async XLA Ops:
  1.6 12.2 %collective-permute-start.3 = (bf16[1,640,128]{2,1,0:T(8,128)(2,1)S(1)}, bf16[1,640,128]{2,1,0:T(8,128)(2,1)}, u32[]{:S(2)}, u32[]{:S(2)}) collective-permute-start(bf16[1,640,128]{2,1,0:T(8,128)(2,1)S(1)} %maximum_bitcast_fusion), channel_id=1, source_target_pairs={{0,2},{1,3},{2,0},{3,1},{4,6},{5,7},{6,4},{7,5},{8,10},{9,11},{10,... | collective-permute-start | bytes 491528 | tf_op jit(solution)/shard_map/ppermute | solution.py:304
  3.7 4.9 %copy-start = (bf16[256,5120]{1,0:T(8,128)(2,1)S(1)}, bf16[256,5120]{1,0:T(8,128)(2,1)}, u32[]{:S(2)}) copy-start(bf16[256,5120]{1,0:T(8,128)(2,1)} %k.3) | copy-start | bytes 7864324
  6.1 21.5 %collective-permute-start.1 = (bf16[64,5120]{1,0:T(8,128)(2,1)}, bf16[64,5120]{1,0:T(8,128)(2,1)S(1)}, u32[]{:S(2)}, u32[]{:S(2)}) collective-permute-start(bf16[64,5120]{1,0:T(8,128)(2,1)} %get-tuple-element.20), channel_id=1, source_target_pairs={{1,2},{2,1},{5,6},{6,5},{9,10},{10,9},{13,14},{14,13},{17,18},{18,... | collective-permute-start | bytes 1966088 | tf_op jit(solution)/shard_map/ppermute | solution.py:301
  9.5 18.1 %collective-permute-start = (bf16[64,5120]{1,0:T(8,128)(2,1)}, bf16[64,5120]{1,0:T(8,128)(2,1)}, u32[]{:S(2)}, u32[]{:S(2)}) collective-permute-start(bf16[64,5120]{1,0:T(8,128)(2,1)} %get-tuple-element.19), channel_id=1, source_target_pairs={{1,2},{2,1},{5,6},{6,5},{9,10},{10,9},{13,14},{14,13},{17,18},{18,... | collective-permute-start | bytes 1966088 | tf_op jit(solution)/shard_map/ppermute | solution.py:301
  13.8 4.8 %copy-start.7 = (s32[256]{0:T(256)S(1)}, s32[256]{0:T(256)}, u32[]{:S(2)}) copy-start(s32[256]{0:T(256)} %lo_ref.5) | copy-start | bytes 3076
  13.8 4.8 %copy-start.8 = (s32[256]{0:T(256)S(1)}, s32[256]{0:T(256)}, u32[]{:S(2)}) copy-start(s32[256]{0:T(256)} %hi_ref.5) | copy-start | bytes 3076
  13.8 4.8 %copy-start.9 = (bf16[2,64,5120]{2,1,0:T(8,128)(2,1)S(1)}, bf16[2,64,5120]{2,1,0:T(8,128)(2,1)}, u32[]{:S(2)}) copy-start(bf16[2,64,5120]{2,1,0:T(8,128)(2,1)} %pad_maximum_fusion.1) | copy-start | bytes 3932164
  14.9 11.1 %collective-permute-start.4 = (bf16[2,320,128]{2,1,0:T(8,128)(2,1)S(1)}, bf16[2,320,128]{2,1,0:T(8,128)(2,1)S(1)}, u32[]{:S(2)}, u32[]{:S(2)}) collective-permute-start(bf16[2,320,128]{2,1,0:T(8,128)(2,1)S(1)} %get-tuple-element.33), channel_id=1, source_target_pairs={{0,8},{1,9},{2,10},{3,11},{4,12},{5,13},{6,14},{7,15},{8,0},{9,1},... | collective-permute-start | bytes 491528 | tf_op jit(solution)/shard_map/ppermute | solution.py:304
  17.3 8.7 %collective-permute-start.5 = (bf16[2,320,128]{2,1,0:T(8,128)(2,1)S(1)}, bf16[2,320,128]{2,1,0:T(8,128)(2,1)S(1)}, u32[]{:S(2)}, u32[]{:S(2)}) collective-permute-start(bf16[2,320,128]{2,1,0:T(8,128)(2,1)S(1)} %get-tuple-element.33), channel_id=1, source_target_pairs={{0,4},{1,5},{2,6},{3,7},{4,0},{5,1},{6,2},{7,3},{8,12},{9,13},{10,... | collective-permute-start | bytes 491528 | tf_op jit(solution)/shard_map/ppermute | solution.py:304
  18.6 11.5 %collective-permute-start.8 = (bf16[2,64,5120]{2,1,0:T(8,128)(2,1)S(1)}, bf16[2,64,5120]{2,1,0:T(8,128)(2,1)S(1)}, u32[]{:S(2)}, u32[]{:S(2)}) collective-permute-start(bf16[2,64,5120]{2,1,0:T(8,128)(2,1)S(1)} %copy-done.9), channel_id=1, source_target_pairs={{0,1},{1,0},{2,3},{3,2},{4,5},{5,4},{6,7},{7,6},{8,9},{9,8},{10,11... | collective-permute-start | bytes 3932168 | tf_op jit(solution)/shard_map/ppermute | solution.py:304
  18.6 1.7 %copy-start.1 = (bf16[256,5120]{1,0:T(8,128)(2,1)S(1)}, bf16[256,5120]{1,0:T(8,128)(2,1)}, u32[]{:S(2)}) copy-start(bf16[256,5120]{1,0:T(8,128)(2,1)} %v.3) | copy-start | bytes 7864324
  20.3 1.7 %copy-start.3 = (bf16[256,5120]{1,0:T(8,128)(2,1)S(1)}, bf16[256,5120]{1,0:T(8,128)(2,1)}, u32[]{:S(2)}) copy-start(bf16[256,5120]{1,0:T(8,128)(2,1)} %q.3) | copy-start | bytes 7864324
  22.1 8.0 %copy-start.4 = (bf16[256,5120]{1,0:T(8,128)(2,1)S(1)}, bf16[256,5120]{1,0:T(8,128)(2,1)}, u32[]{:S(2)}) copy-start(bf16[256,5120]{1,0:T(8,128)(2,1)} %q.3) | copy-start | bytes 7864324
  26.0 6.0 %collective-permute-start.6 = (bf16[2,320,128]{2,1,0:T(8,128)(2,1)S(1)}, bf16[2,320,128]{2,1,0:T(8,128)(2,1)S(1)}, u32[]{:S(2)}, u32[]{:S(2)}) collective-permute-start(bf16[2,320,128]{2,1,0:T(8,128)(2,1)S(1)} %collective-permute-done.4), channel_id=1, source_target_pairs={{0,4},{1,5},{2,6},{3,7},{4,0},{5,1},{6,2},{7,3},{8,12},{9,13},{10,... | collective-permute-start | bytes 491528 | tf_op jit(solution)/shard_map/ppermute | solution.py:304
  26.3 8.5 %collective-permute-start.7 = (bf16[4,320,128]{2,1,0:T(8,128)(2,1)S(1)}, bf16[4,320,128]{2,1,0:T(8,128)(2,1)S(1)}, u32[]{:S(2)}, u32[]{:S(2)}) collective-permute-start(bf16[4,320,128]{2,1,0:T(8,128)(2,1)S(1)} %pad_maximum_fusion.3), channel_id=1, source_target_pairs={{0,16},{16,0},{1,17},{17,1},{2,18},{18,2},{3,19},{19,3},{4,20},{20... | collective-permute-start | bytes 983048 | tf_op jit(solution)/shard_map/ppermute | solution.py:307
  27.6 2.4 %copy-start.2 = (bf16[256,5120]{1,0:T(8,128)(2,1)S(1)}, bf16[256,5120]{1,0:T(8,128)(2,1)}, u32[]{:S(2)}) copy-start(bf16[256,5120]{1,0:T(8,128)(2,1)} %v.3) | copy-start | bytes 7864324
  29.2 19.0 %collective-permute-start.2 = (bf16[2,64,5120]{2,1,0:T(8,128)(2,1)S(1)}, bf16[2,64,5120]{2,1,0:T(8,128)(2,1)S(1)}, u32[]{:S(2)}, u32[]{:S(2)}) collective-permute-start(bf16[2,64,5120]{2,1,0:T(8,128)(2,1)S(1)} %pad_maximum_fusion), channel_id=1, source_target_pairs={{3,4},{4,3},{7,8},{8,7},{11,12},{12,11},{19,20},{20,19},{23,24},{2... | collective-permute-start | bytes 3932168 | tf_op jit(solution)/shard_map/ppermute | solution.py:344
  30.0 14.5 %copy-start.5 = (bf16[320,5120]{1,0:T(8,128)(2,1)S(1)}, bf16[320,5120]{1,0:T(8,128)(2,1)}, u32[]{:S(2)}) copy-start(bf16[320,5120]{1,0:T(8,128)(2,1)} %frozen.1) | copy-start | bytes 9830404
  32.0 12.5 %copy-start.6 = (bf16[320,128]{1,0:T(8,128)(2,1)S(1)}, bf16[320,128]{1,0:T(8,128)(2,1)}, u32[]{:S(2)}) copy-start(bf16[320,128]{1,0:T(8,128)(2,1)} %own_down.1) | copy-start | bytes 245764
  34.8 9.7 %collective-permute-start.9 = (bf16[12,320,128]{2,1,0:T(8,128)(2,1)S(1)}, bf16[12,320,128]{2,1,0:T(8,128)(2,1)S(1)}, u32[]{:S(2)}, u32[]{:S(2)}) collective-permute-start(bf16[12,320,128]{2,1,0:T(8,128)(2,1)S(1)} %constant_dynamic-update-slice_fusion.rest_0_), channel_id=1, source_target_pairs={{0,1},{1,0},{2,3},{3,2},{4,5},{5,4},{6,7},{7,6},{8,9},{9,8},{10,11... | collective-permute-start | bytes 2949128 | tf_op jit(solution)/shard_map/ppermute | solution.py:304
  36.6 5.8 %collective-permute-start.10 = (bf16[2,320,128]{2,1,0:T(8,128)(2,1)S(1)}, bf16[2,320,128]{2,1,0:T(8,128)(2,1)S(1)}, u32[]{:S(2)}, u32[]{:S(2)}) collective-permute-start(bf16[2,320,128]{2,1,0:T(8,128)(2,1)S(1)} %collective-permute-done.6), channel_id=1, source_target_pairs={{0,16},{16,0},{1,17},{17,1},{2,18},{18,2},{3,19},{19,3},{4,20},{20... | collective-permute-start | bytes 491528 | tf_op jit(solution)/shard_map/ppermute | solution.py:307
  42.4 2.2 %collective-permute-start.11 = (bf16[4,320,128]{2,1,0:T(8,128)(2,1)S(1)}, bf16[4,320,128]{2,1,0:T(8,128)(2,1)S(1)}, u32[]{:S(2)}, u32[]{:S(2)}) collective-permute-start(bf16[4,320,128]{2,1,0:T(8,128)(2,1)S(1)} %constant_dynamic-update-slice_fusion.4.rest_2_), channel_id=1, source_target_pairs={{0,1},{1,0},{2,3},{3,2},{4,5},{5,4},{6,7},{7,6},{8,9},{9,8},{10,11... | collective-permute-start | bytes 983048 | tf_op jit(solution)/shard_map/ppermute | solution.py:304

commit v13 on v11

--- a/solution.py
+++ b/solution.py
@@ -337,19 +337,18 @@
         crossed = [jnp.where(first, *halves[::-1])]
         beyond = swap(plane, long)
         beside = swap(plane, short)
-        inner = inner_attention(lo, hi, q, k, v)
-        beyond, beside, inner = barrier((beyond, beside, inner))
-        far_rim, direct, lo_near = barrier((far_rim, direct, lo))
+        beyond, beside = barrier((beyond, beside))
         last = swap(beyond, short)
+        far_rim, direct, last, lo_near = barrier((far_rim, direct, last, lo))
         distant = lax.ppermute(jnp.stack(far_rim), "seq", distant_pairs)
         crossed.append(cross(join([beside, beyond])))
-        near = near_attention(lo, hi, q, k, v, halo)
-        last, crossed[1], near = barrier((last, crossed[1], near))
+        inner = inner_attention(lo_near, hi, q, k, v)
+        near = near_attention(lo_near, hi, q, k, v, halo)
         crossed.append(cross(last))
         masks = [a ^ b for a in (0, short, long) for b in (0, side)]
         late_masks = [short ^ long ^ b for b in (0, side)]
         early = join([plane, beside, beyond, *crossed[:2]])
-        late = join([last, crossed[2]])
+        late, inner, near = barrier((join([last, crossed[2]]), inner, near))
         pieces = [early, swap(early, 1), late, swap(late, 1)]
         layout = [
             [(kind, mask ^ core) for kind in (0, 1) for mask in group]

time: 53.2 us -> 54.4 us (1.023)
  the two profiles are of different devices: /device:TPU:1 before, /device:TPU:24 now
where the time goes in v13:
time: 54.4 us; the launch traced here: 54.1 us
  waiting for transfers between devices  19.1 us (35%)
  Pallas kernels  13.8 us (25%)
  starting transfers between devices  12.2 us (22%)
  other arithmetic  4.79 us (9%)
  local copies, waits for them, and re-layouts  3.45 us (6%)
  between operations  0.8 us (1%)
    ppermute x7, waiting for transfers between devices, swap(): return lax.ppermute(cells, 'seq', [(i, i ^ mask) for i in range(count)])  14.3 us
    ppermute x7, starting transfers between devices, swap(): return lax.ppermute(cells, 'seq', [(i, i ^ mask) for i in range(count)])  5.04 us
    pallas_call x1, Pallas kernels, far_rows(): pl.pallas_call(far_kernel, out_shape=jax.ShapeDtypeStruct((rows, width),...  4.23 us
    pallas_call x1, Pallas kernels, inner_attention(): pl.pallas_call(inner_kernel, grid=(width // WIDE,), out_shape=jax.ShapeDt...  3.93 us
    ppermute x1, waiting for transfers between devices, body(): distant = lax.ppermute(jnp.stack(far_rim), 'seq', distant_pairs)  3.66 us
    pallas_call x1, Pallas kernels, merge(): pl.pallas_call(functools.partial(merge_kernel, layout), out_shape=(jax.Sh...  3.65 us
    another operation x2, local copies, waits for them, and re-layouts, body(): near_rim = jnp.stack(rim((1 - odd) * (rows - FRAME)))  3.32 us
    ppermute x2, starting transfers between devices, cross(): return lax.ppermute(cells, 'group', [(0, 1), (1, 0)])  3.08 us
  transfers between devices with their start and end apart: 12, of which 7 were waited for; matrix products, arithmetic and copies ran while one was open for 13% of the time, Pallas kernels for 18%

profile of v13, /device:TPU:24, one launch (start us, length us, event | category | flops | bytes accessed | tf_op | source)
XLA Modules:
  0.0 54.1 jit_solution(15543888470128110274)
XLA Ops:
  0.6 0.9 %maximum_bitcast_fusion = bf16[1,640,128]{2,1,0:T(8,128)(2,1)S(1)} fusion(bf16[320,128]{1,0:T(8,128)(2,1)} %bitcast.9, bf16[320,128]{1,0:T(8,128)(2,1)} %own_down.1), kind=kLoop, calls=%fused_computation.7 | loop fusion | flops 327680 | bytes 327680 | tf_op jit(solution)/shard_map/broadcast_in_dim | solution.py:328
  1.6 1.6 %collective-permute-start.2 = (bf16[1,640,128]{2,1,0:T(8,128)(2,1)S(1)}, bf16[1,640,128]{2,1,0:T(8,128)(2,1)}, u32[]{:S(2)}, u32[]{:S(2)}) collective-permute-start(bf16[1,640,128]{2,1,0:T(8,128)(2,1)S(1)} %maximum_bitcast_fusion), channel_id=1, source_target_pairs={{0,2},{1,3},{2,0},{3,1},{4,6},{5,7},{6,4},{7,5},{8,10},{9,11},{10,... | collective-permute-start | bytes 491528 | tf_op jit(solution)/shard_map/ppermute | solution.py:304
  3.2 2.4 %dynamic-slice_bitcast_fusion.1 = (bf16[1,64,5120]{2,1,0:T(8,128)(2,1)S(1)}, bf16[64,5120]{1,0:T(8,128)(2,1)}) fusion(bf16[256,5120]{1,0:T(8,128)(2,1)} %k.3, s32[]{:T(128)S(6)} %select_n.22, s32[]{:T(128)S(6)} %select_n.20), kind=kLoop, calls=%fused_computation.3 | loop fusion | bytes 2621448 | tf_op jit(solution)/shard_map/stack | solution.py:314
  5.5 0.7 %collective-permute-start = (bf16[64,5120]{1,0:T(8,128)(2,1)}, bf16[64,5120]{1,0:T(8,128)(2,1)S(1)}, u32[]{:S(2)}, u32[]{:S(2)}) collective-permute-start(bf16[64,5120]{1,0:T(8,128)(2,1)} %get-tuple-element.22), channel_id=1, source_target_pairs={{1,2},{2,1},{5,6},{6,5},{9,10},{10,9},{13,14},{14,13},{17,18},{18,... | collective-permute-start | bytes 1966088 | tf_op jit(solution)/shard_map/ppermute | solution.py:301
  6.2 0.0 copy-done.1
  6.2 1.0 %dynamic-slice_bitcast_fusion = (bf16[1,64,5120]{2,1,0:T(8,128)(2,1)S(1)}, bf16[64,5120]{1,0:T(8,128)(2,1)}) fusion(bf16[256,5120]{1,0:T(8,128)(2,1)S(1)} %copy-done.1, s32[]{:T(128)S(6)} %select_n.22, s32[]{:T(128)S(6)} %select_n.20), kind=kLoop, calls=%fused_computation.2 | loop fusion | bytes 2621448 | tf_op jit(solution)/shard_map/stack | solution.py:314
  7.2 1.5 %collective-permute-start.1 = (bf16[64,5120]{1,0:T(8,128)(2,1)}, bf16[64,5120]{1,0:T(8,128)(2,1)}, u32[]{:S(2)}, u32[]{:S(2)}) collective-permute-start(bf16[64,5120]{1,0:T(8,128)(2,1)} %get-tuple-element.23), channel_id=1, source_target_pairs={{1,2},{2,1},{5,6},{6,5},{9,10},{10,9},{13,14},{14,13},{17,18},{18,... | collective-permute-start | bytes 1966088 | tf_op jit(solution)/shard_map/ppermute | solution.py:301
  8.7 1.2 %pad_maximum_fusion = bf16[2,64,5120]{2,1,0:T(8,128)(2,1)} fusion(bf16[1,64,5120]{2,1,0:T(8,128)(2,1)S(1)} %get-tuple-element.38, bf16[1,64,5120]{2,1,0:T(8,128)(2,1)S(1)} %get-tuple-element.36), kind=kLoop, calls=%fused_computation | loop fusion | flops 655360 | bytes 2621440 | tf_op jit(solution)/shard_map/stack | solution.py:314
  9.9 0.0 collective-permute-done.2
  9.9 0.9 %pad_maximum_fusion.2 = bf16[2,640,128]{2,1,0:T(8,128)(2,1)S(1)} fusion(bf16[1,640,128]{2,1,0:T(8,128)(2,1)} %collective-permute-done.2, bf16[1,640,128]{2,1,0:T(8,128)(2,1)S(1)} %maximum_bitcast_fusion), kind=kLoop, calls=%fused_computation.4 | loop fusion | flops 163840 | bytes 655360 | tf_op jit(solution)/shard_map/concatenate | solution.py:332
  10.8 0.0 copy-start.2
  10.9 0.5 collective-permute-start.4
  11.4 0.3 collective-permute-start.3
  11.7 2.4 %collective-permute-start.8 = (bf16[2,64,5120]{2,1,0:T(8,128)(2,1)}, bf16[2,64,5120]{2,1,0:T(8,128)(2,1)S(1)}, u32[]{:S(2)}, u32[]{:S(2)}) collective-permute-start(bf16[2,64,5120]{2,1,0:T(8,128)(2,1)} %pad_maximum_fusion), channel_id=1, source_target_pairs={{0,1},{1,0},{2,3},{3,2},{4,5},{5,4},{6,7},{7,6},{8,9},{9,8},{10,11... | collective-permute-start | bytes 3932168 | tf_op jit(solution)/shard_map/ppermute | solution.py:304
  14.1 3.9 %collective-permute-done.4 = bf16[2,320,128]{2,1,0:T(8,128)(2,1)S(1)} collective-permute-done((bf16[2,320,128]{2,1,0:T(8,128)(2,1)S(1)}, bf16[2,320,128]{2,1,0:T(8,128)(2,1)S(1)}, u32[]{:S(2)}, u32[]{:S(2)}) %collective-permute-start.4) | collective-permute-done | bytes 163872 | tf_op jit(solution)/shard_map/ppermute | solution.py:304
  18.0 3.6 %collective-permute-done.3 = bf16[2,320,128]{2,1,0:T(8,128)(2,1)S(1)} collective-permute-done((bf16[2,320,128]{2,1,0:T(8,128)(2,1)S(1)}, bf16[2,320,128]{2,1,0:T(8,128)(2,1)S(1)}, u32[]{:S(2)}, u32[]{:S(2)}) %collective-permute-start.3) | collective-permute-done | bytes 163872 | tf_op jit(solution)/shard_map/ppermute | solution.py:304
  21.6 0.0 collective-permute-start.5
  21.7 1.6 %collective-permute-start.9 = (bf16[4,320,128]{2,1,0:T(8,128)(2,1)S(1)}, bf16[4,320,128]{2,1,0:T(8,128)(2,1)S(1)}, u32[]{:S(2)}, u32[]{:S(2)}) collective-permute-start(bf16[4,320,128]{2,1,0:T(8,128)(2,1)S(1)} %pad_maximum_fusion.4), channel_id=1, source_target_pairs={{0,16},{16,0},{1,17},{17,1},{2,18},{18,2},{3,19},{19,3},{4,20},{20... | collective-permute-start | bytes 983048 | tf_op jit(solution)/shard_map/ppermute | solution.py:307
  23.2 5.2 %collective-permute-done.5 = bf16[2,320,128]{2,1,0:T(8,128)(2,1)S(1)} collective-permute-done((bf16[2,320,128]{2,1,0:T(8,128)(2,1)S(1)}, bf16[2,320,128]{2,1,0:T(8,128)(2,1)S(1)}, u32[]{:S(2)}, u32[]{:S(2)}) %collective-permute-start.5) | collective-permute-done | bytes 163872 | tf_op jit(solution)/shard_map/ppermute | solution.py:304
  28.5 0.0 collective-permute-done.rest_0_
  28.5 0.0 collective-permute-done.1.rest_1_
  28.5 0.0 copy-start
  28.5 0.0 copy-start.5
  28.5 0.0 copy-start.6
  28.5 1.6 %pad_maximum_fusion.1 = bf16[2,64,5120]{2,1,0:T(8,128)(2,1)S(1)} fusion(bf16[1,64,5120]{2,1,0:T(8,128)(2,1)} %bitcast.5, bf16[1,64,5120]{2,1,0:T(8,128)(2,1)} %bitcast.4), kind=kLoop, calls=%fused_computation.1 | loop fusion | flops 655360 | bytes 2621440 | tf_op jit(solution)/shard_map/stack | solution.py:343
  30.1 1.9 %collective-permute-start.6 = (bf16[2,64,5120]{2,1,0:T(8,128)(2,1)S(1)}, bf16[2,64,5120]{2,1,0:T(8,128)(2,1)S(1)}, u32[]{:S(2)}, u32[]{:S(2)}) collective-permute-start(bf16[2,64,5120]{2,1,0:T(8,128)(2,1)S(1)} %pad_maximum_fusion.1), channel_id=1, source_target_pairs={{3,4},{4,3},{7,8},{8,7},{11,12},{12,11},{19,20},{20,19},{23,24},{2... | collective-permute-start | bytes 3932168 | tf_op jit(solution)/shard_map/ppermute | solution.py:343
  32.0 0.1 select_dynamic-update-slice_fusion
  32.1 0.1 collective-permute-done.9
  32.2 0.2 collective-permute-start.10
  32.3 1.5 %collective-permute-start.7 = (bf16[2,320,128]{2,1,0:T(8,128)(2,1)S(1)}, bf16[2,320,128]{2,1,0:T(8,128)(2,1)S(1)}, u32[]{:S(2)}, u32[]{:S(2)}) collective-permute-start(bf16[2,320,128]{2,1,0:T(8,128)(2,1)S(1)} %collective-permute-done.5), channel_id=1, source_target_pairs={{0,16},{16,0},{1,17},{17,1},{2,18},{18,2},{3,19},{19,3},{4,20},{20... | collective-permute-start | bytes 491528 | tf_op jit(solution)/shard_map/ppermute | solution.py:307
  33.9 0.0 copy-done.2
  33.9 0.0 copy-done
  33.9 0.0 copy-done.5
  33.9 0.0 copy-done.6
  33.9 3.9 %inner_attention.1.inner = bf16[128,5120]{1,0:T(8,128)(2,1)S(1)} custom-call(s32[256]{0:T(256)S(1)} %copy-done.5, s32[256]{0:T(256)S(1)} %copy-done.6, bf16[256,5120]{1,0:T(8,128)(2,1)S(1)} %copy-done.2, bf16[256,5120]{1,0:T(8,128)(2,1)S(1)} %copy-done, bf16[256,5120]{1,0:T(8,128)(2,1)S(1)} %copy-done.1), custom_call_target="tpu_custom_call" | custom-call | flops 1342177280 | bytes 9175040 | tf_op jit(solution)/shard_map/inner_attention/pallas_call | solution.py:90
  37.8 1.0 %collective-permute-done.7 = bf16[2,320,128]{2,1,0:T(8,128)(2,1)S(1)} collective-permute-done((bf16[2,320,128]{2,1,0:T(8,128)(2,1)S(1)}, bf16[2,320,128]{2,1,0:T(8,128)(2,1)S(1)}, u32[]{:S(2)}, u32[]{:S(2)}) %collective-permute-start.7) | collective-permute-done | bytes 163872 | tf_op jit(solution)/shard_map/ppermute | solution.py:307
  38.9 0.0 copy-start.4
  38.9 0.0 collective-permute-done.8.halo
  38.9 0.0 copy-start.3
  38.9 2.0 %near_edge_attention.1.near = bf16[64,5120]{1,0:T(8,128)(2,1)S(1)} custom-call(s32[256]{0:T(256)S(1)} %copy-done.5, s32[256]{0:T(256)S(1)} %copy-done.6, bf16[256,5120]{1,0:T(8,128)(2,1)S(1)} %copy-done.2, bf16[256,5120]{1,0:T(8,128)(2,1)S(1)} %copy-done, bf16[256,5120]{1,0:T(8,128)(2,1)S(1)} %copy-done.1, bf16[2,64,5120]{2,1,0:T(8,128)(2,1)S(1)} %collective-permute-done.8.halo), custom_call_target="tpu_custom_call" | custom-call | flops 671088640 | bytes 9175040 | tf_op jit(solution)/shard_map/near_edge_attention/pallas_call | solution.py:173
  40.9 0.1 collective-permute-start.11
  41.0 0.0 collective-permute-done.10.rest_1_
  41.0 1.6 %collective-permute-done.11.rest_3_ = bf16[4,320,128]{2,1,0:T(8,128)(2,1)S(1)} collective-permute-done((bf16[4,320,128]{2,1,0:T(8,128)(2,1)S(1)}, bf16[4,320,128]{2,1,0:T(8,128)(2,1)S(1)}, u32[]{:S(2)}, u32[]{:S(2)}) %collective-permute-start.11) | collective-permute-done | bytes 327712 | tf_op jit(solution)/shard_map/ppermute | solution.py:304
  42.6 0.0 copy-done.4
  42.6 0.0 copy-done.3
  42.6 3.6 %merge_and_adapter.1 = (bf16[320,5120]{1,0:T(8,128)(2,1)}, bf16[256,5120]{1,0:T(8,128)(2,1)}, bf16[2,5120,128]{2,1,0:T(8,128)(2,1)S(1)}) custom-call(bf16[320,5120]{1,0:T(8,128)(2,1)S(1)} %copy-done.3, bf16[320,128]{1,0:T(8,128)(2,1)S(1)} %copy-done.4, bf16[128,5120]{1,0:T(8,128)(2,1)S(1)} %inner_attention.1.inner, ...), custom_call_target="tpu_custom_call" | custom-call | flops 1090519040 | bytes 14417920 | tf_op jit(solution)/shard_map/merge_and_adapter/pallas_call | solution.py:228
  46.2 3.7 %collective-permute-done.6.rest_2_ = bf16[2,64,5120]{2,1,0:T(8,128)(2,1)S(1)} collective-permute-done((bf16[2,64,5120]{2,1,0:T(8,128)(2,1)S(1)}, bf16[2,64,5120]{2,1,0:T(8,128)(2,1)S(1)}, u32[]{:S(2)}, u32[]{:S(2)}) %collective-permute-start.6) | collective-permute-done | bytes 1310752 | tf_op jit(solution)/shard_map/ppermute | solution.py:343
  49.9 4.2 %far_edge_rows.1 = bf16[256,5120]{1,0:T(8,128)(2,1)} custom-call(s32[256]{0:T(256)S(1)} %copy-done.5, s32[256]{0:T(256)S(1)} %copy-done.6, bf16[256,5120]{1,0:T(8,128)(2,1)S(1)} %copy-done.2, bf16[256,5120]{1,0:T(8,128)(2,1)S(1)} %copy-done, bf16[256,5120]{1,0:T(8,128)(2,1)S(1)} %copy-done.1, ...), custom_call_target="tpu_custom_call", output_to_operand_aliasing={{}: (9, {})} | custom-call | flops 671088640 | bytes 9175040 | tf_op jit(solution)/shard_map/far_edge_rows/pallas_call | solution.py:275
  (7 shorter events, 0.2 us)
Async XLA Ops:
  1.6 8.3 %collective-permute-start.2 = (bf16[1,640,128]{2,1,0:T(8,128)(2,1)S(1)}, bf16[1,640,128]{2,1,0:T(8,128)(2,1)}, u32[]{:S(2)}, u32[]{:S(2)}) collective-permute-start(bf16[1,640,128]{2,1,0:T(8,128)(2,1)S(1)} %maximum_bitcast_fusion), channel_id=1, source_target_pairs={{0,2},{1,3},{2,0},{3,1},{4,6},{5,7},{6,4},{7,5},{8,10},{9,11},{10,... | collective-permute-start | bytes 491528 | tf_op jit(solution)/shard_map/ppermute | solution.py:304
  3.2 3.1 %copy-start.1 = (bf16[256,5120]{1,0:T(8,128)(2,1)S(1)}, bf16[256,5120]{1,0:T(8,128)(2,1)}, u32[]{:S(2)}) copy-start(bf16[256,5120]{1,0:T(8,128)(2,1)} %v.3) | copy-start | bytes 7864324
  5.5 23.0 %collective-permute-start = (bf16[64,5120]{1,0:T(8,128)(2,1)}, bf16[64,5120]{1,0:T(8,128)(2,1)S(1)}, u32[]{:S(2)}, u32[]{:S(2)}) collective-permute-start(bf16[64,5120]{1,0:T(8,128)(2,1)} %get-tuple-element.22), channel_id=1, source_target_pairs={{1,2},{2,1},{5,6},{6,5},{9,10},{10,9},{13,14},{14,13},{17,18},{18,... | collective-permute-start | bytes 1966088 | tf_op jit(solution)/shard_map/ppermute | solution.py:301
  7.2 21.3 %collective-permute-start.1 = (bf16[64,5120]{1,0:T(8,128)(2,1)}, bf16[64,5120]{1,0:T(8,128)(2,1)}, u32[]{:S(2)}, u32[]{:S(2)}) collective-permute-start(bf16[64,5120]{1,0:T(8,128)(2,1)} %get-tuple-element.23), channel_id=1, source_target_pairs={{1,2},{2,1},{5,6},{6,5},{9,10},{10,9},{13,14},{14,13},{17,18},{18,... | collective-permute-start | bytes 1966088 | tf_op jit(solution)/shard_map/ppermute | solution.py:301
  10.8 23.1 %copy-start.2 = (bf16[256,5120]{1,0:T(8,128)(2,1)S(1)}, bf16[256,5120]{1,0:T(8,128)(2,1)}, u32[]{:S(2)}) copy-start(bf16[256,5120]{1,0:T(8,128)(2,1)} %q.3) | copy-start | bytes 7864324
  10.9 7.2 %collective-permute-start.4 = (bf16[2,320,128]{2,1,0:T(8,128)(2,1)S(1)}, bf16[2,320,128]{2,1,0:T(8,128)(2,1)S(1)}, u32[]{:S(2)}, u32[]{:S(2)}) collective-permute-start(bf16[2,320,128]{2,1,0:T(8,128)(2,1)S(1)} %get-tuple-element.35), channel_id=1, source_target_pairs={{0,4},{1,5},{2,6},{3,7},{4,0},{5,1},{6,2},{7,3},{8,12},{9,13},{10,... | collective-permute-start | bytes 491528 | tf_op jit(solution)/shard_map/ppermute | solution.py:304
  11.4 10.2 %collective-permute-start.3 = (bf16[2,320,128]{2,1,0:T(8,128)(2,1)S(1)}, bf16[2,320,128]{2,1,0:T(8,128)(2,1)S(1)}, u32[]{:S(2)}, u32[]{:S(2)}) collective-permute-start(bf16[2,320,128]{2,1,0:T(8,128)(2,1)S(1)} %get-tuple-element.35), channel_id=1, source_target_pairs={{0,8},{1,9},{2,10},{3,11},{4,12},{5,13},{6,14},{7,15},{8,0},{9,1},... | collective-permute-start | bytes 491528 | tf_op jit(solution)/shard_map/ppermute | solution.py:304
  11.7 27.2 %collective-permute-start.8 = (bf16[2,64,5120]{2,1,0:T(8,128)(2,1)}, bf16[2,64,5120]{2,1,0:T(8,128)(2,1)S(1)}, u32[]{:S(2)}, u32[]{:S(2)}) collective-permute-start(bf16[2,64,5120]{2,1,0:T(8,128)(2,1)} %pad_maximum_fusion), channel_id=1, source_target_pairs={{0,1},{1,0},{2,3},{3,2},{4,5},{5,4},{6,7},{7,6},{8,9},{9,8},{10,11... | collective-permute-start | bytes 3932168 | tf_op jit(solution)/shard_map/ppermute | solution.py:304
  21.6 6.9 %collective-permute-start.5 = (bf16[2,320,128]{2,1,0:T(8,128)(2,1)S(1)}, bf16[2,320,128]{2,1,0:T(8,128)(2,1)S(1)}, u32[]{:S(2)}, u32[]{:S(2)}) collective-permute-start(bf16[2,320,128]{2,1,0:T(8,128)(2,1)S(1)} %collective-permute-done.3), channel_id=1, source_target_pairs={{0,4},{1,5},{2,6},{3,7},{4,0},{5,1},{6,2},{7,3},{8,12},{9,13},{10,... | collective-permute-start | bytes 491528 | tf_op jit(solution)/shard_map/ppermute | solution.py:304
  21.7 10.5 %collective-permute-start.9 = (bf16[4,320,128]{2,1,0:T(8,128)(2,1)S(1)}, bf16[4,320,128]{2,1,0:T(8,128)(2,1)S(1)}, u32[]{:S(2)}, u32[]{:S(2)}) collective-permute-start(bf16[4,320,128]{2,1,0:T(8,128)(2,1)S(1)} %pad_maximum_fusion.4), channel_id=1, source_target_pairs={{0,16},{16,0},{1,17},{17,1},{2,18},{18,2},{3,19},{19,3},{4,20},{20... | collective-permute-start | bytes 983048 | tf_op jit(solution)/shard_map/ppermute | solution.py:307
  28.5 5.4 %copy-start = (bf16[256,5120]{1,0:T(8,128)(2,1)S(1)}, bf16[256,5120]{1,0:T(8,128)(2,1)}, u32[]{:S(2)}) copy-start(bf16[256,5120]{1,0:T(8,128)(2,1)} %k.3) | copy-start | bytes 7864324
  28.5 5.4 %copy-start.5 = (s32[256]{0:T(256)S(1)}, s32[256]{0:T(256)}, u32[]{:S(2)}) copy-start(s32[256]{0:T(256)} %lo_ref.3) | copy-start | bytes 3076
  28.5 5.4 %copy-start.6 = (s32[256]{0:T(256)S(1)}, s32[256]{0:T(256)}, u32[]{:S(2)}) copy-start(s32[256]{0:T(256)} %hi_ref.5) | copy-start | bytes 3076
  30.1 19.8 %collective-permute-start.6 = (bf16[2,64,5120]{2,1,0:T(8,128)(2,1)S(1)}, bf16[2,64,5120]{2,1,0:T(8,128)(2,1)S(1)}, u32[]{:S(2)}, u32[]{:S(2)}) collective-permute-start(bf16[2,64,5120]{2,1,0:T(8,128)(2,1)S(1)} %pad_maximum_fusion.1), channel_id=1, source_target_pairs={{3,4},{4,3},{7,8},{8,7},{11,12},{12,11},{19,20},{20,19},{23,24},{2... | collective-permute-start | bytes 3932168 | tf_op jit(solution)/shard_map/ppermute | solution.py:343
  32.2 8.8 %collective-permute-start.10 = (bf16[12,320,128]{2,1,0:T(8,128)(2,1)S(1)}, bf16[12,320,128]{2,1,0:T(8,128)(2,1)S(1)}, u32[]{:S(2)}, u32[]{:S(2)}) collective-permute-start(bf16[12,320,128]{2,1,0:T(8,128)(2,1)S(1)} %constant_dynamic-update-slice_fusion.rest_0_), channel_id=1, source_target_pairs={{0,1},{1,0},{2,3},{3,2},{4,5},{5,4},{6,7},{7,6},{8,9},{9,8},{10,11... | collective-permute-start | bytes 2949128 | tf_op jit(solution)/shard_map/ppermute | solution.py:304
  32.3 6.5 %collective-permute-start.7 = (bf16[2,320,128]{2,1,0:T(8,128)(2,1)S(1)}, bf16[2,320,128]{2,1,0:T(8,128)(2,1)S(1)}, u32[]{:S(2)}, u32[]{:S(2)}) collective-permute-start(bf16[2,320,128]{2,1,0:T(8,128)(2,1)S(1)} %collective-permute-done.5), channel_id=1, source_target_pairs={{0,16},{16,0},{1,17},{17,1},{2,18},{18,2},{3,19},{19,3},{4,20},{20... | collective-permute-start | bytes 491528 | tf_op jit(solution)/shard_map/ppermute | solution.py:307
  38.9 3.7 %copy-start.4 = (bf16[320,128]{1,0:T(8,128)(2,1)S(1)}, bf16[320,128]{1,0:T(8,128)(2,1)}, u32[]{:S(2)}) copy-start(bf16[320,128]{1,0:T(8,128)(2,1)} %own_down.1) | copy-start | bytes 245764
  38.9 3.7 %copy-start.3 = (bf16[320,5120]{1,0:T(8,128)(2,1)S(1)}, bf16[320,5120]{1,0:T(8,128)(2,1)}, u32[]{:S(2)}) copy-start(bf16[320,5120]{1,0:T(8,128)(2,1)} %frozen.1) | copy-start | bytes 9830404
  40.9 1.7 %collective-permute-start.11 = (bf16[4,320,128]{2,1,0:T(8,128)(2,1)S(1)}, bf16[4,320,128]{2,1,0:T(8,128)(2,1)S(1)}, u32[]{:S(2)}, u32[]{:S(2)}) collective-permute-start(bf16[4,320,128]{2,1,0:T(8,128)(2,1)S(1)} %pad_maximum_fusion.3.rest_2_), channel_id=1, source_target_pairs={{0,1},{1,0},{2,3},{3,2},{4,5},{5,4},{6,7},{7,6},{8,9},{9,8},{10,11... | collective-permute-start | bytes 983048 | tf_op jit(solution)/shard_map/ppermute | solution.py:304

commit v14 on v10

--- a/solution.py
+++ b/solution.py
@@ -136,10 +136,10 @@
 
     bias = clip_bias(lo, hi)
 
-    def step(i, _):
+    for i in range(pairs // unroll):
         loads, parts = [], []
         for pair in range(unroll):
-            part = pl.ds(pl.multiple_of((i * unroll + pair) * 2 * HD, 2 * HD), 2 * HD)
+            part = pl.ds((i * unroll + pair) * 2 * HD, 2 * HD)
             parts.append(part)
             loads.append(
                 (
@@ -151,9 +151,6 @@
             )
         for part, result in zip(parts, attend(loads)):
             out[:, part] = result
-        return 0
-
-    lax.fori_loop(0, pairs // unroll, step, 0)
 
 
 def near_kernel(lo_ref, hi_ref, q, k, v, halo, out):
@@ -209,8 +206,8 @@
         stores.append(pltpu.make_async_copy(source, target, sems.at[len(stores)]))
         stores[-1].start()
 
-    for first in range(0, width, CHUNK):
-        part = pl.ds(first, CHUNK)
+    for first in range(0, width, WIDE):
+        part = pl.ds(first, WIDE)
         factor = up[part, :]
         w[:, part] = adapt(frozen[:, part], own_down[...], factor)
         store(w.at[:, part], merged.at[:, part])

time: 46.3 us -> 45.3 us (0.978)
  Pallas kernels: 13.3 us -> 12.3 us
    pallas_call x1, Pallas kernels: 3.69 us -> 3.06 us  [far_rows(): pl.pallas_call(far_kernel, out_shape=jax.ShapeDtypeStruct((rows, width),...]
  transfers between devices with their start and end apart: 13 -> 13, of which waited for: 5 -> 5; matrix products, arithmetic and copies ran while one was open for 4% -> 5% of each run, Pallas kernels for 21% -> 21%
where the time goes in v14:
time: 45.3 us; the launch traced here: 45 us
  starting transfers between devices  15.2 us (34%)
  waiting for transfers between devices  13 us (29%)
  Pallas kernels  12.3 us (27%)
  local copies, waits for them, and re-layouts  2.49 us (5%)
  other arithmetic  1.24 us (3%)
  between operations  0.87 us (2%)
    ppermute x7, waiting for transfers between devices, swap(): return lax.ppermute(cells, 'seq', [(i, i ^ mask) for i in range(count)])  7.95 us
    ppermute x7, starting transfers between devices, swap(): return lax.ppermute(cells, 'seq', [(i, i ^ mask) for i in range(count)])  5.89 us
    ppermute x2, starting transfers between devices, send(): return [lax.ppermute(x, 'seq', pairs) for x in cells]  5.56 us
    pallas_call x1, Pallas kernels, inner_attention(): pl.pallas_call(inner_kernel, grid=(width // WIDE,), out_shape=jax.ShapeDt...  3.92 us
    pallas_call x1, Pallas kernels, merge(): pl.pallas_call(functools.partial(merge_kernel, layout), out_shape=(jax.Sh...  3.7 us
    pallas_call x1, Pallas kernels, far_rows(): pl.pallas_call(far_kernel, out_shape=jax.ShapeDtypeStruct((rows, width),...  3.06 us
    ppermute x3, waiting for transfers between devices, cross(): return lax.ppermute(cells, 'group', [(0, 1), (1, 0)])  2.85 us
    ppermute x3, starting transfers between devices, cross(): return lax.ppermute(cells, 'group', [(0, 1), (1, 0)])  2.83 us
  transfers between devices with their start and end apart: 13, of which 5 were waited for; matrix products, arithmetic and copies ran while one was open for 5% of the time, Pallas kernels for 21%

profile of v14, /device:TPU:1, one launch (start us, length us, event | category | flops | bytes accessed | tf_op | source)
XLA Modules:
  0.0 45.0 jit_solution(18370990018343549668)
XLA Ops:
  0.6 0.9 %fusion = bf16[1,320,128]{2,1,0:T(8,128)(2,1)S(1)} fusion(bf16[320,128]{1,0:T(8,128)(2,1)} %own_down.1, bf16[128,320]{0,1:T(8,128)(2,1)} %param.14, pred[]{:T(512)S(6)} %eq.3), kind=kLoop, calls=%fused_computation.7 | loop fusion | flops 40960 | bytes 245761 | tf_op jit(solution)/shard_map/broadcast_in_dim | solution.py:326
  1.6 2.1 %collective-permute-start.3 = (bf16[1,320,128]{2,1,0:T(8,128)(2,1)S(1)}, bf16[1,320,128]{2,1,0:T(8,128)(2,1)S(1)}, u32[]{:S(2)}, u32[]{:S(2)}) collective-permute-start(bf16[1,320,128]{2,1,0:T(8,128)(2,1)S(1)} %fusion), channel_id=1, source_target_pairs={{0,2},{1,3},{2,0},{3,1},{4,6},{5,7},{6,4},{7,5},{8,10},{9,11},{10,... | collective-permute-start | bytes 245768 | tf_op jit(solution)/shard_map/ppermute | solution.py:302
  3.7 0.0 copy-start.1
  3.7 1.5 %dynamic-slice_bitcast_fusion.1 = (bf16[1,64,5120]{2,1,0:T(8,128)(2,1)S(1)}, bf16[64,5120]{1,0:T(8,128)(2,1)S(1)}) fusion(bf16[256,5120]{1,0:T(8,128)(2,1)} %k.3, s32[]{:T(128)S(6)} %select_n.19, s32[]{:T(128)S(6)} %select_n.16), kind=kLoop, calls=%fused_computation.3 | loop fusion | bytes 2621448 | tf_op jit(solution)/shard_map/stack | solution.py:312
  5.2 2.5 %collective-permute-start = (bf16[64,5120]{1,0:T(8,128)(2,1)S(1)}, bf16[64,5120]{1,0:T(8,128)(2,1)S(1)}, u32[]{:S(2)}, u32[]{:S(2)}) collective-permute-start(bf16[64,5120]{1,0:T(8,128)(2,1)S(1)} %get-tuple-element.20), channel_id=1, source_target_pairs={{1,2},{2,1},{5,6},{6,5},{9,10},{10,9},{13,14},{14,13},{17,18},{18,... | collective-permute-start | bytes 1966088 | tf_op jit(solution)/shard_map/ppermute | solution.py:299
  7.8 0.0 copy-done.1
  7.8 0.1 dynamic-slice_bitcast_fusion
  7.9 3.1 %collective-permute-start.1 = (bf16[64,5120]{1,0:T(8,128)(2,1)S(1)}, bf16[64,5120]{1,0:T(8,128)(2,1)S(1)}, u32[]{:S(2)}, u32[]{:S(2)}) collective-permute-start(bf16[64,5120]{1,0:T(8,128)(2,1)S(1)} %get-tuple-element.21), channel_id=1, source_target_pairs={{1,2},{2,1},{5,6},{6,5},{9,10},{10,9},{13,14},{14,13},{17,18},{18,... | collective-permute-start | bytes 1966088 | tf_op jit(solution)/shard_map/ppermute | solution.py:299
  10.9 0.0 copy-start.2
  10.9 0.1 pad_maximum_fusion.1
  11.1 0.0 collective-permute-done.3
  11.1 1.2 %collective-permute-start.6 = (bf16[2,320,128]{2,1,0:T(8,128)(2,1)S(1)}, bf16[2,320,128]{2,1,0:T(8,128)(2,1)S(1)}, u32[]{:S(2)}, u32[]{:S(2)}) collective-permute-start(bf16[2,320,128]{2,1,0:T(8,128)(2,1)S(1)} %pad_maximum_fusion.3), channel_id=1, source_target_pairs={{0,16},{16,0},{1,17},{17,1},{2,18},{18,2},{3,19},{19,3},{4,20},{20... | collective-permute-start | bytes 491528 | tf_op jit(solution)/shard_map/ppermute | solution.py:305
  12.4 1.3 %collective-permute-start.5 = (bf16[2,320,128]{2,1,0:T(8,128)(2,1)S(1)}, bf16[2,320,128]{2,1,0:T(8,128)(2,1)S(1)}, u32[]{:S(2)}, u32[]{:S(2)}) collective-permute-start(bf16[2,320,128]{2,1,0:T(8,128)(2,1)S(1)} %pad_maximum_fusion.3), channel_id=1, source_target_pairs={{0,4},{1,5},{2,6},{3,7},{4,0},{5,1},{6,2},{7,3},{8,12},{9,13},{10,... | collective-permute-start | bytes 491528 | tf_op jit(solution)/shard_map/ppermute | solution.py:302
  13.6 2.3 %collective-permute-start.4 = (bf16[2,320,128]{2,1,0:T(8,128)(2,1)S(1)}, bf16[2,320,128]{2,1,0:T(8,128)(2,1)S(1)}, u32[]{:S(2)}, u32[]{:S(2)}) collective-permute-start(bf16[2,320,128]{2,1,0:T(8,128)(2,1)S(1)} %pad_maximum_fusion.3), channel_id=1, source_target_pairs={{0,8},{1,9},{2,10},{3,11},{4,12},{5,13},{6,14},{7,15},{8,0},{9,1},... | collective-permute-start | bytes 491528 | tf_op jit(solution)/shard_map/ppermute | solution.py:302
  16.0 0.0 collective-permute-done.6
  16.0 0.0 collective-permute-start.8
  16.0 2.8 %collective-permute-done.5 = bf16[2,320,128]{2,1,0:T(8,128)(2,1)S(1)} collective-permute-done((bf16[2,320,128]{2,1,0:T(8,128)(2,1)S(1)}, bf16[2,320,128]{2,1,0:T(8,128)(2,1)S(1)}, u32[]{:S(2)}, u32[]{:S(2)}) %collective-permute-start.5) | collective-permute-done | bytes 163872 | tf_op jit(solution)/shard_map/ppermute | solution.py:302
  18.8 3.1 %collective-permute-done.4 = bf16[2,320,128]{2,1,0:T(8,128)(2,1)S(1)} collective-permute-done((bf16[2,320,128]{2,1,0:T(8,128)(2,1)S(1)}, bf16[2,320,128]{2,1,0:T(8,128)(2,1)S(1)}, u32[]{:S(2)}, u32[]{:S(2)}) %collective-permute-start.4) | collective-permute-done | bytes 163872 | tf_op jit(solution)/shard_map/ppermute | solution.py:302
  21.8 0.0 collective-permute-start.7
  21.9 0.4 collective-permute-start.10
  22.3 0.0 collective-permute-done.rest_0_
  22.3 2.2 %collective-permute-done.1.rest_1_ = bf16[64,5120]{1,0:T(8,128)(2,1)S(1)} collective-permute-done((bf16[64,5120]{1,0:T(8,128)(2,1)S(1)}, bf16[64,5120]{1,0:T(8,128)(2,1)S(1)}, u32[]{:S(2)}, u32[]{:S(2)}) %collective-permute-start.1) | collective-permute-done | bytes 655392 | tf_op jit(solution)/shard_map/ppermute | solution.py:299
  24.5 0.0 copy-start
  24.5 0.0 copy-start.5
  24.5 0.1 pad_maximum_fusion
  24.6 0.9 %collective-permute-start.2 = (bf16[2,64,5120]{2,1,0:T(8,128)(2,1)S(1)}, bf16[2,64,5120]{2,1,0:T(8,128)(2,1)S(1)}, u32[]{:S(2)}, u32[]{:S(2)}) collective-permute-start(bf16[2,64,5120]{2,1,0:T(8,128)(2,1)S(1)} %pad_maximum_fusion), channel_id=1, source_target_pairs={{3,4},{4,3},{7,8},{8,7},{11,12},{12,11},{19,20},{20,19},{23,24},{2... | collective-permute-start | bytes 3932168 | tf_op jit(solution)/shard_map/ppermute | solution.py:337
  25.5 0.0 copy-done.2
  25.5 0.7 %copy-done = bf16[256,5120]{1,0:T(8,128)(2,1)S(1)} copy-done((bf16[256,5120]{1,0:T(8,128)(2,1)S(1)}, bf16[256,5120]{1,0:T(8,128)(2,1)}, u32[]{:S(2)}) %copy-start) | copy-done | bytes 2621464
  26.2 0.0 copy-done.5
  26.2 0.0 copy-done.6
  26.2 3.9 %inner_attention.1.inner = bf16[128,5120]{1,0:T(8,128)(2,1)S(1)} custom-call(s32[256]{0:T(256)S(1)} %copy-done.5, s32[256]{0:T(256)S(1)} %copy-done.6, bf16[256,5120]{1,0:T(8,128)(2,1)S(1)} %copy-done.2, bf16[256,5120]{1,0:T(8,128)(2,1)S(1)} %copy-done, bf16[256,5120]{1,0:T(8,128)(2,1)S(1)} %copy-done.1), custom_call_target="tpu_custom_call" | custom-call | flops 1342177280 | bytes 9175040 | tf_op jit(solution)/shard_map/inner_attention/pallas_call | solution.py:90
  30.1 0.0 collective-permute-done.8.halo
  30.2 0.0 copy-start.3
  30.2 1.6 %near_edge_attention.1.near = bf16[64,5120]{1,0:T(8,128)(2,1)S(1)} custom-call(s32[256]{0:T(256)S(1)} %copy-done.5, s32[256]{0:T(256)S(1)} %copy-done.6, bf16[256,5120]{1,0:T(8,128)(2,1)S(1)} %copy-done.2, bf16[256,5120]{1,0:T(8,128)(2,1)S(1)} %copy-done, bf16[256,5120]{1,0:T(8,128)(2,1)S(1)} %copy-done.1, bf16[2,64,5120]{2,1,0:T(8,128)(2,1)S(1)} %collective-permute-done.8.halo), custom_call_target="tpu_custom_call" | custom-call | flops 671088640 | bytes 9175040 | tf_op jit(solution)/shard_map/near_edge_attention/pallas_call | solution.py:170
  31.8 0.0 copy-start.4
  31.8 0.0 collective-permute-done.7
  31.8 1.2 %collective-permute-start.11 = (bf16[2,320,128]{2,1,0:T(8,128)(2,1)S(1)}, bf16[2,320,128]{2,1,0:T(8,128)(2,1)S(1)}, u32[]{:S(2)}, u32[]{:S(2)}) collective-permute-start(bf16[2,320,128]{2,1,0:T(8,128)(2,1)S(1)} %collective-permute-done.7), channel_id=1, source_target_pairs={{0,16},{16,0},{1,17},{17,1},{2,18},{18,2},{3,19},{19,3},{4,20},{20... | collective-permute-start | bytes 491528 | tf_op jit(solution)/shard_map/ppermute | solution.py:305
  33.0 0.0 collective-permute-done.10
  33.1 0.1 collective-permute-start.9
  33.2 2.8 %collective-permute-done.11 = bf16[2,320,128]{2,1,0:T(8,128)(2,1)S(1)} collective-permute-done((bf16[2,320,128]{2,1,0:T(8,128)(2,1)S(1)}, bf16[2,320,128]{2,1,0:T(8,128)(2,1)S(1)}, u32[]{:S(2)}, u32[]{:S(2)}) %collective-permute-start.11) | collective-permute-done | bytes 163872 | tf_op jit(solution)/shard_map/ppermute | solution.py:305
  36.1 0.1 collective-permute-start.12
  36.1 0.0 collective-permute-done.9.rest_1_
  36.2 2.1 %collective-permute-done.12.rest_3_ = bf16[8,320,128]{2,1,0:T(8,128)(2,1)S(1)} collective-permute-done((bf16[8,320,128]{2,1,0:T(8,128)(2,1)S(1)}, bf16[8,320,128]{2,1,0:T(8,128)(2,1)S(1)}, u32[]{:S(2)}, u32[]{:S(2)}) %collective-permute-start.12) | collective-permute-done | bytes 655392 | tf_op jit(solution)/shard_map/ppermute | solution.py:302
  38.2 0.0 copy-done.3
  38.2 0.0 copy-done.4
  38.2 3.7 %merge_and_adapter.1 = (bf16[320,5120]{1,0:T(8,128)(2,1)}, bf16[256,5120]{1,0:T(8,128)(2,1)}, bf16[2,5120,128]{2,1,0:T(8,128)(2,1)S(1)}) custom-call(bf16[320,5120]{1,0:T(8,128)(2,1)S(1)} %copy-done.3, bf16[320,128]{1,0:T(8,128)(2,1)S(1)} %copy-done.4, bf16[128,5120]{1,0:T(8,128)(2,1)S(1)} %inner_attention.1.inner, ...), custom_call_target="tpu_custom_call" | custom-call | flops 1090519040 | bytes 14417920 | tf_op jit(solution)/shard_map/merge_and_adapter/pallas_call | solution.py:226
  41.9 0.0 collective-permute-done.2.rest_2_
  41.9 3.1 %far_edge_rows.1 = bf16[256,5120]{1,0:T(8,128)(2,1)} custom-call(s32[256]{0:T(256)S(1)} %copy-done.5, s32[256]{0:T(256)S(1)} %copy-done.6, bf16[256,5120]{1,0:T(8,128)(2,1)S(1)} %copy-done.2, bf16[256,5120]{1,0:T(8,128)(2,1)S(1)} %copy-done, bf16[256,5120]{1,0:T(8,128)(2,1)S(1)} %copy-done.1, ...), custom_call_target="tpu_custom_call", output_to_operand_aliasing={{}: (9, {})} | custom-call | flops 671088640 | bytes 9175040 | tf_op jit(solution)/shard_map/far_edge_rows/pallas_call | solution.py:273
  (10 shorter events, 0.2 us)
Async XLA Ops:
  1.6 9.5 %collective-permute-start.3 = (bf16[1,320,128]{2,1,0:T(8,128)(2,1)S(1)}, bf16[1,320,128]{2,1,0:T(8,128)(2,1)S(1)}, u32[]{:S(2)}, u32[]{:S(2)}) collective-permute-start(bf16[1,320,128]{2,1,0:T(8,128)(2,1)S(1)} %fusion), channel_id=1, source_target_pairs={{0,2},{1,3},{2,0},{3,1},{4,6},{5,7},{6,4},{7,5},{8,10},{9,11},{10,... | collective-permute-start | bytes 245768 | tf_op jit(solution)/shard_map/ppermute | solution.py:302
  3.7 4.0 %copy-start.1 = (bf16[256,5120]{1,0:T(8,128)(2,1)S(1)}, bf16[256,5120]{1,0:T(8,128)(2,1)}, u32[]{:S(2)}) copy-start(bf16[256,5120]{1,0:T(8,128)(2,1)} %v.3) | copy-start | bytes 7864324
  5.2 17.1 %collective-permute-start = (bf16[64,5120]{1,0:T(8,128)(2,1)S(1)}, bf16[64,5120]{1,0:T(8,128)(2,1)S(1)}, u32[]{:S(2)}, u32[]{:S(2)}) collective-permute-start(bf16[64,5120]{1,0:T(8,128)(2,1)S(1)} %get-tuple-element.20), channel_id=1, source_target_pairs={{1,2},{2,1},{5,6},{6,5},{9,10},{10,9},{13,14},{14,13},{17,18},{18,... | collective-permute-start | bytes 1966088 | tf_op jit(solution)/shard_map/ppermute | solution.py:299
  7.9 16.6 %collective-permute-start.1 = (bf16[64,5120]{1,0:T(8,128)(2,1)S(1)}, bf16[64,5120]{1,0:T(8,128)(2,1)S(1)}, u32[]{:S(2)}, u32[]{:S(2)}) collective-permute-start(bf16[64,5120]{1,0:T(8,128)(2,1)S(1)} %get-tuple-element.21), channel_id=1, source_target_pairs={{1,2},{2,1},{5,6},{6,5},{9,10},{10,9},{13,14},{14,13},{17,18},{18,... | collective-permute-start | bytes 1966088 | tf_op jit(solution)/shard_map/ppermute | solution.py:299
  10.9 14.6 %copy-start.2 = (bf16[256,5120]{1,0:T(8,128)(2,1)S(1)}, bf16[256,5120]{1,0:T(8,128)(2,1)}, u32[]{:S(2)}) copy-start(bf16[256,5120]{1,0:T(8,128)(2,1)} %q.3) | copy-start | bytes 7864324
  11.1 4.8 %collective-permute-start.6 = (bf16[2,320,128]{2,1,0:T(8,128)(2,1)S(1)}, bf16[2,320,128]{2,1,0:T(8,128)(2,1)S(1)}, u32[]{:S(2)}, u32[]{:S(2)}) collective-permute-start(bf16[2,320,128]{2,1,0:T(8,128)(2,1)S(1)} %pad_maximum_fusion.3), channel_id=1, source_target_pairs={{0,16},{16,0},{1,17},{17,1},{2,18},{18,2},{3,19},{19,3},{4,20},{20... | collective-permute-start | bytes 491528 | tf_op jit(solution)/shard_map/ppermute | solution.py:305
  12.4 6.4 %collective-permute-start.5 = (bf16[2,320,128]{2,1,0:T(8,128)(2,1)S(1)}, bf16[2,320,128]{2,1,0:T(8,128)(2,1)S(1)}, u32[]{:S(2)}, u32[]{:S(2)}) collective-permute-start(bf16[2,320,128]{2,1,0:T(8,128)(2,1)S(1)} %pad_maximum_fusion.3), channel_id=1, source_target_pairs={{0,4},{1,5},{2,6},{3,7},{4,0},{5,1},{6,2},{7,3},{8,12},{9,13},{10,... | collective-permute-start | bytes 491528 | tf_op jit(solution)/shard_map/ppermute | solution.py:302
  13.6 8.2 %collective-permute-start.4 = (bf16[2,320,128]{2,1,0:T(8,128)(2,1)S(1)}, bf16[2,320,128]{2,1,0:T(8,128)(2,1)S(1)}, u32[]{:S(2)}, u32[]{:S(2)}) collective-permute-start(bf16[2,320,128]{2,1,0:T(8,128)(2,1)S(1)} %pad_maximum_fusion.3), channel_id=1, source_target_pairs={{0,8},{1,9},{2,10},{3,11},{4,12},{5,13},{6,14},{7,15},{8,0},{9,1},... | collective-permute-start | bytes 491528 | tf_op jit(solution)/shard_map/ppermute | solution.py:302
  16.0 14.2 %collective-permute-start.8 = (bf16[2,64,5120]{2,1,0:T(8,128)(2,1)S(1)}, bf16[2,64,5120]{2,1,0:T(8,128)(2,1)S(1)}, u32[]{:S(2)}, u32[]{:S(2)}) collective-permute-start(bf16[2,64,5120]{2,1,0:T(8,128)(2,1)S(1)} %pad_maximum_fusion.1), channel_id=1, source_target_pairs={{0,1},{1,0},{2,3},{3,2},{4,5},{5,4},{6,7},{7,6},{8,9},{9,8},{10,11... | collective-permute-start | bytes 3932168 | tf_op jit(solution)/shard_map/ppermute | solution.py:302
  21.8 9.9 %collective-permute-start.7 = (bf16[2,320,128]{2,1,0:T(8,128)(2,1)S(1)}, bf16[2,320,128]{2,1,0:T(8,128)(2,1)S(1)}, u32[]{:S(2)}, u32[]{:S(2)}) collective-permute-start(bf16[2,320,128]{2,1,0:T(8,128)(2,1)S(1)} %collective-permute-done.4), channel_id=1, source_target_pairs={{0,4},{1,5},{2,6},{3,7},{4,0},{5,1},{6,2},{7,3},{8,12},{9,13},{10,... | collective-permute-start | bytes 491528 | tf_op jit(solution)/shard_map/ppermute | solution.py:302
  21.9 11.2 %collective-permute-start.10 = (bf16[4,320,128]{2,1,0:T(8,128)(2,1)S(1)}, bf16[4,320,128]{2,1,0:T(8,128)(2,1)S(1)}, u32[]{:S(2)}, u32[]{:S(2)}) collective-permute-start(bf16[4,320,128]{2,1,0:T(8,128)(2,1)S(1)} %pad_maximum_fusion.2), channel_id=1, source_target_pairs={{0,16},{16,0},{1,17},{17,1},{2,18},{18,2},{3,19},{19,3},{4,20},{20... | collective-permute-start | bytes 983048 | tf_op jit(solution)/shard_map/ppermute | solution.py:305
  24.5 1.7 %copy-start = (bf16[256,5120]{1,0:T(8,128)(2,1)S(1)}, bf16[256,5120]{1,0:T(8,128)(2,1)}, u32[]{:S(2)}) copy-start(bf16[256,5120]{1,0:T(8,128)(2,1)} %k.3) | copy-start | bytes 7864324
  24.5 1.7 %copy-start.5 = (s32[256]{0:T(256)S(1)}, s32[256]{0:T(256)}, u32[]{:S(2)}) copy-start(s32[256]{0:T(256)} %lo_ref.3) | copy-start | bytes 3076
  24.5 1.7 %copy-start.6 = (s32[256]{0:T(256)S(1)}, s32[256]{0:T(256)}, u32[]{:S(2)}) copy-start(s32[256]{0:T(256)} %hi_ref.5) | copy-start | bytes 3076
  24.6 17.3 %collective-permute-start.2 = (bf16[2,64,5120]{2,1,0:T(8,128)(2,1)S(1)}, bf16[2,64,5120]{2,1,0:T(8,128)(2,1)S(1)}, u32[]{:S(2)}, u32[]{:S(2)}) collective-permute-start(bf16[2,64,5120]{2,1,0:T(8,128)(2,1)S(1)} %pad_maximum_fusion), channel_id=1, source_target_pairs={{3,4},{4,3},{7,8},{8,7},{11,12},{12,11},{19,20},{20,19},{23,24},{2... | collective-permute-start | bytes 3932168 | tf_op jit(solution)/shard_map/ppermute | solution.py:337
  30.2 8.1 %copy-start.3 = (bf16[320,5120]{1,0:T(8,128)(2,1)S(1)}, bf16[320,5120]{1,0:T(8,128)(2,1)}, u32[]{:S(2)}) copy-start(bf16[320,5120]{1,0:T(8,128)(2,1)} %frozen.1) | copy-start | bytes 9830404
  31.8 6.5 %copy-start.4 = (bf16[320,128]{1,0:T(8,128)(2,1)S(1)}, bf16[320,128]{1,0:T(8,128)(2,1)}, u32[]{:S(2)}) copy-start(bf16[320,128]{1,0:T(8,128)(2,1)} %own_down.1) | copy-start | bytes 245764
  31.8 4.2 %collective-permute-start.11 = (bf16[2,320,128]{2,1,0:T(8,128)(2,1)S(1)}, bf16[2,320,128]{2,1,0:T(8,128)(2,1)S(1)}, u32[]{:S(2)}, u32[]{:S(2)}) collective-permute-start(bf16[2,320,128]{2,1,0:T(8,128)(2,1)S(1)} %collective-permute-done.7), channel_id=1, source_target_pairs={{0,16},{16,0},{1,17},{17,1},{2,18},{18,2},{3,19},{19,3},{4,20},{20... | collective-permute-start | bytes 491528 | tf_op jit(solution)/shard_map/ppermute | solution.py:305
  33.1 3.0 %collective-permute-start.9 = (bf16[8,320,128]{2,1,0:T(8,128)(2,1)S(1)}, bf16[8,320,128]{2,1,0:T(8,128)(2,1)S(1)}, u32[]{:S(2)}, u32[]{:S(2)}) collective-permute-start(bf16[8,320,128]{2,1,0:T(8,128)(2,1)S(1)} %constant_dynamic-update-slice_fusion.rest_0_), channel_id=1, source_target_pairs={{0,1},{1,0},{2,3},{3,2},{4,5},{5,4},{6,7},{7,6},{8,9},{9,8},{10,11... | collective-permute-start | bytes 1966088 | tf_op jit(solution)/shard_map/ppermute | solution.py:302
  36.1 2.2 %collective-permute-start.12 = (bf16[8,320,128]{2,1,0:T(8,128)(2,1)S(1)}, bf16[8,320,128]{2,1,0:T(8,128)(2,1)S(1)}, u32[]{:S(2)}, u32[]{:S(2)}) collective-permute-start(bf16[8,320,128]{2,1,0:T(8,128)(2,1)S(1)} %constant_dynamic-update-slice_fusion.4.rest_2_), channel_id=1, source_target_pairs={{0,1},{1,0},{2,3},{3,2},{4,5},{5,4},{6,7},{7,6},{8,9},{9,8},{10,11... | collective-permute-start | bytes 1966088 | tf_op jit(solution)/shard_map/ppermute | solution.py:302

commit v15 on v14

--- a/solution.py
+++ b/solution.py
@@ -62,38 +62,37 @@
 
 
 def inner_kernel(lo_ref, hi_ref, q_ref, k_ref, v_ref, o_ref):
-    rows = q_ref.shape[0]
+    rows, width = q_ref.shape
     base = lax.axis_index("seq") * rows
-    loads, targets = [], []
     for row in (FRAME, NEAR):
         lo, hi = lo_ref[row], hi_ref[row]
         keys = pl.ds(pl.multiple_of(lo - base, FRAME), NEAR)
         bias = clip_bias(lo, hi)
-        for col in range(0, WIDE, 2 * HD):
-            part = slice(col, col + 2 * HD)
-            targets.append((slice(row - FRAME, row), part))
-            loads.append(
-                (
-                    lambda row=row, part=part: q_ref[row : row + FRAME, part],
-                    lambda keys=keys, part=part: k_ref[keys, part],
-                    lambda keys=keys, part=part: v_ref[keys, part],
-                    bias,
+        for first in range(0, width, width // 2):
+            loads, parts = [], []
+            for col in range(first, first + width // 2, 2 * HD):
+                part = slice(col, col + 2 * HD)
+                parts.append(part)
+                loads.append(
+                    (
+                        lambda row=row, part=part: q_ref[row : row + FRAME, part],
+                        lambda keys=keys, part=part: k_ref[keys, part],
+                        lambda keys=keys, part=part: v_ref[keys, part],
+                        bias,
+                    )
                 )
-            )
-    for target, result in zip(targets, attend(loads)):
-        o_ref[target] = result
+            for part, result in zip(parts, attend(loads)):
+                o_ref[row - FRAME : row, part] = result
 
 
 def inner_attention(lo, hi, q, k, v):
     rows, width = q.shape
-    block = pl.BlockSpec((rows, WIDE), lambda i: (0, i))
     return pl.pallas_call(
         inner_kernel,
-        grid=(width // WIDE,),
         out_shape=jax.ShapeDtypeStruct((NEAR, width), BF16),
-        in_specs=[SMEM, SMEM, block, block, block],
-        out_specs=pl.BlockSpec((NEAR, WIDE), lambda i: (0, i)),
-        compiler_params=pltpu.CompilerParams(vmem_limit_bytes=16 << 20),
+        in_specs=[SMEM, SMEM] + [VMEM] * 3,
+        out_specs=VMEM,
+        compiler_params=pltpu.CompilerParams(vmem_limit_bytes=20 << 20),
         cost_estimate=pl.CostEstimate(
             flops=16 * NEAR * NEAR * width,
             bytes_accessed=7 * rows * width,

time: 45.3 us -> 43.8 us (0.967)
  Pallas kernels: 12.3 us -> 10.8 us
    pallas_call x1, Pallas kernels: 3.92 us -> 2.41 us  [inner_attention(): pl.pallas_call(inner_kernel, out_shape=jax.ShapeDtypeStruct((NEAR, width)...]
  transfers between devices with their start and end apart: 13 -> 13, of which waited for: 5 -> 5; matrix products, arithmetic and copies ran while one was open for 5% -> 5% of each run, Pallas kernels for 21% -> 18%
where the time goes in v15:
time: 43.8 us; the launch traced here: 43.5 us
  starting transfers between devices  15.2 us (35%)
  waiting for transfers between devices  13 us (30%)
  Pallas kernels  10.8 us (25%)
  local copies, waits for them, and re-layouts  2.49 us (6%)
  other arithmetic  1.24 us (3%)
  between operations  0.87 us (2%)
    ppermute x7, waiting for transfers between devices, swap(): return lax.ppermute(cells, 'seq', [(i, i ^ mask) for i in range(count)])  7.95 us
    ppermute x7, starting transfers between devices, swap(): return lax.ppermute(cells, 'seq', [(i, i ^ mask) for i in range(count)])  5.89 us
    ppermute x2, starting transfers between devices, send(): return [lax.ppermute(x, 'seq', pairs) for x in cells]  5.56 us
    pallas_call x1, Pallas kernels, merge(): pl.pallas_call(functools.partial(merge_kernel, layout), out_shape=(jax.Sh...  3.7 us
    pallas_call x1, Pallas kernels, far_rows(): pl.pallas_call(far_kernel, out_shape=jax.ShapeDtypeStruct((rows, width),...  3.07 us
    ppermute x3, waiting for transfers between devices, cross(): return lax.ppermute(cells, 'group', [(0, 1), (1, 0)])  2.84 us
    ppermute x3, starting transfers between devices, cross(): return lax.ppermute(cells, 'group', [(0, 1), (1, 0)])  2.84 us
    pallas_call x1, Pallas kernels, inner_attention(): pl.pallas_call(inner_kernel, out_shape=jax.ShapeDtypeStruct((NEAR, width)...  2.41 us
  transfers between devices with their start and end apart: 13, of which 5 were waited for; matrix products, arithmetic and copies ran while one was open for 5% of the time, Pallas kernels for 18%

profile of v15, /device:TPU:1, one launch (start us, length us, event | category | flops | bytes accessed | tf_op | source)
XLA Modules:
  0.0 43.5 jit_solution(3554004371820713830)
XLA Ops:
  0.6 0.9 %fusion = bf16[1,320,128]{2,1,0:T(8,128)(2,1)S(1)} fusion(bf16[320,128]{1,0:T(8,128)(2,1)} %own_down.1, bf16[128,320]{0,1:T(8,128)(2,1)} %param.14, pred[]{:T(512)S(6)} %eq.3), kind=kLoop, calls=%fused_computation.7 | loop fusion | flops 40960 | bytes 245761 | tf_op jit(solution)/shard_map/broadcast_in_dim | solution.py:325
  1.6 2.1 %collective-permute-start.3 = (bf16[1,320,128]{2,1,0:T(8,128)(2,1)S(1)}, bf16[1,320,128]{2,1,0:T(8,128)(2,1)S(1)}, u32[]{:S(2)}, u32[]{:S(2)}) collective-permute-start(bf16[1,320,128]{2,1,0:T(8,128)(2,1)S(1)} %fusion), channel_id=1, source_target_pairs={{0,2},{1,3},{2,0},{3,1},{4,6},{5,7},{6,4},{7,5},{8,10},{9,11},{10,... | collective-permute-start | bytes 245768 | tf_op jit(solution)/shard_map/ppermute | solution.py:301
  3.7 0.0 copy-start.1
  3.7 1.5 %dynamic-slice_bitcast_fusion.1 = (bf16[1,64,5120]{2,1,0:T(8,128)(2,1)S(1)}, bf16[64,5120]{1,0:T(8,128)(2,1)S(1)}) fusion(bf16[256,5120]{1,0:T(8,128)(2,1)} %k.3, s32[]{:T(128)S(6)} %select_n.19, s32[]{:T(128)S(6)} %select_n.16), kind=kLoop, calls=%fused_computation.3 | loop fusion | bytes 2621448 | tf_op jit(solution)/shard_map/stack | solution.py:311
  5.2 2.5 %collective-permute-start = (bf16[64,5120]{1,0:T(8,128)(2,1)S(1)}, bf16[64,5120]{1,0:T(8,128)(2,1)S(1)}, u32[]{:S(2)}, u32[]{:S(2)}) collective-permute-start(bf16[64,5120]{1,0:T(8,128)(2,1)S(1)} %get-tuple-element.20), channel_id=1, source_target_pairs={{1,2},{2,1},{5,6},{6,5},{9,10},{10,9},{13,14},{14,13},{17,18},{18,... | collective-permute-start | bytes 1966088 | tf_op jit(solution)/shard_map/ppermute | solution.py:298
  7.8 0.0 copy-done.1
  7.8 0.1 dynamic-slice_bitcast_fusion
  7.9 3.1 %collective-permute-start.1 = (bf16[64,5120]{1,0:T(8,128)(2,1)S(1)}, bf16[64,5120]{1,0:T(8,128)(2,1)S(1)}, u32[]{:S(2)}, u32[]{:S(2)}) collective-permute-start(bf16[64,5120]{1,0:T(8,128)(2,1)S(1)} %get-tuple-element.21), channel_id=1, source_target_pairs={{1,2},{2,1},{5,6},{6,5},{9,10},{10,9},{13,14},{14,13},{17,18},{18,... | collective-permute-start | bytes 1966088 | tf_op jit(solution)/shard_map/ppermute | solution.py:298
  10.9 0.0 copy-start.2
  10.9 0.1 pad_maximum_fusion.1
  11.1 0.0 collective-permute-done.3
  11.1 1.2 %collective-permute-start.6 = (bf16[2,320,128]{2,1,0:T(8,128)(2,1)S(1)}, bf16[2,320,128]{2,1,0:T(8,128)(2,1)S(1)}, u32[]{:S(2)}, u32[]{:S(2)}) collective-permute-start(bf16[2,320,128]{2,1,0:T(8,128)(2,1)S(1)} %pad_maximum_fusion.3), channel_id=1, source_target_pairs={{0,16},{16,0},{1,17},{17,1},{2,18},{18,2},{3,19},{19,3},{4,20},{20... | collective-permute-start | bytes 491528 | tf_op jit(solution)/shard_map/ppermute | solution.py:304
  12.4 1.3 %collective-permute-start.5 = (bf16[2,320,128]{2,1,0:T(8,128)(2,1)S(1)}, bf16[2,320,128]{2,1,0:T(8,128)(2,1)S(1)}, u32[]{:S(2)}, u32[]{:S(2)}) collective-permute-start(bf16[2,320,128]{2,1,0:T(8,128)(2,1)S(1)} %pad_maximum_fusion.3), channel_id=1, source_target_pairs={{0,4},{1,5},{2,6},{3,7},{4,0},{5,1},{6,2},{7,3},{8,12},{9,13},{10,... | collective-permute-start | bytes 491528 | tf_op jit(solution)/shard_map/ppermute | solution.py:301
  13.6 2.3 %collective-permute-start.4 = (bf16[2,320,128]{2,1,0:T(8,128)(2,1)S(1)}, bf16[2,320,128]{2,1,0:T(8,128)(2,1)S(1)}, u32[]{:S(2)}, u32[]{:S(2)}) collective-permute-start(bf16[2,320,128]{2,1,0:T(8,128)(2,1)S(1)} %pad_maximum_fusion.3), channel_id=1, source_target_pairs={{0,8},{1,9},{2,10},{3,11},{4,12},{5,13},{6,14},{7,15},{8,0},{9,1},... | collective-permute-start | bytes 491528 | tf_op jit(solution)/shard_map/ppermute | solution.py:301
  16.0 0.0 collective-permute-done.6
  16.0 0.0 collective-permute-start.8
  16.0 2.8 %collective-permute-done.5 = bf16[2,320,128]{2,1,0:T(8,128)(2,1)S(1)} collective-permute-done((bf16[2,320,128]{2,1,0:T(8,128)(2,1)S(1)}, bf16[2,320,128]{2,1,0:T(8,128)(2,1)S(1)}, u32[]{:S(2)}, u32[]{:S(2)}) %collective-permute-start.5) | collective-permute-done | bytes 163872 | tf_op jit(solution)/shard_map/ppermute | solution.py:301
  18.8 3.1 %collective-permute-done.4 = bf16[2,320,128]{2,1,0:T(8,128)(2,1)S(1)} collective-permute-done((bf16[2,320,128]{2,1,0:T(8,128)(2,1)S(1)}, bf16[2,320,128]{2,1,0:T(8,128)(2,1)S(1)}, u32[]{:S(2)}, u32[]{:S(2)}) %collective-permute-start.4) | collective-permute-done | bytes 163872 | tf_op jit(solution)/shard_map/ppermute | solution.py:301
  21.8 0.0 collective-permute-start.7
  21.9 0.4 collective-permute-start.10
  22.3 0.0 collective-permute-done.rest_0_
  22.3 2.2 %collective-permute-done.1.rest_1_ = bf16[64,5120]{1,0:T(8,128)(2,1)S(1)} collective-permute-done((bf16[64,5120]{1,0:T(8,128)(2,1)S(1)}, bf16[64,5120]{1,0:T(8,128)(2,1)S(1)}, u32[]{:S(2)}, u32[]{:S(2)}) %collective-permute-start.1) | collective-permute-done | bytes 655392 | tf_op jit(solution)/shard_map/ppermute | solution.py:298
  24.5 0.0 copy-start
  24.5 0.0 copy-start.5
  24.5 0.1 pad_maximum_fusion
  24.6 0.9 %collective-permute-start.2 = (bf16[2,64,5120]{2,1,0:T(8,128)(2,1)S(1)}, bf16[2,64,5120]{2,1,0:T(8,128)(2,1)S(1)}, u32[]{:S(2)}, u32[]{:S(2)}) collective-permute-start(bf16[2,64,5120]{2,1,0:T(8,128)(2,1)S(1)} %pad_maximum_fusion), channel_id=1, source_target_pairs={{3,4},{4,3},{7,8},{8,7},{11,12},{12,11},{19,20},{20,19},{23,24},{2... | collective-permute-start | bytes 3932168 | tf_op jit(solution)/shard_map/ppermute | solution.py:336
  25.5 0.0 copy-done.2
  25.5 0.7 %copy-done = bf16[256,5120]{1,0:T(8,128)(2,1)S(1)} copy-done((bf16[256,5120]{1,0:T(8,128)(2,1)S(1)}, bf16[256,5120]{1,0:T(8,128)(2,1)}, u32[]{:S(2)}) %copy-start) | copy-done | bytes 2621464
  26.2 0.0 copy-done.5
  26.2 0.0 copy-done.6
  26.2 2.4 %inner_attention.1.inner = bf16[128,5120]{1,0:T(8,128)(2,1)S(1)} custom-call(s32[256]{0:T(256)S(1)} %copy-done.5, s32[256]{0:T(256)S(1)} %copy-done.6, bf16[256,5120]{1,0:T(8,128)(2,1)S(1)} %copy-done.2, bf16[256,5120]{1,0:T(8,128)(2,1)S(1)} %copy-done, bf16[256,5120]{1,0:T(8,128)(2,1)S(1)} %copy-done.1), custom_call_target="tpu_custom_call" | custom-call | flops 1342177280 | bytes 9175040 | tf_op jit(solution)/shard_map/inner_attention/pallas_call | solution.py:90
  28.6 0.0 collective-permute-done.8.halo
  28.6 0.0 copy-start.3
  28.6 1.6 %near_edge_attention.1.near = bf16[64,5120]{1,0:T(8,128)(2,1)S(1)} custom-call(s32[256]{0:T(256)S(1)} %copy-done.5, s32[256]{0:T(256)S(1)} %copy-done.6, bf16[256,5120]{1,0:T(8,128)(2,1)S(1)} %copy-done.2, bf16[256,5120]{1,0:T(8,128)(2,1)S(1)} %copy-done, bf16[256,5120]{1,0:T(8,128)(2,1)S(1)} %copy-done.1, bf16[2,64,5120]{2,1,0:T(8,128)(2,1)S(1)} %collective-permute-done.8.halo), custom_call_target="tpu_custom_call" | custom-call | flops 671088640 | bytes 9175040 | tf_op jit(solution)/shard_map/near_edge_attention/pallas_call | solution.py:169
  30.3 0.0 copy-start.4
  30.3 0.0 collective-permute-done.7
  30.3 1.2 %collective-permute-start.11 = (bf16[2,320,128]{2,1,0:T(8,128)(2,1)S(1)}, bf16[2,320,128]{2,1,0:T(8,128)(2,1)S(1)}, u32[]{:S(2)}, u32[]{:S(2)}) collective-permute-start(bf16[2,320,128]{2,1,0:T(8,128)(2,1)S(1)} %collective-permute-done.7), channel_id=1, source_target_pairs={{0,16},{16,0},{1,17},{17,1},{2,18},{18,2},{3,19},{19,3},{4,20},{20... | collective-permute-start | bytes 491528 | tf_op jit(solution)/shard_map/ppermute | solution.py:304
  31.5 0.0 collective-permute-done.10
  31.6 0.1 collective-permute-start.9
  31.7 2.8 %collective-permute-done.11 = bf16[2,320,128]{2,1,0:T(8,128)(2,1)S(1)} collective-permute-done((bf16[2,320,128]{2,1,0:T(8,128)(2,1)S(1)}, bf16[2,320,128]{2,1,0:T(8,128)(2,1)S(1)}, u32[]{:S(2)}, u32[]{:S(2)}) %collective-permute-start.11) | collective-permute-done | bytes 163872 | tf_op jit(solution)/shard_map/ppermute | solution.py:304
  34.5 0.1 collective-permute-start.12
  34.6 0.0 collective-permute-done.9.rest_1_
  34.6 2.1 %collective-permute-done.12.rest_3_ = bf16[8,320,128]{2,1,0:T(8,128)(2,1)S(1)} collective-permute-done((bf16[8,320,128]{2,1,0:T(8,128)(2,1)S(1)}, bf16[8,320,128]{2,1,0:T(8,128)(2,1)S(1)}, u32[]{:S(2)}, u32[]{:S(2)}) %collective-permute-start.12) | collective-permute-done | bytes 655392 | tf_op jit(solution)/shard_map/ppermute | solution.py:301
  36.7 0.0 copy-done.3
  36.7 0.0 copy-done.4
  36.7 3.7 %merge_and_adapter.1 = (bf16[320,5120]{1,0:T(8,128)(2,1)}, bf16[256,5120]{1,0:T(8,128)(2,1)}, bf16[2,5120,128]{2,1,0:T(8,128)(2,1)S(1)}) custom-call(bf16[320,5120]{1,0:T(8,128)(2,1)S(1)} %copy-done.3, bf16[320,128]{1,0:T(8,128)(2,1)S(1)} %copy-done.4, bf16[128,5120]{1,0:T(8,128)(2,1)S(1)} %inner_attention.1.inner, ...), custom_call_target="tpu_custom_call" | custom-call | flops 1090519040 | bytes 14417920 | tf_op jit(solution)/shard_map/merge_and_adapter/pallas_call | solution.py:225
  40.4 0.0 collective-permute-done.2.rest_2_
  40.4 3.1 %far_edge_rows.1 = bf16[256,5120]{1,0:T(8,128)(2,1)} custom-call(s32[256]{0:T(256)S(1)} %copy-done.5, s32[256]{0:T(256)S(1)} %copy-done.6, bf16[256,5120]{1,0:T(8,128)(2,1)S(1)} %copy-done.2, bf16[256,5120]{1,0:T(8,128)(2,1)S(1)} %copy-done, bf16[256,5120]{1,0:T(8,128)(2,1)S(1)} %copy-done.1, ...), custom_call_target="tpu_custom_call", output_to_operand_aliasing={{}: (9, {})} | custom-call | flops 671088640 | bytes 9175040 | tf_op jit(solution)/shard_map/far_edge_rows/pallas_call | solution.py:272
  (10 shorter events, 0.2 us)
Async XLA Ops:
  1.6 9.5 %collective-permute-start.3 = (bf16[1,320,128]{2,1,0:T(8,128)(2,1)S(1)}, bf16[1,320,128]{2,1,0:T(8,128)(2,1)S(1)}, u32[]{:S(2)}, u32[]{:S(2)}) collective-permute-start(bf16[1,320,128]{2,1,0:T(8,128)(2,1)S(1)} %fusion), channel_id=1, source_target_pairs={{0,2},{1,3},{2,0},{3,1},{4,6},{5,7},{6,4},{7,5},{8,10},{9,11},{10,... | collective-permute-start | bytes 245768 | tf_op jit(solution)/shard_map/ppermute | solution.py:301
  3.7 4.0 %copy-start.1 = (bf16[256,5120]{1,0:T(8,128)(2,1)S(1)}, bf16[256,5120]{1,0:T(8,128)(2,1)}, u32[]{:S(2)}) copy-start(bf16[256,5120]{1,0:T(8,128)(2,1)} %v.3) | copy-start | bytes 7864324
  5.2 17.1 %collective-permute-start = (bf16[64,5120]{1,0:T(8,128)(2,1)S(1)}, bf16[64,5120]{1,0:T(8,128)(2,1)S(1)}, u32[]{:S(2)}, u32[]{:S(2)}) collective-permute-start(bf16[64,5120]{1,0:T(8,128)(2,1)S(1)} %get-tuple-element.20), channel_id=1, source_target_pairs={{1,2},{2,1},{5,6},{6,5},{9,10},{10,9},{13,14},{14,13},{17,18},{18,... | collective-permute-start | bytes 1966088 | tf_op jit(solution)/shard_map/ppermute | solution.py:298
  7.9 16.6 %collective-permute-start.1 = (bf16[64,5120]{1,0:T(8,128)(2,1)S(1)}, bf16[64,5120]{1,0:T(8,128)(2,1)S(1)}, u32[]{:S(2)}, u32[]{:S(2)}) collective-permute-start(bf16[64,5120]{1,0:T(8,128)(2,1)S(1)} %get-tuple-element.21), channel_id=1, source_target_pairs={{1,2},{2,1},{5,6},{6,5},{9,10},{10,9},{13,14},{14,13},{17,18},{18,... | collective-permute-start | bytes 1966088 | tf_op jit(solution)/shard_map/ppermute | solution.py:298
  10.9 14.6 %copy-start.2 = (bf16[256,5120]{1,0:T(8,128)(2,1)S(1)}, bf16[256,5120]{1,0:T(8,128)(2,1)}, u32[]{:S(2)}) copy-start(bf16[256,5120]{1,0:T(8,128)(2,1)} %q.3) | copy-start | bytes 7864324
  11.1 4.8 %collective-permute-start.6 = (bf16[2,320,128]{2,1,0:T(8,128)(2,1)S(1)}, bf16[2,320,128]{2,1,0:T(8,128)(2,1)S(1)}, u32[]{:S(2)}, u32[]{:S(2)}) collective-permute-start(bf16[2,320,128]{2,1,0:T(8,128)(2,1)S(1)} %pad_maximum_fusion.3), channel_id=1, source_target_pairs={{0,16},{16,0},{1,17},{17,1},{2,18},{18,2},{3,19},{19,3},{4,20},{20... | collective-permute-start | bytes 491528 | tf_op jit(solution)/shard_map/ppermute | solution.py:304
  12.4 6.4 %collective-permute-start.5 = (bf16[2,320,128]{2,1,0:T(8,128)(2,1)S(1)}, bf16[2,320,128]{2,1,0:T(8,128)(2,1)S(1)}, u32[]{:S(2)}, u32[]{:S(2)}) collective-permute-start(bf16[2,320,128]{2,1,0:T(8,128)(2,1)S(1)} %pad_maximum_fusion.3), channel_id=1, source_target_pairs={{0,4},{1,5},{2,6},{3,7},{4,0},{5,1},{6,2},{7,3},{8,12},{9,13},{10,... | collective-permute-start | bytes 491528 | tf_op jit(solution)/shard_map/ppermute | solution.py:301
  13.6 8.2 %collective-permute-start.4 = (bf16[2,320,128]{2,1,0:T(8,128)(2,1)S(1)}, bf16[2,320,128]{2,1,0:T(8,128)(2,1)S(1)}, u32[]{:S(2)}, u32[]{:S(2)}) collective-permute-start(bf16[2,320,128]{2,1,0:T(8,128)(2,1)S(1)} %pad_maximum_fusion.3), channel_id=1, source_target_pairs={{0,8},{1,9},{2,10},{3,11},{4,12},{5,13},{6,14},{7,15},{8,0},{9,1},... | collective-permute-start | bytes 491528 | tf_op jit(solution)/shard_map/ppermute | solution.py:301
  16.0 12.7 %collective-permute-start.8 = (bf16[2,64,5120]{2,1,0:T(8,128)(2,1)S(1)}, bf16[2,64,5120]{2,1,0:T(8,128)(2,1)S(1)}, u32[]{:S(2)}, u32[]{:S(2)}) collective-permute-start(bf16[2,64,5120]{2,1,0:T(8,128)(2,1)S(1)} %pad_maximum_fusion.1), channel_id=1, source_target_pairs={{0,1},{1,0},{2,3},{3,2},{4,5},{5,4},{6,7},{7,6},{8,9},{9,8},{10,11... | collective-permute-start | bytes 3932168 | tf_op jit(solution)/shard_map/ppermute | solution.py:301
  21.8 8.4 %collective-permute-start.7 = (bf16[2,320,128]{2,1,0:T(8,128)(2,1)S(1)}, bf16[2,320,128]{2,1,0:T(8,128)(2,1)S(1)}, u32[]{:S(2)}, u32[]{:S(2)}) collective-permute-start(bf16[2,320,128]{2,1,0:T(8,128)(2,1)S(1)} %collective-permute-done.4), channel_id=1, source_target_pairs={{0,4},{1,5},{2,6},{3,7},{4,0},{5,1},{6,2},{7,3},{8,12},{9,13},{10,... | collective-permute-start | bytes 491528 | tf_op jit(solution)/shard_map/ppermute | solution.py:301
  21.9 9.6 %collective-permute-start.10 = (bf16[4,320,128]{2,1,0:T(8,128)(2,1)S(1)}, bf16[4,320,128]{2,1,0:T(8,128)(2,1)S(1)}, u32[]{:S(2)}, u32[]{:S(2)}) collective-permute-start(bf16[4,320,128]{2,1,0:T(8,128)(2,1)S(1)} %pad_maximum_fusion.2), channel_id=1, source_target_pairs={{0,16},{16,0},{1,17},{17,1},{2,18},{18,2},{3,19},{19,3},{4,20},{20... | collective-permute-start | bytes 983048 | tf_op jit(solution)/shard_map/ppermute | solution.py:304
  24.5 1.7 %copy-start = (bf16[256,5120]{1,0:T(8,128)(2,1)S(1)}, bf16[256,5120]{1,0:T(8,128)(2,1)}, u32[]{:S(2)}) copy-start(bf16[256,5120]{1,0:T(8,128)(2,1)} %k.3) | copy-start | bytes 7864324
  24.5 1.7 %copy-start.5 = (s32[256]{0:T(256)S(1)}, s32[256]{0:T(256)}, u32[]{:S(2)}) copy-start(s32[256]{0:T(256)} %lo_ref.3) | copy-start | bytes 3076
  24.5 1.7 %copy-start.6 = (s32[256]{0:T(256)S(1)}, s32[256]{0:T(256)}, u32[]{:S(2)}) copy-start(s32[256]{0:T(256)} %hi_ref.5) | copy-start | bytes 3076
  24.6 15.8 %collective-permute-start.2 = (bf16[2,64,5120]{2,1,0:T(8,128)(2,1)S(1)}, bf16[2,64,5120]{2,1,0:T(8,128)(2,1)S(1)}, u32[]{:S(2)}, u32[]{:S(2)}) collective-permute-start(bf16[2,64,5120]{2,1,0:T(8,128)(2,1)S(1)} %pad_maximum_fusion), channel_id=1, source_target_pairs={{3,4},{4,3},{7,8},{8,7},{11,12},{12,11},{19,20},{20,19},{23,24},{2... | collective-permute-start | bytes 3932168 | tf_op jit(solution)/shard_map/ppermute | solution.py:336
  28.6 8.1 %copy-start.3 = (bf16[320,5120]{1,0:T(8,128)(2,1)S(1)}, bf16[320,5120]{1,0:T(8,128)(2,1)}, u32[]{:S(2)}) copy-start(bf16[320,5120]{1,0:T(8,128)(2,1)} %frozen.1) | copy-start | bytes 9830404
  30.3 6.5 %copy-start.4 = (bf16[320,128]{1,0:T(8,128)(2,1)S(1)}, bf16[320,128]{1,0:T(8,128)(2,1)}, u32[]{:S(2)}) copy-start(bf16[320,128]{1,0:T(8,128)(2,1)} %own_down.1) | copy-start | bytes 245764
  30.3 4.2 %collective-permute-start.11 = (bf16[2,320,128]{2,1,0:T(8,128)(2,1)S(1)}, bf16[2,320,128]{2,1,0:T(8,128)(2,1)S(1)}, u32[]{:S(2)}, u32[]{:S(2)}) collective-permute-start(bf16[2,320,128]{2,1,0:T(8,128)(2,1)S(1)} %collective-permute-done.7), channel_id=1, source_target_pairs={{0,16},{16,0},{1,17},{17,1},{2,18},{18,2},{3,19},{19,3},{4,20},{20... | collective-permute-start | bytes 491528 | tf_op jit(solution)/shard_map/ppermute | solution.py:304
  31.6 3.0 %collective-permute-start.9 = (bf16[8,320,128]{2,1,0:T(8,128)(2,1)S(1)}, bf16[8,320,128]{2,1,0:T(8,128)(2,1)S(1)}, u32[]{:S(2)}, u32[]{:S(2)}) collective-permute-start(bf16[8,320,128]{2,1,0:T(8,128)(2,1)S(1)} %constant_dynamic-update-slice_fusion.rest_0_), channel_id=1, source_target_pairs={{0,1},{1,0},{2,3},{3,2},{4,5},{5,4},{6,7},{7,6},{8,9},{9,8},{10,11... | collective-permute-start | bytes 1966088 | tf_op jit(solution)/shard_map/ppermute | solution.py:301
  34.5 2.2 %collective-permute-start.12 = (bf16[8,320,128]{2,1,0:T(8,128)(2,1)S(1)}, bf16[8,320,128]{2,1,0:T(8,128)(2,1)S(1)}, u32[]{:S(2)}, u32[]{:S(2)}) collective-permute-start(bf16[8,320,128]{2,1,0:T(8,128)(2,1)S(1)} %constant_dynamic-update-slice_fusion.4.rest_2_), channel_id=1, source_target_pairs={{0,1},{1,0},{2,3},{3,2},{4,5},{5,4},{6,7},{7,6},{8,9},{9,8},{10,11... | collective-permute-start | bytes 1966088 | tf_op jit(solution)/shard_map/ppermute | solution.py:301
